TPU v7x, 32 devices: a whole 2x2x4 slice. The times are simulated.
32 devices in a mesh: dp: 2 (over x), lat: 4 (over z), lon: 4 (over y, core).
Axes of the slice: x: 2, y: 2, z: 4, core: 2. Of those that a mesh axis runs over, the one named last changes fastest.
Arguments:
- hidden_in: bfloat16 [2, 120, 240, 384], P('dp', 'lat', 'lon'), may hold values from -6 to 6
- grad_out: bfloat16 [2, 120, 240, 384], P('dp', 'lat', 'lon'), may hold values from -6 to 6
- norm_gain: float32 [384], replicated, may hold values from 0.5 to 1.5
- w_qkv: bfloat16 [384, 1152], replicated, may hold values from -0.3125 to 0.3125
- w_proj: bfloat16 [384, 384], replicated, may hold values from -0.3125 to 0.3125
Outputs:
- grad_in: bfloat16 [2, 120, 240, 384], P('dp', 'lat', 'lon')
- grad_qkv: float32 [384, 1152], P('dp', ('lat', 'lon'))
- grad_proj: float32 [384, 384], P('dp', ('lat', 'lon'))
All inputs are finite; a program needn't handle non-finite values.
Results may differ from a plain program's by a relative error of at most 0.0083.
Values may be sent and summed in bfloat16 or wider, within the bound.
No kernel may reach another device: no remote copies, remote signals or barrier semaphores. Data moves between devices by JAX's collectives and lax.ppermute only.
A program may use at most 64 MiB of HBM per device.

v0:
```python
import jax
import jax.numpy as jnp
from jax import lax
from jax.sharding import PartitionSpec as P

HEADS = 6
WIN = 30
SHIFT = 15


EPSILON = 1e-05


def shifted_2(value, axis, steps):
    count = lax.axis_size(axis)
    pairs = [(source, (source + steps) % count) for source in range(count)]
    return lax.ppermute(value, axis, pairs)


def passed_along(x, axis, by):
    peers = lax.axis_size(axis)
    pairs = [(i, i + by) for i in range(peers) if 0 <= i + by < peers]
    return lax.ppermute(x, axis, pairs)


def attend_head(query_rows, key_rows, value_rows, grad_rows, key_valid, scaling):
    scores = jnp.dot(query_rows, key_rows.T, preferred_element_type=jnp.float32) * scaling
    weights_raw = jnp.exp(scores) * key_valid[None, :]
    attention = weights_raw / jnp.sum(weights_raw, axis=-1, keepdims=True)
    attention_low = attention.astype(jnp.bfloat16)
    outputs = jnp.dot(attention_low, value_rows, preferred_element_type=jnp.float32).astype(
        jnp.bfloat16
    )
    dprobs = jnp.dot(grad_rows, value_rows.T, preferred_element_type=jnp.float32)
    row_total = jnp.sum(attention * dprobs, axis=-1, keepdims=True)
    dscores = (attention * (dprobs - row_total) * scaling).astype(jnp.bfloat16)
    dquery = jnp.dot(dscores, key_rows, preferred_element_type=jnp.float32).astype(jnp.bfloat16)
    dkey_rows = jnp.dot(dscores.T, query_rows, preferred_element_type=jnp.float32).astype(
        jnp.bfloat16
    )
    dvalue = jnp.dot(attention_low.T, grad_rows, preferred_element_type=jnp.float32).astype(
        jnp.bfloat16
    )
    return (outputs, dquery, dkey_rows, dvalue)


def window_grads(window_cells, cotangent, key_valid, norm_gain, w_qkv, w_proj):
    model_width = window_cells.shape[1]
    head_size = model_width // HEADS
    scaling = head_size ** (-0.5)
    values_f = window_cells.astype(jnp.float32)
    average = jnp.mean(values_f, axis=1, keepdims=True)
    centred = values_f - average
    inverse_std = lax.rsqrt(jnp.mean(centred * centred, axis=1, keepdims=True) + EPSILON)
    normed = centred * inverse_std
    normal_low = (normed * norm_gain).astype(jnp.bfloat16)
    qkv = jnp.dot(normal_low, w_qkv, preferred_element_type=jnp.float32).astype(jnp.bfloat16)
    back_rows = jnp.dot(cotangent, w_proj.T, preferred_element_type=jnp.float32).astype(
        jnp.bfloat16
    )

    def split_heads(matrix):
        return matrix.reshape(matrix.shape[0], HEADS, head_size).transpose(1, 0, 2)

    def merge_heads(stacked):
        return stacked.transpose(1, 0, 2).reshape(stacked.shape[1], model_width)

    def one_head(inputs):
        return attend_head(inputs[0], inputs[1], inputs[2], inputs[3], key_valid, scaling)

    heads_in = (
        split_heads(qkv[:, :model_width]),
        split_heads(qkv[:, model_width : 2 * model_width]),
        split_heads(qkv[:, 2 * model_width :]),
        split_heads(back_rows),
    )
    outputs, dquery, dkey_rows, dvalue = lax.map(one_head, heads_in)
    attended = merge_heads(outputs)
    dqkv = jnp.concatenate(
        [merge_heads(dquery), merge_heads(dkey_rows), merge_heads(dvalue)], axis=1
    )
    proj_part = jnp.dot(attended.T, cotangent, preferred_element_type=jnp.float32)
    qkv_part = jnp.dot(normal_low.T, dqkv, preferred_element_type=jnp.float32)
    dnormed = jnp.dot(dqkv, w_qkv.T, preferred_element_type=jnp.float32) * norm_gain
    dcells = inverse_std * (
        dnormed
        - jnp.mean(dnormed, axis=1, keepdims=True)
        - normed * jnp.mean(dnormed * normed, axis=1, keepdims=True)
    )
    return (dcells.astype(jnp.bfloat16), qkv_part, proj_part)


def to_windows(grid_field):
    shape = grid_field.shape
    split = grid_field.reshape(shape[0], shape[1] // WIN, WIN, shape[2] // WIN, WIN, shape[3])
    return split.transpose(0, 1, 3, 2, 4, 5).reshape(-1, WIN * WIN, shape[3])


def from_windows(windows, samples, lat_rows, lon_cols):
    split = windows.reshape(samples, lat_rows // WIN, lon_cols // WIN, WIN, WIN, windows.shape[-1])
    return split.transpose(0, 1, 3, 2, 4, 5).reshape(samples, lat_rows, lon_cols, windows.shape[-1])


def ahead_lon(stacked):
    outgoing = stacked[:, :, :SHIFT]
    incoming = shifted_2(outgoing, "lon", -1)
    return jnp.concatenate([stacked[:, :, SHIFT:], incoming], axis=2)


def ahead_lat(stacked):
    outgoing = stacked[:, :SHIFT]
    incoming = passed_along(outgoing, "lat", -1)
    return jnp.concatenate([stacked[:, SHIFT:], incoming], axis=1)


def behind_lon(stacked):
    outgoing = stacked[:, :, -SHIFT:]
    incoming = shifted_2(outgoing, "lon", 1)
    return jnp.concatenate([incoming, stacked[:, :, :-SHIFT]], axis=2)


def behind_lat(stacked):
    outgoing = stacked[:, -SHIFT:]
    incoming = passed_along(outgoing, "lat", 1)
    return jnp.concatenate([incoming, stacked[:, :-SHIFT]], axis=1)


def per_device(hidden_in, grad_out, norm_gain, w_qkv, w_proj):
    samples, lat_rows, lon_cols, model_width = hidden_in.shape
    stacked = jnp.concatenate([hidden_in, grad_out], axis=0)
    stacked = ahead_lon(ahead_lat(stacked))
    shifted = stacked[:samples]
    cotangent = stacked[samples:]
    grid_rows = lat_rows * lax.axis_size("lat")
    row_index = lax.axis_index("lat") * lat_rows + jnp.arange(lat_rows, dtype=jnp.int32)
    valid_rows = (row_index < grid_rows - SHIFT).astype(jnp.float32)
    valid_field = jnp.broadcast_to(
        valid_rows[None, :, None, None], (samples, lat_rows, lon_cols, 1)
    )
    valid_windows = to_windows(valid_field)[..., 0]

    def step_window(totals, inputs):
        dcells, qkv_part, proj_part = window_grads(
            inputs[0], inputs[1], inputs[2], norm_gain, w_qkv, w_proj
        )
        return ((totals[0] + qkv_part, totals[1] + proj_part), dcells)

    starting = (
        jnp.zeros((model_width, 3 * model_width), jnp.float32),
        jnp.zeros((model_width, model_width), jnp.float32),
    )
    sums, dwindows = lax.scan(
        step_window, starting, (to_windows(shifted), to_windows(cotangent), valid_windows)
    )
    dshift = from_windows(dwindows, samples, lat_rows, lon_cols)
    returned = behind_lon(behind_lat(dshift))
    grad_in = (grad_out.astype(jnp.float32) + returned.astype(jnp.float32)).astype(jnp.bfloat16)
    total_cells = lax.axis_size("dp") * samples * grid_rows * lon_cols * lax.axis_size("lon")
    factor = float(total_cells) ** (-0.5)
    partial_qkv, partial_proj = (
        lax.psum_scatter(sums[0], ("lat", "lon"), scatter_dimension=1, tiled=True),
        lax.psum_scatter(sums[1], ("lat", "lon"), scatter_dimension=1, tiled=True),
    )
    qkv_sum, proj_sum = (
        lax.psum_scatter(partial_qkv, "dp", scatter_dimension=0, tiled=True),
        lax.psum_scatter(partial_proj, "dp", scatter_dimension=0, tiled=True),
    )
    return (grad_in, qkv_sum * factor, proj_sum * factor)


def solution(mesh):
    in_specs = (P("dp", "lat", "lon", None), P("dp", "lat", "lon", None), P(), P(), P())
    out_specs = (P("dp", "lat", "lon", None), P("dp", ("lat", "lon")), P("dp", ("lat", "lon")))
    return jax.shard_map(
        per_device, mesh=mesh, in_specs=in_specs, out_specs=out_specs, check_vma=False
    )
```

profile of v0, /device:TPU:0, one launch (start us, length us, event | category | flops | bytes accessed | tf_op | source)
XLA Modules:
  0.0 412.3 jit_solution(3698998892785344540)
XLA Ops:
  14.0 33.9 %collective-permute-done = bf16[2,15,60,384]{3,0,2,1:T(2,128)(2,1)S(1)} collective-permute-done((bf16[2,15,60,384]{3,0,2,1:T(2,128)(2,1)S(1)}, bf16[2,15,60,384]{3,0,2,1:T(2,128)(2,1)S(1)}, u32[]{:S(2)}, u32[]{:S(2)}) %collective-permute-start) | collective-permute-done | bytes 1382432 | tf_op jit(solution)/shard_map/ppermute | solution.py:23
  52.2 6.6 %collective-permute-done.1 = bf16[2,30,15,384]{3,0,2,1:T(2,128)(2,1)} collective-permute-done((bf16[2,30,15,384]{3,0,2,1:T(2,128)(2,1)}, bf16[2,30,15,384]{3,0,2,1:T(2,128)(2,1)}, u32[]{:S(2)}, u32[]{:S(2)}) %collective-permute-start.1) | collective-permute-done | bytes 691232 | tf_op jit(solution)/shard_map/ppermute | solution.py:17
  65.4 193.0 %while.33 = (s32[]{:T(128)}, f32[384,1152]{1,0:T(8,128)}, f32[384,384]{1,0:T(8,128)S(1)}, bf16[2,900,384]{2,1,0:T(8,128)(2,1)}, bf16[2,900,384]{2,1,0:T(8,128)(2...) while((s32[]{:T(128)}, f32[384,1152]{1,0:T(8,128)}, ...), condition=%wide.region_9.10_spmd.clone, body=%wide.region_0.9_spmd.clone.sunk | while | flops 3586285568 | bytes 79451888 | solution.py:152
  66.0 2.6 convolution_convert_fusion.8
  73.9 2.7 convolution_convert_fusion.9
  79.6 69.4 %while.34 = (s32[]{:T(128)}, bf16[6,900,64]{1,2,0:T(8,128)(2,1)}, bf16[6,900,64]{1,2,0:T(8,128)(2,1)}, bf16[6,900,64]{1,2,0:T(8,128)(2,1)}, bf16[6,900,64]{1,2,0...) while((s32[]{:T(128)}, bf16[6,900,64]{1,2,0:T(8,128)(2,1)}, ...), condition=%wide.region_6.6_spmd, body=%wide.region_3.5_spmd.sunk | while | flops 640938624 | bytes 29625596 | solution.py:77
  86.2 2.6 fusion.124
  97.7 2.6 fusion.124
  144.0 2.6 fusion.124
  149.0 4.2 %fusion.110 = (f32[900]{0:T(1024)S(1)}, f32[900]{0:T(1024)S(1)}, f32[900,384]{1,0:T(8,128)S(1)}) fusion(f32[900]{0:T(1024)} %copy-done.9, f32[900]{0:T(1024)} %copy-done.7, bf16[2,900,384]{2,1,0:T(8,128)(2,1)S(1)} %get-tuple-element.494, s32[]{:T(128)} %get-tuple-element.477, f32[384]{0:T(512)} %get-tuple-element.537, ...), kind=kOutput, calls=%fused_computation.95.clone.1 | convolution fusion | flops 804900608 | bytes 5047876 | tf_op jit(solution)/shard_map/while/body/eval_jaxpr/dot_general | solution.py:84
  155.1 4.6 %convolution_add_fusion.4 = f32[384,1152]{1,0:T(8,128)} fusion(f32[384,1152]{1,0:T(8,128)} %get-tuple-element.478, bf16[900,384]{0,1:T(8,128)(2,1)} %bitcast.189, bf16[900,384]{0,1:T(8,128)(2,1)} %bitcast.221, bf16[900,384]{0,1:T(8,128)(2,1)} %bitcast.219, pred[]{:T(512)S(6)} %compare.3, f32[384]{0:T(512)S(1)} %copy-done.12, ...), kind=kOutput, calls=%fused_computation.44.clone.1 | convolution fusion | flops 805095936 | bytes 6317061 | tf_op jit(solution)/shard_map/while/body/eval_jaxpr/dot_general | solution.py:83
  162.1 2.6 convolution_convert_fusion.8
  170.0 2.7 convolution_convert_fusion.9
  175.7 69.4 %while.34 = (s32[]{:T(128)}, bf16[6,900,64]{1,2,0:T(8,128)(2,1)}, bf16[6,900,64]{1,2,0:T(8,128)(2,1)}, bf16[6,900,64]{1,2,0:T(8,128)(2,1)}, bf16[6,900,64]{1,2,0...) while((s32[]{:T(128)}, bf16[6,900,64]{1,2,0:T(8,128)(2,1)}, ...), condition=%wide.region_6.6_spmd, body=%wide.region_3.5_spmd.sunk | while | flops 640938624 | bytes 29625596 | solution.py:77
  182.3 2.6 fusion.124
  193.8 2.6 fusion.124
  240.1 2.6 fusion.124
  245.1 4.2 %fusion.110 = (f32[900]{0:T(1024)S(1)}, f32[900]{0:T(1024)S(1)}, f32[900,384]{1,0:T(8,128)S(1)}) fusion(f32[900]{0:T(1024)} %copy-done.9, f32[900]{0:T(1024)} %copy-done.7, bf16[2,900,384]{2,1,0:T(8,128)(2,1)S(1)} %get-tuple-element.494, s32[]{:T(128)} %get-tuple-element.477, f32[384]{0:T(512)} %get-tuple-element.537, ...), kind=kOutput, calls=%fused_computation.95.clone.1 | convolution fusion | flops 804900608 | bytes 5047876 | tf_op jit(solution)/shard_map/while/body/eval_jaxpr/dot_general | solution.py:84
  251.2 5.2 %convolution_add_fusion.4 = f32[384,1152]{1,0:T(8,128)} fusion(f32[384,1152]{1,0:T(8,128)} %get-tuple-element.478, bf16[900,384]{0,1:T(8,128)(2,1)} %bitcast.189, bf16[900,384]{0,1:T(8,128)(2,1)} %bitcast.221, bf16[900,384]{0,1:T(8,128)(2,1)} %bitcast.219, pred[]{:T(512)S(6)} %compare.3, f32[384]{0:T(512)S(1)} %copy-done.12, ...), kind=kOutput, calls=%fused_computation.44.clone.1 | convolution fusion | flops 805095936 | bytes 6317061 | tf_op jit(solution)/shard_map/while/body/eval_jaxpr/dot_general | solution.py:83
  259.5 55.6 %reduce-scatter.19.cloned.1.call-done = f32[384,24]{0,1:T(8,128)} async-done(((f32[384,384]{0,1:T(8,128)}), f32[384,24]{0,1:T(8,128)}) %reduce-scatter.19.cloned.1.call-update) | async-done | bytes 36880
  321.6 3.4 collective-permute-start.2
  325.0 13.7 %collective-permute-done.2 = bf16[1,15,60,384]{3,1,2,0:T(8,128)(2,1)S(1)} collective-permute-done((bf16[1,15,60,384]{3,1,2,0:T(8,128)(2,1)S(1)}, bf16[1,15,60,384]{3,1,2,0:T(8,128)(2,1)S(1)}, u32[]{:S(2)}, u32[]{:S(2)}) %collective-permute-start.2) | collective-permute-done | bytes 691232 | tf_op jit(solution)/shard_map/ppermute | solution.py:23
  340.5 51.6 %reduce-scatter.17.cloned.1.call-done = f32[384,72]{0,1:T(8,128)} async-done(((f32[384,1152]{0,1:T(8,128)}), f32[384,72]{0,1:T(8,128)}) %reduce-scatter.17.cloned.1.call-update) | async-done | bytes 110608
  397.5 6.7 %reduce-scatter.13.cloned.1.call-done = f32[192,72]{1,0:T(8,128)} async-done(((f32[384,72]{1,0:T(8,128)}), f32[192,72]{1,0:T(8,128)}) %reduce-scatter.13.cloned.1.call-update) | async-done | bytes 55312
  (202 shorter events, 181.7 us)
Async XLA Ops:
  7.2 2.4 copy-start.1
  7.2 308.0 %reduce-scatter.19.cloned.1.call-start = ((), (), s32[]{:S(2)}) async-start(), calls=%async_computation.7 | async-start | bytes 626688
  12.7 35.2 %collective-permute-start = (bf16[2,15,60,384]{3,0,2,1:T(2,128)(2,1)S(1)}, bf16[2,15,60,384]{3,0,2,1:T(2,128)(2,1)S(1)}, u32[]{:S(2)}, u32[]{:S(2)}) collective-permute-start(bf16[2,15,60,384]{3,0,2,1:T(2,128)(2,1)S(1)} %copy.48), channel_id=1, source_target_pairs={{4,0},{8,4},{12,8},{5,1},{9,5},{13,9},{6,2},{10,6},{14,10},{7,3},{... | collective-permute-start | bytes 4147208 | tf_op jit(solution)/shard_map/ppermute | solution.py:23
  49.8 9.0 %collective-permute-start.1 = (bf16[2,30,15,384]{3,0,2,1:T(2,128)(2,1)}, bf16[2,30,15,384]{3,0,2,1:T(2,128)(2,1)}, u32[]{:S(2)}, u32[]{:S(2)}) collective-permute-start(bf16[2,30,15,384]{3,0,2,1:T(2,128)(2,1)} %copy.50), channel_id=1, source_target_pairs={{0,3},{1,0},{2,1},{3,2},{4,7},{5,4},{6,5},{7,6},{8,11},{9,8},{10,9... | collective-permute-start | bytes 2073608 | tf_op jit(solution)/shard_map/ppermute | solution.py:17
  65.6 3.0 copy-start.7
  66.0 2.6 copy-start.9
  149.0 4.2 %copy-start.4 = (bf16[2,900,384]{2,1,0:T(8,128)(2,1)S(1)}, bf16[2,900,384]{2,1,0:T(8,128)(2,1)}, u32[]{:S(2)}) copy-start(bf16[2,900,384]{2,1,0:T(8,128)(2,1)} %get-tuple-element.480) | copy-start | bytes 4147204 | tf_op jit(solution)/shard_map/while
  149.0 4.2 %copy-start.8 = (f32[900]{0:T(1024)S(1)}, f32[900]{0:T(1024)}, u32[]{:S(2)}) copy-start(f32[900]{0:T(1024)} %copy-done.7) | copy-start | bytes 10804 | tf_op jit(solution)/shard_map/while
  149.0 4.2 %copy-start.10 = (f32[900]{0:T(1024)S(1)}, f32[900]{0:T(1024)}, u32[]{:S(2)}) copy-start(f32[900]{0:T(1024)} %copy-done.9) | copy-start | bytes 10804 | tf_op jit(solution)/shard_map/while
  153.2 1.9 copy-start.12
  155.1 4.6 %copy-start = (bf16[2,900,384]{2,1,0:T(8,128)(2,1)S(1)}, bf16[2,900,384]{2,1,0:T(8,128)(2,1)}, u32[]{:S(2)}) copy-start(bf16[2,900,384]{2,1,0:T(8,128)(2,1)} %get-tuple-element.497) | copy-start | bytes 4147204 | tf_op jit(solution)/shard_map/while
  161.7 3.0 copy-start.7
  162.1 2.7 copy-start.9
  245.1 4.2 %copy-start.4 = (bf16[2,900,384]{2,1,0:T(8,128)(2,1)S(1)}, bf16[2,900,384]{2,1,0:T(8,128)(2,1)}, u32[]{:S(2)}) copy-start(bf16[2,900,384]{2,1,0:T(8,128)(2,1)} %get-tuple-element.480) | copy-start | bytes 4147204 | tf_op jit(solution)/shard_map/while
  245.1 4.2 %copy-start.8 = (f32[900]{0:T(1024)S(1)}, f32[900]{0:T(1024)}, u32[]{:S(2)}) copy-start(f32[900]{0:T(1024)} %copy-done.7) | copy-start | bytes 10804 | tf_op jit(solution)/shard_map/while
  245.1 4.2 %copy-start.10 = (f32[900]{0:T(1024)S(1)}, f32[900]{0:T(1024)}, u32[]{:S(2)}) copy-start(f32[900]{0:T(1024)} %copy-done.9) | copy-start | bytes 10804 | tf_op jit(solution)/shard_map/while
  251.2 5.2 %copy-start = (bf16[2,900,384]{2,1,0:T(8,128)(2,1)S(1)}, bf16[2,900,384]{2,1,0:T(8,128)(2,1)}, u32[]{:S(2)}) copy-start(bf16[2,900,384]{2,1,0:T(8,128)(2,1)} %get-tuple-element.497) | copy-start | bytes 4147204 | tf_op jit(solution)/shard_map/while
  258.4 58.4 %copy-start.3 = (f32[384,1152]{1,0:T(8,128)S(1)}, f32[384,1152]{1,0:T(8,128)}, u32[]{:S(2)}) copy-start(f32[384,1152]{1,0:T(8,128)} %get-tuple-element.525) | copy-start | bytes 5308420
  259.5 79.4 %reduce-scatter.15.cloned.1.call-start = ((), (), s32[]{:S(2)}) async-start(), calls=%async_computation.5 | async-start | bytes 294912
  316.7 75.4 %reduce-scatter.17.cloned.1.call-start = ((), (), s32[]{:S(2)}) async-start(), calls=%async_computation.6 | async-start | bytes 1880064
  318.6 85.6 %reduce-scatter.13.cloned.1.call-start = ((), (), s32[]{:S(2)}) async-start(), calls=%async_computation.4 | async-start | bytes 294912
  321.6 72.3 %copy-start.2 = (bf16[1,30,60,384]{3,2,1,0:T(8,128)(2,1)S(1)}, bf16[1,30,60,384]{3,2,1,0:T(8,128)(2,1)}, u32[]{:S(2)}) copy-start(bf16[1,30,60,384]{3,2,1,0:T(8,128)(2,1)} %param.10) | copy-start | bytes 4147204
  321.6 17.1 %collective-permute-start.2 = (bf16[1,15,60,384]{3,1,2,0:T(8,128)(2,1)S(1)}, bf16[1,15,60,384]{3,1,2,0:T(8,128)(2,1)S(1)}, u32[]{:S(2)}, u32[]{:S(2)}) collective-permute-start(bf16[1,15,60,384]{3,1,2,0:T(8,128)(2,1)S(1)} %get-tuple-element.254), channel_id=1, source_target_pairs={{0,4},{4,8},{8,12},{1,5},{5,9},{9,13},{2,6},{6,10},{10,14},{3,7},{... | collective-permute-start | bytes 2073608 | tf_op jit(solution)/shard_map/ppermute | solution.py:23
  338.8 55.0 %collective-permute-start.3 = (bf16[1,30,15,384]{3,1,2,0:T(8,128)(2,1)S(1)}, bf16[1,30,15,384]{3,1,2,0:T(8,128)(2,1)}, u32[]{:S(2)}, u32[]{:S(2)}) collective-permute-start(bf16[1,30,15,384]{3,1,2,0:T(8,128)(2,1)S(1)} %pad_maximum_fusion.6), channel_id=1, source_target_pairs={{0,1},{1,2},{2,3},{3,0},{4,5},{5,6},{6,7},{7,4},{8,9},{9,10},{10,1... | collective-permute-start | bytes 1036808 | tf_op jit(solution)/shard_map/ppermute | solution.py:17
  (5 other events, 7.3 us)
Sparse Core Ops, SparseCore 0:
  259.6 55.5 reduce-scatter.18
  317.4 9.9 reduce-scatter.14
  331.7 60.3 reduce-scatter.16
  394.3 9.8 reduce-scatter.12
where the time goes:
time: 414 us; the launch traced here: 412 us
  waiting for transfers between devices  168 us (41%)
  matrix products  158 us (38%)
  local copies, waits for them, and re-layouts  45.8 us (11%)
  other arithmetic  20.4 us (5%)
  between operations  14 us (3%)
  starting transfers between devices  5.15 us (1%)
    unnamed x8, waiting for transfers between devices  114 us
    ppermute x2, waiting for transfers between devices, passed_along(): return lax.ppermute(x, axis, pairs)  47.7 us
    dot_general x12, matrix products, attend_head(): jnp.dot(attention_low.T, grad_rows, preferred_element_type=jnp.float32)  31 us
    dot_general x12, matrix products, attend_head(): jnp.dot(attention_low, value_rows, preferred_element_type=jnp.float32)  29 us
    dot_general x12, matrix products, attend_head(): jnp.dot(grad_rows, value_rows.T, preferred_element_type=jnp.float32)  24.9 us
    dot_general x12, matrix products, attend_head(): jnp.dot(dscores.T, query_rows, preferred_element_type=jnp.float32)  16.8 us
    dot_general x12, matrix products, attend_head(): jnp.dot(dscores, key_rows, preferred_element_type=jnp.float32)  13.4 us
    convert_element_type x12, other arithmetic, attend_head(): dscores = (attention * (dprobs - row_total) * scaling).astype(jnp.bfloat16)  13.1 us
  transfers between devices with their start and end apart: 8, of which 6 were waited for; matrix products, arithmetic and copies ran while one was open for 3% of the time, Pallas kernels for 0%

commit v1 on v0

v1 whole, which is shorter than its diff:
```python
import functools, math
import jax, jax.numpy as jnp
from jax import lax
from jax.experimental import pallas as pl
from jax.experimental.pallas import tpu as pltpu

from jax.sharding import PartitionSpec as P

HEADS = 6
WIN = 30
SHIFT = 15
EPSILON = 1e-05
BF = jnp.bfloat16
F32 = jnp.float32
LN2 = math.log(2.0)

def mm(a, b):
    return lax.dot_general(a, b, (((1,), (0,)), ((), ())), preferred_element_type=F32)

def mm_t(a, b):
    return lax.dot_general(a, b, (((1,), (1,)), ((), ())), preferred_element_type=F32)

def blocks_of(n, step):
    return [(at, min(step, n - at)) for at in range(0, n, step)]

def window_kernel(head, x_ref, c_ref, valid_ref, gain_ref, wqkv_ref, wproj_ref,
                  d_ref, gq_ref, gp_ref,
                  nl, q_s, k_s, v_s, b_s, kT, vT, bT, e_s, p_s, ds_s, dqkv, attT):
    cells, width = x_ref.shape
    pair = 2 * head
    pairs = width // pair
    qscale = head ** -0.5 / LN2
    x = x_ref[...].astype(F32)
    mean = jnp.mean(x, axis=1, keepdims=True)
    cen = x - mean
    rstd = lax.rsqrt(jnp.mean(cen * cen, axis=1, keepdims=True) + EPSILON)
    gain = gain_ref[...]
    nl[...] = (cen * rstd * gain).astype(BF)
    qb = blocks_of(cells, 256)

    def one_pair(j, _):
        cols = pl.ds(pl.multiple_of(j * pair, pair), pair)
        colk = pl.ds(pl.multiple_of(width + j * pair, pair), pair)
        colv = pl.ds(pl.multiple_of(2 * width + j * pair, pair), pair)
        q_s[...] = (mm(nl[...], wqkv_ref[:, cols]) * qscale).astype(BF)
        k_s[...] = mm(nl[...], wqkv_ref[:, colk]).astype(BF)
        v_s[...] = mm(nl[...], wqkv_ref[:, colv]).astype(BF)
        b_s[...] = mm_t(c_ref[...], wproj_ref[cols, :]).astype(BF)
        kT[...] = k_s[...].T
        vT[...] = v_s[...].T
        bT[...] = b_s[...].T
        lane = lax.broadcasted_iota(jnp.int32, (cells, pair), 1)
        row = lax.broadcasted_iota(jnp.int32, (pair, cells), 0)
        valid_col = valid_ref[0]
        outs = []
        for h in range(2):
            own = (lane >= head) if h else (lane < head)
            own_r = (row >= head) if h else (row < head)
            aug = 0 if h else head
            bias = jnp.where(lane == aug, (valid_col - 1.0) * 30000.0, 0.0).astype(BF)
            kk = jnp.where(own, k_s[...], bias)
            qq = jnp.where(own, q_s[...], jnp.where(lane == aug, 1.0, 0.0).astype(BF))
            two = (lane == aug) | (lane == aug + 1)
            vv = jnp.where(own, v_s[...], jnp.where(two, 1.0, 0.0).astype(BF))
            vvT = jnp.where(own_r, vT[...], jnp.where(row == aug, 1.0, 0.0).astype(BF))
            for at, n in qb:
                s = mm_t(kk, qq[at:at + n])
                e = jnp.exp2(s).astype(BF)
                oT = mm(vvT, e)
                total = oT[aug:aug + 1]
                inv = 1.0 / total
                aT = oT * inv
                attT[pl.ds(pl.multiple_of(j * pair + h * head, head), head), at:at + n] = aT[h * head:(h + 1) * head].astype(BF)
                bTn = bT[:, at:at + n].astype(F32)
                ownn = own_r[:, :n]
                rown = row[:, :n]
                rt = jnp.sum(jnp.where(ownn, bTn * aT, 0.0), axis=0, keepdims=True)
                hi = rt.astype(BF).astype(F32)
                lo = rt - hi
                baug = jnp.where(ownn, bTn, jnp.where(rown == aug, -hi, jnp.where(rown == aug + 1, -lo, 0.0))).astype(BF)
                p = e * inv.astype(BF)
                p_s[h, :, at:at + n] = p
                dp = mm(vv, baug).astype(BF)
                ds_s[h, :, at:at + n] = p * dp
            dv = mm(p_s[h], b_s[...])
            dk = mm(ds_s[h], q_s[...]) * LN2
            dqT = mm(kT[...], ds_s[h]) * (head ** -0.5)
            outs.append((dqT, dk, dv))
        dqT = jnp.where(row < head, outs[0][0], outs[1][0]).astype(BF)
        dqkv[:, cols] = dqT.T
        dqkv[:, colk] = jnp.where(lane < head, outs[0][1], outs[1][1]).astype(BF)
        dqkv[:, colv] = jnp.where(lane < head, outs[0][2], outs[1][2]).astype(BF)
        return 0

    lax.fori_loop(0, pairs, one_pair, 0)
    gp_ref[...] = mm(attT[...], c_ref[...])
    gq_ref[...] = mm(nl[...].T, dqkv[...])
    dn = mm_t(dqkv[...], wqkv_ref[...]) * gain
    normed = cen * rstd
    d = rstd * (dn - jnp.mean(dn, axis=1, keepdims=True) - normed * jnp.mean(dn * normed, axis=1, keepdims=True))
    d_ref[...] = d.astype(BF)

def window_call(x, c, valid, gain, wqkv, wproj):
    cells, width = x.shape
    head = width // HEADS
    pair = 2 * head
    return pl.pallas_call(
        functools.partial(window_kernel, head),
        out_shape=(jax.ShapeDtypeStruct((cells, width), BF),
                   jax.ShapeDtypeStruct((width, 3 * width), F32),
                   jax.ShapeDtypeStruct((width, width), F32)),
        in_specs=[pl.BlockSpec(memory_space=pltpu.VMEM)] * 6,
        out_specs=[pl.BlockSpec(memory_space=pltpu.VMEM)] * 3,
        scratch_shapes=[pltpu.VMEM((cells, width), BF)]
        + [pltpu.VMEM((cells, pair), BF)] * 4
        + [pltpu.VMEM((pair, cells), BF)] * 3
        + [pltpu.VMEM((1, 128), BF)]
        + [pltpu.VMEM((2, cells, cells), BF)] * 2
        + [pltpu.VMEM((cells, 3 * width), BF), pltpu.VMEM((width, cells), BF)],
        cost_estimate=pl.CostEstimate(flops=24 * cells * width * width + 12 * cells * cells * width, bytes_accessed=8 * 2**20, transcendentals=HEADS * cells * cells),
        compiler_params=pltpu.CompilerParams(vmem_limit_bytes=56 * 2**20),
    )(x, c, valid, gain, wqkv, wproj)


def permuted(value, axes, target):
    sizes = [lax.axis_size(a) for a in axes]
    pairs = []
    for source in range(math.prod(sizes)):
        at, rest = [], source
        for size in reversed(sizes):
            at.append(rest % size)
            rest //= size
        goal = target(*reversed(at))
        if goal is None:
            continue
        flat = 0
        for size, place in zip(sizes, goal):
            flat = flat * size + place
        pairs.append((source, flat))
    return lax.ppermute(value, tuple(axes), pairs)


def from_next(value, lat=False, lon=False):
    rows, cols = lax.axis_size("lat"), lax.axis_size("lon")

    def target(i, j):
        a, b = i - int(lat), (j - int(lon)) % cols
        return (a, b) if a >= 0 else None

    return permuted(value, ("lat", "lon"), target)


def to_next(value, lat=False, lon=False):
    rows, cols = lax.axis_size("lat"), lax.axis_size("lon")

    def target(i, j):
        a, b = i + int(lat), (j + int(lon)) % cols
        return (a, b) if a < rows else None

    return permuted(value, ("lat", "lon"), target)


def scatter_direct(value, axis, dim):
    count = lax.axis_size(axis)
    me = lax.axis_index(axis)
    share = value.shape[dim] // count
    total = lax.dynamic_slice_in_dim(value, me * share, share, dim).astype(F32)
    for step in range(1, count):
        goal = (me + step) % count
        part = lax.dynamic_slice_in_dim(value, goal * share, share, dim).astype(BF)
        got = permuted(part, (axis,), lambda i, s=step: ((i + s) % count,))
        total = total + got.astype(F32)
    return total


def scatter_bit(value, axis, bit, dim):
    me = (lax.axis_index(axis) // bit) % 2
    mine = lax.dynamic_index_in_dim(value, me, dim, keepdims=False).astype(F32)
    other = lax.dynamic_index_in_dim(value, 1 - me, dim, keepdims=False).astype(BF)
    got = permuted(other, (axis,), lambda i: (i ^ bit,))
    return mine + got.astype(F32)


def reduce_weights(gq, gp):
    lats, lons, dps = lax.axis_size("lat"), lax.axis_size("lon"), lax.axis_size("dp")
    width = gq.shape[1]
    parts = lats * lons
    joined = jnp.concatenate(
        [gq.reshape(parts, -1, width), gp.reshape(parts, -1, width)], axis=1
    )
    deep = joined.shape[1]
    total = joined.reshape(lats, lons, deep, width)
    bit = 1
    left = lons
    while left % 2 == 0:
        shape = total.shape
        total = scatter_bit(
            total.reshape(lats, left // 2, 2, deep, total.shape[-1]), "lon", bit, 2
        )
        left //= 2
        bit *= 2
        if bit == 2:
            total = scatter_direct(total, "dp", 3)
    if left > 1:
        raise ValueError("lon size")
    total = total.reshape(lats, deep, total.shape[-1])
    total = scatter_direct(total, "lat", 0)[0]
    cut = gq.shape[0] // parts
    return total[:cut].T, total[cut:].T


def per_device(hidden_in, grad_out, norm_gain, w_qkv, w_proj):
    samples, lat_rows, lon_cols, width = hidden_in.shape
    half = WIN // 2
    nr, nc = lat_rows // WIN, lon_cols // WIN
    short = half + (-half) % 16
    wide = WIN + (-WIN) % 16
    both = jnp.stack([hidden_in, grad_out])
    gain = norm_gain.reshape(1, width)

    def piece(rows_at, cols_at, n, pad_to):
        cut = lax.slice_in_dim(both, rows_at, rows_at + half, axis=2)
        cut = lax.slice_in_dim(cut, cols_at, cols_at + n, axis=3)
        return jnp.pad(cut, ((0, 0), (0, 0), (0, 0), (0, pad_to - n), (0, 0)))

    last = lax.axis_index("lat") == lax.axis_size("lat") - 1
    inner = [wc * WIN + SHIFT for wc in range(nc - 1)]
    edge = (nc - 1) * WIN + SHIFT
    lat_in = [from_next(piece(0, at, WIN, wide), lat=True) for at in inner]
    held = (piece(0, edge, half, short), piece(0, 0, half, short))
    lon_send = [piece(r * half, 0, half, short) for r in range(1, 2 * nr)]
    if lat_in:
        held, lat_in, lon_send = lax.optimization_barrier((held, lat_in, lon_send))
    lat_edge = from_next(held[0], lat=True)
    corner = from_next(held[1], lat=True, lon=True)
    lon_in = [from_next(p, lon=True) for p in lon_send]

    def valid_of(n, pad_to, pieces):
        ok = jnp.broadcast_to((jnp.arange(pad_to) < n)[None], (half, pad_to)).reshape(-1)
        count = len(pieces)
        oks = jnp.stack([ok & jnp.logical_not(p) for p in pieces]).reshape(-1)
        return jnp.broadcast_to(oks.astype(F32)[None, :, None], (1, oks.shape[0], 128))

    sums = None
    out_inner, out_edge = {}, {}
    for b in range(samples):
        for wc in range(nc):
            for wr in range(nr):
                end = wr == nr - 1
                gone = last if end else jnp.bool_(False)
                top = (2 * wr + 1) * half
                if wc < nc - 1:
                    low = lat_in[wc] if end else piece(top + half, inner[wc], WIN, wide)
                    parts = [piece(top, inner[wc], WIN, wide), low]
                    valid = valid_of(WIN, wide, [jnp.bool_(False), gone])
                else:
                    a = lat_edge if end else piece(top + half, edge, half, short)
                    d = corner if end else lon_in[2 * wr + 1]
                    parts = [piece(top, edge, half, short), lon_in[2 * wr], a, d]
                    valid = valid_of(half, short, [jnp.bool_(False)] * 2 + [gone] * 2)
                cells = jnp.concatenate(
                    [p[:, b].reshape(2, -1, width) for p in parts], axis=1
                )
                dcells, gq, gp = window_call(cells[0], cells[1], valid, gain, w_qkv, w_proj)
                sums = (gq, gp) if sums is None else (sums[0] + gq, sums[1] + gp)
                if wc < nc - 1:
                    out_inner[b, wr, wc] = dcells.reshape(2, half, wide, width)[:, :, :WIN]
                else:
                    out_edge[b, wr] = dcells.reshape(2, 2, half, short, width)[:, :, :, :half]

    def over_lat(f):
        halves = [f(wr) for wr in range(nr)]
        carried = halves[nr - 1][1]
        own = [h for pair in halves for h in pair][:-1]
        return carried, own

    samples_out = []
    for b in range(samples):
        columns = []
        for wc in range(nc - 1):
            carried, own = over_lat(lambda wr: (out_inner[b, wr, wc][0], out_inner[b, wr, wc][1]))
            columns.append(jnp.concatenate([to_next(carried, lat=True)] + own, axis=0))
        carried, own = over_lat(lambda wr: (out_edge[b, wr][0, 0], out_edge[b, wr][1, 0]))
        columns.append(jnp.concatenate([to_next(carried, lat=True)] + own, axis=0))
        carried, own = over_lat(lambda wr: (out_edge[b, wr][0, 1], out_edge[b, wr][1, 1]))
        first = jnp.concatenate(
            [to_next(carried, lat=True, lon=True)] + [to_next(o, lon=True) for o in own], axis=0
        )
        samples_out.append(jnp.concatenate([first] + columns, axis=1))
    returned = jnp.stack(samples_out)
    grad_in = (grad_out.astype(F32) + returned.astype(F32)).astype(BF)
    total_cells = (
        lax.axis_size("dp") * samples * lat_rows * lax.axis_size("lat") * lon_cols * lax.axis_size("lon")
    )
    factor = float(total_cells) ** (-0.5)
    gq, gp = reduce_weights(sums[0].T, sums[1].T)
    return (grad_in, gq * factor, gp * factor)


def solution(mesh):
    in_specs = (P("dp", "lat", "lon", None), P("dp", "lat", "lon", None), P(), P(), P())
    out_specs = (P("dp", "lat", "lon", None), P("dp", ("lat", "lon")), P("dp", ("lat", "lon")))
    return jax.shard_map(
        per_device, mesh=mesh, in_specs=in_specs, out_specs=out_specs, check_vma=False
    )
```

time: 414 us -> 157 us (0.38)
  matrix products: 158 us -> 0 us
  waiting for transfers between devices: 168 us -> 32 us
  Pallas kernels: 0 us -> 67.4 us
  local copies, waits for them, and re-layouts: 45.8 us -> 10.1 us
  starting transfers between devices: 5.15 us -> 27.7 us
  between operations: 14 us -> 0.92 us
    dot_general x82 -> x0, matrix products: 158 us -> none  [the longest x12 31 us: attend_head(): jnp.dot(attention_low.T, grad_rows, preferred_element_type=jnp.float32)]
    unnamed x8 -> x0, waiting for transfers between devices: 114 us -> none
    pallas_call x0 -> x2, Pallas kernels: none -> 67.4 us  [window_call(): pl.pallas_call(functools.partial(window_kernel, head), out_shape=(jax.Sha...]
    ppermute x4 -> x14, starting transfers between devices: 4.98 us -> 27.7 us  [permuted(): return lax.ppermute(value, tuple(axes), pairs)]
    ppermute x4 -> x14, waiting for transfers between devices: 54.3 us -> 32 us  [permuted(): return lax.ppermute(value, tuple(axes), pairs)]
    slice x12 -> x0, local copies, waits for them, and re-layouts: 14.4 us -> none  [the longest x4 7.12 us: window_grads(): qkv[:, 2 * model_width:]]
    unnamed x18 -> x14, local copies, waits for them, and re-layouts: 11.8 us -> 0.03 us
    convert_element_type x14 -> x4, other arithmetic: 15.1 us -> 3.76 us  [the longest x1 1.89 us: per_device(): grad_in = (grad_out.astype(F32) + returned.astype(F32)).astype(BF)]
  transfers between devices with their start and end apart: 8 -> 14, of which waited for: 6 -> 6; matrix products, arithmetic and copies ran while one was open for 3% -> 6% of each run, Pallas kernels for 0% -> 21%
where the time goes in v1:
time: 157 us; the launch traced here: 156 us
  Pallas kernels  67.4 us (43%)
  waiting for transfers between devices  32 us (20%)
  starting transfers between devices  27.7 us (18%)
  other arithmetic  18.3 us (12%)
  local copies, waits for them, and re-layouts  10.1 us (6%)
    pallas_call x2, Pallas kernels, window_call(): pl.pallas_call(functools.partial(window_kernel, head), out_shape=(jax.Sha...  67.4 us
    ppermute x14, waiting for transfers between devices, permuted(): return lax.ppermute(value, tuple(axes), pairs)  32 us
    ppermute x14, starting transfers between devices, permuted(): return lax.ppermute(value, tuple(axes), pairs)  27.7 us
    transpose x2, other arithmetic, per_device(): gq, gp = reduce_weights(sums[0].T, sums[1].T)  5.01 us
    transpose x2, local copies, waits for them, and re-layouts, per_device(): gq, gp = reduce_weights(sums[0].T, sums[1].T)  4.31 us
    another operation x1, other arithmetic, per_device(): both = jnp.stack([hidden_in, grad_out])  3.52 us
  transfers between devices with their start and end apart: 14, of which 6 were waited for; matrix products, arithmetic and copies ran while one was open for 6% of the time, Pallas kernels for 21%

profile of v1, /device:TPU:0, one launch (start us, length us, event | category | flops | bytes accessed | tf_op | source)
XLA Modules:
  0.0 156.3 jit_solution(7416542734668724392)
XLA Ops:
  0.7 3.5 %fusion.12 = (bf16[2,1,15,32,384]{4,3,2,1,0:T(8,128)(2,1)}, bf16[2,1,15,32,384]{4,3,2,1,0:T(8,128)(2,1)}) fusion(bf16[1,1,30,60,384]{4,3,2,1,0:T(8,128)(2,1)} %bitcast.70, bf16[1,1,30,60,384]{4,3,2,1,0:T(8,128)(2,1)} %bitcast.72), kind=kLoop, calls=%fused_computation.24 | loop fusion | flops 4792320 | bytes 4239360 | tf_op jit(solution)/shard_map/stack | solution.py:218
  7.0 18.9 %collective-permute-done = bf16[2,1,15,32,384]{4,3,2,1,0:T(8,128)(2,1)} collective-permute-done((bf16[2,1,15,32,384]{4,3,2,1,0:T(8,128)(2,1)}, bf16[2,1,15,32,384]{4,3,2,1,0:T(8,128)(2,1)}, u32[]{:S(2)}, u32[]{:S(2)}) %collective-permute-start) | collective-permute-done | bytes 737312 | tf_op jit(solution)/shard_map/ppermute | solution.py:140
  28.8 2.3 %fusion.13 = (bf16[960,384]{1,0:T(8,128)(2,1)}, bf16[960,384]{1,0:T(8,128)(2,1)}) fusion(bf16[2,480,384]{2,1,0:T(8,128)(2,1)} %bitcast.13, bf16[2,480,384]{2,1,0:T(8,128)(2,1)S(1)} %bitcast.76), kind=kLoop, calls=%fused_computation.26 | loop fusion | flops 2949120 | bytes 2949120 | tf_op jit(solution)/shard_map/squeeze | solution.py:264
  32.1 33.5 %shard_map.77 = (bf16[960,384]{1,0:T(8,128)(2,1)}, f32[384,1152]{1,0:T(8,128)}, f32[384,384]{1,0:T(8,128)}) custom-call(bf16[960,384]{1,0:T(8,128)(2,1)} %get-tuple-element.30.x_ref, bf16[960,384]{1,0:T(8,128)(2,1)} %get-tuple-element.29.c_ref, f32[1,960,128]{2,1,0:T(8,128)} %broadcast_in_dim.33.valid_ref, f32[1,384]{1,0:T(1,128)} %reshape.172.gain_ref, ...), custom_call_target="tpu_custom_call" | custom-call | flops 7644119040 | bytes 8388608 | tf_op jit(solution)/shard_map/pallas_call | solution.py:107
  65.8 1.3 slice_bitcast_fusion
  68.1 33.8 %shard_map.76 = (bf16[960,384]{1,0:T(8,128)(2,1)}, f32[384,1152]{1,0:T(8,128)}, f32[384,384]{1,0:T(8,128)}) custom-call(bf16[960,384]{1,0:T(8,128)(2,1)} %get-tuple-element.32.x_ref, bf16[960,384]{1,0:T(8,128)(2,1)} %get-tuple-element.31.c_ref, f32[1,960,128]{2,1,0:T(8,128)} %broadcast_in_dim.15.valid_ref, f32[1,384]{1,0:T(1,128)} %reshape.172.gain_ref, ...), custom_call_target="tpu_custom_call" | custom-call | flops 7644119040 | bytes 8388608 | tf_op jit(solution)/shard_map/pallas_call | solution.py:107
  101.9 2.9 %add_bitcast_fusion = f32[1152,384]{0,1:T(8,128)} fusion(f32[384,1152]{1,0:T(8,128)S(1)} %copy-done.4, f32[384,1152]{1,0:T(8,128)} %get-tuple-element.20), kind=kLoop, calls=%fused_computation.5 | loop fusion | flops 442368 | bytes 5308416 | tf_op jit(solution)/shard_map/transpose | solution.py:296
  104.8 2.2 %copy.10 = f32[1152,384]{1,0:T(8,128)S(1)} copy(f32[1152,384]{0,1:T(8,128)} %add_bitcast_fusion) | data formatting | bytes 3538944 | tf_op jit(solution)/shard_map/transpose | solution.py:296
  107.0 2.1 %add_bitcast_fusion.1 = f32[384,384]{0,1:T(8,128)} fusion(f32[384,384]{1,0:T(8,128)} %get-tuple-element.21, f32[384,384]{1,0:T(8,128)} %get-tuple-element.22), kind=kLoop, calls=%fused_computation.40 | loop fusion | flops 147456 | bytes 1769472 | tf_op jit(solution)/shard_map/transpose | solution.py:296
  109.1 2.1 %copy.11 = f32[384,384]{1,0:T(8,128)} copy(f32[384,384]{0,1:T(8,128)} %add_bitcast_fusion.1) | data formatting | bytes 1179648 | tf_op jit(solution)/shard_map/transpose | solution.py:296
  111.3 1.8 %fusion.22 = bf16[4,2,96,384]{3,2,1,0:T(8,128)(2,1)} fusion(s32[]{:T(128)S(6)} %select_n.66, f32[4,2,2,24,384]{4,3,2,1,0:T(8,128)} %bitcast.74, f32[4,2,2,72,384]{4,3,2,1,0:T(8,128)S(1)} %bitcast.68), kind=kLoop, calls=%fused_computation.39 | loop fusion | flops 1179648 | bytes 2949124 | tf_op jit(solution)/shard_map/convert_element_type | solution.py:179
  114.6 6.1 %collective-permute-start.6 = (bf16[15,30,384]{2,1,0:T(8,128)(2,1)S(1)}, bf16[15,30,384]{2,1,0:T(8,128)(2,1)S(1)}, u32[]{:S(2)}, u32[]{:S(2)}) collective-permute-start(bf16[15,30,384]{2,1,0:T(8,128)(2,1)S(1)} %get-tuple-element.37), channel_id=1, source_target_pairs={{0,4},{1,5},{2,6},{3,7},{4,8},{5,9},{6,10},{7,11},{8,12},{9,13},{1... | collective-permute-start | bytes 1036808 | tf_op jit(solution)/shard_map/ppermute | solution.py:140
  122.1 1.6 collective-permute-start.9
  123.7 5.5 %collective-permute-done.6 = bf16[15,30,384]{2,1,0:T(8,128)(2,1)S(1)} collective-permute-done((bf16[15,30,384]{2,1,0:T(8,128)(2,1)S(1)}, bf16[15,30,384]{2,1,0:T(8,128)(2,1)S(1)}, u32[]{:S(2)}, u32[]{:S(2)}) %collective-permute-start.6) | collective-permute-done | bytes 345632 | tf_op jit(solution)/shard_map/ppermute | solution.py:140
  129.4 4.4 %collective-permute-start.7 = (bf16[15,15,384]{2,1,0:T(8,128)(2,1)S(1)}, bf16[15,15,384]{2,1,0:T(8,128)(2,1)S(1)}, u32[]{:S(2)}, u32[]{:S(2)}) collective-permute-start(bf16[15,15,384]{2,1,0:T(8,128)(2,1)S(1)} %get-tuple-element.35), channel_id=1, source_target_pairs={{0,4},{1,5},{2,6},{3,7},{4,8},{5,9},{6,10},{7,11},{8,12},{9,13},{1... | collective-permute-start | bytes 518408 | tf_op jit(solution)/shard_map/ppermute | solution.py:140
  133.9 3.7 %collective-permute-start.4 = (bf16[15,15,384]{2,1,0:T(8,128)(2,1)S(1)}, bf16[15,15,384]{2,1,0:T(8,128)(2,1)S(1)}, u32[]{:S(2)}, u32[]{:S(2)}) collective-permute-start(bf16[15,15,384]{2,1,0:T(8,128)(2,1)S(1)} %get-tuple-element.33), channel_id=1, source_target_pairs={{0,5},{1,6},{2,7},{3,4},{4,9},{5,10},{6,11},{7,8},{8,13},{9,14},{1... | collective-permute-start | bytes 518408 | tf_op jit(solution)/shard_map/ppermute | solution.py:140
  137.9 1.7 %collective-permute-start.10 = (bf16[4,1,96,192]{3,2,1,0:T(8,128)(2,1)S(1)}, bf16[4,1,96,192]{3,2,1,0:T(8,128)(2,1)S(1)}, u32[]{:S(2)}, u32[]{:S(2)}) collective-permute-start(bf16[4,1,96,192]{3,2,1,0:T(8,128)(2,1)S(1)} %dynamic-slice_convert_fusion.1), channel_id=1, source_target_pairs={{0,2},{1,3},{2,0},{3,1},{4,6},{5,7},{6,4},{7,5},{8,10},{9,11},{10,... | collective-permute-start | bytes 442376 | tf_op jit(solution)/shard_map/ppermute | solution.py:140
  139.7 2.0 %collective-permute-done.4 = bf16[15,15,384]{2,1,0:T(8,128)(2,1)S(1)} collective-permute-done((bf16[15,15,384]{2,1,0:T(8,128)(2,1)S(1)}, bf16[15,15,384]{2,1,0:T(8,128)(2,1)S(1)}, u32[]{:S(2)}, u32[]{:S(2)}) %collective-permute-start.4) | collective-permute-done | bytes 172832 | tf_op jit(solution)/shard_map/ppermute | solution.py:140
  141.8 2.8 %collective-permute-done.10 = bf16[4,1,96,192]{3,2,1,0:T(8,128)(2,1)S(1)} collective-permute-done((bf16[4,1,96,192]{3,2,1,0:T(8,128)(2,1)S(1)}, bf16[4,1,96,192]{3,2,1,0:T(8,128)(2,1)S(1)}, u32[]{:S(2)}, u32[]{:S(2)}) %collective-permute-start.10) | collective-permute-done | bytes 147488 | tf_op jit(solution)/shard_map/ppermute | solution.py:140
  144.8 2.0 %collective-permute-start.13 = (bf16[1,96,192]{2,1,0:T(8,128)(2,1)S(1)}, bf16[1,96,192]{2,1,0:T(8,128)(2,1)S(1)}, u32[]{:S(2)}, u32[]{:S(2)}) collective-permute-start(bf16[1,96,192]{2,1,0:T(8,128)(2,1)S(1)} %get-tuple-element.40), channel_id=1, source_target_pairs={{0,12},{4,0},{8,4},{12,8},{1,13},{5,1},{9,5},{13,9},{2,14},{6,2},{... | collective-permute-start | bytes 110600 | tf_op jit(solution)/shard_map/ppermute | solution.py:140
  146.7 2.4 %collective-permute-start.12 = (bf16[1,96,192]{2,1,0:T(8,128)(2,1)S(1)}, bf16[1,96,192]{2,1,0:T(8,128)(2,1)S(1)}, u32[]{:S(2)}, u32[]{:S(2)}) collective-permute-start(bf16[1,96,192]{2,1,0:T(8,128)(2,1)S(1)} %get-tuple-element.41), channel_id=1, source_target_pairs={{0,8},{4,12},{8,0},{12,4},{1,9},{5,13},{9,1},{13,5},{2,10},{6,14},... | collective-permute-start | bytes 110600 | tf_op jit(solution)/shard_map/ppermute | solution.py:140
  149.2 1.3 collective-permute-start.11
  150.5 1.9 %add_convert_fusion = bf16[1,30,60,384]{3,2,1,0:T(8,128)(2,1)} fusion(bf16[1,30,60,384]{3,2,1,0:T(8,128)(2,1)S(1)} %copy-done, bf16[1,30,15,384]{3,2,1,0:T(8,128)(2,1)S(1)} %maximum_bitcast_fusion.2, bf16[1,30,30,384]{3,2,1,0:T(8,128)(2,1)S(1)} %maximum_bitcast_fusion, bf16[1,30,15,384]{3,2,1,0:T(8,128)(2,1)S(1)} %maximum_bitcast_fusion.1), kind=kLoop, calls=%fused_computation.2 | loop fusion | flops 6220800 | bytes 4147200 | tf_op jit(solution)/shard_map/convert_element_type | solution.py:291
  153.3 1.7 %collective-permute-done.11 = bf16[1,96,192]{2,1,0:T(8,128)(2,1)S(1)} collective-permute-done((bf16[1,96,192]{2,1,0:T(8,128)(2,1)S(1)}, bf16[1,96,192]{2,1,0:T(8,128)(2,1)S(1)}, u32[]{:S(2)}, u32[]{:S(2)}) %collective-permute-start.11) | collective-permute-done | bytes 36896 | tf_op jit(solution)/shard_map/ppermute | solution.py:140
  (60 shorter events, 13.6 us)
Async XLA Ops:
  0.6 5.1 %copy-start.6 = (f32[384]{0:T(512)S(1)}, f32[384]{0:T(512)}, u32[]{:S(2)}) copy-start(f32[384]{0:T(512)} %param.7) | copy-start | bytes 4612
  0.6 5.8 %copy-start = (bf16[1,30,60,384]{3,2,1,0:T(8,128)(2,1)S(1)}, bf16[1,30,60,384]{3,2,1,0:T(8,128)(2,1)}, u32[]{:S(2)}) copy-start(bf16[1,30,60,384]{3,2,1,0:T(8,128)(2,1)} %param.6) | copy-start | bytes 4147204
  0.7 5.8 %copy-start.1 = (bf16[1,30,60,384]{3,2,1,0:T(8,128)(2,1)S(1)}, bf16[1,30,60,384]{3,2,1,0:T(8,128)(2,1)}, u32[]{:S(2)}) copy-start(bf16[1,30,60,384]{3,2,1,0:T(8,128)(2,1)} %param.5) | copy-start | bytes 4147204
  4.2 21.7 %collective-permute-start = (bf16[2,1,15,32,384]{4,3,2,1,0:T(8,128)(2,1)}, bf16[2,1,15,32,384]{4,3,2,1,0:T(8,128)(2,1)}, u32[]{:S(2)}, u32[]{:S(2)}) collective-permute-start(bf16[2,1,15,32,384]{4,3,2,1,0:T(8,128)(2,1)} %get-tuple-element.24), channel_id=1, source_target_pairs={{4,0},{5,1},{6,2},{7,3},{8,4},{9,5},{10,6},{11,7},{12,8},{13,9},{1... | collective-permute-start | bytes 2211848 | tf_op jit(solution)/shard_map/ppermute | solution.py:140
  6.5 22.3 %copy-start.3 = (bf16[2,1,15,32,384]{4,3,2,1,0:T(8,128)(2,1)S(1)}, bf16[2,1,15,32,384]{4,3,2,1,0:T(8,128)(2,1)}, u32[]{:S(2)}) copy-start(bf16[2,1,15,32,384]{4,3,2,1,0:T(8,128)(2,1)} %get-tuple-element.23) | copy-start | bytes 2211844
  25.9 39.7 %collective-permute-start.3 = (bf16[2,1,15,16,384]{4,3,2,1,0:T(8,128)(2,1)S(1)}, bf16[2,1,15,16,384]{4,3,2,1,0:T(8,128)(2,1)S(1)}, u32[]{:S(2)}, u32[]{:S(2)}) collective-permute-start(bf16[2,1,15,16,384]{4,3,2,1,0:T(8,128)(2,1)S(1)} %get-tuple-element.15), channel_id=1, source_target_pairs={{4,3},{5,0},{6,1},{7,2},{8,7},{9,4},{10,5},{11,6},{12,11},{13,8},{... | collective-permute-start | bytes 1105928 | tf_op jit(solution)/shard_map/ppermute | solution.py:140
  27.2 38.5 %collective-permute-start.2 = (bf16[2,1,15,16,384]{4,3,2,1,0:T(8,128)(2,1)S(1)}, bf16[2,1,15,16,384]{4,3,2,1,0:T(8,128)(2,1)S(1)}, u32[]{:S(2)}, u32[]{:S(2)}) collective-permute-start(bf16[2,1,15,16,384]{4,3,2,1,0:T(8,128)(2,1)S(1)} %get-tuple-element.14), channel_id=1, source_target_pairs={{4,0},{5,1},{6,2},{7,3},{8,4},{9,5},{10,6},{11,7},{12,8},{13,9},{1... | collective-permute-start | bytes 1105928 | tf_op jit(solution)/shard_map/ppermute | solution.py:140
  28.5 37.2 %collective-permute-start.1 = (bf16[2,1,15,16,384]{4,3,2,1,0:T(8,128)(2,1)S(1)}, bf16[2,1,15,16,384]{4,3,2,1,0:T(8,128)(2,1)S(1)}, u32[]{:S(2)}, u32[]{:S(2)}) collective-permute-start(bf16[2,1,15,16,384]{4,3,2,1,0:T(8,128)(2,1)S(1)} %get-tuple-element.13), channel_id=1, source_target_pairs={{0,3},{1,0},{2,1},{3,2},{4,7},{5,4},{6,5},{7,6},{8,11},{9,8},{10,9... | collective-permute-start | bytes 1105928 | tf_op jit(solution)/shard_map/ppermute | solution.py:140
  68.1 33.8 %copy-start.4 = (f32[384,1152]{1,0:T(8,128)S(1)}, f32[384,1152]{1,0:T(8,128)}, u32[]{:S(2)}) copy-start(f32[384,1152]{1,0:T(8,128)} %get-tuple-element.19) | copy-start | bytes 5308420
  113.1 7.6 %collective-permute-start.8 = (bf16[4,2,96,384]{3,2,1,0:T(8,128)(2,1)}, bf16[4,2,96,384]{3,2,1,0:T(8,128)(2,1)}, u32[]{:S(2)}, u32[]{:S(2)}) collective-permute-start(bf16[4,2,96,384]{3,2,1,0:T(8,128)(2,1)} %fusion.22), channel_id=1, source_target_pairs={{0,1},{1,0},{2,3},{3,2},{4,5},{5,4},{6,7},{7,6},{8,9},{9,8},{10,11... | collective-permute-start | bytes 1769480 | tf_op jit(solution)/shard_map/ppermute | solution.py:140
  113.4 7.4 %copy-start.2 = (f32[384,384]{1,0:T(8,128)S(1)}, f32[384,384]{1,0:T(8,128)}, u32[]{:S(2)}) copy-start(f32[384,384]{1,0:T(8,128)} %copy.11) | copy-start | bytes 1769476
  114.6 14.6 %collective-permute-start.6 = (bf16[15,30,384]{2,1,0:T(8,128)(2,1)S(1)}, bf16[15,30,384]{2,1,0:T(8,128)(2,1)S(1)}, u32[]{:S(2)}, u32[]{:S(2)}) collective-permute-start(bf16[15,30,384]{2,1,0:T(8,128)(2,1)S(1)} %get-tuple-element.37), channel_id=1, source_target_pairs={{0,4},{1,5},{2,6},{3,7},{4,8},{5,9},{6,10},{7,11},{8,12},{9,13},{1... | collective-permute-start | bytes 1036808 | tf_op jit(solution)/shard_map/ppermute | solution.py:140
  121.9 7.4 %copy-start.5 = (bf16[960,384]{1,0:T(8,128)(2,1)S(1)}, bf16[960,384]{1,0:T(8,128)(2,1)}, u32[]{:S(2)}) copy-start(bf16[960,384]{1,0:T(8,128)(2,1)} %get-tuple-element.16) | copy-start | bytes 2211844
  122.1 15.5 %collective-permute-start.9 = (bf16[4,2,96,192]{3,2,1,0:T(8,128)(2,1)S(1)}, bf16[4,2,96,192]{3,2,1,0:T(8,128)(2,1)S(1)}, u32[]{:S(2)}, u32[]{:S(2)}) collective-permute-start(bf16[4,2,96,192]{3,2,1,0:T(8,128)(2,1)S(1)} %dynamic-slice_convert_fusion), channel_id=1, source_target_pairs={{0,16},{16,0},{1,17},{17,1},{2,18},{18,2},{3,19},{19,3},{4,20},{20... | collective-permute-start | bytes 884744 | tf_op jit(solution)/shard_map/ppermute | solution.py:140
  129.4 10.3 %collective-permute-start.7 = (bf16[15,15,384]{2,1,0:T(8,128)(2,1)S(1)}, bf16[15,15,384]{2,1,0:T(8,128)(2,1)S(1)}, u32[]{:S(2)}, u32[]{:S(2)}) collective-permute-start(bf16[15,15,384]{2,1,0:T(8,128)(2,1)S(1)} %get-tuple-element.35), channel_id=1, source_target_pairs={{0,4},{1,5},{2,6},{3,7},{4,8},{5,9},{6,10},{7,11},{8,12},{9,13},{1... | collective-permute-start | bytes 518408 | tf_op jit(solution)/shard_map/ppermute | solution.py:140
  133.8 5.9 %collective-permute-start.5 = (bf16[15,15,384]{2,1,0:T(8,128)(2,1)S(1)}, bf16[15,15,384]{2,1,0:T(8,128)(2,1)S(1)}, u32[]{:S(2)}, u32[]{:S(2)}) collective-permute-start(bf16[15,15,384]{2,1,0:T(8,128)(2,1)S(1)} %get-tuple-element.36), channel_id=1, source_target_pairs={{0,1},{1,2},{2,3},{3,0},{4,5},{5,6},{6,7},{7,4},{8,9},{9,10},{10,1... | collective-permute-start | bytes 518408 | tf_op jit(solution)/shard_map/ppermute | solution.py:140
  133.9 7.9 %collective-permute-start.4 = (bf16[15,15,384]{2,1,0:T(8,128)(2,1)S(1)}, bf16[15,15,384]{2,1,0:T(8,128)(2,1)S(1)}, u32[]{:S(2)}, u32[]{:S(2)}) collective-permute-start(bf16[15,15,384]{2,1,0:T(8,128)(2,1)S(1)} %get-tuple-element.33), channel_id=1, source_target_pairs={{0,5},{1,6},{2,7},{3,4},{4,9},{5,10},{6,11},{7,8},{8,13},{9,14},{1... | collective-permute-start | bytes 518408 | tf_op jit(solution)/shard_map/ppermute | solution.py:140
  137.9 6.7 %collective-permute-start.10 = (bf16[4,1,96,192]{3,2,1,0:T(8,128)(2,1)S(1)}, bf16[4,1,96,192]{3,2,1,0:T(8,128)(2,1)S(1)}, u32[]{:S(2)}, u32[]{:S(2)}) collective-permute-start(bf16[4,1,96,192]{3,2,1,0:T(8,128)(2,1)S(1)} %dynamic-slice_convert_fusion.1), channel_id=1, source_target_pairs={{0,2},{1,3},{2,0},{3,1},{4,6},{5,7},{6,4},{7,5},{8,10},{9,11},{10,... | collective-permute-start | bytes 442376 | tf_op jit(solution)/shard_map/ppermute | solution.py:140
  144.8 7.6 %collective-permute-start.13 = (bf16[1,96,192]{2,1,0:T(8,128)(2,1)S(1)}, bf16[1,96,192]{2,1,0:T(8,128)(2,1)S(1)}, u32[]{:S(2)}, u32[]{:S(2)}) collective-permute-start(bf16[1,96,192]{2,1,0:T(8,128)(2,1)S(1)} %get-tuple-element.40), channel_id=1, source_target_pairs={{0,12},{4,0},{8,4},{12,8},{1,13},{5,1},{9,5},{13,9},{2,14},{6,2},{... | collective-permute-start | bytes 110600 | tf_op jit(solution)/shard_map/ppermute | solution.py:140
  146.7 6.6 %collective-permute-start.12 = (bf16[1,96,192]{2,1,0:T(8,128)(2,1)S(1)}, bf16[1,96,192]{2,1,0:T(8,128)(2,1)S(1)}, u32[]{:S(2)}, u32[]{:S(2)}) collective-permute-start(bf16[1,96,192]{2,1,0:T(8,128)(2,1)S(1)} %get-tuple-element.41), channel_id=1, source_target_pairs={{0,8},{4,12},{8,0},{12,4},{1,9},{5,13},{9,1},{13,5},{2,10},{6,14},... | collective-permute-start | bytes 110600 | tf_op jit(solution)/shard_map/ppermute | solution.py:140
  149.2 5.9 %collective-permute-start.11 = (bf16[1,96,192]{2,1,0:T(8,128)(2,1)S(1)}, bf16[1,96,192]{2,1,0:T(8,128)(2,1)S(1)}, u32[]{:S(2)}, u32[]{:S(2)}) collective-permute-start(bf16[1,96,192]{2,1,0:T(8,128)(2,1)S(1)} %get-tuple-element.39), channel_id=1, source_target_pairs={{0,4},{4,8},{8,12},{12,0},{1,5},{5,9},{9,13},{13,1},{2,6},{6,10},{... | collective-permute-start | bytes 110600 | tf_op jit(solution)/shard_map/ppermute | solution.py:140

commit v2 on v1

v2 whole, which is shorter than its diff:
```python
import functools, math
import jax, jax.numpy as jnp
from jax import lax
from jax.experimental import pallas as pl
from jax.experimental.pallas import tpu as pltpu

from jax.sharding import PartitionSpec as P

HEADS = 6
WIN = 30
SHIFT = 15
EPSILON = 1e-05
BF = jnp.bfloat16
F32 = jnp.float32
LN2 = math.log(2.0)

def mm(a, b):
    return lax.dot_general(a, b, (((1,), (0,)), ((), ())), preferred_element_type=F32)

def mm_t(a, b):
    return lax.dot_general(a, b, (((1,), (1,)), ((), ())), preferred_element_type=F32)

def blocks_of(n, step):
    return [(at, min(step, n - at)) for at in range(0, n, step)]

def window_kernel(head, metas, split, flag_ref, *refs):
    count = len(metas)
    pieces, refs = refs[:count], refs[count:]
    gain_ref, wqkv_ref, wproj_ref = refs[:3]
    refs = refs[3:]
    if split[0]:
        prev, refs = refs[:2], refs[2:]
    d_refs, refs = refs[:count], refs[count:]
    (gq_ref, gp_ref), refs = refs[:2], refs[2:]
    c_ref, nl, q_s, k_s, v_s, b_s, kT, vT, bT, p_s, ds_s, dqkv, attT = refs[:13]
    cells, width = c_ref.shape
    pair = 2 * head
    pairs = width // pair
    qscale = head ** -0.5 / LN2
    at = 0
    starts = []
    for p in pieces:
        starts.append(at)
        c_ref[at:at + p.shape[1]] = p[1]
        at += p.shape[1]
    lastf = flag_ref[0].astype(F32)
    oks = []
    for p, (n, pad, gone) in zip(pieces, metas):
        place = lax.broadcasted_iota(jnp.int32, (p.shape[1], pair), 0)
        ok = jnp.where(lax.rem(place, pad) < n, 1.0, 0.0)
        oks.append(ok * (1.0 - lastf) if gone else ok)
    valid_col = jnp.concatenate(oks, axis=0)
    x = jnp.concatenate([p[0] for p in pieces], axis=0).astype(F32)
    mean = jnp.mean(x, axis=1, keepdims=True)
    cen = x - mean
    rstd = lax.rsqrt(jnp.mean(cen * cen, axis=1, keepdims=True) + EPSILON)
    gain = gain_ref[...]
    nl[...] = (cen * rstd * gain).astype(BF)
    qb = blocks_of(cells, cells)

    def one_pair(j, _):
        cols = pl.ds(pl.multiple_of(j * pair, pair), pair)
        colk = pl.ds(pl.multiple_of(width + j * pair, pair), pair)
        colv = pl.ds(pl.multiple_of(2 * width + j * pair, pair), pair)
        q_s[...] = (mm(nl[...], wqkv_ref[:, cols]) * qscale).astype(BF)
        k_s[...] = mm(nl[...], wqkv_ref[:, colk]).astype(BF)
        v_s[...] = mm(nl[...], wqkv_ref[:, colv]).astype(BF)
        b_s[...] = mm_t(c_ref[...], wproj_ref[cols, :]).astype(BF)
        kT[...] = k_s[...].T
        vT[...] = v_s[...].T
        bT[...] = b_s[...].T
        lane = lax.broadcasted_iota(jnp.int32, (cells, pair), 1)
        row = lax.broadcasted_iota(jnp.int32, (pair, cells), 0)
        outs = []
        for h in range(2):
            own = (lane >= head) if h else (lane < head)
            own_r = (row >= head) if h else (row < head)
            aug = 0 if h else head
            bias = jnp.where(lane == aug, (valid_col - 1.0) * 30000.0, 0.0).astype(BF)
            kk = jnp.where(own, k_s[...], bias)
            qq = jnp.where(own, q_s[...], jnp.where(lane == aug, 1.0, 0.0).astype(BF))
            two = (lane == aug) | (lane == aug + 1)
            vv = jnp.where(own, v_s[...], jnp.where(two, 1.0, 0.0).astype(BF))
            vvT = jnp.where(own_r, vT[...], jnp.where(row == aug, 1.0, 0.0).astype(BF))
            for at, n in qb:
                s = mm_t(kk, qq[at:at + n])
                e = jnp.exp2(s).astype(BF)
                oT = mm(vvT, e)
                total = oT[aug:aug + 1]
                inv = 1.0 / total
                aT = oT * inv
                attT[pl.ds(pl.multiple_of(j * pair + h * head, head), head), at:at + n] = aT[h * head:(h + 1) * head].astype(BF)
                bTn = bT[:, at:at + n].astype(F32)
                ownn = own_r[:, :n]
                rown = row[:, :n]
                rt = jnp.sum(jnp.where(ownn, bTn * aT, 0.0), axis=0, keepdims=True)
                hi = rt.astype(BF).astype(F32)
                lo = rt - hi
                baug = jnp.where(ownn, bTn, jnp.where(rown == aug, -hi, jnp.where(rown == aug + 1, -lo, 0.0))).astype(BF)
                p = e * inv.astype(BF)
                p_s[h, :, at:at + n] = p
                dp = mm(vv, baug).astype(BF)
                ds_s[h, :, at:at + n] = p * dp
            dv = mm(p_s[h], b_s[...])
            dk = mm(ds_s[h], q_s[...]) * LN2
            dqT = mm(kT[...], ds_s[h]) * (head ** -0.5)
            outs.append((dqT, dk, dv))
        dqT = jnp.where(row < head, outs[0][0], outs[1][0]).astype(BF)
        dqkv[:, cols] = dqT.T
        dqkv[:, colk] = jnp.where(lane < head, outs[0][1], outs[1][1]).astype(BF)
        dqkv[:, colv] = jnp.where(lane < head, outs[0][2], outs[1][2]).astype(BF)
        return 0

    lax.fori_loop(0, pairs, one_pair, 0)
    gp = mm(attT[...], c_ref[...])
    gq = mm(nl[...].T, dqkv[...])
    if split[0]:
        gq = gq + prev[0][...]
        gp = gp + prev[1][...]
    if split[1] is None:
        gq_ref[...] = gq
        gp_ref[...] = gp
    else:
        joined = refs[13]
        parts = split[1]
        gqT, gpT = gq.T, gp.T
        dq_rows, dp_rows = gqT.shape[0] // parts, gpT.shape[0] // parts
        for i in range(parts):
            joined[i, :dq_rows] = gqT[i * dq_rows:(i + 1) * dq_rows]
            joined[i, dq_rows:] = gpT[i * dp_rows:(i + 1) * dp_rows]
        me = flag_ref[1]
        for i in range(parts // 2):
            gq_ref[i] = joined[2 * i + me]
            gp_ref[i] = joined[2 * i + 1 - me].astype(BF)
    dn = mm_t(dqkv[...], wqkv_ref[...]) * gain
    normed = cen * rstd
    d = rstd * (dn - jnp.mean(dn, axis=1, keepdims=True) - normed * jnp.mean(dn * normed, axis=1, keepdims=True))
    d = d.astype(BF)
    for ref, at in zip(d_refs, starts):
        ref[...] = d[at:at + ref.shape[0]]


def window_call(pieces, metas, flags, gain, wqkv, wproj, prev, parts):
    width = wproj.shape[0]
    head = width // HEADS
    pair = 2 * head
    sizes = [p.shape[1] for p in pieces]
    cells = sum(sizes)
    deep = 4 * width // parts if parts else 0
    if parts is None:
        sums = (jax.ShapeDtypeStruct((width, 3 * width), F32), jax.ShapeDtypeStruct((width, width), F32))
    else:
        sums = (jax.ShapeDtypeStruct((parts // 2, deep, width), F32),
                jax.ShapeDtypeStruct((parts // 2, deep, width), BF))
    scratch = ([pltpu.VMEM((cells, width), BF)] * 2
               + [pltpu.VMEM((cells, pair), BF)] * 4
               + [pltpu.VMEM((pair, cells), BF)] * 3
               + [pltpu.VMEM((2, cells, cells), BF)] * 2
               + [pltpu.VMEM((cells, 3 * width), BF), pltpu.VMEM((width, cells), BF)])
    if parts is not None:
        scratch.append(pltpu.VMEM((parts, deep, width), F32))
    vmem = pl.BlockSpec(memory_space=pltpu.VMEM)
    args = list(pieces) + [gain, wqkv, wproj] + (list(prev) if prev else [])
    outs = pl.pallas_call(
        functools.partial(window_kernel, head, metas, (prev is not None, parts)),
        out_shape=tuple(jax.ShapeDtypeStruct((n, width), BF) for n in sizes) + sums,
        in_specs=[pl.BlockSpec(memory_space=pltpu.SMEM)] + [vmem] * len(args),
        out_specs=[vmem] * (len(sizes) + 2),
        scratch_shapes=scratch,
        cost_estimate=pl.CostEstimate(
            flops=24 * cells * width * width + 12 * cells * cells * width,
            bytes_accessed=8 * 2**20,
            transcendentals=HEADS * cells * cells,
        ),
        compiler_params=pltpu.CompilerParams(vmem_limit_bytes=60 * 2**20),
    )(flags, *args)
    return outs[:len(sizes)], outs[-2:]


def permuted(value, axes, target):
    sizes = [lax.axis_size(a) for a in axes]
    pairs = []
    for source in range(math.prod(sizes)):
        at, rest = [], source
        for size in reversed(sizes):
            at.append(rest % size)
            rest //= size
        goal = target(*reversed(at))
        if goal is None:
            continue
        flat = 0
        for size, place in zip(sizes, goal):
            flat = flat * size + place
        pairs.append((source, flat))
    return lax.ppermute(value, tuple(axes), pairs)


def from_next(value, lat=False, lon=False):
    rows, cols = lax.axis_size("lat"), lax.axis_size("lon")

    def target(i, j):
        a, b = i - int(lat), (j - int(lon)) % cols
        return (a, b) if a >= 0 else None

    return permuted(value, ("lat", "lon"), target)


def to_next(value, lat=False, lon=False):
    rows, cols = lax.axis_size("lat"), lax.axis_size("lon")

    def target(i, j):
        a, b = i + int(lat), (j + int(lon)) % cols
        return (a, b) if a < rows else None

    return permuted(value, ("lat", "lon"), target)


def scatter_direct(value, axis, dim):
    count = lax.axis_size(axis)
    me = lax.axis_index(axis)
    share = value.shape[dim] // count
    total = lax.dynamic_slice_in_dim(value, me * share, share, dim).astype(F32)
    for step in range(1, count):
        goal = (me + step) % count
        part = lax.dynamic_slice_in_dim(value, goal * share, share, dim).astype(BF)
        got = permuted(part, (axis,), lambda i, s=step: ((i + s) % count,))
        total = total + got.astype(F32)
    return total


def scatter_bit(value, axis, bit, dim):
    me = (lax.axis_index(axis) // bit) % 2
    mine = lax.dynamic_index_in_dim(value, me, dim, keepdims=False).astype(F32)
    other = lax.dynamic_index_in_dim(value, 1 - me, dim, keepdims=False).astype(BF)
    got = permuted(other, (axis,), lambda i: (i ^ bit,))
    return mine + got.astype(F32)


def reduce_weights(keep, send, lons):
    half, deep, width = keep.shape
    got = permuted(send, ("lon",), lambda i: (i ^ 1,))
    lats = lax.axis_size("lat")
    total = (keep + got.astype(F32)).reshape(lats, lons // 2, deep, width)
    bit, left = 2, lons // 2
    while left > 1:
        total = scatter_bit(total.reshape(lats, left // 2, 2, deep, width), "lon", bit, 2)
        left //= 2
        bit *= 2
    total = scatter_direct(total.reshape(lats, deep, width), "dp", 2)
    return scatter_direct(total, "lat", 0)[0]


def per_device(hidden_in, grad_out, norm_gain, w_qkv, w_proj):
    samples, lat_rows, lon_cols, width = hidden_in.shape
    half = WIN // 2
    nr, nc = lat_rows // WIN, lon_cols // WIN
    short = half + (-half) % 16
    wide = WIN + (-WIN) % 16
    gain = norm_gain.reshape(1, width)
    lons = lax.axis_size("lon")
    parts = lax.axis_size("lat") * lons
    if lons & (lons - 1) or lons < 2:
        raise ValueError("lon size")

    def pieces_of(x, c):
        def piece(rows_at, cols_at, n, pad_to, rows=half):
            cuts = [v[:, rows_at:rows_at + rows, cols_at:cols_at + n] for v in (x, c)]
            return jnp.pad(jnp.stack(cuts), ((0, 0), (0, 0), (0, 0), (0, pad_to - n), (0, 0)))
        return piece

    at_last = lax.axis_index("lat") == lax.axis_size("lat") - 1
    flags = jnp.stack([at_last.astype(jnp.int32), lax.axis_index("lon") % 2])
    inner = [wc * WIN + SHIFT for wc in range(nc - 1)]
    edge = (nc - 1) * WIN + SHIFT
    first = pieces_of(hidden_in, grad_out)
    lat_send = [first(0, at, WIN, wide) for at in inner]
    hid, got, lat_send = lax.optimization_barrier((hidden_in, grad_out, lat_send))
    lat_in = [from_next(p, lat=True) for p in lat_send]
    piece = pieces_of(hid, got)
    lon_in = from_next(piece(0, 0, half, short, lat_rows), lon=True)
    edge_send = jnp.stack([piece(0, edge, half, short), lon_in[:, :, :half]], axis=2)
    if lat_in:
        edge_send, lat_in = lax.optimization_barrier((edge_send, lat_in))
    edge_in = from_next(edge_send, lat=True)

    order = [(b, wr, wc) for b in range(samples) for wc in range(nc) for wr in range(nr)]
    sums = None
    out = {}
    for step, (b, wr, wc) in enumerate(order):
        end = wr == nr - 1
        top = (2 * wr + 1) * half
        if wc < nc - 1:
            low = lat_in[wc] if end else piece(top + half, inner[wc], WIN, wide)
            cells = [piece(top, inner[wc], WIN, wide), low]
            metas = ((WIN, wide, False), (WIN, wide, end))
        else:
            side = lon_in[:, :, top:top + half]
            if end:
                low = [edge_in[:, :, 0], edge_in[:, :, 1]]
            else:
                low = [piece(top + half, edge, half, short), lon_in[:, :, top + half:top + WIN]]
            cells = [piece(top, edge, half, short), side] + low
            metas = ((half, short, False),) * 2 + ((half, short, end),) * 2
        cells = [p[:, b].reshape(2, -1, width) for p in cells]
        done, sums = window_call(
            cells, metas, flags, gain, w_qkv, w_proj, sums, parts if step == len(order) - 1 else None
        )
        out[b, wr, wc] = [
            d.reshape(half, pad, width)[:, :n] for d, (n, pad, _) in zip(done, metas)
        ]

    rows_out = []
    for b in range(samples):
        columns = []
        for wc in range(nc - 1):
            carried = to_next(out[b, nr - 1, wc][1], lat=True)
            own = [out[b, wr, wc][i] for wr in range(nr) for i in range(2)][:-1]
            columns.append(jnp.concatenate([carried] + own, axis=0))
        carried = to_next(out[b, nr - 1, nc - 1][2], lat=True)
        own = [out[b, wr, nc - 1][i] for wr in range(nr) for i in (0, 2)][:-1]
        columns.append(jnp.concatenate([carried] + own, axis=0))
        carried = to_next(out[b, nr - 1, nc - 1][3], lat=True, lon=True)
        own = [to_next(out[b, wr, nc - 1][i], lon=True) for wr in range(nr) for i in (1, 3)][:-1]
        columns.insert(0, jnp.concatenate([carried] + own, axis=0))
        rows_out.append(jnp.concatenate(columns, axis=1))
    returned = jnp.stack(rows_out)
    grad_in = (grad_out.astype(F32) + returned.astype(F32)).astype(BF)
    total_cells = (
        lax.axis_size("dp") * samples * lat_rows * lax.axis_size("lat") * lon_cols * lons
    )
    factor = float(total_cells) ** (-0.5)
    total = reduce_weights(sums[0], sums[1], lons).T * factor
    cut = 3 * width // parts
    return (grad_in, total[:, :cut], total[:, cut:])


def solution(mesh):
    in_specs = (P("dp", "lat", "lon", None), P("dp", "lat", "lon", None), P(), P(), P())
    out_specs = (P("dp", "lat", "lon", None), P("dp", ("lat", "lon")), P("dp", ("lat", "lon")))
    return jax.shard_map(
        per_device, mesh=mesh, in_specs=in_specs, out_specs=out_specs, check_vma=False
    )
```

time: 157 us -> 128 us (0.82)
  Pallas kernels: 67.4 us -> 57.2 us
  waiting for transfers between devices: 32 us -> 23.3 us
  other arithmetic: 18.3 us -> 10.3 us
  local copies, waits for them, and re-layouts: 10.1 us -> 8.28 us
    pallas_call x2, Pallas kernels: 67.4 us -> 57.2 us  [window_call(): pl.pallas_call(functools.partial(window_kernel, head, metas, (prev is not...]
    ppermute x14 -> x13, waiting for transfers between devices: 32 us -> 23.3 us  [permuted(): return lax.ppermute(value, tuple(axes), pairs)]
    transpose x2 -> x0, other arithmetic: 5.01 us -> none  [per_device(): gq, gp = reduce_weights(sums[0].T, sums[1].T)]
    another operation x2 -> x8, local copies, waits for them, and re-layouts: 0.18 us -> 4.67 us  [the longest x7 2.77 us: piece(): jnp.stack(cuts)]
    transpose x2 -> x0, local copies, waits for them, and re-layouts: 4.31 us -> none  [per_device(): gq, gp = reduce_weights(sums[0].T, sums[1].T)]
    squeeze x3 -> x0, local copies, waits for them, and re-layouts: 2.62 us -> none  [the longest x1 1.31 us: per_device(): dcells, gq, gp = window_call(cells[0], cells[1], valid, gain, w_qkv, w_proj)]
    squeeze x1 -> x0, other arithmetic: 2.35 us -> none  [per_device(): dcells, gq, gp = window_call(cells[0], cells[1], valid, gain, w_qkv, w_proj)]
    slice x0 -> x3, local copies, waits for them, and re-layouts: none -> 2.2 us  [the longest x2 1.25 us: per_device(): return (grad_in, total[:, :cut], total[:, cut:])]
  transfers between devices with their start and end apart: 14 -> 13, of which waited for: 6 -> 6; matrix products, arithmetic and copies ran while one was open for 6% -> 9% of each run, Pallas kernels for 21% -> 22%
where the time goes in v2:
time: 128 us; the launch traced here: 127 us
  Pallas kernels  57.2 us (45%)
  starting transfers between devices  27.2 us (21%)
  waiting for transfers between devices  23.3 us (18%)
  other arithmetic  10.3 us (8%)
  local copies, waits for them, and re-layouts  8.28 us (6%)
    pallas_call x2, Pallas kernels, window_call(): pl.pallas_call(functools.partial(window_kernel, head, metas, (prev is not...  57.2 us
    ppermute x13, starting transfers between devices, permuted(): return lax.ppermute(value, tuple(axes), pairs)  27.2 us
    ppermute x13, waiting for transfers between devices, permuted(): return lax.ppermute(value, tuple(axes), pairs)  23.3 us
    another operation x4, other arithmetic, piece(): jnp.stack(cuts)  3.79 us
    another operation x7, local copies, waits for them, and re-layouts, piece(): jnp.stack(cuts)  2.77 us
  transfers between devices with their start and end apart: 13, of which 6 were waited for; matrix products, arithmetic and copies ran while one was open for 9% of the time, Pallas kernels for 22%

profile of v2, /device:TPU:0, one launch (start us, length us, event | category | flops | bytes accessed | tf_op | source)
XLA Modules:
  0.0 127.2 jit_solution(722182281189652633)
XLA Ops:
  0.6 1.6 %slice_bitcast_fusion.5 = (bf16[1,1,15,30,384]{4,3,2,1,0:T(8,128)(2,1)S(1)}, bf16[1,1,15,30,384]{4,3,2,1,0:T(8,128)(2,1)S(1)}) fusion(bf16[1,30,60,384]{3,2,1,0:T(8,128)(2,1)} %param.6, bf16[1,30,60,384]{3,2,1,0:T(8,128)(2,1)} %param.5), kind=kLoop, calls=%fused_computation.34 | loop fusion | bytes 1382400 | tf_op jit(solution)/shard_map/stack | solution.py:268
  3.9 1.0 fusion.8
  4.9 2.4 %collective-permute-start = (bf16[2,1,30,16,384]{4,3,2,0,1:T(8,128)(2,1)}, bf16[2,1,30,16,384]{4,3,2,0,1:T(8,128)(2,1)}, u32[]{:S(2)}, u32[]{:S(2)}) collective-permute-start(bf16[2,1,30,16,384]{4,3,2,0,1:T(8,128)(2,1)} %fusion.8), channel_id=1, source_target_pairs={{0,3},{1,0},{2,1},{3,2},{4,7},{5,4},{6,5},{7,6},{8,11},{9,8},{10,9... | collective-permute-start | bytes 2211848 | tf_op jit(solution)/shard_map/ppermute | solution.py:195
  7.3 1.3 %collective-permute-start.1 = (bf16[2,1,15,32,384]{4,3,2,1,0:T(8,128)(2,1)}, bf16[2,1,15,32,384]{4,3,2,1,0:T(8,128)(2,1)}, u32[]{:S(2)}, u32[]{:S(2)}) collective-permute-start(bf16[2,1,15,32,384]{4,3,2,1,0:T(8,128)(2,1)} %fusion.6), channel_id=1, source_target_pairs={{4,0},{5,1},{6,2},{7,3},{8,4},{9,5},{10,6},{11,7},{12,8},{13,9},{1... | collective-permute-start | bytes 2211848 | tf_op jit(solution)/shard_map/ppermute | solution.py:195
  12.6 4.1 %collective-permute-done = bf16[2,1,30,16,384]{4,3,2,0,1:T(8,128)(2,1)} collective-permute-done((bf16[2,1,30,16,384]{4,3,2,0,1:T(8,128)(2,1)}, bf16[2,1,30,16,384]{4,3,2,0,1:T(8,128)(2,1)}, u32[]{:S(2)}, u32[]{:S(2)}) %collective-permute-start) | collective-permute-done | bytes 737312 | tf_op jit(solution)/shard_map/ppermute | solution.py:195
  16.6 1.9 %slice_bitcast_fusion = (bf16[2,1,1,15,16,384]{5,4,3,0,2,1:T(8,128)(2,1)S(1)}, bf16[2,1,15,16,384]{4,3,2,0,1:T(8,128)(2,1)}) fusion(bf16[2,1,30,16,384]{4,3,2,0,1:T(8,128)(2,1)} %collective-permute-done), kind=kLoop, calls=%fused_computation.27 | loop fusion | bytes 1474560 | tf_op jit(solution)/shard_map/stack | solution.py:281
  18.6 8.7 %collective-permute-done.1 = bf16[2,1,15,32,384]{4,3,2,1,0:T(8,128)(2,1)} collective-permute-done((bf16[2,1,15,32,384]{4,3,2,1,0:T(8,128)(2,1)}, bf16[2,1,15,32,384]{4,3,2,1,0:T(8,128)(2,1)}, u32[]{:S(2)}, u32[]{:S(2)}) %collective-permute-start.1) | collective-permute-done | bytes 737312 | tf_op jit(solution)/shard_map/ppermute | solution.py:195
  27.3 1.3 %collective-permute-start.2 = (bf16[2,1,2,15,16,384]{5,4,3,0,2,1:T(8,128)(2,1)S(1)}, bf16[2,1,2,15,16,384]{5,4,3,0,2,1:T(8,128)(2,1)S(1)}, u32[]{:S(2)}, u32[]{:S(2)}) collective-permute-start(bf16[2,1,2,15,16,384]{5,4,3,0,2,1:T(8,128)(2,1)S(1)} %pad_maximum_fusion), channel_id=1, source_target_pairs={{4,0},{5,1},{6,2},{7,3},{8,4},{9,5},{10,6},{11,7},{12,8},{13,9},{1... | collective-permute-start | bytes 2211848 | tf_op jit(solution)/shard_map/ppermute | solution.py:195
  29.8 28.2 %shard_map.76 = (bf16[480,384]{1,0:T(8,128)(2,1)}, bf16[480,384]{1,0:T(8,128)(2,1)}, f32[384,1152]{1,0:T(8,128)}, f32[384,384]{1,0:T(8,128)}) custom-call(s32[2]{0:T(128)} %pad_add_fusion.flag_ref, bf16[2,480,384]{2,1,0:T(8,128)(2,1)} %bitcast.69, bf16[2,480,384]{2,1,0:T(8,128)(2,1)} %bitcast.19.refs_1_, f32[1,384]{1,0:T(1,128)} %reshape.89.refs_2_.refs_4_, ...), custom_call_target="tpu_custom_call" | custom-call | flops 7644119040 | bytes 8388608 | tf_op jit(solution)/shard_map/pallas_call | solution.py:164
  59.0 29.0 %shard_map.77 = (bf16[240,384]{1,0:T(8,128)(2,1)}, bf16[240,384]{1,0:T(8,128)(2,1)}, bf16[240,384]{1,0:T(8,128)(2,1)}, bf16[240,384]{1,0:T(8,128)(2,1)}, f32[8,9...) custom-call(s32[2]{0:T(128)} %pad_add_fusion.flag_ref, bf16[2,240,384]{2,1,0:T(8,128)(2,1)} %bitcast.71, ...), custom_call_target="tpu_custom_call" | custom-call | flops 7644119040 | bytes 8388608 | tf_op jit(solution)/shard_map/pallas_call | solution.py:164
  88.0 5.3 %collective-permute-start.5 = (bf16[15,30,384]{2,1,0:T(8,128)(2,1)}, bf16[15,30,384]{2,1,0:T(8,128)(2,1)}, u32[]{:S(2)}, u32[]{:S(2)}) collective-permute-start(bf16[15,30,384]{2,1,0:T(8,128)(2,1)} %bitcast.64), channel_id=1, source_target_pairs={{0,4},{1,5},{2,6},{3,7},{4,8},{5,9},{6,10},{7,11},{8,12},{9,13},{1... | collective-permute-start | bytes 1036808 | tf_op jit(solution)/shard_map/ppermute | solution.py:195
  93.3 1.4 %convert_add_fusion = f32[8,96,384]{2,1,0:T(8,128)S(1)} fusion(f32[8,96,384]{2,1,0:T(8,128)} %get-tuple-element.31, bf16[8,96,384]{2,1,0:T(8,128)(2,1)S(1)} %collective-permute-done.7), kind=kLoop, calls=%fused_computation.9 | loop fusion | flops 589824 | bytes 2949120 | tf_op jit(solution)/shard_map/add | solution.py:243
  94.8 1.7 %collective-permute-start.8 = (bf16[4,1,96,384]{3,2,0,1:T(8,128)(2,1)S(1)}, bf16[4,1,96,384]{3,2,0,1:T(8,128)(2,1)S(1)}, u32[]{:S(2)}, u32[]{:S(2)}) collective-permute-start(bf16[4,1,96,384]{3,2,0,1:T(8,128)(2,1)S(1)} %fusion.16), channel_id=1, source_target_pairs={{0,2},{1,3},{2,0},{3,1},{4,6},{5,7},{6,4},{7,5},{8,10},{9,11},{10,... | collective-permute-start | bytes 884744 | tf_op jit(solution)/shard_map/ppermute | solution.py:195
  96.5 4.8 %collective-permute-done.5 = bf16[15,30,384]{2,1,0:T(8,128)(2,1)} collective-permute-done((bf16[15,30,384]{2,1,0:T(8,128)(2,1)}, bf16[15,30,384]{2,1,0:T(8,128)(2,1)}, u32[]{:S(2)}, u32[]{:S(2)}) %collective-permute-start.5) | collective-permute-done | bytes 345632 | tf_op jit(solution)/shard_map/ppermute | solution.py:195
  101.3 1.2 maximum_bitcast_fusion
  102.6 3.8 %collective-permute-start.3 = (bf16[15,15,384]{2,1,0:T(8,128)(2,1)S(1)}, bf16[15,15,384]{2,1,0:T(8,128)(2,1)S(1)}, u32[]{:S(2)}, u32[]{:S(2)}) collective-permute-start(bf16[15,15,384]{2,1,0:T(8,128)(2,1)S(1)} %bitcast.78), channel_id=1, source_target_pairs={{0,5},{1,6},{2,7},{3,4},{4,9},{5,10},{6,11},{7,8},{8,13},{9,14},{1... | collective-permute-start | bytes 518408 | tf_op jit(solution)/shard_map/ppermute | solution.py:195
  106.4 2.0 %collective-permute-start.4 = (bf16[15,15,384]{2,1,0:T(8,128)(2,1)S(1)}, bf16[15,15,384]{2,1,0:T(8,128)(2,1)S(1)}, u32[]{:S(2)}, u32[]{:S(2)}) collective-permute-start(bf16[15,15,384]{2,1,0:T(8,128)(2,1)S(1)} %bitcast.77), channel_id=1, source_target_pairs={{0,1},{1,2},{2,3},{3,0},{4,5},{5,6},{6,7},{7,4},{8,9},{9,10},{10,1... | collective-permute-start | bytes 518408 | tf_op jit(solution)/shard_map/ppermute | solution.py:195
  108.4 3.5 %collective-permute-start.6 = (bf16[15,15,384]{2,1,0:T(8,128)(2,1)S(1)}, bf16[15,15,384]{2,1,0:T(8,128)(2,1)S(1)}, u32[]{:S(2)}, u32[]{:S(2)}) collective-permute-start(bf16[15,15,384]{2,1,0:T(8,128)(2,1)S(1)} %bitcast.76), channel_id=1, source_target_pairs={{0,4},{1,5},{2,6},{3,7},{4,8},{5,9},{6,10},{7,11},{8,12},{9,13},{1... | collective-permute-start | bytes 518408 | tf_op jit(solution)/shard_map/ppermute | solution.py:195
  112.1 1.6 %collective-permute-start.9 = (bf16[4,96,192]{2,1,0:T(8,128)(2,1)S(1)}, bf16[4,96,192]{2,1,0:T(8,128)(2,1)S(1)}, u32[]{:S(2)}, u32[]{:S(2)}) collective-permute-start(bf16[4,96,192]{2,1,0:T(8,128)(2,1)S(1)} %fusion.17), channel_id=1, source_target_pairs={{0,16},{16,0},{1,17},{17,1},{2,18},{18,2},{3,19},{19,3},{4,20},{20... | collective-permute-start | bytes 442376 | tf_op jit(solution)/shard_map/ppermute | solution.py:195
  113.7 2.2 %collective-permute-done.6 = bf16[15,15,384]{2,1,0:T(8,128)(2,1)S(1)} collective-permute-done((bf16[15,15,384]{2,1,0:T(8,128)(2,1)S(1)}, bf16[15,15,384]{2,1,0:T(8,128)(2,1)S(1)}, u32[]{:S(2)}, u32[]{:S(2)}) %collective-permute-start.6) | collective-permute-done | bytes 172832 | tf_op jit(solution)/shard_map/ppermute | solution.py:195
  116.0 2.7 %collective-permute-done.9 = bf16[4,96,192]{2,1,0:T(8,128)(2,1)S(1)} collective-permute-done((bf16[4,96,192]{2,1,0:T(8,128)(2,1)S(1)}, bf16[4,96,192]{2,1,0:T(8,128)(2,1)S(1)}, u32[]{:S(2)}, u32[]{:S(2)}) %collective-permute-start.9) | collective-permute-done | bytes 147488 | tf_op jit(solution)/shard_map/ppermute | solution.py:195
  118.9 1.7 %collective-permute-start.10 = (bf16[1,96,192]{2,1,0:T(8,128)(2,1)S(1)}, bf16[1,96,192]{2,1,0:T(8,128)(2,1)S(1)}, u32[]{:S(2)}, u32[]{:S(2)}) collective-permute-start(bf16[1,96,192]{2,1,0:T(8,128)(2,1)S(1)} %get-tuple-element.41), channel_id=1, source_target_pairs={{0,4},{4,8},{8,12},{12,0},{1,5},{5,9},{9,13},{13,1},{2,6},{6,10},{... | collective-permute-start | bytes 110600 | tf_op jit(solution)/shard_map/ppermute | solution.py:195
  120.8 2.4 %collective-permute-start.12 = (bf16[1,96,192]{2,1,0:T(8,128)(2,1)S(1)}, bf16[1,96,192]{2,1,0:T(8,128)(2,1)S(1)}, u32[]{:S(2)}, u32[]{:S(2)}) collective-permute-start(bf16[1,96,192]{2,1,0:T(8,128)(2,1)S(1)} %get-tuple-element.42), channel_id=1, source_target_pairs={{0,12},{4,0},{8,4},{12,8},{1,13},{5,1},{9,5},{13,9},{2,14},{6,2},{... | collective-permute-start | bytes 110600 | tf_op jit(solution)/shard_map/ppermute | solution.py:195
  123.2 1.9 %add_convert_fusion = bf16[1,30,60,384]{3,2,1,0:T(8,128)(2,1)} fusion(bf16[1,30,60,384]{3,2,1,0:T(8,128)(2,1)S(1)} %copy-done, bf16[1,30,15,384]{3,2,1,0:T(8,128)(2,1)S(1)} %maximum_bitcast_fusion.2, bf16[1,30,30,384]{3,2,1,0:T(8,128)(2,1)S(1)} %maximum_bitcast_fusion, bf16[1,30,15,384]{3,2,1,0:T(8,128)(2,1)S(1)} %maximum_bitcast_fusion.1), kind=kLoop, calls=%fused_computation | loop fusion | flops 6220800 | bytes 4147200 | tf_op jit(solution)/shard_map/convert_element_type | solution.py:327
  (48 shorter events, 10.8 us)
Async XLA Ops:
  0.6 2.6 %copy-start = (bf16[1,30,60,384]{3,2,1,0:T(8,128)(2,1)S(1)}, bf16[1,30,60,384]{3,2,1,0:T(8,128)(2,1)}, u32[]{:S(2)}) copy-start(bf16[1,30,60,384]{3,2,1,0:T(8,128)(2,1)} %param.6) | copy-start | bytes 4147204
  2.2 1.7 %copy-start.1 = (bf16[1,30,60,384]{3,2,1,0:T(8,128)(2,1)S(1)}, bf16[1,30,60,384]{3,2,1,0:T(8,128)(2,1)}, u32[]{:S(2)}) copy-start(bf16[1,30,60,384]{3,2,1,0:T(8,128)(2,1)} %param.5) | copy-start | bytes 4147204
  4.9 11.7 %collective-permute-start = (bf16[2,1,30,16,384]{4,3,2,0,1:T(8,128)(2,1)}, bf16[2,1,30,16,384]{4,3,2,0,1:T(8,128)(2,1)}, u32[]{:S(2)}, u32[]{:S(2)}) collective-permute-start(bf16[2,1,30,16,384]{4,3,2,0,1:T(8,128)(2,1)} %fusion.8), channel_id=1, source_target_pairs={{0,3},{1,0},{2,1},{3,2},{4,7},{5,4},{6,5},{7,6},{8,11},{9,8},{10,9... | collective-permute-start | bytes 2211848 | tf_op jit(solution)/shard_map/ppermute | solution.py:195
  7.3 20.0 %collective-permute-start.1 = (bf16[2,1,15,32,384]{4,3,2,1,0:T(8,128)(2,1)}, bf16[2,1,15,32,384]{4,3,2,1,0:T(8,128)(2,1)}, u32[]{:S(2)}, u32[]{:S(2)}) collective-permute-start(bf16[2,1,15,32,384]{4,3,2,1,0:T(8,128)(2,1)} %fusion.6), channel_id=1, source_target_pairs={{4,0},{5,1},{6,2},{7,3},{8,4},{9,5},{10,6},{11,7},{12,8},{13,9},{1... | collective-permute-start | bytes 2211848 | tf_op jit(solution)/shard_map/ppermute | solution.py:195
  12.6 16.7 %copy-start.3 = (f32[384]{0:T(512)S(1)}, f32[384]{0:T(512)}, u32[]{:S(2)}) copy-start(f32[384]{0:T(512)} %param.7) | copy-start | bytes 4612
  27.3 30.7 %collective-permute-start.2 = (bf16[2,1,2,15,16,384]{5,4,3,0,2,1:T(8,128)(2,1)S(1)}, bf16[2,1,2,15,16,384]{5,4,3,0,2,1:T(8,128)(2,1)S(1)}, u32[]{:S(2)}, u32[]{:S(2)}) collective-permute-start(bf16[2,1,2,15,16,384]{5,4,3,0,2,1:T(8,128)(2,1)S(1)} %pad_maximum_fusion), channel_id=1, source_target_pairs={{4,0},{5,1},{6,2},{7,3},{8,4},{9,5},{10,6},{11,7},{12,8},{13,9},{1... | collective-permute-start | bytes 2211848 | tf_op jit(solution)/shard_map/ppermute | solution.py:195
  88.0 5.4 %collective-permute-start.7 = (bf16[8,96,384]{2,1,0:T(8,128)(2,1)}, bf16[8,96,384]{2,1,0:T(8,128)(2,1)S(1)}, u32[]{:S(2)}, u32[]{:S(2)}) collective-permute-start(bf16[8,96,384]{2,1,0:T(8,128)(2,1)} %get-tuple-element.32), channel_id=1, source_target_pairs={{0,1},{1,0},{2,3},{3,2},{4,5},{5,4},{6,7},{7,6},{8,9},{9,8},{10,11... | collective-permute-start | bytes 1769480 | tf_op jit(solution)/shard_map/ppermute | solution.py:195
  88.0 13.3 %collective-permute-start.5 = (bf16[15,30,384]{2,1,0:T(8,128)(2,1)}, bf16[15,30,384]{2,1,0:T(8,128)(2,1)}, u32[]{:S(2)}, u32[]{:S(2)}) collective-permute-start(bf16[15,30,384]{2,1,0:T(8,128)(2,1)} %bitcast.64), channel_id=1, source_target_pairs={{0,4},{1,5},{2,6},{3,7},{4,8},{5,9},{6,10},{7,11},{8,12},{9,13},{1... | collective-permute-start | bytes 1036808 | tf_op jit(solution)/shard_map/ppermute | solution.py:195
  94.7 13.7 %copy-start.4 = (bf16[240,384]{1,0:T(8,128)(2,1)S(1)}, bf16[240,384]{1,0:T(8,128)(2,1)}, u32[]{:S(2)}) copy-start(bf16[240,384]{1,0:T(8,128)(2,1)} %get-tuple-element.29) | copy-start | bytes 552964
  94.8 17.1 %collective-permute-start.8 = (bf16[4,1,96,384]{3,2,0,1:T(8,128)(2,1)S(1)}, bf16[4,1,96,384]{3,2,0,1:T(8,128)(2,1)S(1)}, u32[]{:S(2)}, u32[]{:S(2)}) collective-permute-start(bf16[4,1,96,384]{3,2,0,1:T(8,128)(2,1)S(1)} %fusion.16), channel_id=1, source_target_pairs={{0,2},{1,3},{2,0},{3,1},{4,6},{5,7},{6,4},{7,5},{8,10},{9,11},{10,... | collective-permute-start | bytes 884744 | tf_op jit(solution)/shard_map/ppermute | solution.py:195
  96.5 6.0 %copy-start.6 = (bf16[240,384]{1,0:T(8,128)(2,1)S(1)}, bf16[240,384]{1,0:T(8,128)(2,1)}, u32[]{:S(2)}) copy-start(bf16[240,384]{1,0:T(8,128)(2,1)} %get-tuple-element.25) | copy-start | bytes 552964
  96.5 9.9 %copy-start.5 = (bf16[240,384]{1,0:T(8,128)(2,1)S(1)}, bf16[240,384]{1,0:T(8,128)(2,1)}, u32[]{:S(2)}) copy-start(bf16[240,384]{1,0:T(8,128)(2,1)} %get-tuple-element.26) | copy-start | bytes 552964
  102.5 13.4 %copy-start.2 = (bf16[240,384]{1,0:T(8,128)(2,1)S(1)}, bf16[240,384]{1,0:T(8,128)(2,1)}, u32[]{:S(2)}) copy-start(bf16[240,384]{1,0:T(8,128)(2,1)} %get-tuple-element.30) | copy-start | bytes 552964
  102.6 11.1 %collective-permute-start.3 = (bf16[15,15,384]{2,1,0:T(8,128)(2,1)S(1)}, bf16[15,15,384]{2,1,0:T(8,128)(2,1)S(1)}, u32[]{:S(2)}, u32[]{:S(2)}) collective-permute-start(bf16[15,15,384]{2,1,0:T(8,128)(2,1)S(1)} %bitcast.78), channel_id=1, source_target_pairs={{0,5},{1,6},{2,7},{3,4},{4,9},{5,10},{6,11},{7,8},{8,13},{9,14},{1... | collective-permute-start | bytes 518408 | tf_op jit(solution)/shard_map/ppermute | solution.py:195
  106.4 7.3 %collective-permute-start.4 = (bf16[15,15,384]{2,1,0:T(8,128)(2,1)S(1)}, bf16[15,15,384]{2,1,0:T(8,128)(2,1)S(1)}, u32[]{:S(2)}, u32[]{:S(2)}) collective-permute-start(bf16[15,15,384]{2,1,0:T(8,128)(2,1)S(1)} %bitcast.77), channel_id=1, source_target_pairs={{0,1},{1,2},{2,3},{3,0},{4,5},{5,6},{6,7},{7,4},{8,9},{9,10},{10,1... | collective-permute-start | bytes 518408 | tf_op jit(solution)/shard_map/ppermute | solution.py:195
  108.4 7.5 %collective-permute-start.6 = (bf16[15,15,384]{2,1,0:T(8,128)(2,1)S(1)}, bf16[15,15,384]{2,1,0:T(8,128)(2,1)S(1)}, u32[]{:S(2)}, u32[]{:S(2)}) collective-permute-start(bf16[15,15,384]{2,1,0:T(8,128)(2,1)S(1)} %bitcast.76), channel_id=1, source_target_pairs={{0,4},{1,5},{2,6},{3,7},{4,8},{5,9},{6,10},{7,11},{8,12},{9,13},{1... | collective-permute-start | bytes 518408 | tf_op jit(solution)/shard_map/ppermute | solution.py:195
  112.1 6.6 %collective-permute-start.9 = (bf16[4,96,192]{2,1,0:T(8,128)(2,1)S(1)}, bf16[4,96,192]{2,1,0:T(8,128)(2,1)S(1)}, u32[]{:S(2)}, u32[]{:S(2)}) collective-permute-start(bf16[4,96,192]{2,1,0:T(8,128)(2,1)S(1)} %fusion.17), channel_id=1, source_target_pairs={{0,16},{16,0},{1,17},{17,1},{2,18},{18,2},{3,19},{19,3},{4,20},{20... | collective-permute-start | bytes 442376 | tf_op jit(solution)/shard_map/ppermute | solution.py:195
  118.9 6.2 %collective-permute-start.10 = (bf16[1,96,192]{2,1,0:T(8,128)(2,1)S(1)}, bf16[1,96,192]{2,1,0:T(8,128)(2,1)S(1)}, u32[]{:S(2)}, u32[]{:S(2)}) collective-permute-start(bf16[1,96,192]{2,1,0:T(8,128)(2,1)S(1)} %get-tuple-element.41), channel_id=1, source_target_pairs={{0,4},{4,8},{8,12},{12,0},{1,5},{5,9},{9,13},{13,1},{2,6},{6,10},{... | collective-permute-start | bytes 110600 | tf_op jit(solution)/shard_map/ppermute | solution.py:195
  120.6 5.4 %collective-permute-start.11 = (bf16[1,96,192]{2,1,0:T(8,128)(2,1)S(1)}, bf16[1,96,192]{2,1,0:T(8,128)(2,1)S(1)}, u32[]{:S(2)}, u32[]{:S(2)}) collective-permute-start(bf16[1,96,192]{2,1,0:T(8,128)(2,1)S(1)} %get-tuple-element.43), channel_id=1, source_target_pairs={{0,8},{4,12},{8,0},{12,4},{1,9},{5,13},{9,1},{13,5},{2,10},{6,14},... | collective-permute-start | bytes 110600 | tf_op jit(solution)/shard_map/ppermute | solution.py:195
  120.8 5.1 %collective-permute-start.12 = (bf16[1,96,192]{2,1,0:T(8,128)(2,1)S(1)}, bf16[1,96,192]{2,1,0:T(8,128)(2,1)S(1)}, u32[]{:S(2)}, u32[]{:S(2)}) collective-permute-start(bf16[1,96,192]{2,1,0:T(8,128)(2,1)S(1)} %get-tuple-element.42), channel_id=1, source_target_pairs={{0,12},{4,0},{8,4},{12,8},{1,13},{5,1},{9,5},{13,9},{2,14},{6,2},{... | collective-permute-start | bytes 110600 | tf_op jit(solution)/shard_map/ppermute | solution.py:195

commit v3 on v2

--- a/solution.py
+++ b/solution.py
@@ -23,7 +23,7 @@
 def blocks_of(n, step):
     return [(at, min(step, n - at)) for at in range(0, n, step)]
 
-def window_kernel(head, metas, split, flag_ref, *refs):
+def window_kernel(head, metas, split, *refs):
     count = len(metas)
     pieces, refs = refs[:count], refs[count:]
     gain_ref, wqkv_ref, wproj_ref = refs[:3]
@@ -43,18 +43,20 @@
         starts.append(at)
         c_ref[at:at + p.shape[1]] = p[1]
         at += p.shape[1]
-    lastf = flag_ref[0].astype(F32)
-    oks = []
-    for p, (n, pad, gone) in zip(pieces, metas):
+    odd = lax.rem(lax.axis_index("lon"), 2)
+    packed = jnp.where((lax.axis_index("lat") == lax.axis_size("lat") - 1) & (odd == 0), 1.0, 0.0)
+    oks, seconds = [], []
+    for p, (n, pad, other) in zip(pieces, metas):
         place = lax.broadcasted_iota(jnp.int32, (p.shape[1], pair), 0)
-        ok = jnp.where(lax.rem(place, pad) < n, 1.0, 0.0)
-        oks.append(ok * (1.0 - lastf) if gone else ok)
+        oks.append(jnp.where(lax.rem(place, pad) < n, 1.0, 0.0))
+        seconds.append(jnp.full((p.shape[1], pair), packed if other else 0.0, F32))
     valid_col = jnp.concatenate(oks, axis=0)
+    second = jnp.concatenate(seconds, axis=0)
     x = jnp.concatenate([p[0] for p in pieces], axis=0).astype(F32)
     mean = jnp.mean(x, axis=1, keepdims=True)
     cen = x - mean
     rstd = lax.rsqrt(jnp.mean(cen * cen, axis=1, keepdims=True) + EPSILON)
-    gain = gain_ref[...]
+    gain = gain_ref[...][None]
     nl[...] = (cen * rstd * gain).astype(BF)
     qb = blocks_of(cells, cells)
 
@@ -76,10 +78,12 @@
             own = (lane >= head) if h else (lane < head)
             own_r = (row >= head) if h else (row < head)
             aug = 0 if h else head
-            bias = jnp.where(lane == aug, (valid_col - 1.0) * 30000.0, 0.0).astype(BF)
+            seen = jnp.where(lane == aug, valid_col * (1.0 - second), valid_col * second)
+            two = (lane == aug) | (lane == aug + 1)
+            bias = jnp.where(two, (seen - 1.0) * 30000.0, 0.0).astype(BF)
+            group = jnp.where(lane == aug, 1.0 - second, second)
             kk = jnp.where(own, k_s[...], bias)
-            qq = jnp.where(own, q_s[...], jnp.where(lane == aug, 1.0, 0.0).astype(BF))
-            two = (lane == aug) | (lane == aug + 1)
+            qq = jnp.where(own, q_s[...], jnp.where(two, group, 0.0).astype(BF))
             vv = jnp.where(own, v_s[...], jnp.where(two, 1.0, 0.0).astype(BF))
             vvT = jnp.where(own_r, vT[...], jnp.where(row == aug, 1.0, 0.0).astype(BF))
             for at, n in qb:
@@ -128,7 +132,7 @@
         for i in range(parts):
             joined[i, :dq_rows] = gqT[i * dq_rows:(i + 1) * dq_rows]
             joined[i, dq_rows:] = gpT[i * dp_rows:(i + 1) * dp_rows]
-        me = flag_ref[1]
+        me = odd
         for i in range(parts // 2):
             gq_ref[i] = joined[2 * i + me]
             gp_ref[i] = joined[2 * i + 1 - me].astype(BF)
@@ -140,7 +144,7 @@
         ref[...] = d[at:at + ref.shape[0]]
 
 
-def window_call(pieces, metas, flags, gain, wqkv, wproj, prev, parts):
+def window_call(pieces, metas, gain, wqkv, wproj, prev, parts):
     width = wproj.shape[0]
     head = width // HEADS
     pair = 2 * head
@@ -164,7 +168,7 @@
     outs = pl.pallas_call(
         functools.partial(window_kernel, head, metas, (prev is not None, parts)),
         out_shape=tuple(jax.ShapeDtypeStruct((n, width), BF) for n in sizes) + sums,
-        in_specs=[pl.BlockSpec(memory_space=pltpu.SMEM)] + [vmem] * len(args),
+        in_specs=[vmem] * len(args),
         out_specs=[vmem] * (len(sizes) + 2),
         scratch_shapes=scratch,
         cost_estimate=pl.CostEstimate(
@@ -173,7 +177,7 @@
             transcendentals=HEADS * cells * cells,
         ),
         compiler_params=pltpu.CompilerParams(vmem_limit_bytes=60 * 2**20),
-    )(flags, *args)
+    )(*args)
     return outs[:len(sizes)], outs[-2:]
 
 
@@ -195,24 +199,24 @@
     return lax.ppermute(value, tuple(axes), pairs)
 
 
-def from_next(value, lat=False, lon=False):
-    rows, cols = lax.axis_size("lat"), lax.axis_size("lon")
-
-    def target(i, j):
-        a, b = i - int(lat), (j - int(lon)) % cols
-        return (a, b) if a >= 0 else None
-
-    return permuted(value, ("lat", "lon"), target)
-
-
-def to_next(value, lat=False, lon=False):
-    rows, cols = lax.axis_size("lat"), lax.axis_size("lon")
-
-    def target(i, j):
-        a, b = i + int(lat), (j + int(lon)) % cols
-        return (a, b) if a < rows else None
-
-    return permuted(value, ("lat", "lon"), target)
+def shared(value, back=False):
+    lats, lons = lax.axis_size("lat"), lax.axis_size("lon")
+    pairs = []
+    for i in range(lats):
+        for j in range(lons):
+            if j % 2 == 0:
+                goal = (i - 1, j) if i > 0 else None
+            else:
+                goal = (i + 1, j) if i < lats - 1 else (i, j - 1)
+            if goal is not None:
+                pair = (i * lons + j, goal[0] * lons + goal[1])
+                pairs.append(pair[::-1] if back else pair)
+    return lax.ppermute(value, ("lat", "lon"), pairs)
+
+
+def along_lon(value, step):
+    count = lax.axis_size("lon")
+    return lax.ppermute(value, "lon", [(j, (j + step) % count) for j in range(count)])
 
 
 def scatter_direct(value, axis, dim):
@@ -256,72 +260,91 @@
     nr, nc = lat_rows // WIN, lon_cols // WIN
     short = half + (-half) % 16
     wide = WIN + (-WIN) % 16
-    gain = norm_gain.reshape(1, width)
     lons = lax.axis_size("lon")
     parts = lax.axis_size("lat") * lons
     if lons & (lons - 1) or lons < 2:
         raise ValueError("lon size")
 
+    odd = lax.axis_index("lon") % 2
+    idle = (lax.axis_index("lat") == 0) & (odd == 1)
+    end = lat_rows - half
+    own_at, sent_at = jnp.where(odd == 1, 0, end), jnp.where(odd == 1, end, 0)
+
     def pieces_of(x, c):
         def piece(rows_at, cols_at, n, pad_to, rows=half):
-            cuts = [v[:, rows_at:rows_at + rows, cols_at:cols_at + n] for v in (x, c)]
+            cuts = [
+                lax.dynamic_slice_in_dim(v[:, :, cols_at:cols_at + n], rows_at, rows, 1) for v in (x, c)
+            ]
             return jnp.pad(jnp.stack(cuts), ((0, 0), (0, 0), (0, 0), (0, pad_to - n), (0, 0)))
         return piece
 
-    at_last = lax.axis_index("lat") == lax.axis_size("lat") - 1
-    flags = jnp.stack([at_last.astype(jnp.int32), lax.axis_index("lon") % 2])
+    def cleared(value):
+        return jnp.where(idle, jnp.zeros_like(value), value)
+
     inner = [wc * WIN + SHIFT for wc in range(nc - 1)]
     edge = (nc - 1) * WIN + SHIFT
     first = pieces_of(hidden_in, grad_out)
-    lat_send = [first(0, at, WIN, wide) for at in inner]
-    hid, got, lat_send = lax.optimization_barrier((hidden_in, grad_out, lat_send))
-    lat_in = [from_next(p, lat=True) for p in lat_send]
-    piece = pieces_of(hid, got)
-    lon_in = from_next(piece(0, 0, half, short, lat_rows), lon=True)
-    edge_send = jnp.stack([piece(0, edge, half, short), lon_in[:, :, :half]], axis=2)
-    if lat_in:
-        edge_send, lat_in = lax.optimization_barrier((edge_send, lat_in))
-    edge_in = from_next(edge_send, lat=True)
+    sent = [first(sent_at, at, WIN, wide) for at in inner]
+    hid, cot, sent = lax.optimization_barrier((hidden_in, grad_out, sent))
+    inner_in = [shared(p) for p in sent]
+    piece = pieces_of(hid, cot)
+    lon_in = along_lon(piece(0, 0, half, short, lat_rows), -1)
+    own_inner = [cleared(piece(own_at, at, WIN, wide)) for at in inner]
+    own_edge = cleared(piece(own_at, edge, half, short))
+
+    def side(at):
+        return lax.dynamic_slice_in_dim(lon_in, at, half, 2)
+
+    own_side = cleared(side(own_at))
+    edge_sent = jnp.stack([piece(sent_at, edge, half, short), side(sent_at)], axis=2)
+    if inner_in:
+        edge_sent, inner_in = lax.optimization_barrier((edge_sent, inner_in))
+    edge_in = shared(edge_sent)
 
     order = [(b, wr, wc) for b in range(samples) for wc in range(nc) for wr in range(nr)]
     sums = None
     out = {}
     for step, (b, wr, wc) in enumerate(order):
-        end = wr == nr - 1
         top = (2 * wr + 1) * half
-        if wc < nc - 1:
-            low = lat_in[wc] if end else piece(top + half, inner[wc], WIN, wide)
-            cells = [piece(top, inner[wc], WIN, wide), low]
-            metas = ((WIN, wide, False), (WIN, wide, end))
+        if wr < nr - 1 and wc < nc - 1:
+            cells = [piece(top + i * half, inner[wc], WIN, wide) for i in range(2)]
+            metas = ((WIN, wide, False),) * 2
+        elif wr < nr - 1:
+            cells = [
+                f(top + i * half)
+                for i in range(2)
+                for f in (lambda at: piece(at, edge, half, short), side)
+            ]
+            metas = ((half, short, False),) * 4
+        elif wc < nc - 1:
+            cells = [own_inner[wc], inner_in[wc]]
+            metas = ((WIN, wide, False), (WIN, wide, True))
         else:
-            side = lon_in[:, :, top:top + half]
-            if end:
-                low = [edge_in[:, :, 0], edge_in[:, :, 1]]
-            else:
-                low = [piece(top + half, edge, half, short), lon_in[:, :, top + half:top + WIN]]
-            cells = [piece(top, edge, half, short), side] + low
-            metas = ((half, short, False),) * 2 + ((half, short, end),) * 2
+            cells = [own_edge, own_side, edge_in[:, :, 0], edge_in[:, :, 1]]
+            metas = ((half, short, False),) * 2 + ((half, short, True),) * 2
         cells = [p[:, b].reshape(2, -1, width) for p in cells]
         done, sums = window_call(
-            cells, metas, flags, gain, w_qkv, w_proj, sums, parts if step == len(order) - 1 else None
+            cells, metas, norm_gain, w_qkv, w_proj, sums, parts if step == len(order) - 1 else None
         )
-        out[b, wr, wc] = [
-            d.reshape(half, pad, width)[:, :n] for d, (n, pad, _) in zip(done, metas)
-        ]
+        out[b, wr, wc] = [d.reshape(half, pad, width) for d, (n, pad, _) in zip(done, metas)]
 
     rows_out = []
     for b in range(samples):
+        def stacked(own, back, between):
+            upper = jnp.where(odd == 1, own, back)
+            lower = jnp.where(odd == 1, back, own)
+            return jnp.concatenate([upper] + between + [lower], axis=0)
+
         columns = []
         for wc in range(nc - 1):
-            carried = to_next(out[b, nr - 1, wc][1], lat=True)
-            own = [out[b, wr, wc][i] for wr in range(nr) for i in range(2)][:-1]
-            columns.append(jnp.concatenate([carried] + own, axis=0))
-        carried = to_next(out[b, nr - 1, nc - 1][2], lat=True)
-        own = [out[b, wr, nc - 1][i] for wr in range(nr) for i in (0, 2)][:-1]
-        columns.append(jnp.concatenate([carried] + own, axis=0))
-        carried = to_next(out[b, nr - 1, nc - 1][3], lat=True, lon=True)
-        own = [to_next(out[b, wr, nc - 1][i], lon=True) for wr in range(nr) for i in (1, 3)][:-1]
-        columns.insert(0, jnp.concatenate([carried] + own, axis=0))
+            own, other = out[b, nr - 1, wc]
+            between = [out[b, wr, wc][i][:, :WIN] for wr in range(nr - 1) for i in range(2)]
+            columns.append(stacked(own[:, :WIN], shared(other, back=True)[:, :WIN], between))
+        own, own_lon, other, other_lon = out[b, nr - 1, nc - 1]
+        back = shared(jnp.stack([other, other_lon]), back=True)
+        between = [[out[b, wr, nc - 1][i] for wr in range(nr - 1) for i in (k, k + 2)] for k in range(2)]
+        columns.append(stacked(own, back[0], between[0])[:, :half])
+        columns.insert(0, along_lon(stacked(own_lon, back[1], between[1]), 1)[:, :half])
         rows_out.append(jnp.concatenate(columns, axis=1))
     returned = jnp.stack(rows_out)
     grad_in = (grad_out.astype(F32) + returned.astype(F32)).astype(BF)

time: 128 us -> 121 us (0.945)
  waiting for transfers between devices: 23.3 us -> 17.7 us
  local copies, waits for them, and re-layouts: 8.28 us -> 13.1 us
  starting transfers between devices: 27.2 us -> 22.5 us
  other arithmetic: 10.3 us -> 8.59 us
    ppermute x13 -> x6, starting transfers between devices: 27.2 us -> 8.54 us  [permuted(): return lax.ppermute(value, tuple(axes), pairs)]
    ppermute x13 -> x6, waiting for transfers between devices: 23.3 us -> 5.27 us  [permuted(): return lax.ppermute(value, tuple(axes), pairs)]
    ppermute x0 -> x6, starting transfers between devices: none -> 13.9 us  [the longest x4 11 us: shared(): return lax.ppermute(value, ('lat', 'lon'), pairs)]
    ppermute x0 -> x6, waiting for transfers between devices: none -> 12.5 us  [the longest x4 6.53 us: shared(): return lax.ppermute(value, ('lat', 'lon'), pairs)]
    slice x1 -> x5, local copies, waits for them, and re-layouts: 0.95 us -> 7 us  [the longest x4 6.06 us: piece(): v[:, :, cols_at:cols_at + n]]
    select_n x0 -> x4, other arithmetic: none -> 2.06 us  [the longest x2 1.9 us: cleared(): return jnp.where(idle, jnp.zeros_like(value), value)]
    another operation x1 -> x0, local copies, waits for them, and re-layouts: 1.91 us -> none  [per_device(): jnp.stack([piece(0, edge, half, short), lon_in[:, :, :half]], axis=2)]
    another operation x4 -> x2, other arithmetic: 3.79 us -> 1.99 us  [piece(): jnp.stack(cuts)]
  transfers between devices with their start and end apart: 13 -> 12, of which waited for: 6 -> 8; matrix products, arithmetic and copies ran while one was open for 9% -> 9% of each run, Pallas kernels for 22% -> 48%
where the time goes in v3:
time: 121 us
  Pallas kernels  57.6 us (48%)
  starting transfers between devices  22.5 us (19%)
  waiting for transfers between devices  17.7 us (15%)
  local copies, waits for them, and re-layouts  13.1 us (11%)
  other arithmetic  8.59 us (7%)
    pallas_call x2, Pallas kernels, window_call(): pl.pallas_call(functools.partial(window_kernel, head, metas, (prev is not...  57.6 us
    ppermute x4, starting transfers between devices, shared(): return lax.ppermute(value, ('lat', 'lon'), pairs)  11 us
    ppermute x6, starting transfers between devices, permuted(): return lax.ppermute(value, tuple(axes), pairs)  8.54 us
    ppermute x4, waiting for transfers between devices, shared(): return lax.ppermute(value, ('lat', 'lon'), pairs)  6.53 us
    slice x4, local copies, waits for them, and re-layouts, piece(): v[:, :, cols_at:cols_at + n]  6.06 us
    ppermute x2, waiting for transfers between devices, along_lon(): lax.ppermute(value, 'lon', [(j, (j + step) % count) for j in range(count)])  5.94 us
    ppermute x6, waiting for transfers between devices, permuted(): return lax.ppermute(value, tuple(axes), pairs)  5.27 us
    another operation x7, local copies, waits for them, and re-layouts, piece(): jnp.stack(cuts)  3.58 us
  transfers between devices with their start and end apart: 12, of which 8 were waited for; matrix products, arithmetic and copies ran while one was open for 9% of the time, Pallas kernels for 48%

profile of v3, /device:TPU:0, one launch (start us, length us, event | category | flops | bytes accessed | tf_op | source)
XLA Modules:
  0.0 120.5 jit_solution(9339830623342668277)
XLA Ops:
  0.7 2.5 %slice.56 = bf16[1,30,30,384]{3,2,1,0:T(8,128)(2,1)} slice(bf16[1,30,60,384]{3,2,1,0:T(8,128)(2,1)} %param.5), slice={[0:1], [0:30], [15:45], [0:384]} | slice | bytes 1382400 | tf_op jit(solution)/shard_map/slice | solution.py:276
  3.1 1.2 slice.57
  4.3 1.3 %dynamic-slice_bitcast_fusion.3 = (bf16[1,1,15,30,384]{4,3,2,0,1:T(8,128)(2,1)S(1)}, bf16[1,1,15,30,384]{4,3,2,0,1:T(8,128)(2,1)S(1)}) fusion(bf16[1,30,30,384]{3,2,1,0:T(8,128)(2,1)} %slice.57, s32[]{:T(128)S(6)} %select_n.128, bf16[1,30,30,384]{3,2,1,0:T(8,128)(2,1)} %slice.56), kind=kLoop, calls=%fused_computation.41 | loop fusion | bytes 1382404 | tf_op jit(solution)/shard_map/stack | solution.py:278
  8.6 2.4 %collective-permute-start = (bf16[2,1,30,16,384]{4,3,2,1,0:T(8,128)(2,1)}, bf16[2,1,30,16,384]{4,3,2,1,0:T(8,128)(2,1)}, u32[]{:S(2)}, u32[]{:S(2)}) collective-permute-start(bf16[2,1,30,16,384]{4,3,2,1,0:T(8,128)(2,1)} %fusion.9), channel_id=1, source_target_pairs={{0,3},{1,0},{2,1},{3,2},{4,7},{5,4},{6,5},{7,6},{8,11},{9,8},{10,9... | collective-permute-start | bytes 2211848 | tf_op jit(solution)/shard_map/ppermute | solution.py:219
  11.0 1.3 %collective-permute-start.1 = (bf16[2,1,15,32,384]{4,3,2,0,1:T(8,128)(2,1)}, bf16[2,1,15,32,384]{4,3,2,0,1:T(8,128)(2,1)}, u32[]{:S(2)}, u32[]{:S(2)}) collective-permute-start(bf16[2,1,15,32,384]{4,3,2,0,1:T(8,128)(2,1)} %fusion.6), channel_id=1, source_target_pairs={{1,5},{3,7},{4,0},{5,9},{6,2},{7,11},{8,4},{9,13},{10,6},{11,15},{... | collective-permute-start | bytes 2211848 | tf_op jit(solution)/shard_map/ppermute | solution.py:214
  12.3 1.2 slice.65
  13.5 1.2 slice.64
  14.7 1.2 dynamic-slice_bitcast_fusion.6
  17.4 2.9 %collective-permute-done = bf16[2,1,30,16,384]{4,3,2,1,0:T(8,128)(2,1)} collective-permute-done((bf16[2,1,30,16,384]{4,3,2,1,0:T(8,128)(2,1)}, bf16[2,1,30,16,384]{4,3,2,1,0:T(8,128)(2,1)}, u32[]{:S(2)}, u32[]{:S(2)}) %collective-permute-start) | collective-permute-done | bytes 737312 | tf_op jit(solution)/shard_map/ppermute | solution.py:219
  20.3 1.9 %dynamic-slice_bitcast_fusion.2 = (bf16[2,1,1,15,16,384]{5,4,3,0,2,1:T(8,128)(2,1)S(1)}, bf16[2,1,15,16,384]{4,3,2,1,0:T(8,128)(2,1)}) fusion(bf16[2,1,30,16,384]{4,3,2,1,0:T(8,128)(2,1)} %collective-permute-done, s32[]{:T(128)S(6)} %select_n.128, s32[]{:T(128)S(6)} %select_n.129, pred[]{:T(512)S(6)} %and.37), kind=kLoop, calls=%fused_computation.37 | loop fusion | flops 184320 | bytes 1474569 | tf_op jit(solution)/shard_map/stack | solution.py:299
  22.3 2.4 %collective-permute-done.1 = bf16[2,1,15,32,384]{4,3,2,0,1:T(8,128)(2,1)} collective-permute-done((bf16[2,1,15,32,384]{4,3,2,0,1:T(8,128)(2,1)}, bf16[2,1,15,32,384]{4,3,2,0,1:T(8,128)(2,1)}, u32[]{:S(2)}, u32[]{:S(2)}) %collective-permute-start.1) | collective-permute-done | bytes 737312 | tf_op jit(solution)/shard_map/ppermute | solution.py:214
  24.7 1.5 %collective-permute-start.2 = (bf16[2,1,2,15,16,384]{5,4,3,0,2,1:T(8,128)(2,1)S(1)}, bf16[2,1,2,15,16,384]{5,4,3,0,2,1:T(8,128)(2,1)S(1)}, u32[]{:S(2)}, u32[]{:S(2)}) collective-permute-start(bf16[2,1,2,15,16,384]{5,4,3,0,2,1:T(8,128)(2,1)S(1)} %pad_maximum_fusion), channel_id=1, source_target_pairs={{1,5},{3,7},{4,0},{5,9},{6,2},{7,11},{8,4},{9,13},{10,6},{11,15},{... | collective-permute-start | bytes 2211848 | tf_op jit(solution)/shard_map/ppermute | solution.py:214
  27.0 28.3 %shard_map.76 = (bf16[480,384]{1,0:T(8,128)(2,1)}, bf16[480,384]{1,0:T(8,128)(2,1)}, f32[384,1152]{1,0:T(8,128)}, f32[384,384]{1,0:T(8,128)}) custom-call(bf16[2,480,384]{2,1,0:T(8,128)(2,1)} %bitcast.73, bf16[2,480,384]{2,1,0:T(8,128)(2,1)} %bitcast.17.refs_1_, f32[384]{0:T(512)} %refs_4_.3, bf16[384,1152]{1,0:T(8,128)(2,1)} %refs_5_.1, ...), custom_call_target="tpu_custom_call" | custom-call | flops 7644119040 | bytes 8388608 | tf_op jit(solution)/shard_map/pallas_call | solution.py:168
  55.3 4.8 %collective-permute-start.5 = (bf16[15,32,384]{2,1,0:T(8,128)(2,1)}, bf16[15,32,384]{2,1,0:T(8,128)(2,1)S(1)}, u32[]{:S(2)}, u32[]{:S(2)}) collective-permute-start(bf16[15,32,384]{2,1,0:T(8,128)(2,1)} %bitcast.83), channel_id=1, source_target_pairs={{5,1},{7,3},{0,4},{9,5},{2,6},{11,7},{4,8},{13,9},{6,10},{15,11},{... | collective-permute-start | bytes 1105928 | tf_op jit(solution)/shard_map/ppermute | solution.py:214
  61.0 29.3 %shard_map.77 = (bf16[240,384]{1,0:T(8,128)(2,1)}, bf16[240,384]{1,0:T(8,128)(2,1)}, bf16[240,384]{1,0:T(8,128)(2,1)}, bf16[240,384]{1,0:T(8,128)(2,1)}, f32[8,9...) custom-call(bf16[2,240,384]{2,1,0:T(8,128)(2,1)} %bitcast.74, bf16[2,240,384]{2,1,0:T(8,128)(2,1)} %bitcast.76, ...), custom_call_target="tpu_custom_call" | custom-call | flops 7644119040 | bytes 8388608 | tf_op jit(solution)/shard_map/pallas_call | solution.py:168
  91.5 3.5 %collective-permute-start.3 = (bf16[2,15,16,384]{3,2,1,0:T(8,128)(2,1)S(1)}, bf16[2,15,16,384]{3,2,1,0:T(8,128)(2,1)S(1)}, u32[]{:S(2)}, u32[]{:S(2)}) collective-permute-start(bf16[2,15,16,384]{3,2,1,0:T(8,128)(2,1)S(1)} %pad_maximum_fusion.2), channel_id=1, source_target_pairs={{5,1},{7,3},{0,4},{9,5},{2,6},{11,7},{4,8},{13,9},{6,10},{15,11},{... | collective-permute-start | bytes 1105928 | tf_op jit(solution)/shard_map/ppermute | solution.py:214
  95.9 4.2 %collective-permute-done.3 = bf16[2,15,16,384]{3,2,1,0:T(8,128)(2,1)S(1)} collective-permute-done((bf16[2,15,16,384]{3,2,1,0:T(8,128)(2,1)S(1)}, bf16[2,15,16,384]{3,2,1,0:T(8,128)(2,1)S(1)}, u32[]{:S(2)}, u32[]{:S(2)}) %collective-permute-start.3) | collective-permute-done | bytes 368672 | tf_op jit(solution)/shard_map/ppermute | solution.py:214
  100.7 1.7 %collective-permute-done.7 = bf16[4,1,96,384]{3,2,0,1:T(8,128)(2,1)S(1)} collective-permute-done((bf16[4,1,96,384]{3,2,0,1:T(8,128)(2,1)S(1)}, bf16[4,1,96,384]{3,2,0,1:T(8,128)(2,1)S(1)}, u32[]{:S(2)}, u32[]{:S(2)}) %collective-permute-start.7) | collective-permute-done | bytes 294944 | tf_op jit(solution)/shard_map/ppermute | solution.py:199
  102.6 1.6 %collective-permute-start.8 = (bf16[4,96,192]{2,1,0:T(8,128)(2,1)S(1)}, bf16[4,96,192]{2,1,0:T(8,128)(2,1)S(1)}, u32[]{:S(2)}, u32[]{:S(2)}) collective-permute-start(bf16[4,96,192]{2,1,0:T(8,128)(2,1)S(1)} %fusion.20), channel_id=1, source_target_pairs={{0,16},{16,0},{1,17},{17,1},{2,18},{18,2},{3,19},{19,3},{4,20},{20... | collective-permute-start | bytes 442376 | tf_op jit(solution)/shard_map/ppermute | solution.py:199
  104.2 3.0 %collective-permute-done.4 = bf16[30,16,384]{2,1,0:T(8,128)(2,1)S(1)} collective-permute-done((bf16[30,16,384]{2,1,0:T(8,128)(2,1)S(1)}, bf16[30,16,384]{2,1,0:T(8,128)(2,1)S(1)}, u32[]{:S(2)}, u32[]{:S(2)}) %collective-permute-start.4) | collective-permute-done | bytes 368672 | tf_op jit(solution)/shard_map/ppermute | solution.py:219
  108.6 4.3 %collective-permute-start.10 = (bf16[1,96,192]{2,1,0:T(8,128)(2,1)S(1)}, bf16[1,96,192]{2,1,0:T(8,128)(2,1)S(1)}, u32[]{:S(2)}, u32[]{:S(2)}) collective-permute-start(bf16[1,96,192]{2,1,0:T(8,128)(2,1)S(1)} %get-tuple-element.49), channel_id=1, source_target_pairs={{0,8},{4,12},{8,0},{12,4},{1,9},{5,13},{9,1},{13,5},{2,10},{6,14},... | collective-permute-start | bytes 110600 | tf_op jit(solution)/shard_map/ppermute | solution.py:199
  113.3 1.6 %collective-permute-start.9 = (bf16[1,96,192]{2,1,0:T(8,128)(2,1)S(1)}, bf16[1,96,192]{2,1,0:T(8,128)(2,1)S(1)}, u32[]{:S(2)}, u32[]{:S(2)}) collective-permute-start(bf16[1,96,192]{2,1,0:T(8,128)(2,1)S(1)} %get-tuple-element.47), channel_id=1, source_target_pairs={{0,4},{4,8},{8,12},{12,0},{1,5},{5,9},{9,13},{13,1},{2,6},{6,10},{... | collective-permute-start | bytes 110600 | tf_op jit(solution)/shard_map/ppermute | solution.py:199
  114.9 1.9 %add_convert_fusion = bf16[1,30,60,384]{3,2,1,0:T(8,128)(2,1)} fusion(bf16[1,30,60,384]{3,2,1,0:T(8,128)(2,1)S(1)} %copy-done, bf16[1,30,15,384]{3,2,1,0:T(8,128)(2,1)S(1)} %fusion.18, bf16[1,30,30,384]{3,2,1,0:T(8,128)(2,1)S(1)} %maximum_bitcast_fusion, bf16[1,30,15,384]{3,2,1,0:T(8,128)(2,1)S(1)} %slice_bitcast_fusion), kind=kLoop, calls=%fused_computation | loop fusion | flops 6220800 | bytes 4147200 | tf_op jit(solution)/shard_map/convert_element_type | solution.py:350
  117.0 2.3 %collective-permute-done.9 = bf16[1,96,192]{2,1,0:T(8,128)(2,1)S(1)} collective-permute-done((bf16[1,96,192]{2,1,0:T(8,128)(2,1)S(1)}, bf16[1,96,192]{2,1,0:T(8,128)(2,1)S(1)}, u32[]{:S(2)}, u32[]{:S(2)}) %collective-permute-start.9) | collective-permute-done | bytes 36896 | tf_op jit(solution)/shard_map/ppermute | solution.py:199
  (58 shorter events, 12.3 us)
Async XLA Ops:
  0.6 2.5 %copy-start = (bf16[1,30,60,384]{3,2,1,0:T(8,128)(2,1)S(1)}, bf16[1,30,60,384]{3,2,1,0:T(8,128)(2,1)}, u32[]{:S(2)}) copy-start(bf16[1,30,60,384]{3,2,1,0:T(8,128)(2,1)} %param.6) | copy-start | bytes 4147204
  4.3 2.3 %copy-start.1 = (bf16[1,30,60,384]{3,2,1,0:T(8,128)(2,1)S(1)}, bf16[1,30,60,384]{3,2,1,0:T(8,128)(2,1)}, u32[]{:S(2)}) copy-start(bf16[1,30,60,384]{3,2,1,0:T(8,128)(2,1)} %param.5) | copy-start | bytes 4147204
  8.6 11.7 %collective-permute-start = (bf16[2,1,30,16,384]{4,3,2,1,0:T(8,128)(2,1)}, bf16[2,1,30,16,384]{4,3,2,1,0:T(8,128)(2,1)}, u32[]{:S(2)}, u32[]{:S(2)}) collective-permute-start(bf16[2,1,30,16,384]{4,3,2,1,0:T(8,128)(2,1)} %fusion.9), channel_id=1, source_target_pairs={{0,3},{1,0},{2,1},{3,2},{4,7},{5,4},{6,5},{7,6},{8,11},{9,8},{10,9... | collective-permute-start | bytes 2211848 | tf_op jit(solution)/shard_map/ppermute | solution.py:219
  11.0 13.7 %collective-permute-start.1 = (bf16[2,1,15,32,384]{4,3,2,0,1:T(8,128)(2,1)}, bf16[2,1,15,32,384]{4,3,2,0,1:T(8,128)(2,1)}, u32[]{:S(2)}, u32[]{:S(2)}) collective-permute-start(bf16[2,1,15,32,384]{4,3,2,0,1:T(8,128)(2,1)} %fusion.6), channel_id=1, source_target_pairs={{1,5},{3,7},{4,0},{5,9},{6,2},{7,11},{8,4},{9,13},{10,6},{11,15},{... | collective-permute-start | bytes 2211848 | tf_op jit(solution)/shard_map/ppermute | solution.py:214
  14.7 1.3 %copy-start.3 = (bf16[1,30,30,384]{3,2,1,0:T(8,128)(2,1)S(1)}, bf16[1,30,30,384]{3,2,1,0:T(8,128)(2,1)}, u32[]{:S(2)}) copy-start(bf16[1,30,30,384]{3,2,1,0:T(8,128)(2,1)} %slice.65) | copy-start | bytes 2073604
  14.7 1.5 %copy-start.2 = (bf16[1,30,30,384]{3,2,1,0:T(8,128)(2,1)S(1)}, bf16[1,30,30,384]{3,2,1,0:T(8,128)(2,1)}, u32[]{:S(2)}) copy-start(bf16[1,30,30,384]{3,2,1,0:T(8,128)(2,1)} %slice.64) | copy-start | bytes 2073604
  24.7 35.4 %collective-permute-start.2 = (bf16[2,1,2,15,16,384]{5,4,3,0,2,1:T(8,128)(2,1)S(1)}, bf16[2,1,2,15,16,384]{5,4,3,0,2,1:T(8,128)(2,1)S(1)}, u32[]{:S(2)}, u32[]{:S(2)}) collective-permute-start(bf16[2,1,2,15,16,384]{5,4,3,0,2,1:T(8,128)(2,1)S(1)} %pad_maximum_fusion), channel_id=1, source_target_pairs={{1,5},{3,7},{4,0},{5,9},{6,2},{7,11},{8,4},{9,13},{10,6},{11,15},{... | collective-permute-start | bytes 2211848 | tf_op jit(solution)/shard_map/ppermute | solution.py:214
  55.3 35.2 %collective-permute-start.5 = (bf16[15,32,384]{2,1,0:T(8,128)(2,1)}, bf16[15,32,384]{2,1,0:T(8,128)(2,1)S(1)}, u32[]{:S(2)}, u32[]{:S(2)}) collective-permute-start(bf16[15,32,384]{2,1,0:T(8,128)(2,1)} %bitcast.83), channel_id=1, source_target_pairs={{5,1},{7,3},{0,4},{9,5},{2,6},{11,7},{4,8},{13,9},{6,10},{15,11},{... | collective-permute-start | bytes 1105928 | tf_op jit(solution)/shard_map/ppermute | solution.py:214
  61.0 29.5 %copy-start.5 = (bf16[480,384]{1,0:T(8,128)(2,1)S(1)}, bf16[480,384]{1,0:T(8,128)(2,1)}, u32[]{:S(2)}) copy-start(bf16[480,384]{1,0:T(8,128)(2,1)} %get-tuple-element.28) | copy-start | bytes 1105924
  90.4 4.7 %collective-permute-start.6 = (bf16[8,96,384]{2,1,0:T(8,128)(2,1)}, bf16[8,96,384]{2,1,0:T(8,128)(2,1)S(1)}, u32[]{:S(2)}, u32[]{:S(2)}) collective-permute-start(bf16[8,96,384]{2,1,0:T(8,128)(2,1)} %get-tuple-element.32), channel_id=1, source_target_pairs={{0,1},{1,0},{2,3},{3,2},{4,5},{5,4},{6,7},{7,6},{8,9},{9,8},{10,11... | collective-permute-start | bytes 1769480 | tf_op jit(solution)/shard_map/ppermute | solution.py:199
  90.5 0.9 copy-start.8
  90.5 1.0 copy-start.9
  90.6 4.5 %copy-start.4 = (f32[8,96,384]{2,1,0:T(8,128)S(1)}, f32[8,96,384]{2,1,0:T(8,128)}, u32[]{:S(2)}) copy-start(f32[8,96,384]{2,1,0:T(8,128)} %get-tuple-element.31) | copy-start | bytes 3538948
  91.5 8.5 %collective-permute-start.3 = (bf16[2,15,16,384]{3,2,1,0:T(8,128)(2,1)S(1)}, bf16[2,15,16,384]{3,2,1,0:T(8,128)(2,1)S(1)}, u32[]{:S(2)}, u32[]{:S(2)}) collective-permute-start(bf16[2,15,16,384]{3,2,1,0:T(8,128)(2,1)S(1)} %pad_maximum_fusion.2), channel_id=1, source_target_pairs={{5,1},{7,3},{0,4},{9,5},{2,6},{11,7},{4,8},{13,9},{6,10},{15,11},{... | collective-permute-start | bytes 1105928 | tf_op jit(solution)/shard_map/ppermute | solution.py:214
  95.1 5.0 %copy-start.6 = (bf16[240,384]{1,0:T(8,128)(2,1)S(1)}, bf16[240,384]{1,0:T(8,128)(2,1)}, u32[]{:S(2)}) copy-start(bf16[240,384]{1,0:T(8,128)(2,1)} %get-tuple-element.30) | copy-start | bytes 552964
  95.1 5.0 %copy-start.7 = (bf16[240,384]{1,0:T(8,128)(2,1)S(1)}, bf16[240,384]{1,0:T(8,128)(2,1)}, u32[]{:S(2)}) copy-start(bf16[240,384]{1,0:T(8,128)(2,1)} %get-tuple-element.25) | copy-start | bytes 552964
  95.2 7.2 %collective-permute-start.7 = (bf16[4,1,96,384]{3,2,0,1:T(8,128)(2,1)S(1)}, bf16[4,1,96,384]{3,2,0,1:T(8,128)(2,1)S(1)}, u32[]{:S(2)}, u32[]{:S(2)}) collective-permute-start(bf16[4,1,96,384]{3,2,0,1:T(8,128)(2,1)S(1)} %fusion.19), channel_id=1, source_target_pairs={{0,2},{1,3},{2,0},{3,1},{4,6},{5,7},{6,4},{7,5},{8,10},{9,11},{10,... | collective-permute-start | bytes 884744 | tf_op jit(solution)/shard_map/ppermute | solution.py:199
  100.2 7.0 %collective-permute-start.4 = (bf16[30,16,384]{2,1,0:T(8,128)(2,1)S(1)}, bf16[30,16,384]{2,1,0:T(8,128)(2,1)S(1)}, u32[]{:S(2)}, u32[]{:S(2)}) collective-permute-start(bf16[30,16,384]{2,1,0:T(8,128)(2,1)S(1)} %pad_maximum_fusion.3), channel_id=1, source_target_pairs={{0,1},{1,2},{2,3},{3,0},{4,5},{5,6},{6,7},{7,4},{8,9},{9,10},{10,1... | collective-permute-start | bytes 1105928 | tf_op jit(solution)/shard_map/ppermute | solution.py:219
  102.6 5.7 %collective-permute-start.8 = (bf16[4,96,192]{2,1,0:T(8,128)(2,1)S(1)}, bf16[4,96,192]{2,1,0:T(8,128)(2,1)S(1)}, u32[]{:S(2)}, u32[]{:S(2)}) collective-permute-start(bf16[4,96,192]{2,1,0:T(8,128)(2,1)S(1)} %fusion.20), channel_id=1, source_target_pairs={{0,16},{16,0},{1,17},{17,1},{2,18},{18,2},{3,19},{19,3},{4,20},{20... | collective-permute-start | bytes 442376 | tf_op jit(solution)/shard_map/ppermute | solution.py:199
  108.6 8.2 %collective-permute-start.10 = (bf16[1,96,192]{2,1,0:T(8,128)(2,1)S(1)}, bf16[1,96,192]{2,1,0:T(8,128)(2,1)S(1)}, u32[]{:S(2)}, u32[]{:S(2)}) collective-permute-start(bf16[1,96,192]{2,1,0:T(8,128)(2,1)S(1)} %get-tuple-element.49), channel_id=1, source_target_pairs={{0,8},{4,12},{8,0},{12,4},{1,9},{5,13},{9,1},{13,5},{2,10},{6,14},... | collective-permute-start | bytes 110600 | tf_op jit(solution)/shard_map/ppermute | solution.py:199
  112.9 4.1 %collective-permute-start.11 = (bf16[1,96,192]{2,1,0:T(8,128)(2,1)S(1)}, bf16[1,96,192]{2,1,0:T(8,128)(2,1)S(1)}, u32[]{:S(2)}, u32[]{:S(2)}) collective-permute-start(bf16[1,96,192]{2,1,0:T(8,128)(2,1)S(1)} %get-tuple-element.48), channel_id=1, source_target_pairs={{0,12},{4,0},{8,4},{12,8},{1,13},{5,1},{9,5},{13,9},{2,14},{6,2},{... | collective-permute-start | bytes 110600 | tf_op jit(solution)/shard_map/ppermute | solution.py:199
  113.3 5.9 %collective-permute-start.9 = (bf16[1,96,192]{2,1,0:T(8,128)(2,1)S(1)}, bf16[1,96,192]{2,1,0:T(8,128)(2,1)S(1)}, u32[]{:S(2)}, u32[]{:S(2)}) collective-permute-start(bf16[1,96,192]{2,1,0:T(8,128)(2,1)S(1)} %get-tuple-element.47), channel_id=1, source_target_pairs={{0,4},{4,8},{8,12},{12,0},{1,5},{5,9},{9,13},{13,1},{2,6},{6,10},{... | collective-permute-start | bytes 110600 | tf_op jit(solution)/shard_map/ppermute | solution.py:199

commit v4 on v3

--- a/solution.py
+++ b/solution.py
@@ -199,7 +199,7 @@
     return lax.ppermute(value, tuple(axes), pairs)
 
 
-def shared(value, back=False):
+def shared(value, back=False, east=0):
     lats, lons = lax.axis_size("lat"), lax.axis_size("lon")
     pairs = []
     for i in range(lats):
@@ -210,13 +210,47 @@
                 goal = (i + 1, j) if i < lats - 1 else (i, j - 1)
             if goal is not None:
                 pair = (i * lons + j, goal[0] * lons + goal[1])
-                pairs.append(pair[::-1] if back else pair)
+                home = i * lons + (j + east) % lons
+                pairs.append((pair[1], home) if back else pair)
     return lax.ppermute(value, ("lat", "lon"), pairs)
 
 
 def along_lon(value, step):
     count = lax.axis_size("lon")
     return lax.ppermute(value, "lon", [(j, (j + step) % count) for j in range(count)])
+
+
+def cut_kernel(specs, half, hid_ref, cot_ref, *outs):
+    odd = lax.rem(lax.axis_index("lon"), 2)
+    top = lax.axis_index("lat") == 0
+    end = hid_ref.shape[1] - half
+    starts = {"own": (1 - odd) * end, "sent": odd * end}
+    zeroed = {"own": top & (odd == 1), "peer": top & (odd == 0)}
+    for out, (rows, cols, n, pad, clear) in zip(outs, specs):
+        at = starts.get(rows, rows)
+        for k, ref in enumerate((hid_ref, cot_ref)):
+            for b in range(hid_ref.shape[0]):
+                cut = ref[b, pl.ds(at, half)].astype(F32)[:, cols:cols + n]
+                if clear:
+                    cut = jnp.where(zeroed[clear], 0.0, cut)
+                filler = jnp.zeros((half, pad - n, cut.shape[2]), F32)
+                out[k, b] = jnp.concatenate([cut, filler], axis=1).astype(BF)
+
+
+def cut_call(hid, cot, specs, half):
+    samples, _, _, width = hid.shape
+    vmem = pl.BlockSpec(memory_space=pltpu.VMEM)
+    outs = pl.pallas_call(
+        functools.partial(cut_kernel, specs, half),
+        out_shape=tuple(
+            jax.ShapeDtypeStruct((2, samples, half, pad, width), BF) for _, _, _, pad, _ in specs
+        ),
+        in_specs=[vmem] * 2,
+        out_specs=tuple([vmem] * len(specs)),
+        cost_estimate=pl.CostEstimate(flops=0, bytes_accessed=4 * hid.size * 2, transcendentals=0),
+        compiler_params=pltpu.CompilerParams(vmem_limit_bytes=40 * 2**20),
+    )(hid, cot)
+    return list(outs)
 
 
 def scatter_direct(value, axis, dim):
@@ -266,61 +300,43 @@
         raise ValueError("lon size")
 
     odd = lax.axis_index("lon") % 2
-    idle = (lax.axis_index("lat") == 0) & (odd == 1)
-    end = lat_rows - half
-    own_at, sent_at = jnp.where(odd == 1, 0, end), jnp.where(odd == 1, end, 0)
-
-    def pieces_of(x, c):
-        def piece(rows_at, cols_at, n, pad_to, rows=half):
-            cuts = [
-                lax.dynamic_slice_in_dim(v[:, :, cols_at:cols_at + n], rows_at, rows, 1) for v in (x, c)
-            ]
-            return jnp.pad(jnp.stack(cuts), ((0, 0), (0, 0), (0, 0), (0, pad_to - n), (0, 0)))
-        return piece
-
-    def cleared(value):
-        return jnp.where(idle, jnp.zeros_like(value), value)
-
     inner = [wc * WIN + SHIFT for wc in range(nc - 1)]
     edge = (nc - 1) * WIN + SHIFT
-    first = pieces_of(hidden_in, grad_out)
-    sent = [first(sent_at, at, WIN, wide) for at in inner]
+    sent = cut_call(hidden_in, grad_out, [("sent", at, WIN, wide, "") for at in inner], half) if inner else []
     hid, cot, sent = lax.optimization_barrier((hidden_in, grad_out, sent))
     inner_in = [shared(p) for p in sent]
-    piece = pieces_of(hid, cot)
-    lon_in = along_lon(piece(0, 0, half, short, lat_rows), -1)
-    own_inner = [cleared(piece(own_at, at, WIN, wide)) for at in inner]
-    own_edge = cleared(piece(own_at, edge, half, short))
-
-    def side(at):
-        return lax.dynamic_slice_in_dim(lon_in, at, half, 2)
-
-    own_side = cleared(side(own_at))
-    edge_sent = jnp.stack([piece(sent_at, edge, half, short), side(sent_at)], axis=2)
+    specs = [("sent", 0, half, short, "peer"), ("own", 0, half, short, "")]
+    specs += [("own", edge, half, short, "own"), ("sent", edge, half, short, "")]
+    specs += [("own", at, WIN, wide, "own") for at in inner]
+    fixed = [(2 * wr + 1 + i) * half for wr in range(nr - 1) for i in range(2)]
+    specs += [(r, at, WIN, wide, "") for at in inner for r in fixed]
+    specs += [(r, edge, half, short, "") for r in fixed] + [(r, 0, half, short, "") for r in fixed]
+    cuts = cut_call(hid, cot, specs, half)
+    own_side, side_sent = along_lon(cuts[0], -1), along_lon(cuts[1], -1)
+    own_edge, edge_sent = cuts[2:4]
+    own_inner, rest = cuts[4:4 + len(inner)], cuts[4 + len(inner):]
+    whole_inner = [[rest.pop(0) for _ in fixed] for _ in inner]
+    whole_edge = [rest.pop(0) for _ in fixed]
+    whole_side = [along_lon(rest.pop(0), -1) for _ in fixed]
     if inner_in:
-        edge_sent, inner_in = lax.optimization_barrier((edge_sent, inner_in))
-    edge_in = shared(edge_sent)
+        edge_sent, side_sent, inner_in = lax.optimization_barrier((edge_sent, side_sent, inner_in))
+    edge_in, corner_in = shared(edge_sent), shared(side_sent)
 
     order = [(b, wr, wc) for b in range(samples) for wc in range(nc) for wr in range(nr)]
     sums = None
     out = {}
     for step, (b, wr, wc) in enumerate(order):
-        top = (2 * wr + 1) * half
         if wr < nr - 1 and wc < nc - 1:
-            cells = [piece(top + i * half, inner[wc], WIN, wide) for i in range(2)]
+            cells = whole_inner[wc][2 * wr:2 * wr + 2]
             metas = ((WIN, wide, False),) * 2
         elif wr < nr - 1:
-            cells = [
-                f(top + i * half)
-                for i in range(2)
-                for f in (lambda at: piece(at, edge, half, short), side)
-            ]
+            cells = [f[2 * wr + i] for i in range(2) for f in (whole_edge, whole_side)]
             metas = ((half, short, False),) * 4
         elif wc < nc - 1:
             cells = [own_inner[wc], inner_in[wc]]
             metas = ((WIN, wide, False), (WIN, wide, True))
         else:
-            cells = [own_edge, own_side, edge_in[:, :, 0], edge_in[:, :, 1]]
+            cells = [own_edge, own_side, edge_in, corner_in]
             metas = ((half, short, False),) * 2 + ((half, short, True),) * 2
         cells = [p[:, b].reshape(2, -1, width) for p in cells]
         done, sums = window_call(
@@ -330,21 +346,22 @@
 
     rows_out = []
     for b in range(samples):
-        def stacked(own, back, between):
-            upper = jnp.where(odd == 1, own, back)
-            lower = jnp.where(odd == 1, back, own)
-            return jnp.concatenate([upper] + between + [lower], axis=0)
+        def stacked(own, back, between, upper):
+            above = jnp.where(upper, own, back)
+            below = jnp.where(upper, back, own)
+            return jnp.concatenate([above] + between + [below], axis=0)
 
         columns = []
         for wc in range(nc - 1):
             own, other = out[b, nr - 1, wc]
-            between = [out[b, wr, wc][i][:, :WIN] for wr in range(nr - 1) for i in range(2)]
-            columns.append(stacked(own[:, :WIN], shared(other, back=True)[:, :WIN], between))
+            between = [out[b, wr, wc][i] for wr in range(nr - 1) for i in range(2)]
+            columns.append(stacked(own, shared(other, back=True), between, odd == 1)[:, :WIN])
         own, own_lon, other, other_lon = out[b, nr - 1, nc - 1]
-        back = shared(jnp.stack([other, other_lon]), back=True)
-        between = [[out[b, wr, nc - 1][i] for wr in range(nr - 1) for i in (k, k + 2)] for k in range(2)]
-        columns.append(stacked(own, back[0], between[0])[:, :half])
-        columns.insert(0, along_lon(stacked(own_lon, back[1], between[1]), 1)[:, :half])
+        between = [out[b, wr, nc - 1][i] for wr in range(nr - 1) for i in (0, 2)]
+        columns.append(stacked(own, shared(other, back=True), between, odd == 1)[:, :half])
+        between = [along_lon(out[b, wr, nc - 1][i], 1) for wr in range(nr - 1) for i in (1, 3)]
+        near, far = along_lon(own_lon, 1), shared(other_lon, back=True, east=1)
+        columns.insert(0, stacked(near, far, between, odd == 0)[:, :half])
         rows_out.append(jnp.concatenate(columns, axis=1))
     returned = jnp.stack(rows_out)
     grad_in = (grad_out.astype(F32) + returned.astype(F32)).astype(BF)

time: 121 us -> 117 us (0.967)
  starting transfers between devices: 22.5 us -> 30.4 us
  local copies, waits for them, and re-layouts: 13.1 us -> 6.79 us
  other arithmetic: 8.59 us -> 2.55 us
    slice x5 -> x0, local copies, waits for them, and re-layouts: 7 us -> none  [the longest x4 6.06 us: piece(): v[:, :, cols_at:cols_at + n]]
    ppermute x4 -> x6, starting transfers between devices: 11 us -> 17.9 us  [shared(): return lax.ppermute(value, ('lat', 'lon'), pairs)]
    unnamed x20 -> x24, local copies, waits for them, and re-layouts: 1.07 us -> 5.35 us
    another operation x6 -> x0, other arithmetic: 4.1 us -> none  [the longest x3 2.06 us: per_device(): jnp.stack([piece(sent_at, edge, half, short), side(sent_at)], axis=2)]
    ppermute x6, waiting for transfers between devices: 5.27 us -> 8.98 us  [permuted(): return lax.ppermute(value, tuple(axes), pairs)]
    another operation x7 -> x0, local copies, waits for them, and re-layouts: 3.58 us -> none  [piece(): jnp.stack(cuts)]
    ppermute x4 -> x6, waiting for transfers between devices: 6.53 us -> 3.78 us  [shared(): return lax.ppermute(value, ('lat', 'lon'), pairs)]
    select_n x4 -> x3, other arithmetic: 2.06 us -> 0.16 us  [stacked(): above = jnp.where(upper, own, back)]
  transfers between devices with their start and end apart: 12 -> 15, of which waited for: 8 -> 6; matrix products, arithmetic and copies ran while one was open for 9% -> 2% of each run, Pallas kernels for 48% -> 50%
where the time goes in v4:
time: 117 us
  Pallas kernels  58.5 us (50%)
  starting transfers between devices  30.4 us (26%)
  waiting for transfers between devices  17.8 us (15%)
  local copies, waits for them, and re-layouts  6.79 us (6%)
  other arithmetic  2.55 us (2%)
    pallas_call x2, Pallas kernels, window_call(): pl.pallas_call(functools.partial(window_kernel, head, metas, (prev is not...  57.6 us
    ppermute x6, starting transfers between devices, shared(): return lax.ppermute(value, ('lat', 'lon'), pairs)  17.9 us
    ppermute x6, waiting for transfers between devices, permuted(): return lax.ppermute(value, tuple(axes), pairs)  8.98 us
    ppermute x6, starting transfers between devices, permuted(): return lax.ppermute(value, tuple(axes), pairs)  7.68 us
    unnamed x24, local copies, waits for them, and re-layouts  5.35 us
    ppermute x3, waiting for transfers between devices, along_lon(): lax.ppermute(value, 'lon', [(j, (j + step) % count) for j in range(count)])  5 us
    ppermute x3, starting transfers between devices, along_lon(): lax.ppermute(value, 'lon', [(j, (j + step) % count) for j in range(count)])  4.79 us
    ppermute x6, waiting for transfers between devices, shared(): return lax.ppermute(value, ('lat', 'lon'), pairs)  3.78 us
  transfers between devices with their start and end apart: 15, of which 6 were waited for; matrix products, arithmetic and copies ran while one was open for 2% of the time, Pallas kernels for 50%

profile of v4, /device:TPU:0, one launch (start us, length us, event | category | flops | bytes accessed | tf_op | source)
XLA Modules:
  0.0 117.0 jit_solution(13570301102149799857)
XLA Ops:
  0.6 1.4 %copy-done = bf16[1,30,60,384]{3,2,1,0:T(8,128)(2,1)S(1)} copy-done((bf16[1,30,60,384]{3,2,1,0:T(8,128)(2,1)S(1)}, bf16[1,30,60,384]{3,2,1,0:T(8,128)(2,1)}, u32[]{:S(2)}) %copy-start) | copy-done | bytes 1382424
  2.0 1.4 %copy-done.2 = bf16[1,30,60,384]{3,2,1,0:T(8,128)(2,1)S(1)} copy-done((bf16[1,30,60,384]{3,2,1,0:T(8,128)(2,1)S(1)}, bf16[1,30,60,384]{3,2,1,0:T(8,128)(2,1)}, u32[]{:S(2)}) %copy-start.2) | copy-done | bytes 1382424
  3.6 1.3 %collective-permute-start.2 = (bf16[2,1,15,32,384]{4,3,2,1,0:T(8,128)(2,1)S(1)}, bf16[2,1,15,32,384]{4,3,2,1,0:T(8,128)(2,1)S(1)}, u32[]{:S(2)}, u32[]{:S(2)}) collective-permute-start(bf16[2,1,15,32,384]{4,3,2,1,0:T(8,128)(2,1)S(1)} %shard_map.76), channel_id=1, source_target_pairs={{1,5},{3,7},{4,0},{5,9},{6,2},{7,11},{8,4},{9,13},{10,6},{11,15},{... | collective-permute-start | bytes 2211848 | tf_op jit(solution)/shard_map/ppermute | solution.py:215
  5.6 0.9 copy-done.3
  6.4 0.7 copy-done.4
  7.2 4.4 %collective-permute-start.1 = (bf16[2,1,15,16,384]{4,3,2,1,0:T(8,128)(2,1)S(1)}, bf16[2,1,15,16,384]{4,3,2,1,0:T(8,128)(2,1)S(1)}, u32[]{:S(2)}, u32[]{:S(2)}) collective-permute-start(bf16[2,1,15,16,384]{4,3,2,1,0:T(8,128)(2,1)S(1)} %get-tuple-element.29), channel_id=1, source_target_pairs={{0,3},{1,0},{2,1},{3,2},{4,7},{5,4},{6,5},{7,6},{8,11},{9,8},{10,9... | collective-permute-start | bytes 1105928 | tf_op jit(solution)/shard_map/ppermute | solution.py:220
  11.6 5.0 %collective-permute-done.1 = bf16[2,1,15,16,384]{4,3,2,1,0:T(8,128)(2,1)S(1)} collective-permute-done((bf16[2,1,15,16,384]{4,3,2,1,0:T(8,128)(2,1)S(1)}, bf16[2,1,15,16,384]{4,3,2,1,0:T(8,128)(2,1)S(1)}, u32[]{:S(2)}, u32[]{:S(2)}) %collective-permute-start.1) | collective-permute-done | bytes 368672 | tf_op jit(solution)/shard_map/ppermute | solution.py:220
  16.6 1.4 %collective-permute-done.2 = bf16[2,1,15,32,384]{4,3,2,1,0:T(8,128)(2,1)S(1)} collective-permute-done((bf16[2,1,15,32,384]{4,3,2,1,0:T(8,128)(2,1)S(1)}, bf16[2,1,15,32,384]{4,3,2,1,0:T(8,128)(2,1)S(1)}, u32[]{:S(2)}, u32[]{:S(2)}) %collective-permute-start.2) | collective-permute-done | bytes 737312 | tf_op jit(solution)/shard_map/ppermute | solution.py:215
  18.0 1.3 %collective-permute-start.3 = (bf16[2,1,15,16,384]{4,3,2,1,0:T(8,128)(2,1)S(1)}, bf16[2,1,15,16,384]{4,3,2,1,0:T(8,128)(2,1)S(1)}, u32[]{:S(2)}, u32[]{:S(2)}) collective-permute-start(bf16[2,1,15,16,384]{4,3,2,1,0:T(8,128)(2,1)S(1)} %get-tuple-element.31), channel_id=1, source_target_pairs={{1,5},{3,7},{4,0},{5,9},{6,2},{7,11},{8,4},{9,13},{10,6},{11,15},{... | collective-permute-start | bytes 1105928 | tf_op jit(solution)/shard_map/ppermute | solution.py:215
  19.3 1.3 %collective-permute-start.4 = (bf16[2,1,15,16,384]{4,3,2,1,0:T(8,128)(2,1)S(1)}, bf16[2,1,15,16,384]{4,3,2,1,0:T(8,128)(2,1)S(1)}, u32[]{:S(2)}, u32[]{:S(2)}) collective-permute-start(bf16[2,1,15,16,384]{4,3,2,1,0:T(8,128)(2,1)S(1)} %collective-permute-done.1), channel_id=1, source_target_pairs={{1,5},{3,7},{4,0},{5,9},{6,2},{7,11},{8,4},{9,13},{10,6},{11,15},{... | collective-permute-start | bytes 1105928 | tf_op jit(solution)/shard_map/ppermute | solution.py:215
  20.6 28.3 %shard_map.78 = (bf16[480,384]{1,0:T(8,128)(2,1)}, bf16[480,384]{1,0:T(8,128)(2,1)}, f32[384,1152]{1,0:T(8,128)}, f32[384,384]{1,0:T(8,128)}) custom-call(bf16[2,480,384]{2,1,0:T(8,128)(2,1)} %bitcast.35, bf16[2,480,384]{2,1,0:T(8,128)(2,1)} %bitcast.41, f32[384]{0:T(512)} %refs_4_.3, bf16[384,1152]{1,0:T(8,128)(2,1)} %refs_5_.1, bf16[384,384]{1,0:T(8,128)(2,1)} %refs_6_.1), custom_call_target="tpu_custom_call" | custom-call | flops 7644119040 | bytes 8388608 | tf_op jit(solution)/shard_map/pallas_call | solution.py:168
  48.8 5.4 %collective-permute-start.7 = (bf16[15,32,384]{2,1,0:T(8,128)(2,1)}, bf16[15,32,384]{2,1,0:T(8,128)(2,1)S(1)}, u32[]{:S(2)}, u32[]{:S(2)}) collective-permute-start(bf16[15,32,384]{2,1,0:T(8,128)(2,1)} %bitcast.42), channel_id=1, source_target_pairs={{5,1},{7,3},{0,4},{9,5},{2,6},{11,7},{4,8},{13,9},{6,10},{15,11},{... | collective-permute-start | bytes 1105928 | tf_op jit(solution)/shard_map/ppermute | solution.py:215
  55.2 29.3 %shard_map.79 = (bf16[240,384]{1,0:T(8,128)(2,1)}, bf16[240,384]{1,0:T(8,128)(2,1)}, bf16[240,384]{1,0:T(8,128)(2,1)}, bf16[240,384]{1,0:T(8,128)(2,1)}, f32[8,9...) custom-call(bf16[2,240,384]{2,1,0:T(8,128)(2,1)} %bitcast.36, bf16[2,240,384]{2,1,0:T(8,128)(2,1)} %bitcast.43, ...), custom_call_target="tpu_custom_call" | custom-call | flops 7644119040 | bytes 8388608 | tf_op jit(solution)/shard_map/pallas_call | solution.py:168
  85.2 5.2 %collective-permute-start.6 = (bf16[15,16,384]{2,1,0:T(8,128)(2,1)}, bf16[15,16,384]{2,1,0:T(8,128)(2,1)S(1)}, u32[]{:S(2)}, u32[]{:S(2)}) collective-permute-start(bf16[15,16,384]{2,1,0:T(8,128)(2,1)} %bitcast.46), channel_id=1, source_target_pairs={{5,2},{7,0},{0,5},{9,6},{2,7},{11,4},{4,9},{13,10},{6,11},{15,8},{... | collective-permute-start | bytes 552968 | tf_op jit(solution)/shard_map/ppermute | solution.py:215
  90.4 3.5 %collective-permute-start.8 = (bf16[15,16,384]{2,1,0:T(8,128)(2,1)}, bf16[15,16,384]{2,1,0:T(8,128)(2,1)S(1)}, u32[]{:S(2)}, u32[]{:S(2)}) collective-permute-start(bf16[15,16,384]{2,1,0:T(8,128)(2,1)} %bitcast.48), channel_id=1, source_target_pairs={{5,1},{7,3},{0,4},{9,5},{2,6},{11,7},{4,8},{13,9},{6,10},{15,11},{... | collective-permute-start | bytes 552968 | tf_op jit(solution)/shard_map/ppermute | solution.py:215
  94.8 2.4 %collective-permute-done.8 = bf16[15,16,384]{2,1,0:T(8,128)(2,1)S(1)} collective-permute-done((bf16[15,16,384]{2,1,0:T(8,128)(2,1)}, bf16[15,16,384]{2,1,0:T(8,128)(2,1)S(1)}, u32[]{:S(2)}, u32[]{:S(2)}) %collective-permute-start.8) | collective-permute-done | bytes 184352 | tf_op jit(solution)/shard_map/ppermute | solution.py:215
  97.3 3.7 %collective-permute-done.10 = bf16[4,1,96,384]{3,2,0,1:T(8,128)(2,1)S(1)} collective-permute-done((bf16[4,1,96,384]{3,2,0,1:T(8,128)(2,1)S(1)}, bf16[4,1,96,384]{3,2,0,1:T(8,128)(2,1)S(1)}, u32[]{:S(2)}, u32[]{:S(2)}) %collective-permute-start.10) | collective-permute-done | bytes 294944 | tf_op jit(solution)/shard_map/ppermute | solution.py:199
  101.2 1.6 %collective-permute-start.11 = (bf16[4,96,192]{2,1,0:T(8,128)(2,1)S(1)}, bf16[4,96,192]{2,1,0:T(8,128)(2,1)S(1)}, u32[]{:S(2)}, u32[]{:S(2)}) collective-permute-start(bf16[4,96,192]{2,1,0:T(8,128)(2,1)S(1)} %fusion.4), channel_id=1, source_target_pairs={{0,16},{16,0},{1,17},{17,1},{2,18},{18,2},{3,19},{19,3},{4,20},{20... | collective-permute-start | bytes 442376 | tf_op jit(solution)/shard_map/ppermute | solution.py:199
  102.9 4.0 %collective-permute-done.11 = bf16[4,96,192]{2,1,0:T(8,128)(2,1)S(1)} collective-permute-done((bf16[4,96,192]{2,1,0:T(8,128)(2,1)S(1)}, bf16[4,96,192]{2,1,0:T(8,128)(2,1)S(1)}, u32[]{:S(2)}, u32[]{:S(2)}) %collective-permute-start.11) | collective-permute-done | bytes 147488 | tf_op jit(solution)/shard_map/ppermute | solution.py:199
  107.1 1.1 collective-permute-start.12
  108.2 3.5 %collective-permute-start.13 = (bf16[1,96,192]{2,1,0:T(8,128)(2,1)S(1)}, bf16[1,96,192]{2,1,0:T(8,128)(2,1)S(1)}, u32[]{:S(2)}, u32[]{:S(2)}) collective-permute-start(bf16[1,96,192]{2,1,0:T(8,128)(2,1)S(1)} %get-tuple-element.49), channel_id=1, source_target_pairs={{0,8},{4,12},{8,0},{12,4},{1,9},{5,13},{9,1},{13,5},{2,10},{6,14},... | collective-permute-start | bytes 110600 | tf_op jit(solution)/shard_map/ppermute | solution.py:199
  111.7 0.9 collective-permute-start.14
  112.6 1.9 %add_convert_fusion = bf16[1,30,60,384]{3,2,1,0:T(8,128)(2,1)} fusion(bf16[1,30,60,384]{3,2,1,0:T(8,128)(2,1)S(1)} %copy-done.1, bf16[1,30,15,384]{3,2,1,0:T(8,128)(2,1)S(1)} %get-tuple-element.54, bf16[1,30,30,384]{3,2,1,0:T(8,128)(2,1)S(1)} %fusion, bf16[1,30,15,384]{3,2,1,0:T(8,128)(2,1)S(1)} %get-tuple-element.55), kind=kLoop, calls=%fused_computation | loop fusion | flops 6220800 | bytes 4147200 | tf_op jit(solution)/shard_map/convert_element_type | solution.py:367
  114.5 1.3 %collective-permute-done.14 = bf16[1,96,192]{2,1,0:T(8,128)(2,1)S(1)} collective-permute-done((bf16[1,96,192]{2,1,0:T(8,128)(2,1)S(1)}, bf16[1,96,192]{2,1,0:T(8,128)(2,1)S(1)}, u32[]{:S(2)}, u32[]{:S(2)}) %collective-permute-start.14) | collective-permute-done | bytes 36896 | tf_op jit(solution)/shard_map/ppermute | solution.py:199
  (49 shorter events, 5.1 us)
Async XLA Ops:
  0.6 1.4 %copy-start = (bf16[1,30,60,384]{3,2,1,0:T(8,128)(2,1)S(1)}, bf16[1,30,60,384]{3,2,1,0:T(8,128)(2,1)}, u32[]{:S(2)}) copy-start(bf16[1,30,60,384]{3,2,1,0:T(8,128)(2,1)} %cot_ref.2) | copy-start | bytes 4147204
  2.0 1.4 %copy-start.2 = (bf16[1,30,60,384]{3,2,1,0:T(8,128)(2,1)S(1)}, bf16[1,30,60,384]{3,2,1,0:T(8,128)(2,1)}, u32[]{:S(2)}) copy-start(bf16[1,30,60,384]{3,2,1,0:T(8,128)(2,1)} %hid_ref.2) | copy-start | bytes 4147204
  3.6 14.4 %collective-permute-start.2 = (bf16[2,1,15,32,384]{4,3,2,1,0:T(8,128)(2,1)S(1)}, bf16[2,1,15,32,384]{4,3,2,1,0:T(8,128)(2,1)S(1)}, u32[]{:S(2)}, u32[]{:S(2)}) collective-permute-start(bf16[2,1,15,32,384]{4,3,2,1,0:T(8,128)(2,1)S(1)} %shard_map.76), channel_id=1, source_target_pairs={{1,5},{3,7},{4,0},{5,9},{6,2},{7,11},{8,4},{9,13},{10,6},{11,15},{... | collective-permute-start | bytes 2211848 | tf_op jit(solution)/shard_map/ppermute | solution.py:215
  7.2 9.4 %collective-permute-start.1 = (bf16[2,1,15,16,384]{4,3,2,1,0:T(8,128)(2,1)S(1)}, bf16[2,1,15,16,384]{4,3,2,1,0:T(8,128)(2,1)S(1)}, u32[]{:S(2)}, u32[]{:S(2)}) collective-permute-start(bf16[2,1,15,16,384]{4,3,2,1,0:T(8,128)(2,1)S(1)} %get-tuple-element.29), channel_id=1, source_target_pairs={{0,3},{1,0},{2,1},{3,2},{4,7},{5,4},{6,5},{7,6},{8,11},{9,8},{10,9... | collective-permute-start | bytes 1105928 | tf_op jit(solution)/shard_map/ppermute | solution.py:220
  11.6 42.6 %collective-permute-start = (bf16[2,1,15,16,384]{4,3,2,1,0:T(8,128)(2,1)S(1)}, bf16[2,1,15,16,384]{4,3,2,1,0:T(8,128)(2,1)S(1)}, u32[]{:S(2)}, u32[]{:S(2)}) collective-permute-start(bf16[2,1,15,16,384]{4,3,2,1,0:T(8,128)(2,1)S(1)} %get-tuple-element.27), channel_id=1, source_target_pairs={{0,3},{1,0},{2,1},{3,2},{4,7},{5,4},{6,5},{7,6},{8,11},{9,8},{10,9... | collective-permute-start | bytes 1105928 | tf_op jit(solution)/shard_map/ppermute | solution.py:220
  18.0 2.6 %copy-start.8 = (bf16[2,1,15,32,384]{4,3,2,1,0:T(8,128)(2,1)}, bf16[2,1,15,32,384]{4,3,2,1,0:T(8,128)(2,1)S(1)}, u32[]{:S(2)}) copy-start(bf16[2,1,15,32,384]{4,3,2,1,0:T(8,128)(2,1)S(1)} %collective-permute-done.2) | copy-start | bytes 2211844
  18.0 36.3 %collective-permute-start.3 = (bf16[2,1,15,16,384]{4,3,2,1,0:T(8,128)(2,1)S(1)}, bf16[2,1,15,16,384]{4,3,2,1,0:T(8,128)(2,1)S(1)}, u32[]{:S(2)}, u32[]{:S(2)}) collective-permute-start(bf16[2,1,15,16,384]{4,3,2,1,0:T(8,128)(2,1)S(1)} %get-tuple-element.31), channel_id=1, source_target_pairs={{1,5},{3,7},{4,0},{5,9},{6,2},{7,11},{8,4},{9,13},{10,6},{11,15},{... | collective-permute-start | bytes 1105928 | tf_op jit(solution)/shard_map/ppermute | solution.py:215
  19.3 35.0 %collective-permute-start.4 = (bf16[2,1,15,16,384]{4,3,2,1,0:T(8,128)(2,1)S(1)}, bf16[2,1,15,16,384]{4,3,2,1,0:T(8,128)(2,1)S(1)}, u32[]{:S(2)}, u32[]{:S(2)}) collective-permute-start(bf16[2,1,15,16,384]{4,3,2,1,0:T(8,128)(2,1)S(1)} %collective-permute-done.1), channel_id=1, source_target_pairs={{1,5},{3,7},{4,0},{5,9},{6,2},{7,11},{8,4},{9,13},{10,6},{11,15},{... | collective-permute-start | bytes 1105928 | tf_op jit(solution)/shard_map/ppermute | solution.py:215
  48.8 45.1 %collective-permute-start.7 = (bf16[15,32,384]{2,1,0:T(8,128)(2,1)}, bf16[15,32,384]{2,1,0:T(8,128)(2,1)S(1)}, u32[]{:S(2)}, u32[]{:S(2)}) collective-permute-start(bf16[15,32,384]{2,1,0:T(8,128)(2,1)} %bitcast.42), channel_id=1, source_target_pairs={{5,1},{7,3},{0,4},{9,5},{2,6},{11,7},{4,8},{13,9},{6,10},{15,11},{... | collective-permute-start | bytes 1105928 | tf_op jit(solution)/shard_map/ppermute | solution.py:215
  54.2 0.9 copy-start.10
  54.3 1.0 copy-start.11
  55.2 38.7 %copy-start.6 = (bf16[480,384]{1,0:T(8,128)(2,1)S(1)}, bf16[480,384]{1,0:T(8,128)(2,1)}, u32[]{:S(2)}) copy-start(bf16[480,384]{1,0:T(8,128)(2,1)} %get-tuple-element.39) | copy-start | bytes 1105924
  84.6 9.4 %copy-start.5 = (f32[8,96,384]{2,1,0:T(8,128)S(1)}, f32[8,96,384]{2,1,0:T(8,128)}, u32[]{:S(2)}) copy-start(f32[8,96,384]{2,1,0:T(8,128)} %get-tuple-element.43) | copy-start | bytes 3538948
  84.6 9.4 %collective-permute-start.9 = (bf16[8,96,384]{2,1,0:T(8,128)(2,1)}, bf16[8,96,384]{2,1,0:T(8,128)(2,1)S(1)}, u32[]{:S(2)}, u32[]{:S(2)}) collective-permute-start(bf16[8,96,384]{2,1,0:T(8,128)(2,1)} %get-tuple-element.44), channel_id=1, source_target_pairs={{0,1},{1,0},{2,3},{3,2},{4,5},{5,4},{6,7},{7,6},{8,9},{9,8},{10,11... | collective-permute-start | bytes 1769480 | tf_op jit(solution)/shard_map/ppermute | solution.py:199
  84.8 18.0 %collective-permute-start.5 = (bf16[15,16,384]{2,1,0:T(8,128)(2,1)}, bf16[15,16,384]{2,1,0:T(8,128)(2,1)S(1)}, u32[]{:S(2)}, u32[]{:S(2)}) collective-permute-start(bf16[15,16,384]{2,1,0:T(8,128)(2,1)} %bitcast.47), channel_id=1, source_target_pairs={{0,1},{1,2},{2,3},{3,0},{4,5},{5,6},{6,7},{7,4},{8,9},{9,10},{10,1... | collective-permute-start | bytes 552968 | tf_op jit(solution)/shard_map/ppermute | solution.py:220
  85.2 17.6 %collective-permute-start.6 = (bf16[15,16,384]{2,1,0:T(8,128)(2,1)}, bf16[15,16,384]{2,1,0:T(8,128)(2,1)S(1)}, u32[]{:S(2)}, u32[]{:S(2)}) collective-permute-start(bf16[15,16,384]{2,1,0:T(8,128)(2,1)} %bitcast.46), channel_id=1, source_target_pairs={{5,2},{7,0},{0,5},{9,6},{2,7},{11,4},{4,9},{13,10},{6,11},{15,8},{... | collective-permute-start | bytes 552968 | tf_op jit(solution)/shard_map/ppermute | solution.py:215
  90.4 6.8 %collective-permute-start.8 = (bf16[15,16,384]{2,1,0:T(8,128)(2,1)}, bf16[15,16,384]{2,1,0:T(8,128)(2,1)S(1)}, u32[]{:S(2)}, u32[]{:S(2)}) collective-permute-start(bf16[15,16,384]{2,1,0:T(8,128)(2,1)} %bitcast.48), channel_id=1, source_target_pairs={{5,1},{7,3},{0,4},{9,5},{2,6},{11,7},{4,8},{13,9},{6,10},{15,11},{... | collective-permute-start | bytes 552968 | tf_op jit(solution)/shard_map/ppermute | solution.py:215
  94.1 3.1 %copy-start.7 = (bf16[240,384]{1,0:T(8,128)(2,1)S(1)}, bf16[240,384]{1,0:T(8,128)(2,1)}, u32[]{:S(2)}) copy-start(bf16[240,384]{1,0:T(8,128)(2,1)} %get-tuple-element.41) | copy-start | bytes 552964
  94.2 6.8 %collective-permute-start.10 = (bf16[4,1,96,384]{3,2,0,1:T(8,128)(2,1)S(1)}, bf16[4,1,96,384]{3,2,0,1:T(8,128)(2,1)S(1)}, u32[]{:S(2)}, u32[]{:S(2)}) collective-permute-start(bf16[4,1,96,384]{3,2,0,1:T(8,128)(2,1)S(1)} %fusion.3), channel_id=1, source_target_pairs={{0,2},{1,3},{2,0},{3,1},{4,6},{5,7},{6,4},{7,5},{8,10},{9,11},{10,... | collective-permute-start | bytes 884744 | tf_op jit(solution)/shard_map/ppermute | solution.py:199
  101.2 5.7 %collective-permute-start.11 = (bf16[4,96,192]{2,1,0:T(8,128)(2,1)S(1)}, bf16[4,96,192]{2,1,0:T(8,128)(2,1)S(1)}, u32[]{:S(2)}, u32[]{:S(2)}) collective-permute-start(bf16[4,96,192]{2,1,0:T(8,128)(2,1)S(1)} %fusion.4), channel_id=1, source_target_pairs={{0,16},{16,0},{1,17},{17,1},{2,18},{18,2},{3,19},{19,3},{4,20},{20... | collective-permute-start | bytes 442376 | tf_op jit(solution)/shard_map/ppermute | solution.py:199
  102.8 9.8 %copy-start.1 = (bf16[1,30,60,384]{3,2,1,0:T(8,128)(2,1)S(1)}, bf16[1,30,60,384]{3,2,1,0:T(8,128)(2,1)}, u32[]{:S(2)}) copy-start(bf16[1,30,60,384]{3,2,1,0:T(8,128)(2,1)} %cot_ref.2) | copy-start | bytes 4147204
  107.1 7.4 %collective-permute-start.12 = (bf16[1,96,192]{2,1,0:T(8,128)(2,1)S(1)}, bf16[1,96,192]{2,1,0:T(8,128)(2,1)S(1)}, u32[]{:S(2)}, u32[]{:S(2)}) collective-permute-start(bf16[1,96,192]{2,1,0:T(8,128)(2,1)S(1)} %get-tuple-element.47), channel_id=1, source_target_pairs={{0,4},{4,8},{8,12},{12,0},{1,5},{5,9},{9,13},{13,1},{2,6},{6,10},{... | collective-permute-start | bytes 110600 | tf_op jit(solution)/shard_map/ppermute | solution.py:199
  108.2 6.3 %collective-permute-start.13 = (bf16[1,96,192]{2,1,0:T(8,128)(2,1)S(1)}, bf16[1,96,192]{2,1,0:T(8,128)(2,1)S(1)}, u32[]{:S(2)}, u32[]{:S(2)}) collective-permute-start(bf16[1,96,192]{2,1,0:T(8,128)(2,1)S(1)} %get-tuple-element.49), channel_id=1, source_target_pairs={{0,8},{4,12},{8,0},{12,4},{1,9},{5,13},{9,1},{13,5},{2,10},{6,14},... | collective-permute-start | bytes 110600 | tf_op jit(solution)/shard_map/ppermute | solution.py:199
  111.7 4.1 %collective-permute-start.14 = (bf16[1,96,192]{2,1,0:T(8,128)(2,1)S(1)}, bf16[1,96,192]{2,1,0:T(8,128)(2,1)S(1)}, u32[]{:S(2)}, u32[]{:S(2)}) collective-permute-start(bf16[1,96,192]{2,1,0:T(8,128)(2,1)S(1)} %get-tuple-element.48), channel_id=1, source_target_pairs={{0,12},{4,0},{8,4},{12,8},{1,13},{5,1},{9,5},{13,9},{2,14},{6,2},{... | collective-permute-start | bytes 110600 | tf_op jit(solution)/shard_map/ppermute | solution.py:199
  (3 other events, 2.4 us)

commit v5 on v4

--- a/solution.py
+++ b/solution.py
@@ -176,7 +176,7 @@
             bytes_accessed=8 * 2**20,
             transcendentals=HEADS * cells * cells,
         ),
-        compiler_params=pltpu.CompilerParams(vmem_limit_bytes=60 * 2**20),
+        compiler_params=pltpu.CompilerParams(vmem_limit_bytes=32 * 2**20),
     )(*args)
     return outs[:len(sizes)], outs[-2:]
 
@@ -211,7 +211,7 @@
             if goal is not None:
                 pair = (i * lons + j, goal[0] * lons + goal[1])
                 home = i * lons + (j + east) % lons
-                pairs.append((pair[1], home) if back else pair)
+                pairs.append((pair[1], home) if back else (home, pair[1]))
     return lax.ppermute(value, ("lat", "lon"), pairs)
 
 
@@ -274,18 +274,29 @@
     return mine + got.astype(F32)
 
 
-def reduce_weights(keep, send, lons):
+def reduce_weights(keep, send, lons, returns):
     half, deep, width = keep.shape
+    lats = lax.axis_size("lat")
+    moved, waiting = [], list(returns)
+
+    def release(value, count=1):
+        for _ in range(min(count, len(waiting))):
+            held, move = waiting.pop(0)
+            value, held = lax.optimization_barrier((value, held))
+            moved.append(move(held))
+        return value
+
     got = permuted(send, ("lon",), lambda i: (i ^ 1,))
-    lats = lax.axis_size("lat")
-    total = (keep + got.astype(F32)).reshape(lats, lons // 2, deep, width)
+    moved.append(waiting[0][1](waiting.pop(0)[0]))
+    total = release((keep + got.astype(F32)).reshape(lats, lons // 2, deep, width))
     bit, left = 2, lons // 2
     while left > 1:
         total = scatter_bit(total.reshape(lats, left // 2, 2, deep, width), "lon", bit, 2)
         left //= 2
         bit *= 2
-    total = scatter_direct(total.reshape(lats, deep, width), "dp", 2)
-    return scatter_direct(total, "lat", 0)[0]
+    total = release(total.reshape(lats, deep, width), len(waiting))
+    total = scatter_direct(total, "dp", 2)
+    return scatter_direct(total, "lat", 0)[0], moved
 
 
 def per_device(hidden_in, grad_out, norm_gain, w_qkv, w_proj):
@@ -312,15 +323,16 @@
     specs += [(r, at, WIN, wide, "") for at in inner for r in fixed]
     specs += [(r, edge, half, short, "") for r in fixed] + [(r, 0, half, short, "") for r in fixed]
     cuts = cut_call(hid, cot, specs, half)
-    own_side, side_sent = along_lon(cuts[0], -1), along_lon(cuts[1], -1)
-    own_edge, edge_sent = cuts[2:4]
+    side_sent, corner_sent, own_edge, edge_sent = cuts[:4]
     own_inner, rest = cuts[4:4 + len(inner)], cuts[4 + len(inner):]
     whole_inner = [[rest.pop(0) for _ in fixed] for _ in inner]
     whole_edge = [rest.pop(0) for _ in fixed]
     whole_side = [along_lon(rest.pop(0), -1) for _ in fixed]
     if inner_in:
-        edge_sent, side_sent, inner_in = lax.optimization_barrier((edge_sent, side_sent, inner_in))
-    edge_in, corner_in = shared(edge_sent), shared(side_sent)
+        edge_sent, side_sent, corner_sent, inner_in = lax.optimization_barrier(
+            (edge_sent, side_sent, corner_sent, inner_in)
+        )
+    own_side, edge_in, corner_in = along_lon(side_sent, -1), shared(edge_sent), shared(corner_sent, east=1)
 
     order = [(b, wr, wc) for b in range(samples) for wc in range(nc) for wr in range(nr)]
     sums = None
@@ -344,6 +356,14 @@
         )
         out[b, wr, wc] = [d.reshape(half, pad, width) for d, (n, pad, _) in zip(done, metas)]
 
+    late = []
+    for b in range(samples):
+        own, own_lon, other, other_lon = out[b, nr - 1, nc - 1]
+        late.append((other, lambda v: shared(v, back=True)))
+        late.append((other_lon, lambda v: shared(v, back=True, east=1)))
+        late.append((own_lon, lambda v: along_lon(v, 1)))
+    total, moved = reduce_weights(sums[0], sums[1], lons, late)
+
     rows_out = []
     for b in range(samples):
         def stacked(own, back, between, upper):
@@ -356,11 +376,11 @@
             own, other = out[b, nr - 1, wc]
             between = [out[b, wr, wc][i] for wr in range(nr - 1) for i in range(2)]
             columns.append(stacked(own, shared(other, back=True), between, odd == 1)[:, :WIN])
-        own, own_lon, other, other_lon = out[b, nr - 1, nc - 1]
+        own = out[b, nr - 1, nc - 1][0]
+        back, far, near = moved[3 * b:3 * b + 3]
         between = [out[b, wr, nc - 1][i] for wr in range(nr - 1) for i in (0, 2)]
-        columns.append(stacked(own, shared(other, back=True), between, odd == 1)[:, :half])
+        columns.append(stacked(own, back, between, odd == 1)[:, :half])
         between = [along_lon(out[b, wr, nc - 1][i], 1) for wr in range(nr - 1) for i in (1, 3)]
-        near, far = along_lon(own_lon, 1), shared(other_lon, back=True, east=1)
         columns.insert(0, stacked(near, far, between, odd == 0)[:, :half])
         rows_out.append(jnp.concatenate(columns, axis=1))
     returned = jnp.stack(rows_out)
@@ -369,7 +389,7 @@
         lax.axis_size("dp") * samples * lat_rows * lax.axis_size("lat") * lon_cols * lons
     )
     factor = float(total_cells) ** (-0.5)
-    total = reduce_weights(sums[0], sums[1], lons).T * factor
+    total = total.T * factor
     cut = 3 * width // parts
     return (grad_in, total[:, :cut], total[:, cut:])
 

time: 117 us -> 114 us (0.974)
  waiting for transfers between devices: 17.8 us -> 27.6 us
  starting transfers between devices: 30.4 us -> 23.3 us
  Pallas kernels: 58.5 us -> 51.7 us
  other arithmetic: 2.55 us -> 4.67 us
  local copies, waits for them, and re-layouts: 6.79 us -> 5.21 us
    ppermute x6, waiting for transfers between devices: 3.78 us -> 16.5 us  [shared(): return lax.ppermute(value, ('lat', 'lon'), pairs)]
    pallas_call x2, Pallas kernels: 57.6 us -> 50.8 us  [window_call(): pl.pallas_call(functools.partial(window_kernel, head, metas, (prev is not...]
    ppermute x3 -> x2, starting transfers between devices: 4.79 us -> 0.06 us  [along_lon(): lax.ppermute(value, 'lon', [(j, (j + step) % count) for j in range(count)])]
    ppermute x3 -> x2, waiting for transfers between devices: 5 us -> 1.06 us  [along_lon(): lax.ppermute(value, 'lon', [(j, (j + step) % count) for j in range(count)])]
    ppermute x6, starting transfers between devices: 7.68 us -> 6.07 us  [permuted(): return lax.ppermute(value, tuple(axes), pairs)]
    unnamed x24 -> x14, local copies, waits for them, and re-layouts: 5.35 us -> 3.77 us
  transfers between devices with their start and end apart: 15 -> 14, of which waited for: 6 -> 7; matrix products, arithmetic and copies ran while one was open for 2% -> 3% of each run, Pallas kernels for 50% -> 23%
where the time goes in v5:
time: 114 us; the launch traced here: 113 us
  Pallas kernels  51.7 us (45%)
  waiting for transfers between devices  27.6 us (24%)
  starting transfers between devices  23.3 us (20%)
  local copies, waits for them, and re-layouts  5.21 us (5%)
  other arithmetic  4.67 us (4%)
    pallas_call x2, Pallas kernels, window_call(): pl.pallas_call(functools.partial(window_kernel, head, metas, (prev is not...  50.8 us
    ppermute x6, starting transfers between devices, shared(): return lax.ppermute(value, ('lat', 'lon'), pairs)  17.1 us
    ppermute x6, waiting for transfers between devices, shared(): return lax.ppermute(value, ('lat', 'lon'), pairs)  16.5 us
    ppermute x6, waiting for transfers between devices, permuted(): return lax.ppermute(value, tuple(axes), pairs)  10 us
    ppermute x6, starting transfers between devices, permuted(): return lax.ppermute(value, tuple(axes), pairs)  6.07 us
    unnamed x14, local copies, waits for them, and re-layouts  3.77 us
  transfers between devices with their start and end apart: 14, of which 7 were waited for; matrix products, arithmetic and copies ran while one was open for 3% of the time, Pallas kernels for 23%

profile of v5, /device:TPU:0, one launch (start us, length us, event | category | flops | bytes accessed | tf_op | source)
XLA Modules:
  0.0 113.4 jit_solution(13735289983985750484)
XLA Ops:
  0.6 1.4 %copy-done = bf16[1,30,60,384]{3,2,1,0:T(8,128)(2,1)S(1)} copy-done((bf16[1,30,60,384]{3,2,1,0:T(8,128)(2,1)S(1)}, bf16[1,30,60,384]{3,2,1,0:T(8,128)(2,1)}, u32[]{:S(2)}) %copy-start) | copy-done | bytes 1382424
  2.0 1.4 %copy-done.2 = bf16[1,30,60,384]{3,2,1,0:T(8,128)(2,1)S(1)} copy-done((bf16[1,30,60,384]{3,2,1,0:T(8,128)(2,1)S(1)}, bf16[1,30,60,384]{3,2,1,0:T(8,128)(2,1)}, u32[]{:S(2)}) %copy-start.2) | copy-done | bytes 1382424
  3.6 1.4 %collective-permute-start = (bf16[2,1,15,32,384]{4,3,2,1,0:T(8,128)(2,1)S(1)}, bf16[2,1,15,32,384]{4,3,2,1,0:T(8,128)(2,1)S(1)}, u32[]{:S(2)}, u32[]{:S(2)}) collective-permute-start(bf16[2,1,15,32,384]{4,3,2,1,0:T(8,128)(2,1)S(1)} %shard_map.76), channel_id=1, source_target_pairs={{1,5},{3,7},{4,0},{5,9},{6,2},{7,11},{8,4},{9,13},{10,6},{11,15},{... | collective-permute-start | bytes 2211848 | tf_op jit(solution)/shard_map/ppermute | solution.py:215
  5.1 0.7 shard_map.77
  5.7 12.4 %collective-permute-done = bf16[2,1,15,32,384]{4,3,2,1,0:T(8,128)(2,1)S(1)} collective-permute-done((bf16[2,1,15,32,384]{4,3,2,1,0:T(8,128)(2,1)S(1)}, bf16[2,1,15,32,384]{4,3,2,1,0:T(8,128)(2,1)S(1)}, u32[]{:S(2)}, u32[]{:S(2)}) %collective-permute-start) | collective-permute-done | bytes 737312 | tf_op jit(solution)/shard_map/ppermute | solution.py:215
  18.1 1.3 %collective-permute-start.2 = (bf16[2,1,15,16,384]{4,3,2,1,0:T(8,128)(2,1)S(1)}, bf16[2,1,15,16,384]{4,3,2,1,0:T(8,128)(2,1)S(1)}, u32[]{:S(2)}, u32[]{:S(2)}) collective-permute-start(bf16[2,1,15,16,384]{4,3,2,1,0:T(8,128)(2,1)S(1)} %get-tuple-element.37), channel_id=1, source_target_pairs={{1,5},{3,7},{4,0},{5,9},{6,2},{7,11},{8,4},{9,13},{10,6},{11,15},{... | collective-permute-start | bytes 1105928 | tf_op jit(solution)/shard_map/ppermute | solution.py:215
  19.4 6.9 %collective-permute-start.3 = (bf16[2,1,15,16,384]{4,3,2,1,0:T(8,128)(2,1)S(1)}, bf16[2,1,15,16,384]{4,3,2,1,0:T(8,128)(2,1)S(1)}, u32[]{:S(2)}, u32[]{:S(2)}) collective-permute-start(bf16[2,1,15,16,384]{4,3,2,1,0:T(8,128)(2,1)S(1)} %get-tuple-element.38), channel_id=1, source_target_pairs={{2,5},{0,7},{5,0},{6,9},{7,2},{4,11},{9,4},{10,13},{11,6},{8,15},{... | collective-permute-start | bytes 1105928 | tf_op jit(solution)/shard_map/ppermute | solution.py:215
  26.4 25.1 %shard_map.78 = (bf16[480,384]{1,0:T(8,128)(2,1)S(1)}, bf16[480,384]{1,0:T(8,128)(2,1)S(1)}, f32[384,1152]{1,0:T(8,128)S(1)}, f32[384,384]{1,0:T(8,128)S(1)}) custom-call(bf16[2,480,384]{2,1,0:T(8,128)(2,1)S(1)} %bitcast.28, bf16[2,480,384]{2,1,0:T(8,128)(2,1)S(1)} %bitcast.27, f32[384]{0:T(512)S(1)} %copy-done.5, bf16[384,1152]{1,0:T(8,128)(2,1)S(1)} %copy-done.3, ...), custom_call_target="tpu_custom_call" | custom-call | flops 7644119040 | bytes 8388608 | tf_op jit(solution)/shard_map/pallas_call | solution.py:168
  51.5 25.8 %shard_map.79 = (bf16[240,384]{1,0:T(8,128)(2,1)S(1)}, bf16[240,384]{1,0:T(8,128)(2,1)S(1)}, bf16[240,384]{1,0:T(8,128)(2,1)S(1)}, bf16[240,384]{1,0:T(8,128)(2,...) custom-call(bf16[2,240,384]{2,1,0:T(8,128)(2,1)S(1)} %bitcast.30, bf16[2,240,384]{2,1,0:T(8,128)(2,1)S(1)} %bitcast.31, ...), custom_call_target="tpu_custom_call" | custom-call | flops 7644119040 | bytes 8388608 | tf_op jit(solution)/shard_map/pallas_call | solution.py:168
  77.4 2.1 %collective-permute-done.4 = bf16[8,96,384]{2,1,0:T(8,128)(2,1)} collective-permute-done((bf16[8,96,384]{2,1,0:T(8,128)(2,1)S(1)}, bf16[8,96,384]{2,1,0:T(8,128)(2,1)}, u32[]{:S(2)}, u32[]{:S(2)}) %collective-permute-start.4) | collective-permute-done | bytes 589856 | tf_op jit(solution)/shard_map/ppermute | solution.py:199
  79.4 1.2 %convert_add_fusion = f32[8,96,384]{2,1,0:T(8,128)S(1)} fusion(f32[8,96,384]{2,1,0:T(8,128)S(1)} %get-tuple-element.43, bf16[8,96,384]{2,1,0:T(8,128)(2,1)} %collective-permute-done.4), kind=kLoop, calls=%fused_computation.1 | loop fusion | flops 589824 | bytes 2949120 | tf_op jit(solution)/shard_map/add | solution.py:291
  80.6 1.0 copy-done.6
  82.2 2.2 %collective-permute-start.8 = (bf16[15,32,384]{2,1,0:T(8,128)(2,1)S(1)}, bf16[15,32,384]{2,1,0:T(8,128)(2,1)S(1)}, u32[]{:S(2)}, u32[]{:S(2)}) collective-permute-start(bf16[15,32,384]{2,1,0:T(8,128)(2,1)S(1)} %bitcast.29), channel_id=1, source_target_pairs={{5,1},{7,3},{0,4},{9,5},{2,6},{11,7},{4,8},{13,9},{6,10},{15,11},{... | collective-permute-start | bytes 1105928 | tf_op jit(solution)/shard_map/ppermute | solution.py:215
  84.5 3.3 %collective-permute-start.9 = (bf16[15,16,384]{2,1,0:T(8,128)(2,1)S(1)}, bf16[15,16,384]{2,1,0:T(8,128)(2,1)S(1)}, u32[]{:S(2)}, u32[]{:S(2)}) collective-permute-start(bf16[15,16,384]{2,1,0:T(8,128)(2,1)S(1)} %bitcast.36), channel_id=1, source_target_pairs={{5,1},{7,3},{0,4},{9,5},{2,6},{11,7},{4,8},{13,9},{6,10},{15,11},{... | collective-permute-start | bytes 552968 | tf_op jit(solution)/shard_map/ppermute | solution.py:215
  87.7 3.0 %collective-permute-done.5 = bf16[4,1,96,384]{3,2,0,1:T(8,128)(2,1)S(1)} collective-permute-done((bf16[4,1,96,384]{3,2,0,1:T(8,128)(2,1)S(1)}, bf16[4,1,96,384]{3,2,0,1:T(8,128)(2,1)S(1)}, u32[]{:S(2)}, u32[]{:S(2)}) %collective-permute-start.5) | collective-permute-done | bytes 294944 | tf_op jit(solution)/shard_map/ppermute | solution.py:199
  90.8 1.1 add_bitcast_fusion
  92.0 1.6 %collective-permute-start.10 = (bf16[4,96,192]{2,1,0:T(8,128)(2,1)S(1)}, bf16[4,96,192]{2,1,0:T(8,128)(2,1)S(1)}, u32[]{:S(2)}, u32[]{:S(2)}) collective-permute-start(bf16[4,96,192]{2,1,0:T(8,128)(2,1)S(1)} %dynamic-slice_convert_fusion.1), channel_id=1, source_target_pairs={{0,16},{16,0},{1,17},{17,1},{2,18},{18,2},{3,19},{19,3},{4,20},{20... | collective-permute-start | bytes 442376 | tf_op jit(solution)/shard_map/ppermute | solution.py:199
  93.8 4.5 %collective-permute-done.10 = bf16[4,96,192]{2,1,0:T(8,128)(2,1)S(1)} collective-permute-done((bf16[4,96,192]{2,1,0:T(8,128)(2,1)S(1)}, bf16[4,96,192]{2,1,0:T(8,128)(2,1)S(1)}, u32[]{:S(2)}, u32[]{:S(2)}) %collective-permute-start.10) | collective-permute-done | bytes 147488 | tf_op jit(solution)/shard_map/ppermute | solution.py:199
  98.8 1.9 %collective-permute-start.12 = (bf16[1,96,192]{2,1,0:T(8,128)(2,1)S(1)}, bf16[1,96,192]{2,1,0:T(8,128)(2,1)S(1)}, u32[]{:S(2)}, u32[]{:S(2)}) collective-permute-start(bf16[1,96,192]{2,1,0:T(8,128)(2,1)S(1)} %get-tuple-element.59), channel_id=1, source_target_pairs={{0,8},{4,12},{8,0},{12,4},{1,9},{5,13},{9,1},{13,5},{2,10},{6,14},... | collective-permute-start | bytes 110600 | tf_op jit(solution)/shard_map/ppermute | solution.py:199
  100.7 1.6 %collective-permute-start.13 = (bf16[1,96,192]{2,1,0:T(8,128)(2,1)S(1)}, bf16[1,96,192]{2,1,0:T(8,128)(2,1)S(1)}, u32[]{:S(2)}, u32[]{:S(2)}) collective-permute-start(bf16[1,96,192]{2,1,0:T(8,128)(2,1)S(1)} %get-tuple-element.58), channel_id=1, source_target_pairs={{0,12},{4,0},{8,4},{12,8},{1,13},{5,1},{9,5},{13,9},{2,14},{6,2},{... | collective-permute-start | bytes 110600 | tf_op jit(solution)/shard_map/ppermute | solution.py:199
  102.4 2.1 %collective-permute-start.7 = (bf16[15,16,384]{2,1,0:T(8,128)(2,1)S(1)}, bf16[15,16,384]{2,1,0:T(8,128)(2,1)S(1)}, u32[]{:S(2)}, u32[]{:S(2)}) collective-permute-start(bf16[15,16,384]{2,1,0:T(8,128)(2,1)S(1)} %bitcast.35), channel_id=1, source_target_pairs={{5,2},{7,0},{0,5},{9,6},{2,7},{11,4},{4,9},{13,10},{6,11},{15,8},{... | collective-permute-start | bytes 552968 | tf_op jit(solution)/shard_map/ppermute | solution.py:215
  106.2 4.2 %collective-permute-done.7 = bf16[15,16,384]{2,1,0:T(8,128)(2,1)S(1)} collective-permute-done((bf16[15,16,384]{2,1,0:T(8,128)(2,1)S(1)}, bf16[15,16,384]{2,1,0:T(8,128)(2,1)S(1)}, u32[]{:S(2)}, u32[]{:S(2)}) %collective-permute-start.7) | collective-permute-done | bytes 184352 | tf_op jit(solution)/shard_map/ppermute | solution.py:215
  110.4 1.1 collective-permute-done.6
  111.6 1.9 %add_convert_fusion = bf16[1,30,60,384]{3,2,1,0:T(8,128)(2,1)} fusion(bf16[1,30,60,384]{3,2,1,0:T(8,128)(2,1)S(1)} %copy-done.1, bf16[1,30,15,384]{3,2,1,0:T(8,128)(2,1)S(1)} %get-tuple-element.64, bf16[1,30,30,384]{3,2,1,0:T(8,128)(2,1)S(1)} %fusion, bf16[1,30,15,384]{3,2,1,0:T(8,128)(2,1)S(1)} %get-tuple-element.65), kind=kLoop, calls=%fused_computation | loop fusion | flops 6220800 | bytes 4147200 | tf_op jit(solution)/shard_map/convert_element_type | solution.py:387
  (37 shorter events, 3.7 us)
Async XLA Ops:
  0.6 1.4 %copy-start = (bf16[1,30,60,384]{3,2,1,0:T(8,128)(2,1)S(1)}, bf16[1,30,60,384]{3,2,1,0:T(8,128)(2,1)}, u32[]{:S(2)}) copy-start(bf16[1,30,60,384]{3,2,1,0:T(8,128)(2,1)} %cot_ref.2) | copy-start | bytes 4147204
  2.0 1.4 %copy-start.2 = (bf16[1,30,60,384]{3,2,1,0:T(8,128)(2,1)S(1)}, bf16[1,30,60,384]{3,2,1,0:T(8,128)(2,1)}, u32[]{:S(2)}) copy-start(bf16[1,30,60,384]{3,2,1,0:T(8,128)(2,1)} %hid_ref.2) | copy-start | bytes 4147204
  3.6 22.7 %copy-start.3 = (bf16[384,1152]{1,0:T(8,128)(2,1)S(1)}, bf16[384,1152]{1,0:T(8,128)(2,1)}, u32[]{:S(2)}) copy-start(bf16[384,1152]{1,0:T(8,128)(2,1)} %refs_5_.1) | copy-start | bytes 2654212
  3.6 22.7 %copy-start.4 = (bf16[384,384]{1,0:T(8,128)(2,1)S(1)}, bf16[384,384]{1,0:T(8,128)(2,1)}, u32[]{:S(2)}) copy-start(bf16[384,384]{1,0:T(8,128)(2,1)} %refs_6_.1) | copy-start | bytes 884740
  3.6 22.7 %copy-start.5 = (f32[384]{0:T(512)S(1)}, f32[384]{0:T(512)}, u32[]{:S(2)}) copy-start(f32[384]{0:T(512)} %refs_4_.3) | copy-start | bytes 4612
  3.6 14.5 %collective-permute-start = (bf16[2,1,15,32,384]{4,3,2,1,0:T(8,128)(2,1)S(1)}, bf16[2,1,15,32,384]{4,3,2,1,0:T(8,128)(2,1)S(1)}, u32[]{:S(2)}, u32[]{:S(2)}) collective-permute-start(bf16[2,1,15,32,384]{4,3,2,1,0:T(8,128)(2,1)S(1)} %shard_map.76), channel_id=1, source_target_pairs={{1,5},{3,7},{4,0},{5,9},{6,2},{7,11},{8,4},{9,13},{10,6},{11,15},{... | collective-permute-start | bytes 2211848 | tf_op jit(solution)/shard_map/ppermute | solution.py:215
  18.1 33.3 %collective-permute-start.1 = (bf16[2,1,15,16,384]{4,3,2,1,0:T(8,128)(2,1)S(1)}, bf16[2,1,15,16,384]{4,3,2,1,0:T(8,128)(2,1)S(1)}, u32[]{:S(2)}, u32[]{:S(2)}) collective-permute-start(bf16[2,1,15,16,384]{4,3,2,1,0:T(8,128)(2,1)S(1)} %get-tuple-element.36), channel_id=1, source_target_pairs={{0,3},{1,0},{2,1},{3,2},{4,7},{5,4},{6,5},{7,6},{8,11},{9,8},{10,9... | collective-permute-start | bytes 1105928 | tf_op jit(solution)/shard_map/ppermute | solution.py:220
  18.1 33.3 %collective-permute-start.2 = (bf16[2,1,15,16,384]{4,3,2,1,0:T(8,128)(2,1)S(1)}, bf16[2,1,15,16,384]{4,3,2,1,0:T(8,128)(2,1)S(1)}, u32[]{:S(2)}, u32[]{:S(2)}) collective-permute-start(bf16[2,1,15,16,384]{4,3,2,1,0:T(8,128)(2,1)S(1)} %get-tuple-element.37), channel_id=1, source_target_pairs={{1,5},{3,7},{4,0},{5,9},{6,2},{7,11},{8,4},{9,13},{10,6},{11,15},{... | collective-permute-start | bytes 1105928 | tf_op jit(solution)/shard_map/ppermute | solution.py:215
  19.4 32.0 %collective-permute-start.3 = (bf16[2,1,15,16,384]{4,3,2,1,0:T(8,128)(2,1)S(1)}, bf16[2,1,15,16,384]{4,3,2,1,0:T(8,128)(2,1)S(1)}, u32[]{:S(2)}, u32[]{:S(2)}) collective-permute-start(bf16[2,1,15,16,384]{4,3,2,1,0:T(8,128)(2,1)S(1)} %get-tuple-element.38), channel_id=1, source_target_pairs={{2,5},{0,7},{5,0},{6,9},{7,2},{4,11},{9,4},{10,13},{11,6},{8,15},{... | collective-permute-start | bytes 1105928 | tf_op jit(solution)/shard_map/ppermute | solution.py:215
  77.2 2.2 %collective-permute-start.4 = (bf16[8,96,384]{2,1,0:T(8,128)(2,1)S(1)}, bf16[8,96,384]{2,1,0:T(8,128)(2,1)}, u32[]{:S(2)}, u32[]{:S(2)}) collective-permute-start(bf16[8,96,384]{2,1,0:T(8,128)(2,1)S(1)} %get-tuple-element.44), channel_id=1, source_target_pairs={{0,1},{1,0},{2,3},{3,2},{4,5},{5,4},{6,7},{7,6},{8,9},{9,8},{10,11... | collective-permute-start | bytes 1769480 | tf_op jit(solution)/shard_map/ppermute | solution.py:199
  80.6 1.0 copy-start.6
  81.7 9.1 %collective-permute-start.5 = (bf16[4,1,96,384]{3,2,0,1:T(8,128)(2,1)S(1)}, bf16[4,1,96,384]{3,2,0,1:T(8,128)(2,1)S(1)}, u32[]{:S(2)}, u32[]{:S(2)}) collective-permute-start(bf16[4,1,96,384]{3,2,0,1:T(8,128)(2,1)S(1)} %dynamic-slice_convert_fusion), channel_id=1, source_target_pairs={{0,2},{1,3},{2,0},{3,1},{4,6},{5,7},{6,4},{7,5},{8,10},{9,11},{10,... | collective-permute-start | bytes 884744 | tf_op jit(solution)/shard_map/ppermute | solution.py:199
  82.2 11.4 %collective-permute-start.8 = (bf16[15,32,384]{2,1,0:T(8,128)(2,1)S(1)}, bf16[15,32,384]{2,1,0:T(8,128)(2,1)S(1)}, u32[]{:S(2)}, u32[]{:S(2)}) collective-permute-start(bf16[15,32,384]{2,1,0:T(8,128)(2,1)S(1)} %bitcast.29), channel_id=1, source_target_pairs={{5,1},{7,3},{0,4},{9,5},{2,6},{11,7},{4,8},{13,9},{6,10},{15,11},{... | collective-permute-start | bytes 1105928 | tf_op jit(solution)/shard_map/ppermute | solution.py:215
  84.5 17.9 %collective-permute-start.9 = (bf16[15,16,384]{2,1,0:T(8,128)(2,1)S(1)}, bf16[15,16,384]{2,1,0:T(8,128)(2,1)S(1)}, u32[]{:S(2)}, u32[]{:S(2)}) collective-permute-start(bf16[15,16,384]{2,1,0:T(8,128)(2,1)S(1)} %bitcast.36), channel_id=1, source_target_pairs={{5,1},{7,3},{0,4},{9,5},{2,6},{11,7},{4,8},{13,9},{6,10},{15,11},{... | collective-permute-start | bytes 552968 | tf_op jit(solution)/shard_map/ppermute | solution.py:215
  92.0 6.2 %collective-permute-start.10 = (bf16[4,96,192]{2,1,0:T(8,128)(2,1)S(1)}, bf16[4,96,192]{2,1,0:T(8,128)(2,1)S(1)}, u32[]{:S(2)}, u32[]{:S(2)}) collective-permute-start(bf16[4,96,192]{2,1,0:T(8,128)(2,1)S(1)} %dynamic-slice_convert_fusion.1), channel_id=1, source_target_pairs={{0,16},{16,0},{1,17},{17,1},{2,18},{18,2},{3,19},{19,3},{4,20},{20... | collective-permute-start | bytes 442376 | tf_op jit(solution)/shard_map/ppermute | solution.py:199
  98.4 6.1 %collective-permute-start.11 = (bf16[1,96,192]{2,1,0:T(8,128)(2,1)S(1)}, bf16[1,96,192]{2,1,0:T(8,128)(2,1)S(1)}, u32[]{:S(2)}, u32[]{:S(2)}) collective-permute-start(bf16[1,96,192]{2,1,0:T(8,128)(2,1)S(1)} %get-tuple-element.57), channel_id=1, source_target_pairs={{0,4},{4,8},{8,12},{12,0},{1,5},{5,9},{9,13},{13,1},{2,6},{6,10},{... | collective-permute-start | bytes 110600 | tf_op jit(solution)/shard_map/ppermute | solution.py:199
  98.8 5.7 %collective-permute-start.12 = (bf16[1,96,192]{2,1,0:T(8,128)(2,1)S(1)}, bf16[1,96,192]{2,1,0:T(8,128)(2,1)S(1)}, u32[]{:S(2)}, u32[]{:S(2)}) collective-permute-start(bf16[1,96,192]{2,1,0:T(8,128)(2,1)S(1)} %get-tuple-element.59), channel_id=1, source_target_pairs={{0,8},{4,12},{8,0},{12,4},{1,9},{5,13},{9,1},{13,5},{2,10},{6,14},... | collective-permute-start | bytes 110600 | tf_op jit(solution)/shard_map/ppermute | solution.py:199
  100.7 4.3 %collective-permute-start.13 = (bf16[1,96,192]{2,1,0:T(8,128)(2,1)S(1)}, bf16[1,96,192]{2,1,0:T(8,128)(2,1)S(1)}, u32[]{:S(2)}, u32[]{:S(2)}) collective-permute-start(bf16[1,96,192]{2,1,0:T(8,128)(2,1)S(1)} %get-tuple-element.58), channel_id=1, source_target_pairs={{0,12},{4,0},{8,4},{12,8},{1,13},{5,1},{9,5},{13,9},{2,14},{6,2},{... | collective-permute-start | bytes 110600 | tf_op jit(solution)/shard_map/ppermute | solution.py:199
  102.4 9.2 %copy-start.1 = (bf16[1,30,60,384]{3,2,1,0:T(8,128)(2,1)S(1)}, bf16[1,30,60,384]{3,2,1,0:T(8,128)(2,1)}, u32[]{:S(2)}) copy-start(bf16[1,30,60,384]{3,2,1,0:T(8,128)(2,1)} %cot_ref.2) | copy-start | bytes 4147204
  102.4 8.0 %collective-permute-start.7 = (bf16[15,16,384]{2,1,0:T(8,128)(2,1)S(1)}, bf16[15,16,384]{2,1,0:T(8,128)(2,1)S(1)}, u32[]{:S(2)}, u32[]{:S(2)}) collective-permute-start(bf16[15,16,384]{2,1,0:T(8,128)(2,1)S(1)} %bitcast.35), channel_id=1, source_target_pairs={{5,2},{7,0},{0,5},{9,6},{2,7},{11,4},{4,9},{13,10},{6,11},{15,8},{... | collective-permute-start | bytes 552968 | tf_op jit(solution)/shard_map/ppermute | solution.py:215
  104.4 7.0 %collective-permute-start.6 = (bf16[15,16,384]{2,1,0:T(8,128)(2,1)S(1)}, bf16[15,16,384]{2,1,0:T(8,128)(2,1)S(1)}, u32[]{:S(2)}, u32[]{:S(2)}) collective-permute-start(bf16[15,16,384]{2,1,0:T(8,128)(2,1)S(1)} %bitcast.34), channel_id=1, source_target_pairs={{0,1},{1,2},{2,3},{3,0},{4,5},{5,6},{6,7},{7,4},{8,9},{9,10},{10,1... | collective-permute-start | bytes 552968 | tf_op jit(solution)/shard_map/ppermute | solution.py:220

commit v6 on v5

--- a/solution.py
+++ b/solution.py
@@ -287,15 +287,17 @@
         return value
 
     got = permuted(send, ("lon",), lambda i: (i ^ 1,))
-    moved.append(waiting[0][1](waiting.pop(0)[0]))
-    total = release((keep + got.astype(F32)).reshape(lats, lons // 2, deep, width))
+    keep = release(keep, len(waiting) // 2)
+    early = len(moved)
+    total = release((keep + got.astype(F32)).reshape(lats, lons // 2, deep, width), len(waiting))
     bit, left = 2, lons // 2
     while left > 1:
         total = scatter_bit(total.reshape(lats, left // 2, 2, deep, width), "lon", bit, 2)
         left //= 2
         bit *= 2
-    total = release(total.reshape(lats, deep, width), len(waiting))
+    total, moved[:early] = lax.optimization_barrier((total.reshape(lats, deep, width), moved[:early]))
     total = scatter_direct(total, "dp", 2)
+    total, moved[early:] = lax.optimization_barrier((total, moved[early:]))
     return scatter_direct(total, "lat", 0)[0], moved
 
 
@@ -328,10 +330,6 @@
     whole_inner = [[rest.pop(0) for _ in fixed] for _ in inner]
     whole_edge = [rest.pop(0) for _ in fixed]
     whole_side = [along_lon(rest.pop(0), -1) for _ in fixed]
-    if inner_in:
-        edge_sent, side_sent, corner_sent, inner_in = lax.optimization_barrier(
-            (edge_sent, side_sent, corner_sent, inner_in)
-        )
     own_side, edge_in, corner_in = along_lon(side_sent, -1), shared(edge_sent), shared(corner_sent, east=1)
 
     order = [(b, wr, wc) for b in range(samples) for wc in range(nc) for wr in range(nr)]
@@ -356,7 +354,7 @@
         )
         out[b, wr, wc] = [d.reshape(half, pad, width) for d, (n, pad, _) in zip(done, metas)]
 
-    late = []
+    late = [(out[b, nr - 1, wc][1], lambda v: shared(v, back=True)) for b in range(samples) for wc in range(nc - 1)]
     for b in range(samples):
         own, own_lon, other, other_lon = out[b, nr - 1, nc - 1]
         late.append((other, lambda v: shared(v, back=True)))
@@ -375,9 +373,9 @@
         for wc in range(nc - 1):
             own, other = out[b, nr - 1, wc]
             between = [out[b, wr, wc][i] for wr in range(nr - 1) for i in range(2)]
-            columns.append(stacked(own, shared(other, back=True), between, odd == 1)[:, :WIN])
+            columns.append(stacked(own, moved[b * (nc - 1) + wc], between, odd == 1)[:, :WIN])
         own = out[b, nr - 1, nc - 1][0]
-        back, far, near = moved[3 * b:3 * b + 3]
+        back, far, near = moved[samples * (nc - 1) + 3 * b:][:3]
         between = [out[b, wr, nc - 1][i] for wr in range(nr - 1) for i in (0, 2)]
         columns.append(stacked(own, back, between, odd == 1)[:, :half])
         between = [along_lon(out[b, wr, nc - 1][i], 1) for wr in range(nr - 1) for i in (1, 3)]

time: 114 us -> 104 us (0.912)
  waiting for transfers between devices: 27.6 us -> 10.3 us
  starting transfers between devices: 23.3 us -> 31.2 us
    ppermute x6, waiting for transfers between devices: 16.5 us -> 3.6 us  [shared(): return lax.ppermute(value, ('lat', 'lon'), pairs)]
    ppermute x2, starting transfers between devices: 0.06 us -> 4.47 us  [along_lon(): lax.ppermute(value, 'lon', [(j, (j + step) % count) for j in range(count)])]
    ppermute x6, starting transfers between devices: 6.07 us -> 10.1 us  [permuted(): return lax.ppermute(value, tuple(axes), pairs)]
    ppermute x6, waiting for transfers between devices: 10 us -> 6.65 us  [permuted(): return lax.ppermute(value, tuple(axes), pairs)]
  transfers between devices with their start and end apart: 14 -> 14, of which waited for: 7 -> 4; matrix products, arithmetic and copies ran while one was open for 3% -> 3% of each run, Pallas kernels for 23% -> 25%
where the time goes in v6:
time: 104 us
  Pallas kernels  51.7 us (50%)
  starting transfers between devices  31.2 us (30%)
  waiting for transfers between devices  10.3 us (10%)
  local copies, waits for them, and re-layouts  5.16 us (5%)
  other arithmetic  4.7 us (5%)
    pallas_call x2, Pallas kernels, window_call(): pl.pallas_call(functools.partial(window_kernel, head, metas, (prev is not...  50.8 us
    ppermute x6, starting transfers between devices, shared(): return lax.ppermute(value, ('lat', 'lon'), pairs)  16.6 us
    ppermute x6, starting transfers between devices, permuted(): return lax.ppermute(value, tuple(axes), pairs)  10.1 us
    ppermute x6, waiting for transfers between devices, permuted(): return lax.ppermute(value, tuple(axes), pairs)  6.65 us
    ppermute x2, starting transfers between devices, along_lon(): lax.ppermute(value, 'lon', [(j, (j + step) % count) for j in range(count)])  4.47 us
    unnamed x14, local copies, waits for them, and re-layouts  3.72 us
    ppermute x6, waiting for transfers between devices, shared(): return lax.ppermute(value, ('lat', 'lon'), pairs)  3.6 us
  transfers between devices with their start and end apart: 14, of which 4 were waited for; matrix products, arithmetic and copies ran while one was open for 3% of the time, Pallas kernels for 25%

profile of v6, /device:TPU:0, one launch (start us, length us, event | category | flops | bytes accessed | tf_op | source)
XLA Modules:
  0.0 104.0 jit_solution(14706138061782256632)
XLA Ops:
  0.6 1.4 %copy-done = bf16[1,30,60,384]{3,2,1,0:T(8,128)(2,1)S(1)} copy-done((bf16[1,30,60,384]{3,2,1,0:T(8,128)(2,1)S(1)}, bf16[1,30,60,384]{3,2,1,0:T(8,128)(2,1)}, u32[]{:S(2)}) %copy-start) | copy-done | bytes 1382424
  2.0 1.4 %copy-done.2 = bf16[1,30,60,384]{3,2,1,0:T(8,128)(2,1)S(1)} copy-done((bf16[1,30,60,384]{3,2,1,0:T(8,128)(2,1)S(1)}, bf16[1,30,60,384]{3,2,1,0:T(8,128)(2,1)}, u32[]{:S(2)}) %copy-start.2) | copy-done | bytes 1382424
  3.6 1.4 %collective-permute-start.3 = (bf16[2,1,15,32,384]{4,3,2,1,0:T(8,128)(2,1)S(1)}, bf16[2,1,15,32,384]{4,3,2,1,0:T(8,128)(2,1)S(1)}, u32[]{:S(2)}, u32[]{:S(2)}) collective-permute-start(bf16[2,1,15,32,384]{4,3,2,1,0:T(8,128)(2,1)S(1)} %shard_map.76), channel_id=1, source_target_pairs={{1,5},{3,7},{4,0},{5,9},{6,2},{7,11},{8,4},{9,13},{10,6},{11,15},{... | collective-permute-start | bytes 2211848 | tf_op jit(solution)/shard_map/ppermute | solution.py:215
  5.1 0.7 shard_map.77
  5.7 4.4 %collective-permute-start = (bf16[2,1,15,16,384]{4,3,2,1,0:T(8,128)(2,1)S(1)}, bf16[2,1,15,16,384]{4,3,2,1,0:T(8,128)(2,1)S(1)}, u32[]{:S(2)}, u32[]{:S(2)}) collective-permute-start(bf16[2,1,15,16,384]{4,3,2,1,0:T(8,128)(2,1)S(1)} %get-tuple-element.38), channel_id=1, source_target_pairs={{0,3},{1,0},{2,1},{3,2},{4,7},{5,4},{6,5},{7,6},{8,11},{9,8},{10,9... | collective-permute-start | bytes 1105928 | tf_op jit(solution)/shard_map/ppermute | solution.py:220
  10.2 1.3 %collective-permute-start.1 = (bf16[2,1,15,16,384]{4,3,2,1,0:T(8,128)(2,1)S(1)}, bf16[2,1,15,16,384]{4,3,2,1,0:T(8,128)(2,1)S(1)}, u32[]{:S(2)}, u32[]{:S(2)}) collective-permute-start(bf16[2,1,15,16,384]{4,3,2,1,0:T(8,128)(2,1)S(1)} %get-tuple-element.39), channel_id=1, source_target_pairs={{1,5},{3,7},{4,0},{5,9},{6,2},{7,11},{8,4},{9,13},{10,6},{11,15},{... | collective-permute-start | bytes 1105928 | tf_op jit(solution)/shard_map/ppermute | solution.py:215
  11.4 4.8 %collective-permute-start.2 = (bf16[2,1,15,16,384]{4,3,2,1,0:T(8,128)(2,1)S(1)}, bf16[2,1,15,16,384]{4,3,2,1,0:T(8,128)(2,1)S(1)}, u32[]{:S(2)}, u32[]{:S(2)}) collective-permute-start(bf16[2,1,15,16,384]{4,3,2,1,0:T(8,128)(2,1)S(1)} %get-tuple-element.40), channel_id=1, source_target_pairs={{2,5},{0,7},{5,0},{6,9},{7,2},{4,11},{9,4},{10,13},{11,6},{8,15},{... | collective-permute-start | bytes 1105928 | tf_op jit(solution)/shard_map/ppermute | solution.py:215
  16.3 3.4 %collective-permute-done.3 = bf16[2,1,15,32,384]{4,3,2,1,0:T(8,128)(2,1)S(1)} collective-permute-done((bf16[2,1,15,32,384]{4,3,2,1,0:T(8,128)(2,1)S(1)}, bf16[2,1,15,32,384]{4,3,2,1,0:T(8,128)(2,1)S(1)}, u32[]{:S(2)}, u32[]{:S(2)}) %collective-permute-start.3) | collective-permute-done | bytes 737312 | tf_op jit(solution)/shard_map/ppermute | solution.py:215
  19.7 25.1 %shard_map.78 = (bf16[480,384]{1,0:T(8,128)(2,1)S(1)}, bf16[480,384]{1,0:T(8,128)(2,1)S(1)}, f32[384,1152]{1,0:T(8,128)S(1)}, f32[384,384]{1,0:T(8,128)S(1)}) custom-call(bf16[2,480,384]{2,1,0:T(8,128)(2,1)S(1)} %bitcast.28, bf16[2,480,384]{2,1,0:T(8,128)(2,1)S(1)} %bitcast.27, f32[384]{0:T(512)S(1)} %copy-done.5, bf16[384,1152]{1,0:T(8,128)(2,1)S(1)} %copy-done.3, ...), custom_call_target="tpu_custom_call" | custom-call | flops 7644119040 | bytes 8388608 | tf_op jit(solution)/shard_map/pallas_call | solution.py:168
  44.7 25.8 %shard_map.79 = (bf16[240,384]{1,0:T(8,128)(2,1)S(1)}, bf16[240,384]{1,0:T(8,128)(2,1)S(1)}, bf16[240,384]{1,0:T(8,128)(2,1)S(1)}, bf16[240,384]{1,0:T(8,128)(2,...) custom-call(bf16[2,240,384]{2,1,0:T(8,128)(2,1)S(1)} %bitcast.30, bf16[2,240,384]{2,1,0:T(8,128)(2,1)S(1)} %bitcast.31, ...), custom_call_target="tpu_custom_call" | custom-call | flops 7644119040 | bytes 8388608 | tf_op jit(solution)/shard_map/pallas_call | solution.py:168
  70.6 2.1 %collective-permute-done.4 = bf16[8,96,384]{2,1,0:T(8,128)(2,1)} collective-permute-done((bf16[8,96,384]{2,1,0:T(8,128)(2,1)S(1)}, bf16[8,96,384]{2,1,0:T(8,128)(2,1)}, u32[]{:S(2)}, u32[]{:S(2)}) %collective-permute-start.4) | collective-permute-done | bytes 589856 | tf_op jit(solution)/shard_map/ppermute | solution.py:199
  72.7 1.2 %convert_add_fusion = f32[8,96,384]{2,1,0:T(8,128)S(1)} fusion(f32[8,96,384]{2,1,0:T(8,128)S(1)} %get-tuple-element.49, bf16[8,96,384]{2,1,0:T(8,128)(2,1)} %collective-permute-done.4), kind=kLoop, calls=%fused_computation.1 | loop fusion | flops 589824 | bytes 2949120 | tf_op jit(solution)/shard_map/add | solution.py:292
  74.0 1.0 copy-done.6
  74.9 2.4 %collective-permute-start.5 = (bf16[4,1,96,384]{3,2,0,1:T(8,128)(2,1)S(1)}, bf16[4,1,96,384]{3,2,0,1:T(8,128)(2,1)S(1)}, u32[]{:S(2)}, u32[]{:S(2)}) collective-permute-start(bf16[4,1,96,384]{3,2,0,1:T(8,128)(2,1)S(1)} %dynamic-slice_convert_fusion), channel_id=1, source_target_pairs={{0,2},{1,3},{2,0},{3,1},{4,6},{5,7},{6,4},{7,5},{8,10},{9,11},{10,... | collective-permute-start | bytes 884744 | tf_op jit(solution)/shard_map/ppermute | solution.py:199
  77.3 3.7 %collective-permute-start.6 = (bf16[15,32,384]{2,1,0:T(8,128)(2,1)S(1)}, bf16[15,32,384]{2,1,0:T(8,128)(2,1)S(1)}, u32[]{:S(2)}, u32[]{:S(2)}) collective-permute-start(bf16[15,32,384]{2,1,0:T(8,128)(2,1)S(1)} %bitcast.29), channel_id=1, source_target_pairs={{5,1},{7,3},{0,4},{9,5},{2,6},{11,7},{4,8},{13,9},{6,10},{15,11},{... | collective-permute-start | bytes 1105928 | tf_op jit(solution)/shard_map/ppermute | solution.py:215
  81.1 3.5 %collective-permute-start.7 = (bf16[15,16,384]{2,1,0:T(8,128)(2,1)S(1)}, bf16[15,16,384]{2,1,0:T(8,128)(2,1)S(1)}, u32[]{:S(2)}, u32[]{:S(2)}) collective-permute-start(bf16[15,16,384]{2,1,0:T(8,128)(2,1)S(1)} %bitcast.36), channel_id=1, source_target_pairs={{5,1},{7,3},{0,4},{9,5},{2,6},{11,7},{4,8},{13,9},{6,10},{15,11},{... | collective-permute-start | bytes 552968 | tf_op jit(solution)/shard_map/ppermute | solution.py:215
  84.6 1.9 %collective-permute-start.9 = (bf16[15,16,384]{2,1,0:T(8,128)(2,1)S(1)}, bf16[15,16,384]{2,1,0:T(8,128)(2,1)S(1)}, u32[]{:S(2)}, u32[]{:S(2)}) collective-permute-start(bf16[15,16,384]{2,1,0:T(8,128)(2,1)S(1)} %bitcast.34), channel_id=1, source_target_pairs={{5,2},{7,0},{0,5},{9,6},{2,7},{11,4},{4,9},{13,10},{6,11},{15,8},{... | collective-permute-start | bytes 552968 | tf_op jit(solution)/shard_map/ppermute | solution.py:215
  86.6 1.1 %add_bitcast_fusion = f32[4,96,384]{2,1,0:T(8,128)S(1)} fusion(bf16[4,1,96,384]{3,2,0,1:T(8,128)(2,1)S(1)} %collective-permute-done.5, s32[]{:T(128)S(6)} %select_n.94, f32[4,2,96,384]{3,2,1,0:T(8,128)} %bitcast.38), kind=kLoop, calls=%fused_computation.4 | loop fusion | flops 294912 | bytes 1474564 | tf_op jit(solution)/shard_map/reshape | solution.py:298
  88.1 1.6 %collective-permute-start.8 = (bf16[4,96,192]{2,1,0:T(8,128)(2,1)S(1)}, bf16[4,96,192]{2,1,0:T(8,128)(2,1)S(1)}, u32[]{:S(2)}, u32[]{:S(2)}) collective-permute-start(bf16[4,96,192]{2,1,0:T(8,128)(2,1)S(1)} %dynamic-slice_convert_fusion.1), channel_id=1, source_target_pairs={{0,16},{16,0},{1,17},{17,1},{2,18},{18,2},{3,19},{19,3},{4,20},{20... | collective-permute-start | bytes 442376 | tf_op jit(solution)/shard_map/ppermute | solution.py:199
  89.9 4.6 %collective-permute-done.8 = bf16[4,96,192]{2,1,0:T(8,128)(2,1)S(1)} collective-permute-done((bf16[4,96,192]{2,1,0:T(8,128)(2,1)S(1)}, bf16[4,96,192]{2,1,0:T(8,128)(2,1)S(1)}, u32[]{:S(2)}, u32[]{:S(2)}) %collective-permute-start.8) | collective-permute-done | bytes 147488 | tf_op jit(solution)/shard_map/ppermute | solution.py:199
  94.7 2.1 %collective-permute-start.11 = (bf16[1,96,192]{2,1,0:T(8,128)(2,1)S(1)}, bf16[1,96,192]{2,1,0:T(8,128)(2,1)S(1)}, u32[]{:S(2)}, u32[]{:S(2)}) collective-permute-start(bf16[1,96,192]{2,1,0:T(8,128)(2,1)S(1)} %get-tuple-element.69), channel_id=1, source_target_pairs={{0,4},{4,8},{8,12},{12,0},{1,5},{5,9},{9,13},{13,1},{2,6},{6,10},{... | collective-permute-start | bytes 110600 | tf_op jit(solution)/shard_map/ppermute | solution.py:199
  96.7 1.1 %collective-permute-start.12 = (bf16[1,96,192]{2,1,0:T(8,128)(2,1)S(1)}, bf16[1,96,192]{2,1,0:T(8,128)(2,1)S(1)}, u32[]{:S(2)}, u32[]{:S(2)}) collective-permute-start(bf16[1,96,192]{2,1,0:T(8,128)(2,1)S(1)} %get-tuple-element.71), channel_id=1, source_target_pairs={{0,8},{4,12},{8,0},{12,4},{1,9},{5,13},{9,1},{13,5},{2,10},{6,14},... | collective-permute-start | bytes 110600 | tf_op jit(solution)/shard_map/ppermute | solution.py:199
  97.9 2.8 %collective-permute-start.13 = (bf16[1,96,192]{2,1,0:T(8,128)(2,1)S(1)}, bf16[1,96,192]{2,1,0:T(8,128)(2,1)S(1)}, u32[]{:S(2)}, u32[]{:S(2)}) collective-permute-start(bf16[1,96,192]{2,1,0:T(8,128)(2,1)S(1)} %get-tuple-element.70), channel_id=1, source_target_pairs={{0,12},{4,0},{8,4},{12,8},{1,13},{5,1},{9,5},{13,9},{2,14},{6,2},{... | collective-permute-start | bytes 110600 | tf_op jit(solution)/shard_map/ppermute | solution.py:199
  100.9 1.9 %add_convert_fusion = bf16[1,30,60,384]{3,2,1,0:T(8,128)(2,1)} fusion(bf16[1,30,60,384]{3,2,1,0:T(8,128)(2,1)S(1)} %copy-done.1, bf16[1,30,15,384]{3,2,1,0:T(8,128)(2,1)S(1)} %get-tuple-element.76, bf16[1,30,30,384]{3,2,1,0:T(8,128)(2,1)S(1)} %fusion, bf16[1,30,15,384]{3,2,1,0:T(8,128)(2,1)S(1)} %get-tuple-element.77), kind=kLoop, calls=%fused_computation | loop fusion | flops 6220800 | bytes 4147200 | tf_op jit(solution)/shard_map/convert_element_type | solution.py:385
  (37 shorter events, 2.6 us)
Async XLA Ops:
  0.6 1.4 %copy-start = (bf16[1,30,60,384]{3,2,1,0:T(8,128)(2,1)S(1)}, bf16[1,30,60,384]{3,2,1,0:T(8,128)(2,1)}, u32[]{:S(2)}) copy-start(bf16[1,30,60,384]{3,2,1,0:T(8,128)(2,1)} %cot_ref.2) | copy-start | bytes 4147204
  2.0 1.4 %copy-start.2 = (bf16[1,30,60,384]{3,2,1,0:T(8,128)(2,1)S(1)}, bf16[1,30,60,384]{3,2,1,0:T(8,128)(2,1)}, u32[]{:S(2)}) copy-start(bf16[1,30,60,384]{3,2,1,0:T(8,128)(2,1)} %hid_ref.2) | copy-start | bytes 4147204
  3.6 16.0 %copy-start.3 = (bf16[384,1152]{1,0:T(8,128)(2,1)S(1)}, bf16[384,1152]{1,0:T(8,128)(2,1)}, u32[]{:S(2)}) copy-start(bf16[384,1152]{1,0:T(8,128)(2,1)} %refs_5_.1) | copy-start | bytes 2654212
  3.6 16.0 %copy-start.4 = (bf16[384,384]{1,0:T(8,128)(2,1)S(1)}, bf16[384,384]{1,0:T(8,128)(2,1)}, u32[]{:S(2)}) copy-start(bf16[384,384]{1,0:T(8,128)(2,1)} %refs_6_.1) | copy-start | bytes 884740
  3.6 16.0 %copy-start.5 = (f32[384]{0:T(512)S(1)}, f32[384]{0:T(512)}, u32[]{:S(2)}) copy-start(f32[384]{0:T(512)} %refs_4_.3) | copy-start | bytes 4612
  3.6 16.0 %collective-permute-start.3 = (bf16[2,1,15,32,384]{4,3,2,1,0:T(8,128)(2,1)S(1)}, bf16[2,1,15,32,384]{4,3,2,1,0:T(8,128)(2,1)S(1)}, u32[]{:S(2)}, u32[]{:S(2)}) collective-permute-start(bf16[2,1,15,32,384]{4,3,2,1,0:T(8,128)(2,1)S(1)} %shard_map.76), channel_id=1, source_target_pairs={{1,5},{3,7},{4,0},{5,9},{6,2},{7,11},{8,4},{9,13},{10,6},{11,15},{... | collective-permute-start | bytes 2211848 | tf_op jit(solution)/shard_map/ppermute | solution.py:215
  5.7 39.0 %collective-permute-start = (bf16[2,1,15,16,384]{4,3,2,1,0:T(8,128)(2,1)S(1)}, bf16[2,1,15,16,384]{4,3,2,1,0:T(8,128)(2,1)S(1)}, u32[]{:S(2)}, u32[]{:S(2)}) collective-permute-start(bf16[2,1,15,16,384]{4,3,2,1,0:T(8,128)(2,1)S(1)} %get-tuple-element.38), channel_id=1, source_target_pairs={{0,3},{1,0},{2,1},{3,2},{4,7},{5,4},{6,5},{7,6},{8,11},{9,8},{10,9... | collective-permute-start | bytes 1105928 | tf_op jit(solution)/shard_map/ppermute | solution.py:220
  10.2 34.6 %collective-permute-start.1 = (bf16[2,1,15,16,384]{4,3,2,1,0:T(8,128)(2,1)S(1)}, bf16[2,1,15,16,384]{4,3,2,1,0:T(8,128)(2,1)S(1)}, u32[]{:S(2)}, u32[]{:S(2)}) collective-permute-start(bf16[2,1,15,16,384]{4,3,2,1,0:T(8,128)(2,1)S(1)} %get-tuple-element.39), channel_id=1, source_target_pairs={{1,5},{3,7},{4,0},{5,9},{6,2},{7,11},{8,4},{9,13},{10,6},{11,15},{... | collective-permute-start | bytes 1105928 | tf_op jit(solution)/shard_map/ppermute | solution.py:215
  11.4 33.3 %collective-permute-start.2 = (bf16[2,1,15,16,384]{4,3,2,1,0:T(8,128)(2,1)S(1)}, bf16[2,1,15,16,384]{4,3,2,1,0:T(8,128)(2,1)S(1)}, u32[]{:S(2)}, u32[]{:S(2)}) collective-permute-start(bf16[2,1,15,16,384]{4,3,2,1,0:T(8,128)(2,1)S(1)} %get-tuple-element.40), channel_id=1, source_target_pairs={{2,5},{0,7},{5,0},{6,9},{7,2},{4,11},{9,4},{10,13},{11,6},{8,15},{... | collective-permute-start | bytes 1105928 | tf_op jit(solution)/shard_map/ppermute | solution.py:215
  70.5 2.2 %collective-permute-start.4 = (bf16[8,96,384]{2,1,0:T(8,128)(2,1)S(1)}, bf16[8,96,384]{2,1,0:T(8,128)(2,1)}, u32[]{:S(2)}, u32[]{:S(2)}) collective-permute-start(bf16[8,96,384]{2,1,0:T(8,128)(2,1)S(1)} %get-tuple-element.50), channel_id=1, source_target_pairs={{0,1},{1,0},{2,3},{3,2},{4,5},{5,4},{6,7},{7,6},{8,9},{9,8},{10,11... | collective-permute-start | bytes 1769480 | tf_op jit(solution)/shard_map/ppermute | solution.py:199
  73.9 1.0 copy-start.6
  74.9 11.7 %collective-permute-start.5 = (bf16[4,1,96,384]{3,2,0,1:T(8,128)(2,1)S(1)}, bf16[4,1,96,384]{3,2,0,1:T(8,128)(2,1)S(1)}, u32[]{:S(2)}, u32[]{:S(2)}) collective-permute-start(bf16[4,1,96,384]{3,2,0,1:T(8,128)(2,1)S(1)} %dynamic-slice_convert_fusion), channel_id=1, source_target_pairs={{0,2},{1,3},{2,0},{3,1},{4,6},{5,7},{6,4},{7,5},{8,10},{9,11},{10,... | collective-permute-start | bytes 884744 | tf_op jit(solution)/shard_map/ppermute | solution.py:199
  77.3 10.6 %collective-permute-start.6 = (bf16[15,32,384]{2,1,0:T(8,128)(2,1)S(1)}, bf16[15,32,384]{2,1,0:T(8,128)(2,1)S(1)}, u32[]{:S(2)}, u32[]{:S(2)}) collective-permute-start(bf16[15,32,384]{2,1,0:T(8,128)(2,1)S(1)} %bitcast.29), channel_id=1, source_target_pairs={{5,1},{7,3},{0,4},{9,5},{2,6},{11,7},{4,8},{13,9},{6,10},{15,11},{... | collective-permute-start | bytes 1105928 | tf_op jit(solution)/shard_map/ppermute | solution.py:215
  81.1 6.9 %collective-permute-start.7 = (bf16[15,16,384]{2,1,0:T(8,128)(2,1)S(1)}, bf16[15,16,384]{2,1,0:T(8,128)(2,1)S(1)}, u32[]{:S(2)}, u32[]{:S(2)}) collective-permute-start(bf16[15,16,384]{2,1,0:T(8,128)(2,1)S(1)} %bitcast.36), channel_id=1, source_target_pairs={{5,1},{7,3},{0,4},{9,5},{2,6},{11,7},{4,8},{13,9},{6,10},{15,11},{... | collective-permute-start | bytes 552968 | tf_op jit(solution)/shard_map/ppermute | solution.py:215
  84.6 10.0 %collective-permute-start.10 = (bf16[15,16,384]{2,1,0:T(8,128)(2,1)S(1)}, bf16[15,16,384]{2,1,0:T(8,128)(2,1)S(1)}, u32[]{:S(2)}, u32[]{:S(2)}) collective-permute-start(bf16[15,16,384]{2,1,0:T(8,128)(2,1)S(1)} %bitcast.35), channel_id=1, source_target_pairs={{0,1},{1,2},{2,3},{3,0},{4,5},{5,6},{6,7},{7,4},{8,9},{9,10},{10,1... | collective-permute-start | bytes 552968 | tf_op jit(solution)/shard_map/ppermute | solution.py:220
  84.6 10.0 %collective-permute-start.9 = (bf16[15,16,384]{2,1,0:T(8,128)(2,1)S(1)}, bf16[15,16,384]{2,1,0:T(8,128)(2,1)S(1)}, u32[]{:S(2)}, u32[]{:S(2)}) collective-permute-start(bf16[15,16,384]{2,1,0:T(8,128)(2,1)S(1)} %bitcast.34), channel_id=1, source_target_pairs={{5,2},{7,0},{0,5},{9,6},{2,7},{11,4},{4,9},{13,10},{6,11},{15,8},{... | collective-permute-start | bytes 552968 | tf_op jit(solution)/shard_map/ppermute | solution.py:215
  88.1 6.3 %collective-permute-start.8 = (bf16[4,96,192]{2,1,0:T(8,128)(2,1)S(1)}, bf16[4,96,192]{2,1,0:T(8,128)(2,1)S(1)}, u32[]{:S(2)}, u32[]{:S(2)}) collective-permute-start(bf16[4,96,192]{2,1,0:T(8,128)(2,1)S(1)} %dynamic-slice_convert_fusion.1), channel_id=1, source_target_pairs={{0,16},{16,0},{1,17},{17,1},{2,18},{18,2},{3,19},{19,3},{4,20},{20... | collective-permute-start | bytes 442376 | tf_op jit(solution)/shard_map/ppermute | solution.py:199
  94.6 6.3 %copy-start.1 = (bf16[1,30,60,384]{3,2,1,0:T(8,128)(2,1)S(1)}, bf16[1,30,60,384]{3,2,1,0:T(8,128)(2,1)}, u32[]{:S(2)}) copy-start(bf16[1,30,60,384]{3,2,1,0:T(8,128)(2,1)} %cot_ref.2) | copy-start | bytes 4147204
  94.7 8.1 %collective-permute-start.11 = (bf16[1,96,192]{2,1,0:T(8,128)(2,1)S(1)}, bf16[1,96,192]{2,1,0:T(8,128)(2,1)S(1)}, u32[]{:S(2)}, u32[]{:S(2)}) collective-permute-start(bf16[1,96,192]{2,1,0:T(8,128)(2,1)S(1)} %get-tuple-element.69), channel_id=1, source_target_pairs={{0,4},{4,8},{8,12},{12,0},{1,5},{5,9},{9,13},{13,1},{2,6},{6,10},{... | collective-permute-start | bytes 110600 | tf_op jit(solution)/shard_map/ppermute | solution.py:199
  96.7 6.0 %collective-permute-start.12 = (bf16[1,96,192]{2,1,0:T(8,128)(2,1)S(1)}, bf16[1,96,192]{2,1,0:T(8,128)(2,1)S(1)}, u32[]{:S(2)}, u32[]{:S(2)}) collective-permute-start(bf16[1,96,192]{2,1,0:T(8,128)(2,1)S(1)} %get-tuple-element.71), channel_id=1, source_target_pairs={{0,8},{4,12},{8,0},{12,4},{1,9},{5,13},{9,1},{13,5},{2,10},{6,14},... | collective-permute-start | bytes 110600 | tf_op jit(solution)/shard_map/ppermute | solution.py:199
  97.9 4.9 %collective-permute-start.13 = (bf16[1,96,192]{2,1,0:T(8,128)(2,1)S(1)}, bf16[1,96,192]{2,1,0:T(8,128)(2,1)S(1)}, u32[]{:S(2)}, u32[]{:S(2)}) collective-permute-start(bf16[1,96,192]{2,1,0:T(8,128)(2,1)S(1)} %get-tuple-element.70), channel_id=1, source_target_pairs={{0,12},{4,0},{8,4},{12,8},{1,13},{5,1},{9,5},{13,9},{2,14},{6,2},{... | collective-permute-start | bytes 110600 | tf_op jit(solution)/shard_map/ppermute | solution.py:199

commit v7 on v6

--- a/solution.py
+++ b/solution.py
@@ -253,19 +253,6 @@
     return list(outs)
 
 
-def scatter_direct(value, axis, dim):
-    count = lax.axis_size(axis)
-    me = lax.axis_index(axis)
-    share = value.shape[dim] // count
-    total = lax.dynamic_slice_in_dim(value, me * share, share, dim).astype(F32)
-    for step in range(1, count):
-        goal = (me + step) % count
-        part = lax.dynamic_slice_in_dim(value, goal * share, share, dim).astype(BF)
-        got = permuted(part, (axis,), lambda i, s=step: ((i + s) % count,))
-        total = total + got.astype(F32)
-    return total
-
-
 def scatter_bit(value, axis, bit, dim):
     me = (lax.axis_index(axis) // bit) % 2
     mine = lax.dynamic_index_in_dim(value, me, dim, keepdims=False).astype(F32)
@@ -296,9 +283,32 @@
         left //= 2
         bit *= 2
     total, moved[:early] = lax.optimization_barrier((total.reshape(lats, deep, width), moved[:early]))
-    total = scatter_direct(total, "dp", 2)
-    total, moved[early:] = lax.optimization_barrier((total, moved[early:]))
-    return scatter_direct(total, "lat", 0)[0], moved
+    dps = lax.axis_size("dp")
+    blocks = total.astype(BF).reshape(lats, deep, dps, width // dps).transpose(2, 0, 1, 3)
+    blocks, moved[early:] = lax.optimization_barrier((blocks, moved[early:]))
+    blocks = blocks.reshape(dps * lats, deep, width // dps)
+    return lax.all_to_all(blocks, ("dp", "lat"), 0, 0, tiled=True), moved
+
+
+def finish_kernel(factor, cut, in_ref, gq_ref, gp_ref):
+    total = in_ref[0].astype(F32)
+    for i in range(1, in_ref.shape[0]):
+        total = total + in_ref[i].astype(F32)
+    total = (total * factor).T
+    gq_ref[...] = total[:, :cut]
+    gp_ref[...] = total[:, cut:]
+
+
+def finish_call(blocks, factor, cut):
+    _, deep, rows = blocks.shape
+    vmem = pl.BlockSpec(memory_space=pltpu.VMEM)
+    return pl.pallas_call(
+        functools.partial(finish_kernel, factor, cut),
+        out_shape=(jax.ShapeDtypeStruct((rows, cut), F32), jax.ShapeDtypeStruct((rows, deep - cut), F32)),
+        in_specs=[vmem],
+        out_specs=(vmem, vmem),
+        compiler_params=pltpu.CompilerParams(vmem_limit_bytes=16 * 2**20),
+    )(blocks)
 
 
 def per_device(hidden_in, grad_out, norm_gain, w_qkv, w_proj):
@@ -387,9 +397,8 @@
         lax.axis_size("dp") * samples * lat_rows * lax.axis_size("lat") * lon_cols * lons
     )
     factor = float(total_cells) ** (-0.5)
-    total = total.T * factor
-    cut = 3 * width // parts
-    return (grad_in, total[:, :cut], total[:, cut:])
+    gq, gp = finish_call(total, factor, 3 * width // parts)
+    return (grad_in, gq, gp)
 
 
 def solution(mesh):

time: 104 us -> 111 us (1.067)
  waiting for transfers between devices: 10.3 us -> 18.9 us
  starting transfers between devices: 31.2 us -> 27 us
  local copies, waits for them, and re-layouts: 5.16 us -> 7.36 us
    all_to_all x0 -> x1, waiting for transfers between devices: none -> 9.02 us  [reduce_weights(): return (lax.all_to_all(blocks, ('dp', 'lat'), 0, 0, tiled=True), moved)]
    ppermute x6 -> x2, starting transfers between devices: 10.1 us -> 2.47 us  [permuted(): return lax.ppermute(value, tuple(axes), pairs)]
    ppermute x6 -> x2, waiting for transfers between devices: 6.65 us -> 2.09 us  [permuted(): return lax.ppermute(value, tuple(axes), pairs)]
    all_to_all x0 -> x1, starting transfers between devices: none -> 3.45 us  [reduce_weights(): return (lax.all_to_all(blocks, ('dp', 'lat'), 0, 0, tiled=True), moved)]
    ppermute x6, waiting for transfers between devices: 3.6 us -> 6.45 us  [shared(): return lax.ppermute(value, ('lat', 'lon'), pairs)]
    unnamed x14 -> x16, local copies, waits for them, and re-layouts: 3.72 us -> 6.3 us
    ppermute x2, waiting for transfers between devices: 0.01 us -> 1.35 us  [along_lon(): lax.ppermute(value, 'lon', [(j, (j + step) % count) for j in range(count)])]
    slice x2 -> x0, local copies, waits for them, and re-layouts: 1.25 us -> none  [per_device(): return (grad_in, total[:, :cut], total[:, cut:])]
  transfers between devices with their start and end apart: 14 -> 11, of which waited for: 4 -> 6; matrix products, arithmetic and copies ran while one was open for 3% -> 3% of each run, Pallas kernels for 25% -> 23%
where the time goes in v7:
time: 111 us
  Pallas kernels  52 us (47%)
  starting transfers between devices  27 us (24%)
  waiting for transfers between devices  18.9 us (17%)
  local copies, waits for them, and re-layouts  7.36 us (7%)
  other arithmetic  4.49 us (4%)
    pallas_call x2, Pallas kernels, window_call(): pl.pallas_call(functools.partial(window_kernel, head, metas, (prev is not...  50.9 us
    ppermute x6, starting transfers between devices, shared(): return lax.ppermute(value, ('lat', 'lon'), pairs)  16.6 us
    all_to_all x1, waiting for transfers between devices, reduce_weights(): return (lax.all_to_all(blocks, ('dp', 'lat'), 0, 0, tiled=True), moved)  9.02 us
    ppermute x6, waiting for transfers between devices, shared(): return lax.ppermute(value, ('lat', 'lon'), pairs)  6.45 us
    unnamed x16, local copies, waits for them, and re-layouts  6.3 us
    ppermute x2, starting transfers between devices, along_lon(): lax.ppermute(value, 'lon', [(j, (j + step) % count) for j in range(count)])  4.47 us
    all_to_all x1, starting transfers between devices, reduce_weights(): return (lax.all_to_all(blocks, ('dp', 'lat'), 0, 0, tiled=True), moved)  3.45 us
    ppermute x2, starting transfers between devices, permuted(): return lax.ppermute(value, tuple(axes), pairs)  2.47 us
  transfers between devices with their start and end apart: 11, of which 6 were waited for; matrix products, arithmetic and copies ran while one was open for 3% of the time, Pallas kernels for 23%

profile of v7, /device:TPU:0, one launch (start us, length us, event | category | flops | bytes accessed | tf_op | source)
XLA Modules:
  0.0 110.6 jit_solution(9224784031636100578)
XLA Ops:
  0.6 1.4 %copy-done = bf16[1,30,60,384]{3,2,1,0:T(8,128)(2,1)S(1)} copy-done((bf16[1,30,60,384]{3,2,1,0:T(8,128)(2,1)S(1)}, bf16[1,30,60,384]{3,2,1,0:T(8,128)(2,1)}, u32[]{:S(2)}) %copy-start) | copy-done | bytes 1382424
  2.0 1.4 %copy-done.2 = bf16[1,30,60,384]{3,2,1,0:T(8,128)(2,1)S(1)} copy-done((bf16[1,30,60,384]{3,2,1,0:T(8,128)(2,1)S(1)}, bf16[1,30,60,384]{3,2,1,0:T(8,128)(2,1)}, u32[]{:S(2)}) %copy-start.2) | copy-done | bytes 1382424
  3.6 1.4 %collective-permute-start.3 = (bf16[2,1,15,32,384]{4,3,2,1,0:T(8,128)(2,1)S(1)}, bf16[2,1,15,32,384]{4,3,2,1,0:T(8,128)(2,1)S(1)}, u32[]{:S(2)}, u32[]{:S(2)}) collective-permute-start(bf16[2,1,15,32,384]{4,3,2,1,0:T(8,128)(2,1)S(1)} %shard_map.76), channel_id=1, source_target_pairs={{1,5},{3,7},{4,0},{5,9},{6,2},{7,11},{8,4},{9,13},{10,6},{11,15},{... | collective-permute-start | bytes 2211848 | tf_op jit(solution)/shard_map/ppermute | solution.py:215
  5.7 4.4 %collective-permute-start = (bf16[2,1,15,16,384]{4,3,2,1,0:T(8,128)(2,1)S(1)}, bf16[2,1,15,16,384]{4,3,2,1,0:T(8,128)(2,1)S(1)}, u32[]{:S(2)}, u32[]{:S(2)}) collective-permute-start(bf16[2,1,15,16,384]{4,3,2,1,0:T(8,128)(2,1)S(1)} %get-tuple-element.40), channel_id=1, source_target_pairs={{0,3},{1,0},{2,1},{3,2},{4,7},{5,4},{6,5},{7,6},{8,11},{9,8},{10,9... | collective-permute-start | bytes 1105928 | tf_op jit(solution)/shard_map/ppermute | solution.py:220
  10.2 1.3 %collective-permute-start.1 = (bf16[2,1,15,16,384]{4,3,2,1,0:T(8,128)(2,1)S(1)}, bf16[2,1,15,16,384]{4,3,2,1,0:T(8,128)(2,1)S(1)}, u32[]{:S(2)}, u32[]{:S(2)}) collective-permute-start(bf16[2,1,15,16,384]{4,3,2,1,0:T(8,128)(2,1)S(1)} %get-tuple-element.41), channel_id=1, source_target_pairs={{1,5},{3,7},{4,0},{5,9},{6,2},{7,11},{8,4},{9,13},{10,6},{11,15},{... | collective-permute-start | bytes 1105928 | tf_op jit(solution)/shard_map/ppermute | solution.py:215
  11.4 4.8 %collective-permute-start.2 = (bf16[2,1,15,16,384]{4,3,2,1,0:T(8,128)(2,1)S(1)}, bf16[2,1,15,16,384]{4,3,2,1,0:T(8,128)(2,1)S(1)}, u32[]{:S(2)}, u32[]{:S(2)}) collective-permute-start(bf16[2,1,15,16,384]{4,3,2,1,0:T(8,128)(2,1)S(1)} %get-tuple-element.42), channel_id=1, source_target_pairs={{2,5},{0,7},{5,0},{6,9},{7,2},{4,11},{9,4},{10,13},{11,6},{8,15},{... | collective-permute-start | bytes 1105928 | tf_op jit(solution)/shard_map/ppermute | solution.py:215
  16.3 3.4 %collective-permute-done.3 = bf16[2,1,15,32,384]{4,3,2,1,0:T(8,128)(2,1)S(1)} collective-permute-done((bf16[2,1,15,32,384]{4,3,2,1,0:T(8,128)(2,1)S(1)}, bf16[2,1,15,32,384]{4,3,2,1,0:T(8,128)(2,1)S(1)}, u32[]{:S(2)}, u32[]{:S(2)}) %collective-permute-start.3) | collective-permute-done | bytes 737312 | tf_op jit(solution)/shard_map/ppermute | solution.py:215
  19.7 25.1 %shard_map.78 = (bf16[480,384]{1,0:T(8,128)(2,1)S(1)}, bf16[480,384]{1,0:T(8,128)(2,1)S(1)}, f32[384,1152]{1,0:T(8,128)S(1)}, f32[384,384]{1,0:T(8,128)S(1)}) custom-call(bf16[2,480,384]{2,1,0:T(8,128)(2,1)S(1)} %bitcast.26, bf16[2,480,384]{2,1,0:T(8,128)(2,1)S(1)} %bitcast.25, f32[384]{0:T(512)S(1)} %copy-done.5, bf16[384,1152]{1,0:T(8,128)(2,1)S(1)} %copy-done.3, ...), custom_call_target="tpu_custom_call" | custom-call | flops 7644119040 | bytes 8388608 | tf_op jit(solution)/shard_map/pallas_call | solution.py:168
  44.8 25.8 %shard_map.79 = (bf16[240,384]{1,0:T(8,128)(2,1)S(1)}, bf16[240,384]{1,0:T(8,128)(2,1)S(1)}, bf16[240,384]{1,0:T(8,128)(2,1)S(1)}, bf16[240,384]{1,0:T(8,128)(2,...) custom-call(bf16[2,240,384]{2,1,0:T(8,128)(2,1)S(1)} %bitcast.28, bf16[2,240,384]{2,1,0:T(8,128)(2,1)S(1)} %bitcast.29, ...), custom_call_target="tpu_custom_call" | custom-call | flops 7644119040 | bytes 8388608 | tf_op jit(solution)/shard_map/pallas_call | solution.py:168
  70.7 2.1 %collective-permute-done.4 = bf16[8,96,384]{2,1,0:T(8,128)(2,1)} collective-permute-done((bf16[8,96,384]{2,1,0:T(8,128)(2,1)S(1)}, bf16[8,96,384]{2,1,0:T(8,128)(2,1)}, u32[]{:S(2)}, u32[]{:S(2)}) %collective-permute-start.4) | collective-permute-done | bytes 589856 | tf_op jit(solution)/shard_map/ppermute | solution.py:199
  72.8 1.2 %convert_add_fusion = f32[8,96,384]{2,1,0:T(8,128)S(1)} fusion(f32[8,96,384]{2,1,0:T(8,128)S(1)} %get-tuple-element.51, bf16[8,96,384]{2,1,0:T(8,128)(2,1)} %collective-permute-done.4), kind=kLoop, calls=%fused_computation.1 | loop fusion | flops 589824 | bytes 2949120 | tf_op jit(solution)/shard_map/add | solution.py:279
  74.0 1.0 copy-done.6
  74.9 2.4 %collective-permute-start.5 = (bf16[4,1,96,384]{3,2,0,1:T(8,128)(2,1)S(1)}, bf16[4,1,96,384]{3,2,0,1:T(8,128)(2,1)S(1)}, u32[]{:S(2)}, u32[]{:S(2)}) collective-permute-start(bf16[4,1,96,384]{3,2,0,1:T(8,128)(2,1)S(1)} %dynamic-slice_convert_fusion), channel_id=1, source_target_pairs={{0,2},{1,3},{2,0},{3,1},{4,6},{5,7},{6,4},{7,5},{8,10},{9,11},{10,... | collective-permute-start | bytes 884744 | tf_op jit(solution)/shard_map/ppermute | solution.py:199
  77.3 3.7 %collective-permute-start.6 = (bf16[15,32,384]{2,1,0:T(8,128)(2,1)S(1)}, bf16[15,32,384]{2,1,0:T(8,128)(2,1)S(1)}, u32[]{:S(2)}, u32[]{:S(2)}) collective-permute-start(bf16[15,32,384]{2,1,0:T(8,128)(2,1)S(1)} %bitcast.27), channel_id=1, source_target_pairs={{5,1},{7,3},{0,4},{9,5},{2,6},{11,7},{4,8},{13,9},{6,10},{15,11},{... | collective-permute-start | bytes 1105928 | tf_op jit(solution)/shard_map/ppermute | solution.py:215
  81.0 3.5 %collective-permute-start.7 = (bf16[15,16,384]{2,1,0:T(8,128)(2,1)S(1)}, bf16[15,16,384]{2,1,0:T(8,128)(2,1)S(1)}, u32[]{:S(2)}, u32[]{:S(2)}) collective-permute-start(bf16[15,16,384]{2,1,0:T(8,128)(2,1)S(1)} %bitcast.34), channel_id=1, source_target_pairs={{5,1},{7,3},{0,4},{9,5},{2,6},{11,7},{4,8},{13,9},{6,10},{15,11},{... | collective-permute-start | bytes 552968 | tf_op jit(solution)/shard_map/ppermute | solution.py:215
  84.6 1.9 %collective-permute-start.8 = (bf16[15,16,384]{2,1,0:T(8,128)(2,1)S(1)}, bf16[15,16,384]{2,1,0:T(8,128)(2,1)S(1)}, u32[]{:S(2)}, u32[]{:S(2)}) collective-permute-start(bf16[15,16,384]{2,1,0:T(8,128)(2,1)S(1)} %bitcast.32), channel_id=1, source_target_pairs={{5,2},{7,0},{0,5},{9,6},{2,7},{11,4},{4,9},{13,10},{6,11},{15,8},{... | collective-permute-start | bytes 552968 | tf_op jit(solution)/shard_map/ppermute | solution.py:215
  86.6 1.1 %add_bitcast_fusion = bf16[4,96,384]{2,1,0:T(8,128)(2,1)S(1)} fusion(bf16[4,1,96,384]{3,2,0,1:T(8,128)(2,1)S(1)} %collective-permute-done.5, s32[]{:T(128)S(6)} %select_n.60, f32[4,2,96,384]{3,2,1,0:T(8,128)} %bitcast.36), kind=kLoop, calls=%fused_computation.4 | loop fusion | flops 442368 | bytes 1179652 | tf_op jit(solution)/shard_map/reshape | solution.py:285
  88.2 1.3 %collective-permute-done.9 = bf16[15,16,384]{2,1,0:T(8,128)(2,1)S(1)} collective-permute-done((bf16[15,16,384]{2,1,0:T(8,128)(2,1)S(1)}, bf16[15,16,384]{2,1,0:T(8,128)(2,1)S(1)}, u32[]{:S(2)}, u32[]{:S(2)}) %collective-permute-start.9) | collective-permute-done | bytes 184352 | tf_op jit(solution)/shard_map/ppermute | solution.py:220
  89.6 2.8 %collective-permute-done.8 = bf16[15,16,384]{2,1,0:T(8,128)(2,1)S(1)} collective-permute-done((bf16[15,16,384]{2,1,0:T(8,128)(2,1)S(1)}, bf16[15,16,384]{2,1,0:T(8,128)(2,1)S(1)}, u32[]{:S(2)}, u32[]{:S(2)}) %collective-permute-start.8) | collective-permute-done | bytes 184352 | tf_op jit(solution)/shard_map/ppermute | solution.py:215
  92.4 0.8 copy.12
  93.2 3.5 %all-to-all-start = ((bf16[8,96,192]{2,1,0:T(8,128)(2,1)}), bf16[8,96,192]{2,1,0:T(8,128)(2,1)S(1)}, u32[]{:S(2)}, u32[]{:S(2)}) async-start(bf16[8,96,192]{2,1,0:T(8,128)(2,1)} %bitcast.18), calls=%async_computation | async-start | bytes 786432 | tf_op jit(solution)/shard_map/all_to_all | solution.py:290
  97.0 1.2 %copy-done.1 = bf16[1,30,60,384]{3,2,1,0:T(8,128)(2,1)S(1)} copy-done((bf16[1,30,60,384]{3,2,1,0:T(8,128)(2,1)S(1)}, bf16[1,30,60,384]{3,2,1,0:T(8,128)(2,1)}, u32[]{:S(2)}) %copy-start.1) | copy-done | bytes 1382424
  98.2 1.8 %add_convert_fusion = bf16[1,30,60,384]{3,2,1,0:T(8,128)(2,1)} fusion(bf16[1,30,60,384]{3,2,1,0:T(8,128)(2,1)S(1)} %copy-done.1, bf16[1,30,15,384]{3,2,1,0:T(8,128)(2,1)S(1)} %get-tuple-element.83, bf16[1,30,30,384]{3,2,1,0:T(8,128)(2,1)S(1)} %fusion, bf16[1,30,15,384]{3,2,1,0:T(8,128)(2,1)S(1)} %get-tuple-element.84), kind=kLoop, calls=%fused_computation | loop fusion | flops 6220800 | bytes 4147200 | tf_op jit(solution)/shard_map/convert_element_type | solution.py:395
  100.0 9.0 %all-to-all-done.in_ref = bf16[8,96,192]{2,1,0:T(8,128)(2,1)S(1)} async-done(((bf16[8,96,192]{2,1,0:T(8,128)(2,1)}), bf16[8,96,192]{2,1,0:T(8,128)(2,1)S(1)}, u32[]{:S(2)}, u32[]{:S(2)}) %all-to-all-start) | async-done | bytes 294944 | tf_op jit(solution)/shard_map/all_to_all | solution.py:290
  (30 shorter events, 3.6 us)
Async XLA Ops:
  0.6 1.4 %copy-start = (bf16[1,30,60,384]{3,2,1,0:T(8,128)(2,1)S(1)}, bf16[1,30,60,384]{3,2,1,0:T(8,128)(2,1)}, u32[]{:S(2)}) copy-start(bf16[1,30,60,384]{3,2,1,0:T(8,128)(2,1)} %cot_ref.2) | copy-start | bytes 4147204
  2.0 1.4 %copy-start.2 = (bf16[1,30,60,384]{3,2,1,0:T(8,128)(2,1)S(1)}, bf16[1,30,60,384]{3,2,1,0:T(8,128)(2,1)}, u32[]{:S(2)}) copy-start(bf16[1,30,60,384]{3,2,1,0:T(8,128)(2,1)} %hid_ref.2) | copy-start | bytes 4147204
  3.6 16.0 %copy-start.3 = (bf16[384,1152]{1,0:T(8,128)(2,1)S(1)}, bf16[384,1152]{1,0:T(8,128)(2,1)}, u32[]{:S(2)}) copy-start(bf16[384,1152]{1,0:T(8,128)(2,1)} %refs_5_.1) | copy-start | bytes 2654212
  3.6 16.0 %copy-start.4 = (bf16[384,384]{1,0:T(8,128)(2,1)S(1)}, bf16[384,384]{1,0:T(8,128)(2,1)}, u32[]{:S(2)}) copy-start(bf16[384,384]{1,0:T(8,128)(2,1)} %refs_6_.1) | copy-start | bytes 884740
  3.6 16.0 %copy-start.5 = (f32[384]{0:T(512)S(1)}, f32[384]{0:T(512)}, u32[]{:S(2)}) copy-start(f32[384]{0:T(512)} %refs_4_.3) | copy-start | bytes 4612
  3.6 16.0 %collective-permute-start.3 = (bf16[2,1,15,32,384]{4,3,2,1,0:T(8,128)(2,1)S(1)}, bf16[2,1,15,32,384]{4,3,2,1,0:T(8,128)(2,1)S(1)}, u32[]{:S(2)}, u32[]{:S(2)}) collective-permute-start(bf16[2,1,15,32,384]{4,3,2,1,0:T(8,128)(2,1)S(1)} %shard_map.76), channel_id=1, source_target_pairs={{1,5},{3,7},{4,0},{5,9},{6,2},{7,11},{8,4},{9,13},{10,6},{11,15},{... | collective-permute-start | bytes 2211848 | tf_op jit(solution)/shard_map/ppermute | solution.py:215
  5.7 39.0 %collective-permute-start = (bf16[2,1,15,16,384]{4,3,2,1,0:T(8,128)(2,1)S(1)}, bf16[2,1,15,16,384]{4,3,2,1,0:T(8,128)(2,1)S(1)}, u32[]{:S(2)}, u32[]{:S(2)}) collective-permute-start(bf16[2,1,15,16,384]{4,3,2,1,0:T(8,128)(2,1)S(1)} %get-tuple-element.40), channel_id=1, source_target_pairs={{0,3},{1,0},{2,1},{3,2},{4,7},{5,4},{6,5},{7,6},{8,11},{9,8},{10,9... | collective-permute-start | bytes 1105928 | tf_op jit(solution)/shard_map/ppermute | solution.py:220
  10.2 34.6 %collective-permute-start.1 = (bf16[2,1,15,16,384]{4,3,2,1,0:T(8,128)(2,1)S(1)}, bf16[2,1,15,16,384]{4,3,2,1,0:T(8,128)(2,1)S(1)}, u32[]{:S(2)}, u32[]{:S(2)}) collective-permute-start(bf16[2,1,15,16,384]{4,3,2,1,0:T(8,128)(2,1)S(1)} %get-tuple-element.41), channel_id=1, source_target_pairs={{1,5},{3,7},{4,0},{5,9},{6,2},{7,11},{8,4},{9,13},{10,6},{11,15},{... | collective-permute-start | bytes 1105928 | tf_op jit(solution)/shard_map/ppermute | solution.py:215
  11.4 33.3 %collective-permute-start.2 = (bf16[2,1,15,16,384]{4,3,2,1,0:T(8,128)(2,1)S(1)}, bf16[2,1,15,16,384]{4,3,2,1,0:T(8,128)(2,1)S(1)}, u32[]{:S(2)}, u32[]{:S(2)}) collective-permute-start(bf16[2,1,15,16,384]{4,3,2,1,0:T(8,128)(2,1)S(1)} %get-tuple-element.42), channel_id=1, source_target_pairs={{2,5},{0,7},{5,0},{6,9},{7,2},{4,11},{9,4},{10,13},{11,6},{8,15},{... | collective-permute-start | bytes 1105928 | tf_op jit(solution)/shard_map/ppermute | solution.py:215
  70.6 2.2 %collective-permute-start.4 = (bf16[8,96,384]{2,1,0:T(8,128)(2,1)S(1)}, bf16[8,96,384]{2,1,0:T(8,128)(2,1)}, u32[]{:S(2)}, u32[]{:S(2)}) collective-permute-start(bf16[8,96,384]{2,1,0:T(8,128)(2,1)S(1)} %get-tuple-element.52), channel_id=1, source_target_pairs={{0,1},{1,0},{2,3},{3,2},{4,5},{5,4},{6,7},{7,6},{8,9},{9,8},{10,11... | collective-permute-start | bytes 1769480 | tf_op jit(solution)/shard_map/ppermute | solution.py:199
  73.9 1.0 copy-start.6
  74.9 11.6 %collective-permute-start.5 = (bf16[4,1,96,384]{3,2,0,1:T(8,128)(2,1)S(1)}, bf16[4,1,96,384]{3,2,0,1:T(8,128)(2,1)S(1)}, u32[]{:S(2)}, u32[]{:S(2)}) collective-permute-start(bf16[4,1,96,384]{3,2,0,1:T(8,128)(2,1)S(1)} %dynamic-slice_convert_fusion), channel_id=1, source_target_pairs={{0,2},{1,3},{2,0},{3,1},{4,6},{5,7},{6,4},{7,5},{8,10},{9,11},{10,... | collective-permute-start | bytes 884744 | tf_op jit(solution)/shard_map/ppermute | solution.py:199
  77.3 10.6 %collective-permute-start.6 = (bf16[15,32,384]{2,1,0:T(8,128)(2,1)S(1)}, bf16[15,32,384]{2,1,0:T(8,128)(2,1)S(1)}, u32[]{:S(2)}, u32[]{:S(2)}) collective-permute-start(bf16[15,32,384]{2,1,0:T(8,128)(2,1)S(1)} %bitcast.27), channel_id=1, source_target_pairs={{5,1},{7,3},{0,4},{9,5},{2,6},{11,7},{4,8},{13,9},{6,10},{15,11},{... | collective-permute-start | bytes 1105928 | tf_op jit(solution)/shard_map/ppermute | solution.py:215
  81.0 6.9 %collective-permute-start.7 = (bf16[15,16,384]{2,1,0:T(8,128)(2,1)S(1)}, bf16[15,16,384]{2,1,0:T(8,128)(2,1)S(1)}, u32[]{:S(2)}, u32[]{:S(2)}) collective-permute-start(bf16[15,16,384]{2,1,0:T(8,128)(2,1)S(1)} %bitcast.34), channel_id=1, source_target_pairs={{5,1},{7,3},{0,4},{9,5},{2,6},{11,7},{4,8},{13,9},{6,10},{15,11},{... | collective-permute-start | bytes 552968 | tf_op jit(solution)/shard_map/ppermute | solution.py:215
  84.5 5.0 %collective-permute-start.9 = (bf16[15,16,384]{2,1,0:T(8,128)(2,1)S(1)}, bf16[15,16,384]{2,1,0:T(8,128)(2,1)S(1)}, u32[]{:S(2)}, u32[]{:S(2)}) collective-permute-start(bf16[15,16,384]{2,1,0:T(8,128)(2,1)S(1)} %bitcast.33), channel_id=1, source_target_pairs={{0,1},{1,2},{2,3},{3,0},{4,5},{5,6},{6,7},{7,4},{8,9},{9,10},{10,1... | collective-permute-start | bytes 552968 | tf_op jit(solution)/shard_map/ppermute | solution.py:220
  84.6 7.8 %collective-permute-start.8 = (bf16[15,16,384]{2,1,0:T(8,128)(2,1)S(1)}, bf16[15,16,384]{2,1,0:T(8,128)(2,1)S(1)}, u32[]{:S(2)}, u32[]{:S(2)}) collective-permute-start(bf16[15,16,384]{2,1,0:T(8,128)(2,1)S(1)} %bitcast.32), channel_id=1, source_target_pairs={{5,2},{7,0},{0,5},{9,6},{2,7},{11,4},{4,9},{13,10},{6,11},{15,8},{... | collective-permute-start | bytes 552968 | tf_op jit(solution)/shard_map/ppermute | solution.py:215
  93.2 15.9 %all-to-all-start = ((bf16[8,96,192]{2,1,0:T(8,128)(2,1)}), bf16[8,96,192]{2,1,0:T(8,128)(2,1)S(1)}, u32[]{:S(2)}, u32[]{:S(2)}) async-start(bf16[8,96,192]{2,1,0:T(8,128)(2,1)} %bitcast.18), calls=%async_computation | async-start | bytes 786432 | tf_op jit(solution)/shard_map/all_to_all | solution.py:290
  96.8 1.4 %copy-start.1 = (bf16[1,30,60,384]{3,2,1,0:T(8,128)(2,1)S(1)}, bf16[1,30,60,384]{3,2,1,0:T(8,128)(2,1)}, u32[]{:S(2)}) copy-start(bf16[1,30,60,384]{3,2,1,0:T(8,128)(2,1)} %cot_ref.2) | copy-start | bytes 4147204

commit v8 on v6

--- a/solution.py
+++ b/solution.py
@@ -274,7 +274,7 @@
     return mine + got.astype(F32)
 
 
-def reduce_weights(keep, send, lons, returns):
+def reduce_weights(keep, send, lons, inner_moved, returns):
     half, deep, width = keep.shape
     lats = lax.axis_size("lat")
     moved, waiting = [], list(returns)
@@ -287,17 +287,20 @@
         return value
 
     got = permuted(send, ("lon",), lambda i: (i ^ 1,))
-    keep = release(keep, len(waiting) // 2)
+    keep = release(keep, len(waiting) // 3)
     early = len(moved)
-    total = release((keep + got.astype(F32)).reshape(lats, lons // 2, deep, width), len(waiting))
+    total = (keep + got.astype(F32)).reshape(lats, lons // 2, deep, width)
+    total, inner_moved = lax.optimization_barrier((total, inner_moved))
     bit, left = 2, lons // 2
     while left > 1:
         total = scatter_bit(total.reshape(lats, left // 2, 2, deep, width), "lon", bit, 2)
         left //= 2
         bit *= 2
     total, moved[:early] = lax.optimization_barrier((total.reshape(lats, deep, width), moved[:early]))
+    total = release(total, len(waiting))
     total = scatter_direct(total, "dp", 2)
     total, moved[early:] = lax.optimization_barrier((total, moved[early:]))
+    moved = inner_moved + moved
     return scatter_direct(total, "lat", 0)[0], moved
 
 
@@ -354,14 +357,18 @@
         )
         out[b, wr, wc] = [d.reshape(half, pad, width) for d, (n, pad, _) in zip(done, metas)]
 
-    late = [(out[b, nr - 1, wc][1], lambda v: shared(v, back=True)) for b in range(samples) for wc in range(nc - 1)]
+    inner_moved = [
+        shared(out[b, nr - 1, wc][1], back=True) for b in range(samples) for wc in range(nc - 1)
+    ]
+    late = []
     for b in range(samples):
         own, own_lon, other, other_lon = out[b, nr - 1, nc - 1]
-        late.append((other, lambda v: shared(v, back=True)))
+        late.insert(b, (other, lambda v: shared(v, back=True)))
         late.append((other_lon, lambda v: shared(v, back=True, east=1)))
         late.append((own_lon, lambda v: along_lon(v, 1)))
-    total, moved = reduce_weights(sums[0], sums[1], lons, late)
-
+    total, moved = reduce_weights(sums[0], sums[1], lons, inner_moved, late)
+
+    edge_moved = moved[samples * (nc - 1):]
     rows_out = []
     for b in range(samples):
         def stacked(own, back, between, upper):
@@ -375,7 +382,8 @@
             between = [out[b, wr, wc][i] for wr in range(nr - 1) for i in range(2)]
             columns.append(stacked(own, moved[b * (nc - 1) + wc], between, odd == 1)[:, :WIN])
         own = out[b, nr - 1, nc - 1][0]
-        back, far, near = moved[samples * (nc - 1) + 3 * b:][:3]
+        back = edge_moved[b]
+        far, near = edge_moved[samples + 2 * b:][:2]
         between = [out[b, wr, nc - 1][i] for wr in range(nr - 1) for i in (0, 2)]
         columns.append(stacked(own, back, between, odd == 1)[:, :half])
         between = [along_lon(out[b, wr, nc - 1][i], 1) for wr in range(nr - 1) for i in (1, 3)]

time: 104 us -> 111 us (1.067)
  waiting for transfers between devices: 10.3 us -> 18.7 us
    ppermute x6, waiting for transfers between devices: 6.65 us -> 11.1 us  [permuted(): return lax.ppermute(value, tuple(axes), pairs)]
    ppermute x6, waiting for transfers between devices: 3.6 us -> 6.33 us  [shared(): return lax.ppermute(value, ('lat', 'lon'), pairs)]
    ppermute x2, waiting for transfers between devices: 0.01 us -> 1.24 us  [along_lon(): lax.ppermute(value, 'lon', [(j, (j + step) % count) for j in range(count)])]
    unnamed x14 -> x12, local copies, waits for them, and re-layouts: 3.72 us -> 2.77 us
  transfers between devices with their start and end apart: 14 -> 14, of which waited for: 4 -> 8; matrix products, arithmetic and copies ran while one was open for 3% -> 4% of each run, Pallas kernels for 25% -> 23%
where the time goes in v8:
time: 111 us
  Pallas kernels  51.7 us (47%)
  starting transfers between devices  30.5 us (27%)
  waiting for transfers between devices  18.7 us (17%)
  other arithmetic  4.6 us (4%)
  local copies, waits for them, and re-layouts  4.19 us (4%)
    pallas_call x2, Pallas kernels, window_call(): pl.pallas_call(functools.partial(window_kernel, head, metas, (prev is not...  50.8 us
    ppermute x6, starting transfers between devices, shared(): return lax.ppermute(value, ('lat', 'lon'), pairs)  16.8 us
    ppermute x6, waiting for transfers between devices, permuted(): return lax.ppermute(value, tuple(axes), pairs)  11.1 us
    ppermute x6, starting transfers between devices, permuted(): return lax.ppermute(value, tuple(axes), pairs)  9.2 us
    ppermute x6, waiting for transfers between devices, shared(): return lax.ppermute(value, ('lat', 'lon'), pairs)  6.33 us
    ppermute x2, starting transfers between devices, along_lon(): lax.ppermute(value, 'lon', [(j, (j + step) % count) for j in range(count)])  4.47 us
    unnamed x12, local copies, waits for them, and re-layouts  2.77 us
  transfers between devices with their start and end apart: 14, of which 8 were waited for; matrix products, arithmetic and copies ran while one was open for 4% of the time, Pallas kernels for 23%

profile of v8, /device:TPU:0, one launch (start us, length us, event | category | flops | bytes accessed | tf_op | source)
XLA Modules:
  0.0 110.5 jit_solution(11854304829158722101)
XLA Ops:
  0.6 1.4 %copy-done = bf16[1,30,60,384]{3,2,1,0:T(8,128)(2,1)S(1)} copy-done((bf16[1,30,60,384]{3,2,1,0:T(8,128)(2,1)S(1)}, bf16[1,30,60,384]{3,2,1,0:T(8,128)(2,1)}, u32[]{:S(2)}) %copy-start) | copy-done | bytes 1382424
  2.0 1.4 %copy-done.2 = bf16[1,30,60,384]{3,2,1,0:T(8,128)(2,1)S(1)} copy-done((bf16[1,30,60,384]{3,2,1,0:T(8,128)(2,1)S(1)}, bf16[1,30,60,384]{3,2,1,0:T(8,128)(2,1)}, u32[]{:S(2)}) %copy-start.2) | copy-done | bytes 1382424
  3.6 1.4 %collective-permute-start.3 = (bf16[2,1,15,32,384]{4,3,2,1,0:T(8,128)(2,1)S(1)}, bf16[2,1,15,32,384]{4,3,2,1,0:T(8,128)(2,1)S(1)}, u32[]{:S(2)}, u32[]{:S(2)}) collective-permute-start(bf16[2,1,15,32,384]{4,3,2,1,0:T(8,128)(2,1)S(1)} %shard_map.76), channel_id=1, source_target_pairs={{1,5},{3,7},{4,0},{5,9},{6,2},{7,11},{8,4},{9,13},{10,6},{11,15},{... | collective-permute-start | bytes 2211848 | tf_op jit(solution)/shard_map/ppermute | solution.py:215
  5.7 4.4 %collective-permute-start = (bf16[2,1,15,16,384]{4,3,2,1,0:T(8,128)(2,1)S(1)}, bf16[2,1,15,16,384]{4,3,2,1,0:T(8,128)(2,1)S(1)}, u32[]{:S(2)}, u32[]{:S(2)}) collective-permute-start(bf16[2,1,15,16,384]{4,3,2,1,0:T(8,128)(2,1)S(1)} %get-tuple-element.37), channel_id=1, source_target_pairs={{0,3},{1,0},{2,1},{3,2},{4,7},{5,4},{6,5},{7,6},{8,11},{9,8},{10,9... | collective-permute-start | bytes 1105928 | tf_op jit(solution)/shard_map/ppermute | solution.py:220
  10.2 1.3 %collective-permute-start.1 = (bf16[2,1,15,16,384]{4,3,2,1,0:T(8,128)(2,1)S(1)}, bf16[2,1,15,16,384]{4,3,2,1,0:T(8,128)(2,1)S(1)}, u32[]{:S(2)}, u32[]{:S(2)}) collective-permute-start(bf16[2,1,15,16,384]{4,3,2,1,0:T(8,128)(2,1)S(1)} %get-tuple-element.38), channel_id=1, source_target_pairs={{1,5},{3,7},{4,0},{5,9},{6,2},{7,11},{8,4},{9,13},{10,6},{11,15},{... | collective-permute-start | bytes 1105928 | tf_op jit(solution)/shard_map/ppermute | solution.py:215
  11.4 4.8 %collective-permute-start.2 = (bf16[2,1,15,16,384]{4,3,2,1,0:T(8,128)(2,1)S(1)}, bf16[2,1,15,16,384]{4,3,2,1,0:T(8,128)(2,1)S(1)}, u32[]{:S(2)}, u32[]{:S(2)}) collective-permute-start(bf16[2,1,15,16,384]{4,3,2,1,0:T(8,128)(2,1)S(1)} %get-tuple-element.39), channel_id=1, source_target_pairs={{2,5},{0,7},{5,0},{6,9},{7,2},{4,11},{9,4},{10,13},{11,6},{8,15},{... | collective-permute-start | bytes 1105928 | tf_op jit(solution)/shard_map/ppermute | solution.py:215
  16.3 3.4 %collective-permute-done.3 = bf16[2,1,15,32,384]{4,3,2,1,0:T(8,128)(2,1)S(1)} collective-permute-done((bf16[2,1,15,32,384]{4,3,2,1,0:T(8,128)(2,1)S(1)}, bf16[2,1,15,32,384]{4,3,2,1,0:T(8,128)(2,1)S(1)}, u32[]{:S(2)}, u32[]{:S(2)}) %collective-permute-start.3) | collective-permute-done | bytes 737312 | tf_op jit(solution)/shard_map/ppermute | solution.py:215
  19.7 25.0 %shard_map.78 = (bf16[480,384]{1,0:T(8,128)(2,1)S(1)}, bf16[480,384]{1,0:T(8,128)(2,1)S(1)}, f32[384,1152]{1,0:T(8,128)S(1)}, f32[384,384]{1,0:T(8,128)S(1)}) custom-call(bf16[2,480,384]{2,1,0:T(8,128)(2,1)S(1)} %bitcast.28, bf16[2,480,384]{2,1,0:T(8,128)(2,1)S(1)} %bitcast.27, f32[384]{0:T(512)S(1)} %copy-done.5, bf16[384,1152]{1,0:T(8,128)(2,1)S(1)} %copy-done.3, ...), custom_call_target="tpu_custom_call" | custom-call | flops 7644119040 | bytes 8388608 | tf_op jit(solution)/shard_map/pallas_call | solution.py:168
  44.7 25.8 %shard_map.79 = (bf16[240,384]{1,0:T(8,128)(2,1)S(1)}, bf16[240,384]{1,0:T(8,128)(2,1)S(1)}, bf16[240,384]{1,0:T(8,128)(2,1)S(1)}, bf16[240,384]{1,0:T(8,128)(2,...) custom-call(bf16[2,240,384]{2,1,0:T(8,128)(2,1)S(1)} %bitcast.30, bf16[2,240,384]{2,1,0:T(8,128)(2,1)S(1)} %bitcast.31, ...), custom_call_target="tpu_custom_call" | custom-call | flops 7644119040 | bytes 8388608 | tf_op jit(solution)/shard_map/pallas_call | solution.py:168
  70.6 4.3 %collective-permute-start.5 = (bf16[15,32,384]{2,1,0:T(8,128)(2,1)S(1)}, bf16[15,32,384]{2,1,0:T(8,128)(2,1)}, u32[]{:S(2)}, u32[]{:S(2)}) collective-permute-start(bf16[15,32,384]{2,1,0:T(8,128)(2,1)S(1)} %bitcast.29), channel_id=1, source_target_pairs={{5,1},{7,3},{0,4},{9,5},{2,6},{11,7},{4,8},{13,9},{6,10},{15,11},{... | collective-permute-start | bytes 1105928 | tf_op jit(solution)/shard_map/ppermute | solution.py:215
  74.9 2.9 %collective-permute-start.7 = (bf16[15,16,384]{2,1,0:T(8,128)(2,1)S(1)}, bf16[15,16,384]{2,1,0:T(8,128)(2,1)S(1)}, u32[]{:S(2)}, u32[]{:S(2)}) collective-permute-start(bf16[15,16,384]{2,1,0:T(8,128)(2,1)S(1)} %bitcast.36), channel_id=1, source_target_pairs={{5,1},{7,3},{0,4},{9,5},{2,6},{11,7},{4,8},{13,9},{6,10},{15,11},{... | collective-permute-start | bytes 552968 | tf_op jit(solution)/shard_map/ppermute | solution.py:215
  77.8 1.2 %convert_add_fusion = f32[8,96,384]{2,1,0:T(8,128)S(1)} fusion(f32[8,96,384]{2,1,0:T(8,128)S(1)} %get-tuple-element.46, bf16[8,96,384]{2,1,0:T(8,128)(2,1)} %collective-permute-done.4), kind=kLoop, calls=%fused_computation.1 | loop fusion | flops 589824 | bytes 2949120 | tf_op jit(solution)/shard_map/add | solution.py:292
  79.2 2.6 %collective-permute-start.6 = (bf16[4,1,96,384]{3,2,0,1:T(8,128)(2,1)S(1)}, bf16[4,1,96,384]{3,2,0,1:T(8,128)(2,1)S(1)}, u32[]{:S(2)}, u32[]{:S(2)}) collective-permute-start(bf16[4,1,96,384]{3,2,0,1:T(8,128)(2,1)S(1)} %dynamic-slice_convert_fusion), channel_id=1, source_target_pairs={{0,2},{1,3},{2,0},{3,1},{4,6},{5,7},{6,4},{7,5},{8,10},{9,11},{10,... | collective-permute-start | bytes 884744 | tf_op jit(solution)/shard_map/ppermute | solution.py:199
  81.8 1.1 broadcast_select_fusion.1
  82.9 6.2 %collective-permute-done.6 = bf16[4,1,96,384]{3,2,0,1:T(8,128)(2,1)S(1)} collective-permute-done((bf16[4,1,96,384]{3,2,0,1:T(8,128)(2,1)S(1)}, bf16[4,1,96,384]{3,2,0,1:T(8,128)(2,1)S(1)}, u32[]{:S(2)}, u32[]{:S(2)}) %collective-permute-start.6) | collective-permute-done | bytes 294944 | tf_op jit(solution)/shard_map/ppermute | solution.py:199
  89.3 1.8 %collective-permute-start.8 = (bf16[4,96,192]{2,1,0:T(8,128)(2,1)S(1)}, bf16[4,96,192]{2,1,0:T(8,128)(2,1)S(1)}, u32[]{:S(2)}, u32[]{:S(2)}) collective-permute-start(bf16[4,96,192]{2,1,0:T(8,128)(2,1)S(1)} %dynamic-slice_convert_fusion.1), channel_id=1, source_target_pairs={{0,16},{16,0},{1,17},{17,1},{2,18},{18,2},{3,19},{19,3},{4,20},{20... | collective-permute-start | bytes 442376 | tf_op jit(solution)/shard_map/ppermute | solution.py:199
  91.1 2.1 %collective-permute-start.9 = (bf16[15,16,384]{2,1,0:T(8,128)(2,1)S(1)}, bf16[15,16,384]{2,1,0:T(8,128)(2,1)S(1)}, u32[]{:S(2)}, u32[]{:S(2)}) collective-permute-start(bf16[15,16,384]{2,1,0:T(8,128)(2,1)S(1)} %bitcast.35), channel_id=1, source_target_pairs={{5,2},{7,0},{0,5},{9,6},{2,7},{11,4},{4,9},{13,10},{6,11},{15,8},{... | collective-permute-start | bytes 552968 | tf_op jit(solution)/shard_map/ppermute | solution.py:215
  93.3 2.7 %collective-permute-done.8 = bf16[4,96,192]{2,1,0:T(8,128)(2,1)S(1)} collective-permute-done((bf16[4,96,192]{2,1,0:T(8,128)(2,1)S(1)}, bf16[4,96,192]{2,1,0:T(8,128)(2,1)S(1)}, u32[]{:S(2)}, u32[]{:S(2)}) %collective-permute-start.8) | collective-permute-done | bytes 147488 | tf_op jit(solution)/shard_map/ppermute | solution.py:199
  96.2 2.8 %collective-permute-done.9 = bf16[15,16,384]{2,1,0:T(8,128)(2,1)S(1)} collective-permute-done((bf16[15,16,384]{2,1,0:T(8,128)(2,1)S(1)}, bf16[15,16,384]{2,1,0:T(8,128)(2,1)S(1)}, u32[]{:S(2)}, u32[]{:S(2)}) %collective-permute-start.9) | collective-permute-done | bytes 184352 | tf_op jit(solution)/shard_map/ppermute | solution.py:215
  98.9 1.2 %collective-permute-done.10 = bf16[15,16,384]{2,1,0:T(8,128)(2,1)S(1)} collective-permute-done((bf16[15,16,384]{2,1,0:T(8,128)(2,1)S(1)}, bf16[15,16,384]{2,1,0:T(8,128)(2,1)S(1)}, u32[]{:S(2)}, u32[]{:S(2)}) %collective-permute-start.10) | collective-permute-done | bytes 184352 | tf_op jit(solution)/shard_map/ppermute | solution.py:220
  100.2 2.1 %collective-permute-start.13 = (bf16[1,96,192]{2,1,0:T(8,128)(2,1)S(1)}, bf16[1,96,192]{2,1,0:T(8,128)(2,1)S(1)}, u32[]{:S(2)}, u32[]{:S(2)}) collective-permute-start(bf16[1,96,192]{2,1,0:T(8,128)(2,1)S(1)} %get-tuple-element.68), channel_id=1, source_target_pairs={{0,12},{4,0},{8,4},{12,8},{1,13},{5,1},{9,5},{13,9},{2,14},{6,2},{... | collective-permute-start | bytes 110600 | tf_op jit(solution)/shard_map/ppermute | solution.py:199
  103.4 1.6 %collective-permute-start.11 = (bf16[1,96,192]{2,1,0:T(8,128)(2,1)S(1)}, bf16[1,96,192]{2,1,0:T(8,128)(2,1)S(1)}, u32[]{:S(2)}, u32[]{:S(2)}) collective-permute-start(bf16[1,96,192]{2,1,0:T(8,128)(2,1)S(1)} %get-tuple-element.67), channel_id=1, source_target_pairs={{0,4},{4,8},{8,12},{12,0},{1,5},{5,9},{9,13},{13,1},{2,6},{6,10},{... | collective-permute-start | bytes 110600 | tf_op jit(solution)/shard_map/ppermute | solution.py:199
  105.1 1.9 %add_convert_fusion = bf16[1,30,60,384]{3,2,1,0:T(8,128)(2,1)} fusion(bf16[1,30,60,384]{3,2,1,0:T(8,128)(2,1)S(1)} %copy-done.1, bf16[1,30,15,384]{3,2,1,0:T(8,128)(2,1)S(1)} %get-tuple-element.74, bf16[1,30,30,384]{3,2,1,0:T(8,128)(2,1)S(1)} %fusion, bf16[1,30,15,384]{3,2,1,0:T(8,128)(2,1)S(1)} %get-tuple-element.75), kind=kLoop, calls=%fused_computation | loop fusion | flops 6220800 | bytes 4147200 | tf_op jit(solution)/shard_map/convert_element_type | solution.py:393
  108.1 1.2 %collective-permute-done.11 = bf16[1,96,192]{2,1,0:T(8,128)(2,1)S(1)} collective-permute-done((bf16[1,96,192]{2,1,0:T(8,128)(2,1)S(1)}, bf16[1,96,192]{2,1,0:T(8,128)(2,1)S(1)}, u32[]{:S(2)}, u32[]{:S(2)}) %collective-permute-start.11) | collective-permute-done | bytes 36896 | tf_op jit(solution)/shard_map/ppermute | solution.py:199
  (35 shorter events, 5.3 us)
Async XLA Ops:
  0.6 1.4 %copy-start = (bf16[1,30,60,384]{3,2,1,0:T(8,128)(2,1)S(1)}, bf16[1,30,60,384]{3,2,1,0:T(8,128)(2,1)}, u32[]{:S(2)}) copy-start(bf16[1,30,60,384]{3,2,1,0:T(8,128)(2,1)} %cot_ref.2) | copy-start | bytes 4147204
  2.0 1.4 %copy-start.2 = (bf16[1,30,60,384]{3,2,1,0:T(8,128)(2,1)S(1)}, bf16[1,30,60,384]{3,2,1,0:T(8,128)(2,1)}, u32[]{:S(2)}) copy-start(bf16[1,30,60,384]{3,2,1,0:T(8,128)(2,1)} %hid_ref.2) | copy-start | bytes 4147204
  3.6 16.0 %copy-start.3 = (bf16[384,1152]{1,0:T(8,128)(2,1)S(1)}, bf16[384,1152]{1,0:T(8,128)(2,1)}, u32[]{:S(2)}) copy-start(bf16[384,1152]{1,0:T(8,128)(2,1)} %refs_5_.1) | copy-start | bytes 2654212
  3.6 16.0 %copy-start.4 = (bf16[384,384]{1,0:T(8,128)(2,1)S(1)}, bf16[384,384]{1,0:T(8,128)(2,1)}, u32[]{:S(2)}) copy-start(bf16[384,384]{1,0:T(8,128)(2,1)} %refs_6_.1) | copy-start | bytes 884740
  3.6 16.0 %copy-start.5 = (f32[384]{0:T(512)S(1)}, f32[384]{0:T(512)}, u32[]{:S(2)}) copy-start(f32[384]{0:T(512)} %refs_4_.3) | copy-start | bytes 4612
  3.6 16.0 %collective-permute-start.3 = (bf16[2,1,15,32,384]{4,3,2,1,0:T(8,128)(2,1)S(1)}, bf16[2,1,15,32,384]{4,3,2,1,0:T(8,128)(2,1)S(1)}, u32[]{:S(2)}, u32[]{:S(2)}) collective-permute-start(bf16[2,1,15,32,384]{4,3,2,1,0:T(8,128)(2,1)S(1)} %shard_map.76), channel_id=1, source_target_pairs={{1,5},{3,7},{4,0},{5,9},{6,2},{7,11},{8,4},{9,13},{10,6},{11,15},{... | collective-permute-start | bytes 2211848 | tf_op jit(solution)/shard_map/ppermute | solution.py:215
  5.7 39.0 %collective-permute-start = (bf16[2,1,15,16,384]{4,3,2,1,0:T(8,128)(2,1)S(1)}, bf16[2,1,15,16,384]{4,3,2,1,0:T(8,128)(2,1)S(1)}, u32[]{:S(2)}, u32[]{:S(2)}) collective-permute-start(bf16[2,1,15,16,384]{4,3,2,1,0:T(8,128)(2,1)S(1)} %get-tuple-element.37), channel_id=1, source_target_pairs={{0,3},{1,0},{2,1},{3,2},{4,7},{5,4},{6,5},{7,6},{8,11},{9,8},{10,9... | collective-permute-start | bytes 1105928 | tf_op jit(solution)/shard_map/ppermute | solution.py:220
  10.2 34.6 %collective-permute-start.1 = (bf16[2,1,15,16,384]{4,3,2,1,0:T(8,128)(2,1)S(1)}, bf16[2,1,15,16,384]{4,3,2,1,0:T(8,128)(2,1)S(1)}, u32[]{:S(2)}, u32[]{:S(2)}) collective-permute-start(bf16[2,1,15,16,384]{4,3,2,1,0:T(8,128)(2,1)S(1)} %get-tuple-element.38), channel_id=1, source_target_pairs={{1,5},{3,7},{4,0},{5,9},{6,2},{7,11},{8,4},{9,13},{10,6},{11,15},{... | collective-permute-start | bytes 1105928 | tf_op jit(solution)/shard_map/ppermute | solution.py:215
  11.4 33.3 %collective-permute-start.2 = (bf16[2,1,15,16,384]{4,3,2,1,0:T(8,128)(2,1)S(1)}, bf16[2,1,15,16,384]{4,3,2,1,0:T(8,128)(2,1)S(1)}, u32[]{:S(2)}, u32[]{:S(2)}) collective-permute-start(bf16[2,1,15,16,384]{4,3,2,1,0:T(8,128)(2,1)S(1)} %get-tuple-element.39), channel_id=1, source_target_pairs={{2,5},{0,7},{5,0},{6,9},{7,2},{4,11},{9,4},{10,13},{11,6},{8,15},{... | collective-permute-start | bytes 1105928 | tf_op jit(solution)/shard_map/ppermute | solution.py:215
  70.5 7.3 %collective-permute-start.4 = (bf16[8,96,384]{2,1,0:T(8,128)(2,1)S(1)}, bf16[8,96,384]{2,1,0:T(8,128)(2,1)}, u32[]{:S(2)}, u32[]{:S(2)}) collective-permute-start(bf16[8,96,384]{2,1,0:T(8,128)(2,1)S(1)} %get-tuple-element.47), channel_id=1, source_target_pairs={{0,1},{1,0},{2,3},{3,2},{4,5},{5,4},{6,7},{7,6},{8,9},{9,8},{10,11... | collective-permute-start | bytes 1769480 | tf_op jit(solution)/shard_map/ppermute | solution.py:199
  70.6 8.5 %collective-permute-start.5 = (bf16[15,32,384]{2,1,0:T(8,128)(2,1)S(1)}, bf16[15,32,384]{2,1,0:T(8,128)(2,1)}, u32[]{:S(2)}, u32[]{:S(2)}) collective-permute-start(bf16[15,32,384]{2,1,0:T(8,128)(2,1)S(1)} %bitcast.29), channel_id=1, source_target_pairs={{5,1},{7,3},{0,4},{9,5},{2,6},{11,7},{4,8},{13,9},{6,10},{15,11},{... | collective-permute-start | bytes 1105928 | tf_op jit(solution)/shard_map/ppermute | solution.py:215
  74.9 14.3 %collective-permute-start.7 = (bf16[15,16,384]{2,1,0:T(8,128)(2,1)S(1)}, bf16[15,16,384]{2,1,0:T(8,128)(2,1)S(1)}, u32[]{:S(2)}, u32[]{:S(2)}) collective-permute-start(bf16[15,16,384]{2,1,0:T(8,128)(2,1)S(1)} %bitcast.36), channel_id=1, source_target_pairs={{5,1},{7,3},{0,4},{9,5},{2,6},{11,7},{4,8},{13,9},{6,10},{15,11},{... | collective-permute-start | bytes 552968 | tf_op jit(solution)/shard_map/ppermute | solution.py:215
  79.2 10.0 %collective-permute-start.6 = (bf16[4,1,96,384]{3,2,0,1:T(8,128)(2,1)S(1)}, bf16[4,1,96,384]{3,2,0,1:T(8,128)(2,1)S(1)}, u32[]{:S(2)}, u32[]{:S(2)}) collective-permute-start(bf16[4,1,96,384]{3,2,0,1:T(8,128)(2,1)S(1)} %dynamic-slice_convert_fusion), channel_id=1, source_target_pairs={{0,2},{1,3},{2,0},{3,1},{4,6},{5,7},{6,4},{7,5},{8,10},{9,11},{10,... | collective-permute-start | bytes 884744 | tf_op jit(solution)/shard_map/ppermute | solution.py:199
  89.3 6.6 %collective-permute-start.8 = (bf16[4,96,192]{2,1,0:T(8,128)(2,1)S(1)}, bf16[4,96,192]{2,1,0:T(8,128)(2,1)S(1)}, u32[]{:S(2)}, u32[]{:S(2)}) collective-permute-start(bf16[4,96,192]{2,1,0:T(8,128)(2,1)S(1)} %dynamic-slice_convert_fusion.1), channel_id=1, source_target_pairs={{0,16},{16,0},{1,17},{17,1},{2,18},{18,2},{3,19},{19,3},{4,20},{20... | collective-permute-start | bytes 442376 | tf_op jit(solution)/shard_map/ppermute | solution.py:199
  91.1 7.8 %collective-permute-start.9 = (bf16[15,16,384]{2,1,0:T(8,128)(2,1)S(1)}, bf16[15,16,384]{2,1,0:T(8,128)(2,1)S(1)}, u32[]{:S(2)}, u32[]{:S(2)}) collective-permute-start(bf16[15,16,384]{2,1,0:T(8,128)(2,1)S(1)} %bitcast.35), channel_id=1, source_target_pairs={{5,2},{7,0},{0,5},{9,6},{2,7},{11,4},{4,9},{13,10},{6,11},{15,8},{... | collective-permute-start | bytes 552968 | tf_op jit(solution)/shard_map/ppermute | solution.py:215
  93.2 7.0 %collective-permute-start.10 = (bf16[15,16,384]{2,1,0:T(8,128)(2,1)S(1)}, bf16[15,16,384]{2,1,0:T(8,128)(2,1)S(1)}, u32[]{:S(2)}, u32[]{:S(2)}) collective-permute-start(bf16[15,16,384]{2,1,0:T(8,128)(2,1)S(1)} %bitcast.34), channel_id=1, source_target_pairs={{0,1},{1,2},{2,3},{3,0},{4,5},{5,6},{6,7},{7,4},{8,9},{9,10},{10,1... | collective-permute-start | bytes 552968 | tf_op jit(solution)/shard_map/ppermute | solution.py:220
  96.2 8.9 %copy-start.1 = (bf16[1,30,60,384]{3,2,1,0:T(8,128)(2,1)S(1)}, bf16[1,30,60,384]{3,2,1,0:T(8,128)(2,1)}, u32[]{:S(2)}) copy-start(bf16[1,30,60,384]{3,2,1,0:T(8,128)(2,1)} %cot_ref.2) | copy-start | bytes 4147204
  100.2 6.8 %collective-permute-start.13 = (bf16[1,96,192]{2,1,0:T(8,128)(2,1)S(1)}, bf16[1,96,192]{2,1,0:T(8,128)(2,1)S(1)}, u32[]{:S(2)}, u32[]{:S(2)}) collective-permute-start(bf16[1,96,192]{2,1,0:T(8,128)(2,1)S(1)} %get-tuple-element.68), channel_id=1, source_target_pairs={{0,12},{4,0},{8,4},{12,8},{1,13},{5,1},{9,5},{13,9},{2,14},{6,2},{... | collective-permute-start | bytes 110600 | tf_op jit(solution)/shard_map/ppermute | solution.py:199
  102.3 5.7 %collective-permute-start.12 = (bf16[1,96,192]{2,1,0:T(8,128)(2,1)S(1)}, bf16[1,96,192]{2,1,0:T(8,128)(2,1)S(1)}, u32[]{:S(2)}, u32[]{:S(2)}) collective-permute-start(bf16[1,96,192]{2,1,0:T(8,128)(2,1)S(1)} %get-tuple-element.69), channel_id=1, source_target_pairs={{0,8},{4,12},{8,0},{12,4},{1,9},{5,13},{9,1},{13,5},{2,10},{6,14},... | collective-permute-start | bytes 110600 | tf_op jit(solution)/shard_map/ppermute | solution.py:199
  103.4 5.9 %collective-permute-start.11 = (bf16[1,96,192]{2,1,0:T(8,128)(2,1)S(1)}, bf16[1,96,192]{2,1,0:T(8,128)(2,1)S(1)}, u32[]{:S(2)}, u32[]{:S(2)}) collective-permute-start(bf16[1,96,192]{2,1,0:T(8,128)(2,1)S(1)} %get-tuple-element.67), channel_id=1, source_target_pairs={{0,4},{4,8},{8,12},{12,0},{1,5},{5,9},{9,13},{13,1},{2,6},{6,10},{... | collective-permute-start | bytes 110600 | tf_op jit(solution)/shard_map/ppermute | solution.py:199

commit v9 on v6

--- a/solution.py
+++ b/solution.py
@@ -253,6 +253,41 @@
     return list(outs)
 
 
+def cut_sent_kernel(specs, half, hid_ref, cot_ref, *refs):
+    outs, (held, sems) = refs[:len(specs)], refs[len(specs):]
+    samples = hid_ref.shape[0]
+    at = lax.rem(lax.axis_index("lon"), 2) * (hid_ref.shape[1] - half)
+    copies = [
+        (k, b, pltpu.make_async_copy(ref.at[b, pl.ds(at, half)], held.at[k, b], sems.at[k, b]))
+        for b in range(samples)
+        for k, ref in enumerate((hid_ref, cot_ref))
+    ]
+    for _, _, copy in copies:
+        copy.start()
+    for k, b, copy in copies:
+        copy.wait()
+        rows = held[k, b].astype(F32)
+        for out, (cols, n, pad) in zip(outs, specs):
+            filler = jnp.zeros((half, pad - n, rows.shape[2]), F32)
+            out[k, b] = jnp.concatenate([rows[:, cols:cols + n], filler], axis=1).astype(BF)
+
+
+def cut_sent_call(hid, cot, specs, half):
+    samples, _, lon_cols, width = hid.shape
+    outs = pl.pallas_call(
+        functools.partial(cut_sent_kernel, specs, half),
+        out_shape=tuple(jax.ShapeDtypeStruct((2, samples, half, pad, width), BF) for _, _, pad in specs),
+        in_specs=[pl.BlockSpec(memory_space=pl.ANY)] * 2,
+        out_specs=tuple([pl.BlockSpec(memory_space=pltpu.VMEM)] * len(specs)),
+        scratch_shapes=[
+            pltpu.VMEM((2, samples, half, lon_cols, width), BF),
+            pltpu.SemaphoreType.DMA((2, samples)),
+        ],
+        compiler_params=pltpu.CompilerParams(vmem_limit_bytes=60 * 2**20),
+    )(hid, cot)
+    return list(outs)
+
+
 def scatter_direct(value, axis, dim):
     count = lax.axis_size(axis)
     me = lax.axis_index(axis)
@@ -274,7 +309,7 @@
     return mine + got.astype(F32)
 
 
-def reduce_weights(keep, send, lons, returns):
+def reduce_weights(keep, send, lons, samples, returns):
     half, deep, width = keep.shape
     lats = lax.axis_size("lat")
     moved, waiting = [], list(returns)
@@ -287,15 +322,16 @@
         return value
 
     got = permuted(send, ("lon",), lambda i: (i ^ 1,))
-    keep = release(keep, len(waiting) // 2)
+    keep = release(keep, len(waiting) - 2 * samples)
     early = len(moved)
-    total = release((keep + got.astype(F32)).reshape(lats, lons // 2, deep, width), len(waiting))
+    total = release((keep + got.astype(F32)).reshape(lats, lons // 2, deep, width), len(waiting) - samples)
     bit, left = 2, lons // 2
     while left > 1:
         total = scatter_bit(total.reshape(lats, left // 2, 2, deep, width), "lon", bit, 2)
         left //= 2
         bit *= 2
     total, moved[:early] = lax.optimization_barrier((total.reshape(lats, deep, width), moved[:early]))
+    total = release(total, len(waiting))
     total = scatter_direct(total, "dp", 2)
     total, moved[early:] = lax.optimization_barrier((total, moved[early:]))
     return scatter_direct(total, "lat", 0)[0], moved
@@ -315,7 +351,7 @@
     odd = lax.axis_index("lon") % 2
     inner = [wc * WIN + SHIFT for wc in range(nc - 1)]
     edge = (nc - 1) * WIN + SHIFT
-    sent = cut_call(hidden_in, grad_out, [("sent", at, WIN, wide, "") for at in inner], half) if inner else []
+    sent = cut_sent_call(hidden_in, grad_out, [(at, WIN, wide) for at in inner], half) if inner else []
     hid, cot, sent = lax.optimization_barrier((hidden_in, grad_out, sent))
     inner_in = [shared(p) for p in sent]
     specs = [("sent", 0, half, short, "peer"), ("own", 0, half, short, "")]
@@ -355,12 +391,11 @@
         out[b, wr, wc] = [d.reshape(half, pad, width) for d, (n, pad, _) in zip(done, metas)]
 
     late = [(out[b, nr - 1, wc][1], lambda v: shared(v, back=True)) for b in range(samples) for wc in range(nc - 1)]
-    for b in range(samples):
-        own, own_lon, other, other_lon = out[b, nr - 1, nc - 1]
-        late.append((other, lambda v: shared(v, back=True)))
-        late.append((other_lon, lambda v: shared(v, back=True, east=1)))
-        late.append((own_lon, lambda v: along_lon(v, 1)))
-    total, moved = reduce_weights(sums[0], sums[1], lons, late)
+    corners = [out[b, nr - 1, nc - 1] for b in range(samples)]
+    late += [(c[2], lambda v: shared(v, back=True)) for c in corners]
+    late += [(c[3], lambda v: shared(v, back=True, east=1)) for c in corners]
+    late += [(c[1], lambda v: along_lon(v, 1)) for c in corners]
+    total, moved = reduce_weights(sums[0], sums[1], lons, samples, late)
 
     rows_out = []
     for b in range(samples):
@@ -375,7 +410,7 @@
             between = [out[b, wr, wc][i] for wr in range(nr - 1) for i in range(2)]
             columns.append(stacked(own, moved[b * (nc - 1) + wc], between, odd == 1)[:, :WIN])
         own = out[b, nr - 1, nc - 1][0]
-        back, far, near = moved[samples * (nc - 1) + 3 * b:][:3]
+        back, far, near = moved[samples * (nc - 1) + b::samples]
         between = [out[b, wr, nc - 1][i] for wr in range(nr - 1) for i in (0, 2)]
         columns.append(stacked(own, back, between, odd == 1)[:, :half])
         between = [along_lon(out[b, wr, nc - 1][i], 1) for wr in range(nr - 1) for i in (1, 3)]

time: 104 us -> 108 us (1.038)
  Pallas kernels: 51.7 us -> 55.1 us
  local copies, waits for them, and re-layouts: 5.16 us -> 3.83 us
    pallas_call x0 -> x1, Pallas kernels: none -> 2.49 us  [cut_sent_call(): pl.pallas_call(functools.partial(cut_sent_kernel, specs, half), out_shape...]
    unnamed x14 -> x16, local copies, waits for them, and re-layouts: 3.72 us -> 2.41 us
    pallas_call x2, Pallas kernels: 50.8 us -> 52 us  [window_call(): pl.pallas_call(functools.partial(window_kernel, head, metas, (prev is not...]
  transfers between devices with their start and end apart: 14 -> 14, of which waited for: 4 -> 5; matrix products, arithmetic and copies ran while one was open for 3% -> 3% of each run, Pallas kernels for 25% -> 25%
where the time goes in v9:
time: 108 us; the launch traced here: 107 us
  Pallas kernels  55.1 us (51%)
  starting transfers between devices  31.5 us (29%)
  waiting for transfers between devices  11.3 us (10%)
  other arithmetic  4.7 us (4%)
  local copies, waits for them, and re-layouts  3.83 us (4%)
    pallas_call x2, Pallas kernels, window_call(): pl.pallas_call(functools.partial(window_kernel, head, metas, (prev is not...  52 us
    ppermute x6, starting transfers between devices, shared(): return lax.ppermute(value, ('lat', 'lon'), pairs)  16.6 us
    ppermute x6, starting transfers between devices, permuted(): return lax.ppermute(value, tuple(axes), pairs)  10.4 us
    ppermute x6, waiting for transfers between devices, permuted(): return lax.ppermute(value, tuple(axes), pairs)  6.81 us
    ppermute x2, starting transfers between devices, along_lon(): lax.ppermute(value, 'lon', [(j, (j + step) % count) for j in range(count)])  4.42 us
    ppermute x6, waiting for transfers between devices, shared(): return lax.ppermute(value, ('lat', 'lon'), pairs)  4.36 us
    pallas_call x1, Pallas kernels, cut_sent_call(): pl.pallas_call(functools.partial(cut_sent_kernel, specs, half), out_shape...  2.49 us
    unnamed x16, local copies, waits for them, and re-layouts  2.41 us
  transfers between devices with their start and end apart: 14, of which 5 were waited for; matrix products, arithmetic and copies ran while one was open for 3% of the time, Pallas kernels for 25%

profile of v9, /device:TPU:0, one launch (start us, length us, event | category | flops | bytes accessed | tf_op | source)
XLA Modules:
  0.0 107.3 jit_solution(18188972341232895579)
XLA Ops:
  0.6 2.5 %shard_map.76 = bf16[2,1,15,32,384]{4,3,2,1,0:T(8,128)(2,1)} custom-call(bf16[1,30,60,384]{3,2,1,0:T(8,128)(2,1)} %hid_ref.2, bf16[1,30,60,384]{3,2,1,0:T(8,128)(2,1)} %cot_ref.2), custom_call_target="tpu_custom_call" | custom-call | tf_op jit(solution)/shard_map/pallas_call | solution.py:277
  3.2 1.4 %collective-permute-start.3 = (bf16[2,1,15,32,384]{4,3,2,1,0:T(8,128)(2,1)}, bf16[2,1,15,32,384]{4,3,2,1,0:T(8,128)(2,1)S(1)}, u32[]{:S(2)}, u32[]{:S(2)}) collective-permute-start(bf16[2,1,15,32,384]{4,3,2,1,0:T(8,128)(2,1)} %shard_map.76), channel_id=1, source_target_pairs={{1,5},{3,7},{4,0},{5,9},{6,2},{7,11},{8,4},{9,13},{10,6},{11,15},{... | collective-permute-start | bytes 2211848 | tf_op jit(solution)/shard_map/ppermute | solution.py:215
  5.3 4.4 %collective-permute-start = (bf16[2,1,15,16,384]{4,3,2,1,0:T(8,128)(2,1)S(1)}, bf16[2,1,15,16,384]{4,3,2,1,0:T(8,128)(2,1)S(1)}, u32[]{:S(2)}, u32[]{:S(2)}) collective-permute-start(bf16[2,1,15,16,384]{4,3,2,1,0:T(8,128)(2,1)S(1)} %get-tuple-element.38), channel_id=1, source_target_pairs={{0,3},{1,0},{2,1},{3,2},{4,7},{5,4},{6,5},{7,6},{8,11},{9,8},{10,9... | collective-permute-start | bytes 1105928 | tf_op jit(solution)/shard_map/ppermute | solution.py:220
  9.7 1.3 %collective-permute-start.1 = (bf16[2,1,15,16,384]{4,3,2,1,0:T(8,128)(2,1)S(1)}, bf16[2,1,15,16,384]{4,3,2,1,0:T(8,128)(2,1)S(1)}, u32[]{:S(2)}, u32[]{:S(2)}) collective-permute-start(bf16[2,1,15,16,384]{4,3,2,1,0:T(8,128)(2,1)S(1)} %get-tuple-element.39), channel_id=1, source_target_pairs={{1,5},{3,7},{4,0},{5,9},{6,2},{7,11},{8,4},{9,13},{10,6},{11,15},{... | collective-permute-start | bytes 1105928 | tf_op jit(solution)/shard_map/ppermute | solution.py:215
  11.0 4.8 %collective-permute-start.2 = (bf16[2,1,15,16,384]{4,3,2,1,0:T(8,128)(2,1)S(1)}, bf16[2,1,15,16,384]{4,3,2,1,0:T(8,128)(2,1)S(1)}, u32[]{:S(2)}, u32[]{:S(2)}) collective-permute-start(bf16[2,1,15,16,384]{4,3,2,1,0:T(8,128)(2,1)S(1)} %get-tuple-element.40), channel_id=1, source_target_pairs={{2,5},{0,7},{5,0},{6,9},{7,2},{4,11},{9,4},{10,13},{11,6},{8,15},{... | collective-permute-start | bytes 1105928 | tf_op jit(solution)/shard_map/ppermute | solution.py:215
  15.8 3.7 %collective-permute-done.3 = bf16[2,1,15,32,384]{4,3,2,1,0:T(8,128)(2,1)S(1)} collective-permute-done((bf16[2,1,15,32,384]{4,3,2,1,0:T(8,128)(2,1)}, bf16[2,1,15,32,384]{4,3,2,1,0:T(8,128)(2,1)S(1)}, u32[]{:S(2)}, u32[]{:S(2)}) %collective-permute-start.3) | collective-permute-done | bytes 737312 | tf_op jit(solution)/shard_map/ppermute | solution.py:215
  19.6 25.8 %shard_map.78 = (bf16[480,384]{1,0:T(8,128)(2,1)S(1)}, bf16[480,384]{1,0:T(8,128)(2,1)}, f32[384,1152]{1,0:T(8,128)S(1)}, f32[384,384]{1,0:T(8,128)S(1)}) custom-call(bf16[2,480,384]{2,1,0:T(8,128)(2,1)S(1)} %bitcast.28, bf16[2,480,384]{2,1,0:T(8,128)(2,1)S(1)} %bitcast.27, f32[384]{0:T(512)S(1)} %copy-done.6, bf16[384,1152]{1,0:T(8,128)(2,1)S(1)} %copy-done.2, ...), custom_call_target="tpu_custom_call" | custom-call | flops 7644119040 | bytes 8388608 | tf_op jit(solution)/shard_map/pallas_call | solution.py:168
  45.4 26.2 %shard_map.79 = (bf16[240,384]{1,0:T(8,128)(2,1)S(1)}, bf16[240,384]{1,0:T(8,128)(2,1)S(1)}, bf16[240,384]{1,0:T(8,128)(2,1)S(1)}, bf16[240,384]{1,0:T(8,128)(2,...) custom-call(bf16[2,240,384]{2,1,0:T(8,128)(2,1)S(1)} %bitcast.29, bf16[2,240,384]{2,1,0:T(8,128)(2,1)S(1)} %bitcast.30, ...), custom_call_target="tpu_custom_call" | custom-call | flops 7644119040 | bytes 8388608 | tf_op jit(solution)/shard_map/pallas_call | solution.py:168
  71.6 0.7 copy-done.4
  72.3 0.7 copy-done.5
  73.0 2.3 %collective-permute-done.4 = bf16[8,96,384]{2,1,0:T(8,128)(2,1)} collective-permute-done((bf16[8,96,384]{2,1,0:T(8,128)(2,1)}, bf16[8,96,384]{2,1,0:T(8,128)(2,1)}, u32[]{:S(2)}, u32[]{:S(2)}) %collective-permute-start.4) | collective-permute-done | bytes 589856 | tf_op jit(solution)/shard_map/ppermute | solution.py:199
  75.3 1.2 %convert_add_fusion = f32[8,96,384]{2,1,0:T(8,128)S(1)} fusion(f32[8,96,384]{2,1,0:T(8,128)S(1)} %get-tuple-element.49, bf16[8,96,384]{2,1,0:T(8,128)(2,1)} %collective-permute-done.4), kind=kLoop, calls=%fused_computation.1 | loop fusion | flops 589824 | bytes 2949120 | tf_op jit(solution)/shard_map/add | solution.py:327
  76.5 1.0 copy-done.7
  77.5 2.5 %collective-permute-start.5 = (bf16[4,1,96,384]{3,2,0,1:T(8,128)(2,1)S(1)}, bf16[4,1,96,384]{3,2,0,1:T(8,128)(2,1)S(1)}, u32[]{:S(2)}, u32[]{:S(2)}) collective-permute-start(bf16[4,1,96,384]{3,2,0,1:T(8,128)(2,1)S(1)} %dynamic-slice_convert_fusion), channel_id=1, source_target_pairs={{0,2},{1,3},{2,0},{3,1},{4,6},{5,7},{6,4},{7,5},{8,10},{9,11},{10,... | collective-permute-start | bytes 884744 | tf_op jit(solution)/shard_map/ppermute | solution.py:199
  80.0 3.7 %collective-permute-start.6 = (bf16[15,32,384]{2,1,0:T(8,128)(2,1)}, bf16[15,32,384]{2,1,0:T(8,128)(2,1)S(1)}, u32[]{:S(2)}, u32[]{:S(2)}) collective-permute-start(bf16[15,32,384]{2,1,0:T(8,128)(2,1)} %bitcast.6), channel_id=1, source_target_pairs={{5,1},{7,3},{0,4},{9,5},{2,6},{11,7},{4,8},{13,9},{6,10},{15,11},{... | collective-permute-start | bytes 1105928 | tf_op jit(solution)/shard_map/ppermute | solution.py:215
  83.7 3.5 %collective-permute-start.7 = (bf16[15,16,384]{2,1,0:T(8,128)(2,1)}, bf16[15,16,384]{2,1,0:T(8,128)(2,1)S(1)}, u32[]{:S(2)}, u32[]{:S(2)}) collective-permute-start(bf16[15,16,384]{2,1,0:T(8,128)(2,1)} %bitcast.35), channel_id=1, source_target_pairs={{5,1},{7,3},{0,4},{9,5},{2,6},{11,7},{4,8},{13,9},{6,10},{15,11},{... | collective-permute-start | bytes 552968 | tf_op jit(solution)/shard_map/ppermute | solution.py:215
  87.3 1.9 %collective-permute-start.9 = (bf16[15,16,384]{2,1,0:T(8,128)(2,1)}, bf16[15,16,384]{2,1,0:T(8,128)(2,1)S(1)}, u32[]{:S(2)}, u32[]{:S(2)}) collective-permute-start(bf16[15,16,384]{2,1,0:T(8,128)(2,1)} %bitcast.34), channel_id=1, source_target_pairs={{5,2},{7,0},{0,5},{9,6},{2,7},{11,4},{4,9},{13,10},{6,11},{15,8},{... | collective-permute-start | bytes 552968 | tf_op jit(solution)/shard_map/ppermute | solution.py:215
  89.2 1.1 %add_bitcast_fusion = f32[4,96,384]{2,1,0:T(8,128)S(1)} fusion(bf16[4,1,96,384]{3,2,0,1:T(8,128)(2,1)S(1)} %collective-permute-done.5, s32[]{:T(128)S(6)} %select_n.94, f32[4,2,96,384]{3,2,1,0:T(8,128)} %bitcast.37), kind=kLoop, calls=%fused_computation.4 | loop fusion | flops 294912 | bytes 1474564 | tf_op jit(solution)/shard_map/reshape | solution.py:333
  91.1 1.6 %collective-permute-start.8 = (bf16[4,96,192]{2,1,0:T(8,128)(2,1)S(1)}, bf16[4,96,192]{2,1,0:T(8,128)(2,1)S(1)}, u32[]{:S(2)}, u32[]{:S(2)}) collective-permute-start(bf16[4,96,192]{2,1,0:T(8,128)(2,1)S(1)} %dynamic-slice_convert_fusion.1), channel_id=1, source_target_pairs={{0,16},{16,0},{1,17},{17,1},{2,18},{18,2},{3,19},{19,3},{4,20},{20... | collective-permute-start | bytes 442376 | tf_op jit(solution)/shard_map/ppermute | solution.py:199
  92.8 4.5 %collective-permute-done.8 = bf16[4,96,192]{2,1,0:T(8,128)(2,1)S(1)} collective-permute-done((bf16[4,96,192]{2,1,0:T(8,128)(2,1)S(1)}, bf16[4,96,192]{2,1,0:T(8,128)(2,1)S(1)}, u32[]{:S(2)}, u32[]{:S(2)}) %collective-permute-start.8) | collective-permute-done | bytes 147488 | tf_op jit(solution)/shard_map/ppermute | solution.py:199
  97.6 2.4 %collective-permute-start.11 = (bf16[1,96,192]{2,1,0:T(8,128)(2,1)S(1)}, bf16[1,96,192]{2,1,0:T(8,128)(2,1)S(1)}, u32[]{:S(2)}, u32[]{:S(2)}) collective-permute-start(bf16[1,96,192]{2,1,0:T(8,128)(2,1)S(1)} %get-tuple-element.69), channel_id=1, source_target_pairs={{0,4},{4,8},{8,12},{12,0},{1,5},{5,9},{9,13},{13,1},{2,6},{6,10},{... | collective-permute-start | bytes 110600 | tf_op jit(solution)/shard_map/ppermute | solution.py:199
  100.0 1.1 %collective-permute-start.12 = (bf16[1,96,192]{2,1,0:T(8,128)(2,1)S(1)}, bf16[1,96,192]{2,1,0:T(8,128)(2,1)S(1)}, u32[]{:S(2)}, u32[]{:S(2)}) collective-permute-start(bf16[1,96,192]{2,1,0:T(8,128)(2,1)S(1)} %get-tuple-element.71), channel_id=1, source_target_pairs={{0,8},{4,12},{8,0},{12,4},{1,9},{5,13},{9,1},{13,5},{2,10},{6,14},... | collective-permute-start | bytes 110600 | tf_op jit(solution)/shard_map/ppermute | solution.py:199
  101.2 2.8 %collective-permute-start.13 = (bf16[1,96,192]{2,1,0:T(8,128)(2,1)S(1)}, bf16[1,96,192]{2,1,0:T(8,128)(2,1)S(1)}, u32[]{:S(2)}, u32[]{:S(2)}) collective-permute-start(bf16[1,96,192]{2,1,0:T(8,128)(2,1)S(1)} %get-tuple-element.70), channel_id=1, source_target_pairs={{0,12},{4,0},{8,4},{12,8},{1,13},{5,1},{9,5},{13,9},{2,14},{6,2},{... | collective-permute-start | bytes 110600 | tf_op jit(solution)/shard_map/ppermute | solution.py:199
  104.1 1.9 %add_convert_fusion = bf16[1,30,60,384]{3,2,1,0:T(8,128)(2,1)} fusion(bf16[1,30,60,384]{3,2,1,0:T(8,128)(2,1)S(1)} %copy-done, bf16[1,30,15,384]{3,2,1,0:T(8,128)(2,1)S(1)} %get-tuple-element.76, bf16[1,30,30,384]{3,2,1,0:T(8,128)(2,1)S(1)} %fusion, bf16[1,30,15,384]{3,2,1,0:T(8,128)(2,1)S(1)} %get-tuple-element.77), kind=kLoop, calls=%fused_computation | loop fusion | flops 6220800 | bytes 4147200 | tf_op jit(solution)/shard_map/convert_element_type | solution.py:420
  (39 shorter events, 3.4 us)
Async XLA Ops:
  0.6 4.0 %copy-start.1 = (bf16[1,30,60,384]{3,2,1,0:T(8,128)(2,1)S(1)}, bf16[1,30,60,384]{3,2,1,0:T(8,128)(2,1)}, u32[]{:S(2)}) copy-start(bf16[1,30,60,384]{3,2,1,0:T(8,128)(2,1)} %hid_ref.2) | copy-start | bytes 4147204
  0.6 4.0 %copy-start = (bf16[1,30,60,384]{3,2,1,0:T(8,128)(2,1)S(1)}, bf16[1,30,60,384]{3,2,1,0:T(8,128)(2,1)}, u32[]{:S(2)}) copy-start(bf16[1,30,60,384]{3,2,1,0:T(8,128)(2,1)} %cot_ref.2) | copy-start | bytes 4147204
  3.1 16.4 %copy-start.2 = (bf16[384,1152]{1,0:T(8,128)(2,1)S(1)}, bf16[384,1152]{1,0:T(8,128)(2,1)}, u32[]{:S(2)}) copy-start(bf16[384,1152]{1,0:T(8,128)(2,1)} %refs_5_.1) | copy-start | bytes 2654212
  3.2 16.4 %copy-start.3 = (bf16[384,384]{1,0:T(8,128)(2,1)S(1)}, bf16[384,384]{1,0:T(8,128)(2,1)}, u32[]{:S(2)}) copy-start(bf16[384,384]{1,0:T(8,128)(2,1)} %refs_6_.1) | copy-start | bytes 884740
  3.2 16.4 %copy-start.6 = (f32[384]{0:T(512)S(1)}, f32[384]{0:T(512)}, u32[]{:S(2)}) copy-start(f32[384]{0:T(512)} %refs_4_.3) | copy-start | bytes 4612
  3.2 16.4 %collective-permute-start.3 = (bf16[2,1,15,32,384]{4,3,2,1,0:T(8,128)(2,1)}, bf16[2,1,15,32,384]{4,3,2,1,0:T(8,128)(2,1)S(1)}, u32[]{:S(2)}, u32[]{:S(2)}) collective-permute-start(bf16[2,1,15,32,384]{4,3,2,1,0:T(8,128)(2,1)} %shard_map.76), channel_id=1, source_target_pairs={{1,5},{3,7},{4,0},{5,9},{6,2},{7,11},{8,4},{9,13},{10,6},{11,15},{... | collective-permute-start | bytes 2211848 | tf_op jit(solution)/shard_map/ppermute | solution.py:215
  5.3 40.1 %collective-permute-start = (bf16[2,1,15,16,384]{4,3,2,1,0:T(8,128)(2,1)S(1)}, bf16[2,1,15,16,384]{4,3,2,1,0:T(8,128)(2,1)S(1)}, u32[]{:S(2)}, u32[]{:S(2)}) collective-permute-start(bf16[2,1,15,16,384]{4,3,2,1,0:T(8,128)(2,1)S(1)} %get-tuple-element.38), channel_id=1, source_target_pairs={{0,3},{1,0},{2,1},{3,2},{4,7},{5,4},{6,5},{7,6},{8,11},{9,8},{10,9... | collective-permute-start | bytes 1105928 | tf_op jit(solution)/shard_map/ppermute | solution.py:220
  9.7 35.7 %collective-permute-start.1 = (bf16[2,1,15,16,384]{4,3,2,1,0:T(8,128)(2,1)S(1)}, bf16[2,1,15,16,384]{4,3,2,1,0:T(8,128)(2,1)S(1)}, u32[]{:S(2)}, u32[]{:S(2)}) collective-permute-start(bf16[2,1,15,16,384]{4,3,2,1,0:T(8,128)(2,1)S(1)} %get-tuple-element.39), channel_id=1, source_target_pairs={{1,5},{3,7},{4,0},{5,9},{6,2},{7,11},{8,4},{9,13},{10,6},{11,15},{... | collective-permute-start | bytes 1105928 | tf_op jit(solution)/shard_map/ppermute | solution.py:215
  11.0 34.4 %collective-permute-start.2 = (bf16[2,1,15,16,384]{4,3,2,1,0:T(8,128)(2,1)S(1)}, bf16[2,1,15,16,384]{4,3,2,1,0:T(8,128)(2,1)S(1)}, u32[]{:S(2)}, u32[]{:S(2)}) collective-permute-start(bf16[2,1,15,16,384]{4,3,2,1,0:T(8,128)(2,1)S(1)} %get-tuple-element.40), channel_id=1, source_target_pairs={{2,5},{0,7},{5,0},{6,9},{7,2},{4,11},{9,4},{10,13},{11,6},{8,15},{... | collective-permute-start | bytes 1105928 | tf_op jit(solution)/shard_map/ppermute | solution.py:215
  71.6 0.7 copy-start.4
  72.3 0.7 copy-start.5
  73.0 2.3 %collective-permute-start.4 = (bf16[8,96,384]{2,1,0:T(8,128)(2,1)}, bf16[8,96,384]{2,1,0:T(8,128)(2,1)}, u32[]{:S(2)}, u32[]{:S(2)}) collective-permute-start(bf16[8,96,384]{2,1,0:T(8,128)(2,1)} %get-tuple-element.50), channel_id=1, source_target_pairs={{0,1},{1,0},{2,3},{3,2},{4,5},{5,4},{6,7},{7,6},{8,9},{9,8},{10,11... | collective-permute-start | bytes 1769480 | tf_op jit(solution)/shard_map/ppermute | solution.py:199
  76.5 1.0 copy-start.7
  77.5 11.7 %collective-permute-start.5 = (bf16[4,1,96,384]{3,2,0,1:T(8,128)(2,1)S(1)}, bf16[4,1,96,384]{3,2,0,1:T(8,128)(2,1)S(1)}, u32[]{:S(2)}, u32[]{:S(2)}) collective-permute-start(bf16[4,1,96,384]{3,2,0,1:T(8,128)(2,1)S(1)} %dynamic-slice_convert_fusion), channel_id=1, source_target_pairs={{0,2},{1,3},{2,0},{3,1},{4,6},{5,7},{6,4},{7,5},{8,10},{9,11},{10,... | collective-permute-start | bytes 884744 | tf_op jit(solution)/shard_map/ppermute | solution.py:199
  80.0 10.9 %collective-permute-start.6 = (bf16[15,32,384]{2,1,0:T(8,128)(2,1)}, bf16[15,32,384]{2,1,0:T(8,128)(2,1)S(1)}, u32[]{:S(2)}, u32[]{:S(2)}) collective-permute-start(bf16[15,32,384]{2,1,0:T(8,128)(2,1)} %bitcast.6), channel_id=1, source_target_pairs={{5,1},{7,3},{0,4},{9,5},{2,6},{11,7},{4,8},{13,9},{6,10},{15,11},{... | collective-permute-start | bytes 1105928 | tf_op jit(solution)/shard_map/ppermute | solution.py:215
  83.7 7.2 %collective-permute-start.7 = (bf16[15,16,384]{2,1,0:T(8,128)(2,1)}, bf16[15,16,384]{2,1,0:T(8,128)(2,1)S(1)}, u32[]{:S(2)}, u32[]{:S(2)}) collective-permute-start(bf16[15,16,384]{2,1,0:T(8,128)(2,1)} %bitcast.35), channel_id=1, source_target_pairs={{5,1},{7,3},{0,4},{9,5},{2,6},{11,7},{4,8},{13,9},{6,10},{15,11},{... | collective-permute-start | bytes 552968 | tf_op jit(solution)/shard_map/ppermute | solution.py:215
  87.3 10.2 %collective-permute-start.9 = (bf16[15,16,384]{2,1,0:T(8,128)(2,1)}, bf16[15,16,384]{2,1,0:T(8,128)(2,1)S(1)}, u32[]{:S(2)}, u32[]{:S(2)}) collective-permute-start(bf16[15,16,384]{2,1,0:T(8,128)(2,1)} %bitcast.34), channel_id=1, source_target_pairs={{5,2},{7,0},{0,5},{9,6},{2,7},{11,4},{4,9},{13,10},{6,11},{15,8},{... | collective-permute-start | bytes 552968 | tf_op jit(solution)/shard_map/ppermute | solution.py:215
  91.1 6.2 %collective-permute-start.8 = (bf16[4,96,192]{2,1,0:T(8,128)(2,1)S(1)}, bf16[4,96,192]{2,1,0:T(8,128)(2,1)S(1)}, u32[]{:S(2)}, u32[]{:S(2)}) collective-permute-start(bf16[4,96,192]{2,1,0:T(8,128)(2,1)S(1)} %dynamic-slice_convert_fusion.1), channel_id=1, source_target_pairs={{0,16},{16,0},{1,17},{17,1},{2,18},{18,2},{3,19},{19,3},{4,20},{20... | collective-permute-start | bytes 442376 | tf_op jit(solution)/shard_map/ppermute | solution.py:199
  92.6 5.0 %collective-permute-start.10 = (bf16[15,16,384]{2,1,0:T(8,128)(2,1)S(1)}, bf16[15,16,384]{2,1,0:T(8,128)(2,1)S(1)}, u32[]{:S(2)}, u32[]{:S(2)}) collective-permute-start(bf16[15,16,384]{2,1,0:T(8,128)(2,1)S(1)} %bitcast.33), channel_id=1, source_target_pairs={{0,1},{1,2},{2,3},{3,0},{4,5},{5,6},{6,7},{7,4},{8,9},{9,10},{10,1... | collective-permute-start | bytes 552968 | tf_op jit(solution)/shard_map/ppermute | solution.py:220
  97.6 8.4 %collective-permute-start.11 = (bf16[1,96,192]{2,1,0:T(8,128)(2,1)S(1)}, bf16[1,96,192]{2,1,0:T(8,128)(2,1)S(1)}, u32[]{:S(2)}, u32[]{:S(2)}) collective-permute-start(bf16[1,96,192]{2,1,0:T(8,128)(2,1)S(1)} %get-tuple-element.69), channel_id=1, source_target_pairs={{0,4},{4,8},{8,12},{12,0},{1,5},{5,9},{9,13},{13,1},{2,6},{6,10},{... | collective-permute-start | bytes 110600 | tf_op jit(solution)/shard_map/ppermute | solution.py:199
  100.0 6.0 %collective-permute-start.12 = (bf16[1,96,192]{2,1,0:T(8,128)(2,1)S(1)}, bf16[1,96,192]{2,1,0:T(8,128)(2,1)S(1)}, u32[]{:S(2)}, u32[]{:S(2)}) collective-permute-start(bf16[1,96,192]{2,1,0:T(8,128)(2,1)S(1)} %get-tuple-element.71), channel_id=1, source_target_pairs={{0,8},{4,12},{8,0},{12,4},{1,9},{5,13},{9,1},{13,5},{2,10},{6,14},... | collective-permute-start | bytes 110600 | tf_op jit(solution)/shard_map/ppermute | solution.py:199
  101.2 4.9 %collective-permute-start.13 = (bf16[1,96,192]{2,1,0:T(8,128)(2,1)S(1)}, bf16[1,96,192]{2,1,0:T(8,128)(2,1)S(1)}, u32[]{:S(2)}, u32[]{:S(2)}) collective-permute-start(bf16[1,96,192]{2,1,0:T(8,128)(2,1)S(1)} %get-tuple-element.70), channel_id=1, source_target_pairs={{0,12},{4,0},{8,4},{12,8},{1,13},{5,1},{9,5},{13,9},{2,14},{6,2},{... | collective-permute-start | bytes 110600 | tf_op jit(solution)/shard_map/ppermute | solution.py:199

commit v10 on v6

--- a/solution.py
+++ b/solution.py
@@ -132,10 +132,13 @@
         for i in range(parts):
             joined[i, :dq_rows] = gqT[i * dq_rows:(i + 1) * dq_rows]
             joined[i, dq_rows:] = gpT[i * dp_rows:(i + 1) * dp_rows]
-        me = odd
-        for i in range(parts // 2):
-            gq_ref[i] = joined[2 * i + me]
-            gp_ref[i] = joined[2 * i + 1 - me].astype(BF)
+        lats, lons = lax.axis_size("lat"), lax.axis_size("lon")
+        own_lon, own_lat = lax.axis_index("lon") // 2, lax.axis_index("lat")
+        for p in range(lons // 2):
+            for step in range(lats):
+                source = lax.rem(own_lat + step, lats) * lons + 2 * (own_lon ^ p)
+                gq_ref[p * lats + step] = joined[source + odd]
+                gp_ref[p * lats + step] = joined[source + 1 - odd].astype(BF)
     dn = mm_t(dqkv[...], wqkv_ref[...]) * gain
     normed = cen * rstd
     d = rstd * (dn - jnp.mean(dn, axis=1, keepdims=True) - normed * jnp.mean(dn * normed, axis=1, keepdims=True))
@@ -253,33 +256,12 @@
     return list(outs)
 
 
-def scatter_direct(value, axis, dim):
-    count = lax.axis_size(axis)
-    me = lax.axis_index(axis)
-    share = value.shape[dim] // count
-    total = lax.dynamic_slice_in_dim(value, me * share, share, dim).astype(F32)
-    for step in range(1, count):
-        goal = (me + step) % count
-        part = lax.dynamic_slice_in_dim(value, goal * share, share, dim).astype(BF)
-        got = permuted(part, (axis,), lambda i, s=step: ((i + s) % count,))
-        total = total + got.astype(F32)
-    return total
-
-
-def scatter_bit(value, axis, bit, dim):
-    me = (lax.axis_index(axis) // bit) % 2
-    mine = lax.dynamic_index_in_dim(value, me, dim, keepdims=False).astype(F32)
-    other = lax.dynamic_index_in_dim(value, 1 - me, dim, keepdims=False).astype(BF)
-    got = permuted(other, (axis,), lambda i: (i ^ bit,))
-    return mine + got.astype(F32)
-
-
 def reduce_weights(keep, send, lons, returns):
-    half, deep, width = keep.shape
-    lats = lax.axis_size("lat")
+    _, _, width = keep.shape
+    lats, dps = lax.axis_size("lat"), lax.axis_size("dp")
     moved, waiting = [], list(returns)
 
-    def release(value, count=1):
+    def release(value, count):
         for _ in range(min(count, len(waiting))):
             held, move = waiting.pop(0)
             value, held = lax.optimization_barrier((value, held))
@@ -289,16 +271,33 @@
     got = permuted(send, ("lon",), lambda i: (i ^ 1,))
     keep = release(keep, len(waiting) // 2)
     early = len(moved)
-    total = release((keep + got.astype(F32)).reshape(lats, lons // 2, deep, width), len(waiting))
-    bit, left = 2, lons // 2
-    while left > 1:
-        total = scatter_bit(total.reshape(lats, left // 2, 2, deep, width), "lon", bit, 2)
-        left //= 2
-        bit *= 2
-    total, moved[:early] = lax.optimization_barrier((total.reshape(lats, deep, width), moved[:early]))
-    total = scatter_direct(total, "dp", 2)
-    total, moved[early:] = lax.optimization_barrier((total, moved[early:]))
-    return scatter_direct(total, "lat", 0)[0], moved
+    got = release(got, len(waiting))
+    total = [keep[i * lats:(i + 1) * lats] + got[i * lats:(i + 1) * lats].astype(F32) for i in range(lons // 2)]
+    while len(total) > 1:
+        left = len(total) // 2
+        payload = jnp.concatenate(total[left:], axis=0).astype(BF)
+        got = permuted(payload, ("lon",), lambda i, bit=2 * left: (i ^ bit,))
+        if left == 1:
+            got, moved[:early] = lax.optimization_barrier((got, moved[:early]))
+        total = [total[i] + got[i * lats:(i + 1) * lats].astype(F32) for i in range(left)]
+    total = total[0]
+
+    share = width // dps
+    me, mine = lax.axis_index("dp"), None
+    for step in range(1, dps):
+        part = lax.dynamic_slice_in_dim(total, ((me + step) % dps) * share, share, 2).astype(BF)
+        got = permuted(part, ("dp",), lambda i, step=step: ((i + step) % dps,))
+        if step == dps - 1:
+            got, moved[early:] = lax.optimization_barrier((got, moved[early:]))
+        mine = got.astype(F32) if mine is None else mine + got.astype(F32)
+    own = lax.dynamic_slice_in_dim(total, me * share, share, 2)
+    total = own if mine is None else own + mine
+
+    mine = total[0]
+    for step in range(1, lats):
+        got = permuted(total[step].astype(BF), ("lat",), lambda i, step=step: ((i + step) % lats,))
+        mine = mine + got.astype(F32)
+    return mine, moved
 
 
 def per_device(hidden_in, grad_out, norm_gain, w_qkv, w_proj):
@@ -387,9 +386,8 @@
         lax.axis_size("dp") * samples * lat_rows * lax.axis_size("lat") * lon_cols * lons
     )
     factor = float(total_cells) ** (-0.5)
-    total = total.T * factor
     cut = 3 * width // parts
-    return (grad_in, total[:, :cut], total[:, cut:])
+    return (grad_in, total[:cut].T * factor, total[cut:].T * factor)
 
 
 def solution(mesh):

time: 104 us -> 102 us (0.981)
  waiting for transfers between devices: 10.3 us -> 6.44 us
  local copies, waits for them, and re-layouts: 5.16 us -> 2.91 us
  starting transfers between devices: 31.2 us -> 33.3 us
  other arithmetic: 4.7 us -> 6.41 us
    ppermute x6, waiting for transfers between devices: 6.65 us -> 1.15 us  [permuted(): return lax.ppermute(value, tuple(axes), pairs)]
    select_n x3, other arithmetic: 0.16 us -> 2.07 us  [stacked(): above = jnp.where(upper, own, back)]
    ppermute x6, waiting for transfers between devices: 3.6 us -> 5.29 us  [shared(): return lax.ppermute(value, ('lat', 'lon'), pairs)]
    ppermute x6, starting transfers between devices: 10.1 us -> 11.8 us  [permuted(): return lax.ppermute(value, tuple(axes), pairs)]
    slice x2 -> x0, local copies, waits for them, and re-layouts: 1.25 us -> none  [per_device(): return (grad_in, total[:, :cut], total[:, cut:])]
    add x2, other arithmetic: 1.34 us -> 0.1 us  [the longest x1 0.08 us: reduce_weights(): total[i] + got[i * lats:(i + 1) * lats].astype(F32)]
    mul x1 -> x2, other arithmetic: 0.03 us -> 1.25 us  [per_device(): return (grad_in, total[:cut].T * factor, total[cut:].T * factor)]
    reshape x1 -> x0, other arithmetic: 1.14 us -> none  [reduce_weights(): total.reshape(lats, deep, width)]
  transfers between devices with their start and end apart: 14 -> 14, of which waited for: 4 -> 5; matrix products, arithmetic and copies ran while one was open for 3% -> 5% of each run, Pallas kernels for 25% -> 25%
where the time goes in v10:
time: 102 us; the launch traced here: 101 us
  Pallas kernels  51.3 us (50%)
  starting transfers between devices  33.3 us (33%)
  waiting for transfers between devices  6.44 us (6%)
  other arithmetic  6.41 us (6%)
  local copies, waits for them, and re-layouts  2.91 us (3%)
    pallas_call x2, Pallas kernels, window_call(): pl.pallas_call(functools.partial(window_kernel, head, metas, (prev is not...  50.5 us
    ppermute x6, starting transfers between devices, shared(): return lax.ppermute(value, ('lat', 'lon'), pairs)  17.1 us
    ppermute x6, starting transfers between devices, permuted(): return lax.ppermute(value, tuple(axes), pairs)  11.8 us
    ppermute x6, waiting for transfers between devices, shared(): return lax.ppermute(value, ('lat', 'lon'), pairs)  5.29 us
    ppermute x2, starting transfers between devices, along_lon(): lax.ppermute(value, 'lon', [(j, (j + step) % count) for j in range(count)])  4.42 us
    unnamed x12, local copies, waits for them, and re-layouts  2.77 us
    select_n x3, other arithmetic, stacked(): above = jnp.where(upper, own, back)  2.07 us
  transfers between devices with their start and end apart: 14, of which 5 were waited for; matrix products, arithmetic and copies ran while one was open for 5% of the time, Pallas kernels for 25%

profile of v10, /device:TPU:0, one launch (start us, length us, event | category | flops | bytes accessed | tf_op | source)
XLA Modules:
  0.0 101.3 jit_solution(13481635658370025294)
XLA Ops:
  0.6 1.4 %copy-done = bf16[1,30,60,384]{3,2,1,0:T(8,128)(2,1)S(1)} copy-done((bf16[1,30,60,384]{3,2,1,0:T(8,128)(2,1)S(1)}, bf16[1,30,60,384]{3,2,1,0:T(8,128)(2,1)}, u32[]{:S(2)}) %copy-start) | copy-done | bytes 1382424
  2.0 1.4 %copy-done.2 = bf16[1,30,60,384]{3,2,1,0:T(8,128)(2,1)S(1)} copy-done((bf16[1,30,60,384]{3,2,1,0:T(8,128)(2,1)S(1)}, bf16[1,30,60,384]{3,2,1,0:T(8,128)(2,1)}, u32[]{:S(2)}) %copy-start.2) | copy-done | bytes 1382424
  3.6 1.4 %collective-permute-start.3 = (bf16[2,1,15,32,384]{4,3,2,1,0:T(8,128)(2,1)S(1)}, bf16[2,1,15,32,384]{4,3,2,1,0:T(8,128)(2,1)S(1)}, u32[]{:S(2)}, u32[]{:S(2)}) collective-permute-start(bf16[2,1,15,32,384]{4,3,2,1,0:T(8,128)(2,1)S(1)} %shard_map.76), channel_id=1, source_target_pairs={{1,5},{3,7},{4,0},{5,9},{6,2},{7,11},{8,4},{9,13},{10,6},{11,15},{... | collective-permute-start | bytes 2211848 | tf_op jit(solution)/shard_map/ppermute | solution.py:218
  5.1 0.7 shard_map.77
  5.7 4.4 %collective-permute-start = (bf16[2,1,15,16,384]{4,3,2,1,0:T(8,128)(2,1)S(1)}, bf16[2,1,15,16,384]{4,3,2,1,0:T(8,128)(2,1)S(1)}, u32[]{:S(2)}, u32[]{:S(2)}) collective-permute-start(bf16[2,1,15,16,384]{4,3,2,1,0:T(8,128)(2,1)S(1)} %get-tuple-element.38), channel_id=1, source_target_pairs={{0,3},{1,0},{2,1},{3,2},{4,7},{5,4},{6,5},{7,6},{8,11},{9,8},{10,9... | collective-permute-start | bytes 1105928 | tf_op jit(solution)/shard_map/ppermute | solution.py:223
  10.2 1.3 %collective-permute-start.1 = (bf16[2,1,15,16,384]{4,3,2,1,0:T(8,128)(2,1)S(1)}, bf16[2,1,15,16,384]{4,3,2,1,0:T(8,128)(2,1)S(1)}, u32[]{:S(2)}, u32[]{:S(2)}) collective-permute-start(bf16[2,1,15,16,384]{4,3,2,1,0:T(8,128)(2,1)S(1)} %get-tuple-element.39), channel_id=1, source_target_pairs={{1,5},{3,7},{4,0},{5,9},{6,2},{7,11},{8,4},{9,13},{10,6},{11,15},{... | collective-permute-start | bytes 1105928 | tf_op jit(solution)/shard_map/ppermute | solution.py:218
  11.4 4.8 %collective-permute-start.2 = (bf16[2,1,15,16,384]{4,3,2,1,0:T(8,128)(2,1)S(1)}, bf16[2,1,15,16,384]{4,3,2,1,0:T(8,128)(2,1)S(1)}, u32[]{:S(2)}, u32[]{:S(2)}) collective-permute-start(bf16[2,1,15,16,384]{4,3,2,1,0:T(8,128)(2,1)S(1)} %get-tuple-element.40), channel_id=1, source_target_pairs={{2,5},{0,7},{5,0},{6,9},{7,2},{4,11},{9,4},{10,13},{11,6},{8,15},{... | collective-permute-start | bytes 1105928 | tf_op jit(solution)/shard_map/ppermute | solution.py:218
  16.3 3.4 %collective-permute-done.3 = bf16[2,1,15,32,384]{4,3,2,1,0:T(8,128)(2,1)S(1)} collective-permute-done((bf16[2,1,15,32,384]{4,3,2,1,0:T(8,128)(2,1)S(1)}, bf16[2,1,15,32,384]{4,3,2,1,0:T(8,128)(2,1)S(1)}, u32[]{:S(2)}, u32[]{:S(2)}) %collective-permute-start.3) | collective-permute-done | bytes 737312 | tf_op jit(solution)/shard_map/ppermute | solution.py:218
  19.7 25.0 %shard_map.78 = (bf16[480,384]{1,0:T(8,128)(2,1)S(1)}, bf16[480,384]{1,0:T(8,128)(2,1)S(1)}, f32[384,1152]{1,0:T(8,128)S(1)}, f32[384,384]{1,0:T(8,128)S(1)}) custom-call(bf16[2,480,384]{2,1,0:T(8,128)(2,1)S(1)} %bitcast.39, bf16[2,480,384]{2,1,0:T(8,128)(2,1)S(1)} %bitcast.38, f32[384]{0:T(512)S(1)} %copy-done.5, bf16[384,1152]{1,0:T(8,128)(2,1)S(1)} %copy-done.3, ...), custom_call_target="tpu_custom_call" | custom-call | flops 7644119040 | bytes 8388608 | tf_op jit(solution)/shard_map/pallas_call | solution.py:171
  44.7 25.4 %shard_map.79 = (bf16[240,384]{1,0:T(8,128)(2,1)S(1)}, bf16[240,384]{1,0:T(8,128)(2,1)S(1)}, bf16[240,384]{1,0:T(8,128)(2,1)S(1)}, bf16[240,384]{1,0:T(8,128)(2,...) custom-call(bf16[2,240,384]{2,1,0:T(8,128)(2,1)S(1)} %bitcast.41, bf16[2,240,384]{2,1,0:T(8,128)(2,1)S(1)} %bitcast.42, ...), custom_call_target="tpu_custom_call" | custom-call | flops 7644119040 | bytes 8388608 | tf_op jit(solution)/shard_map/pallas_call | solution.py:171
  70.2 4.3 %collective-permute-start.6 = (bf16[15,32,384]{2,1,0:T(8,128)(2,1)S(1)}, bf16[15,32,384]{2,1,0:T(8,128)(2,1)}, u32[]{:S(2)}, u32[]{:S(2)}) collective-permute-start(bf16[15,32,384]{2,1,0:T(8,128)(2,1)S(1)} %bitcast.40), channel_id=1, source_target_pairs={{5,1},{7,3},{0,4},{9,5},{2,6},{11,7},{4,8},{13,9},{6,10},{15,11},{... | collective-permute-start | bytes 1105928 | tf_op jit(solution)/shard_map/ppermute | solution.py:218
  74.5 0.8 add_convert_fusion.1
  75.3 2.5 %collective-permute-start.5 = (bf16[4,96,384]{2,1,0:T(8,128)(2,1)}, bf16[4,96,384]{2,1,0:T(8,128)(2,1)S(1)}, u32[]{:S(2)}, u32[]{:S(2)}) collective-permute-start(bf16[4,96,384]{2,1,0:T(8,128)(2,1)} %add_convert_fusion.1), channel_id=1, source_target_pairs={{0,2},{1,3},{2,0},{3,1},{4,6},{5,7},{6,4},{7,5},{8,10},{9,11},{10,... | collective-permute-start | bytes 884744 | tf_op jit(solution)/shard_map/ppermute | solution.py:202
  77.8 3.5 %collective-permute-start.7 = (bf16[15,16,384]{2,1,0:T(8,128)(2,1)S(1)}, bf16[15,16,384]{2,1,0:T(8,128)(2,1)}, u32[]{:S(2)}, u32[]{:S(2)}) collective-permute-start(bf16[15,16,384]{2,1,0:T(8,128)(2,1)S(1)} %bitcast.47), channel_id=1, source_target_pairs={{5,1},{7,3},{0,4},{9,5},{2,6},{11,7},{4,8},{13,9},{6,10},{15,11},{... | collective-permute-start | bytes 552968 | tf_op jit(solution)/shard_map/ppermute | solution.py:218
  81.3 1.9 %collective-permute-start.9 = (bf16[15,16,384]{2,1,0:T(8,128)(2,1)S(1)}, bf16[15,16,384]{2,1,0:T(8,128)(2,1)S(1)}, u32[]{:S(2)}, u32[]{:S(2)}) collective-permute-start(bf16[15,16,384]{2,1,0:T(8,128)(2,1)S(1)} %bitcast.45), channel_id=1, source_target_pairs={{5,2},{7,0},{0,5},{9,6},{2,7},{11,4},{4,9},{13,10},{6,11},{15,8},{... | collective-permute-start | bytes 552968 | tf_op jit(solution)/shard_map/ppermute | solution.py:218
  83.9 1.6 %collective-permute-start.8 = (bf16[4,96,192]{2,1,0:T(8,128)(2,1)S(1)}, bf16[4,96,192]{2,1,0:T(8,128)(2,1)S(1)}, u32[]{:S(2)}, u32[]{:S(2)}) collective-permute-start(bf16[4,96,192]{2,1,0:T(8,128)(2,1)S(1)} %dynamic-slice_convert_fusion), channel_id=1, source_target_pairs={{0,16},{16,0},{1,17},{17,1},{2,18},{18,2},{3,19},{19,3},{4,20},{20... | collective-permute-start | bytes 442376 | tf_op jit(solution)/shard_map/ppermute | solution.py:202
  85.4 1.1 %broadcast_select_fusion.1 = (bf16[15,32,384]{2,1,0:T(8,128)(2,1)S(1)}, bf16[15,32,384]{2,1,0:T(8,128)(2,1)S(1)}) fusion(bf16[15,32,384]{2,1,0:T(8,128)(2,1)S(1)} %bitcast.36, bf16[15,32,384]{2,1,0:T(8,128)(2,1)} %collective-permute-done.6, pred[]{:T(512)S(6)} %eq.11), kind=kLoop, calls=%fused_computation.12 | loop fusion | flops 368640 | bytes 1474561 | tf_op jit(solution)/shard_map/jit(_where)/select_n | solution.py:367
  86.5 1.0 broadcast_select_fusion.3
  87.5 1.5 %collective-permute-done.9 = bf16[15,16,384]{2,1,0:T(8,128)(2,1)S(1)} collective-permute-done((bf16[15,16,384]{2,1,0:T(8,128)(2,1)S(1)}, bf16[15,16,384]{2,1,0:T(8,128)(2,1)S(1)}, u32[]{:S(2)}, u32[]{:S(2)}) %collective-permute-start.9) | collective-permute-done | bytes 184352 | tf_op jit(solution)/shard_map/ppermute | solution.py:218
  89.8 4.7 %collective-permute-start.11 = (bf16[96,192]{1,0:T(8,128)(2,1)S(1)}, bf16[96,192]{1,0:T(8,128)(2,1)S(1)}, u32[]{:S(2)}, u32[]{:S(2)}) collective-permute-start(bf16[96,192]{1,0:T(8,128)(2,1)S(1)} %get-tuple-element.75), channel_id=1, source_target_pairs={{0,4},{4,8},{8,12},{12,0},{1,5},{5,9},{9,13},{13,1},{2,6},{6,10},{... | collective-permute-start | bytes 110600 | tf_op jit(solution)/shard_map/ppermute | solution.py:202
  94.5 2.8 %collective-permute-start.13 = (bf16[96,192]{1,0:T(8,128)(2,1)S(1)}, bf16[96,192]{1,0:T(8,128)(2,1)S(1)}, u32[]{:S(2)}, u32[]{:S(2)}) collective-permute-start(bf16[96,192]{1,0:T(8,128)(2,1)S(1)} %get-tuple-element.76), channel_id=1, source_target_pairs={{0,12},{4,0},{8,4},{12,8},{1,13},{5,1},{9,5},{13,9},{2,14},{6,2},{... | collective-permute-start | bytes 110600 | tf_op jit(solution)/shard_map/ppermute | solution.py:202
  97.5 1.9 %add_convert_fusion = bf16[1,30,60,384]{3,2,1,0:T(8,128)(2,1)} fusion(bf16[1,30,60,384]{3,2,1,0:T(8,128)(2,1)S(1)} %copy-done.1, bf16[1,30,15,384]{3,2,1,0:T(8,128)(2,1)S(1)} %get-tuple-element.78, bf16[1,30,30,384]{3,2,1,0:T(8,128)(2,1)S(1)} %fusion, bf16[1,30,15,384]{3,2,1,0:T(8,128)(2,1)S(1)} %get-tuple-element.79), kind=kLoop, calls=%fused_computation | loop fusion | flops 6220800 | bytes 4147200 | tf_op jit(solution)/shard_map/convert_element_type | solution.py:384
  100.0 0.6 fusion.6
  100.7 0.6 fusion.7
  (34 shorter events, 2.6 us)
Async XLA Ops:
  0.6 1.4 %copy-start = (bf16[1,30,60,384]{3,2,1,0:T(8,128)(2,1)S(1)}, bf16[1,30,60,384]{3,2,1,0:T(8,128)(2,1)}, u32[]{:S(2)}) copy-start(bf16[1,30,60,384]{3,2,1,0:T(8,128)(2,1)} %cot_ref.2) | copy-start | bytes 4147204
  2.0 1.4 %copy-start.2 = (bf16[1,30,60,384]{3,2,1,0:T(8,128)(2,1)S(1)}, bf16[1,30,60,384]{3,2,1,0:T(8,128)(2,1)}, u32[]{:S(2)}) copy-start(bf16[1,30,60,384]{3,2,1,0:T(8,128)(2,1)} %hid_ref.2) | copy-start | bytes 4147204
  3.6 16.0 %copy-start.3 = (bf16[384,1152]{1,0:T(8,128)(2,1)S(1)}, bf16[384,1152]{1,0:T(8,128)(2,1)}, u32[]{:S(2)}) copy-start(bf16[384,1152]{1,0:T(8,128)(2,1)} %refs_5_.1) | copy-start | bytes 2654212
  3.6 16.0 %copy-start.4 = (bf16[384,384]{1,0:T(8,128)(2,1)S(1)}, bf16[384,384]{1,0:T(8,128)(2,1)}, u32[]{:S(2)}) copy-start(bf16[384,384]{1,0:T(8,128)(2,1)} %refs_6_.1) | copy-start | bytes 884740
  3.6 16.0 %copy-start.5 = (f32[384]{0:T(512)S(1)}, f32[384]{0:T(512)}, u32[]{:S(2)}) copy-start(f32[384]{0:T(512)} %refs_4_.3) | copy-start | bytes 4612
  3.6 16.0 %collective-permute-start.3 = (bf16[2,1,15,32,384]{4,3,2,1,0:T(8,128)(2,1)S(1)}, bf16[2,1,15,32,384]{4,3,2,1,0:T(8,128)(2,1)S(1)}, u32[]{:S(2)}, u32[]{:S(2)}) collective-permute-start(bf16[2,1,15,32,384]{4,3,2,1,0:T(8,128)(2,1)S(1)} %shard_map.76), channel_id=1, source_target_pairs={{1,5},{3,7},{4,0},{5,9},{6,2},{7,11},{8,4},{9,13},{10,6},{11,15},{... | collective-permute-start | bytes 2211848 | tf_op jit(solution)/shard_map/ppermute | solution.py:218
  5.7 39.0 %collective-permute-start = (bf16[2,1,15,16,384]{4,3,2,1,0:T(8,128)(2,1)S(1)}, bf16[2,1,15,16,384]{4,3,2,1,0:T(8,128)(2,1)S(1)}, u32[]{:S(2)}, u32[]{:S(2)}) collective-permute-start(bf16[2,1,15,16,384]{4,3,2,1,0:T(8,128)(2,1)S(1)} %get-tuple-element.38), channel_id=1, source_target_pairs={{0,3},{1,0},{2,1},{3,2},{4,7},{5,4},{6,5},{7,6},{8,11},{9,8},{10,9... | collective-permute-start | bytes 1105928 | tf_op jit(solution)/shard_map/ppermute | solution.py:223
  10.2 34.6 %collective-permute-start.1 = (bf16[2,1,15,16,384]{4,3,2,1,0:T(8,128)(2,1)S(1)}, bf16[2,1,15,16,384]{4,3,2,1,0:T(8,128)(2,1)S(1)}, u32[]{:S(2)}, u32[]{:S(2)}) collective-permute-start(bf16[2,1,15,16,384]{4,3,2,1,0:T(8,128)(2,1)S(1)} %get-tuple-element.39), channel_id=1, source_target_pairs={{1,5},{3,7},{4,0},{5,9},{6,2},{7,11},{8,4},{9,13},{10,6},{11,15},{... | collective-permute-start | bytes 1105928 | tf_op jit(solution)/shard_map/ppermute | solution.py:218
  11.4 33.3 %collective-permute-start.2 = (bf16[2,1,15,16,384]{4,3,2,1,0:T(8,128)(2,1)S(1)}, bf16[2,1,15,16,384]{4,3,2,1,0:T(8,128)(2,1)S(1)}, u32[]{:S(2)}, u32[]{:S(2)}) collective-permute-start(bf16[2,1,15,16,384]{4,3,2,1,0:T(8,128)(2,1)S(1)} %get-tuple-element.40), channel_id=1, source_target_pairs={{2,5},{0,7},{5,0},{6,9},{7,2},{4,11},{9,4},{10,13},{11,6},{8,15},{... | collective-permute-start | bytes 1105928 | tf_op jit(solution)/shard_map/ppermute | solution.py:218
  70.1 4.3 %collective-permute-start.4 = (bf16[8,96,384]{2,1,0:T(8,128)(2,1)S(1)}, bf16[8,96,384]{2,1,0:T(8,128)(2,1)S(1)}, u32[]{:S(2)}, u32[]{:S(2)}) collective-permute-start(bf16[8,96,384]{2,1,0:T(8,128)(2,1)S(1)} %get-tuple-element.50), channel_id=1, source_target_pairs={{0,1},{1,0},{2,3},{3,2},{4,5},{5,4},{6,7},{7,6},{8,9},{9,8},{10,11... | collective-permute-start | bytes 1769480 | tf_op jit(solution)/shard_map/ppermute | solution.py:202
  70.2 13.4 %collective-permute-start.6 = (bf16[15,32,384]{2,1,0:T(8,128)(2,1)S(1)}, bf16[15,32,384]{2,1,0:T(8,128)(2,1)}, u32[]{:S(2)}, u32[]{:S(2)}) collective-permute-start(bf16[15,32,384]{2,1,0:T(8,128)(2,1)S(1)} %bitcast.40), channel_id=1, source_target_pairs={{5,1},{7,3},{0,4},{9,5},{2,6},{11,7},{4,8},{13,9},{6,10},{15,11},{... | collective-permute-start | bytes 1105928 | tf_op jit(solution)/shard_map/ppermute | solution.py:218
  75.3 8.4 %collective-permute-start.5 = (bf16[4,96,384]{2,1,0:T(8,128)(2,1)}, bf16[4,96,384]{2,1,0:T(8,128)(2,1)S(1)}, u32[]{:S(2)}, u32[]{:S(2)}) collective-permute-start(bf16[4,96,384]{2,1,0:T(8,128)(2,1)} %add_convert_fusion.1), channel_id=1, source_target_pairs={{0,2},{1,3},{2,0},{3,1},{4,6},{5,7},{6,4},{7,5},{8,10},{9,11},{10,... | collective-permute-start | bytes 884744 | tf_op jit(solution)/shard_map/ppermute | solution.py:202
  77.8 5.8 %collective-permute-start.7 = (bf16[15,16,384]{2,1,0:T(8,128)(2,1)S(1)}, bf16[15,16,384]{2,1,0:T(8,128)(2,1)}, u32[]{:S(2)}, u32[]{:S(2)}) collective-permute-start(bf16[15,16,384]{2,1,0:T(8,128)(2,1)S(1)} %bitcast.47), channel_id=1, source_target_pairs={{5,1},{7,3},{0,4},{9,5},{2,6},{11,7},{4,8},{13,9},{6,10},{15,11},{... | collective-permute-start | bytes 552968 | tf_op jit(solution)/shard_map/ppermute | solution.py:218
  81.3 6.3 %collective-permute-start.10 = (bf16[15,16,384]{2,1,0:T(8,128)(2,1)S(1)}, bf16[15,16,384]{2,1,0:T(8,128)(2,1)S(1)}, u32[]{:S(2)}, u32[]{:S(2)}) collective-permute-start(bf16[15,16,384]{2,1,0:T(8,128)(2,1)S(1)} %bitcast.46), channel_id=1, source_target_pairs={{0,1},{1,2},{2,3},{3,0},{4,5},{5,6},{6,7},{7,4},{8,9},{9,10},{10,1... | collective-permute-start | bytes 552968 | tf_op jit(solution)/shard_map/ppermute | solution.py:223
  81.3 7.7 %collective-permute-start.9 = (bf16[15,16,384]{2,1,0:T(8,128)(2,1)S(1)}, bf16[15,16,384]{2,1,0:T(8,128)(2,1)S(1)}, u32[]{:S(2)}, u32[]{:S(2)}) collective-permute-start(bf16[15,16,384]{2,1,0:T(8,128)(2,1)S(1)} %bitcast.45), channel_id=1, source_target_pairs={{5,2},{7,0},{0,5},{9,6},{2,7},{11,4},{4,9},{13,10},{6,11},{15,8},{... | collective-permute-start | bytes 552968 | tf_op jit(solution)/shard_map/ppermute | solution.py:218
  83.9 5.7 %collective-permute-start.8 = (bf16[4,96,192]{2,1,0:T(8,128)(2,1)S(1)}, bf16[4,96,192]{2,1,0:T(8,128)(2,1)S(1)}, u32[]{:S(2)}, u32[]{:S(2)}) collective-permute-start(bf16[4,96,192]{2,1,0:T(8,128)(2,1)S(1)} %dynamic-slice_convert_fusion), channel_id=1, source_target_pairs={{0,16},{16,0},{1,17},{17,1},{2,18},{18,2},{3,19},{19,3},{4,20},{20... | collective-permute-start | bytes 442376 | tf_op jit(solution)/shard_map/ppermute | solution.py:202
  89.8 7.7 %copy-start.1 = (bf16[1,30,60,384]{3,2,1,0:T(8,128)(2,1)S(1)}, bf16[1,30,60,384]{3,2,1,0:T(8,128)(2,1)}, u32[]{:S(2)}) copy-start(bf16[1,30,60,384]{3,2,1,0:T(8,128)(2,1)} %cot_ref.2) | copy-start | bytes 4147204
  89.8 9.6 %collective-permute-start.11 = (bf16[96,192]{1,0:T(8,128)(2,1)S(1)}, bf16[96,192]{1,0:T(8,128)(2,1)S(1)}, u32[]{:S(2)}, u32[]{:S(2)}) collective-permute-start(bf16[96,192]{1,0:T(8,128)(2,1)S(1)} %get-tuple-element.75), channel_id=1, source_target_pairs={{0,4},{4,8},{8,12},{12,0},{1,5},{5,9},{9,13},{13,1},{2,6},{6,10},{... | collective-permute-start | bytes 110600 | tf_op jit(solution)/shard_map/ppermute | solution.py:202
  94.5 5.5 %collective-permute-start.12 = (bf16[96,192]{1,0:T(8,128)(2,1)S(1)}, bf16[96,192]{1,0:T(8,128)(2,1)S(1)}, u32[]{:S(2)}, u32[]{:S(2)}) collective-permute-start(bf16[96,192]{1,0:T(8,128)(2,1)S(1)} %get-tuple-element.77), channel_id=1, source_target_pairs={{0,8},{4,12},{8,0},{12,4},{1,9},{5,13},{9,1},{13,5},{2,10},{6,14},... | collective-permute-start | bytes 110600 | tf_op jit(solution)/shard_map/ppermute | solution.py:202
  94.5 5.4 %collective-permute-start.13 = (bf16[96,192]{1,0:T(8,128)(2,1)S(1)}, bf16[96,192]{1,0:T(8,128)(2,1)S(1)}, u32[]{:S(2)}, u32[]{:S(2)}) collective-permute-start(bf16[96,192]{1,0:T(8,128)(2,1)S(1)} %get-tuple-element.76), channel_id=1, source_target_pairs={{0,12},{4,0},{8,4},{12,8},{1,13},{5,1},{9,5},{13,9},{2,14},{6,2},{... | collective-permute-start | bytes 110600 | tf_op jit(solution)/shard_map/ppermute | solution.py:202

commit v11 on v10

--- a/solution.py
+++ b/solution.py
@@ -270,28 +270,29 @@
 
     got = permuted(send, ("lon",), lambda i: (i ^ 1,))
     keep = release(keep, len(waiting) // 2)
-    early = len(moved)
     got = release(got, len(waiting))
     total = [keep[i * lats:(i + 1) * lats] + got[i * lats:(i + 1) * lats].astype(F32) for i in range(lons // 2)]
-    while len(total) > 1:
+    while len(total) > 2:
         left = len(total) // 2
         payload = jnp.concatenate(total[left:], axis=0).astype(BF)
         got = permuted(payload, ("lon",), lambda i, bit=2 * left: (i ^ bit,))
-        if left == 1:
-            got, moved[:early] = lax.optimization_barrier((got, moved[:early]))
         total = [total[i] + got[i * lats:(i + 1) * lats].astype(F32) for i in range(left)]
-    total = total[0]
 
     share = width // dps
-    me, mine = lax.axis_index("dp"), None
-    for step in range(1, dps):
-        part = lax.dynamic_slice_in_dim(total, ((me + step) % dps) * share, share, 2).astype(BF)
-        got = permuted(part, ("dp",), lambda i, step=step: ((i + step) % dps,))
-        if step == dps - 1:
-            got, moved[early:] = lax.optimization_barrier((got, moved[early:]))
-        mine = got.astype(F32) if mine is None else mine + got.astype(F32)
-    own = lax.dynamic_slice_in_dim(total, me * share, share, 2)
-    total = own if mine is None else own + mine
+    me = lax.axis_index("dp")
+    arrived = []
+    for pair in range(len(total)):
+        for step in range(dps):
+            if pair == 0 and step == 0:
+                continue
+            part = lax.dynamic_slice_in_dim(total[pair], ((me + step) % dps) * share, share, 2).astype(BF)
+            arrived.append(
+                permuted(part, ("dp", "lon"), lambda d, j, s=step, p=pair: ((d + s) % dps, j ^ (2 * p)))
+            )
+    arrived, moved = lax.optimization_barrier((arrived, moved))
+    total = lax.dynamic_slice_in_dim(total[0], me * share, share, 2)
+    for got in arrived:
+        total = total + got.astype(F32)
 
     mine = total[0]
     for step in range(1, lats):

time: 102 us -> 107 us (1.049)
  waiting for transfers between devices: 6.44 us -> 12.2 us
  starting transfers between devices: 33.3 us -> 30.7 us
  local copies, waits for them, and re-layouts: 2.91 us -> 5.07 us
    ppermute x6 -> x7, waiting for transfers between devices: 1.15 us -> 8.79 us  [permuted(): return lax.ppermute(value, tuple(axes), pairs)]
    unnamed x12 -> x16, local copies, waits for them, and re-layouts: 2.77 us -> 4.74 us
    ppermute x6 -> x7, starting transfers between devices: 11.8 us -> 9.79 us  [permuted(): return lax.ppermute(value, tuple(axes), pairs)]
    add x1 -> x2, other arithmetic: 0.08 us -> 2.04 us  [reduce_weights(): keep[i * lats:(i + 1) * lats] + got[i * lats:(i + 1) * lats].astype(F32)]
    ppermute x6, waiting for transfers between devices: 5.29 us -> 3.38 us  [shared(): return lax.ppermute(value, ('lat', 'lon'), pairs)]
  transfers between devices with their start and end apart: 14 -> 15, of which waited for: 5 -> 4; matrix products, arithmetic and copies ran while one was open for 5% -> 5% of each run, Pallas kernels for 25% -> 24%
where the time goes in v11:
time: 107 us
  Pallas kernels  51.3 us (48%)
  starting transfers between devices  30.7 us (29%)
  waiting for transfers between devices  12.2 us (11%)
  other arithmetic  6.7 us (6%)
  local copies, waits for them, and re-layouts  5.07 us (5%)
    pallas_call x2, Pallas kernels, window_call(): pl.pallas_call(functools.partial(window_kernel, head, metas, (prev is not...  50.4 us
    ppermute x6, starting transfers between devices, shared(): return lax.ppermute(value, ('lat', 'lon'), pairs)  16.5 us
    ppermute x7, starting transfers between devices, permuted(): return lax.ppermute(value, tuple(axes), pairs)  9.79 us
    ppermute x7, waiting for transfers between devices, permuted(): return lax.ppermute(value, tuple(axes), pairs)  8.79 us
    unnamed x16, local copies, waits for them, and re-layouts  4.74 us
    ppermute x2, starting transfers between devices, along_lon(): lax.ppermute(value, 'lon', [(j, (j + step) % count) for j in range(count)])  4.42 us
    ppermute x6, waiting for transfers between devices, shared(): return lax.ppermute(value, ('lat', 'lon'), pairs)  3.38 us
  transfers between devices with their start and end apart: 15, of which 4 were waited for; matrix products, arithmetic and copies ran while one was open for 5% of the time, Pallas kernels for 24%

profile of v11, /device:TPU:0, one launch (start us, length us, event | category | flops | bytes accessed | tf_op | source)
XLA Modules:
  0.0 106.9 jit_solution(5414849844629576609)
XLA Ops:
  0.6 1.4 %copy-done = bf16[1,30,60,384]{3,2,1,0:T(8,128)(2,1)S(1)} copy-done((bf16[1,30,60,384]{3,2,1,0:T(8,128)(2,1)S(1)}, bf16[1,30,60,384]{3,2,1,0:T(8,128)(2,1)}, u32[]{:S(2)}) %copy-start) | copy-done | bytes 1382424
  2.0 1.4 %copy-done.2 = bf16[1,30,60,384]{3,2,1,0:T(8,128)(2,1)S(1)} copy-done((bf16[1,30,60,384]{3,2,1,0:T(8,128)(2,1)S(1)}, bf16[1,30,60,384]{3,2,1,0:T(8,128)(2,1)}, u32[]{:S(2)}) %copy-start.2) | copy-done | bytes 1382424
  3.6 1.4 %collective-permute-start.3 = (bf16[2,1,15,32,384]{4,3,2,1,0:T(8,128)(2,1)S(1)}, bf16[2,1,15,32,384]{4,3,2,1,0:T(8,128)(2,1)S(1)}, u32[]{:S(2)}, u32[]{:S(2)}) collective-permute-start(bf16[2,1,15,32,384]{4,3,2,1,0:T(8,128)(2,1)S(1)} %shard_map.76), channel_id=1, source_target_pairs={{1,5},{3,7},{4,0},{5,9},{6,2},{7,11},{8,4},{9,13},{10,6},{11,15},{... | collective-permute-start | bytes 2211848 | tf_op jit(solution)/shard_map/ppermute | solution.py:218
  5.7 4.4 %collective-permute-start = (bf16[2,1,15,16,384]{4,3,2,1,0:T(8,128)(2,1)S(1)}, bf16[2,1,15,16,384]{4,3,2,1,0:T(8,128)(2,1)S(1)}, u32[]{:S(2)}, u32[]{:S(2)}) collective-permute-start(bf16[2,1,15,16,384]{4,3,2,1,0:T(8,128)(2,1)S(1)} %get-tuple-element.39), channel_id=1, source_target_pairs={{0,3},{1,0},{2,1},{3,2},{4,7},{5,4},{6,5},{7,6},{8,11},{9,8},{10,9... | collective-permute-start | bytes 1105928 | tf_op jit(solution)/shard_map/ppermute | solution.py:223
  10.2 1.3 %collective-permute-start.1 = (bf16[2,1,15,16,384]{4,3,2,1,0:T(8,128)(2,1)S(1)}, bf16[2,1,15,16,384]{4,3,2,1,0:T(8,128)(2,1)S(1)}, u32[]{:S(2)}, u32[]{:S(2)}) collective-permute-start(bf16[2,1,15,16,384]{4,3,2,1,0:T(8,128)(2,1)S(1)} %get-tuple-element.40), channel_id=1, source_target_pairs={{1,5},{3,7},{4,0},{5,9},{6,2},{7,11},{8,4},{9,13},{10,6},{11,15},{... | collective-permute-start | bytes 1105928 | tf_op jit(solution)/shard_map/ppermute | solution.py:218
  11.4 4.8 %collective-permute-start.2 = (bf16[2,1,15,16,384]{4,3,2,1,0:T(8,128)(2,1)S(1)}, bf16[2,1,15,16,384]{4,3,2,1,0:T(8,128)(2,1)S(1)}, u32[]{:S(2)}, u32[]{:S(2)}) collective-permute-start(bf16[2,1,15,16,384]{4,3,2,1,0:T(8,128)(2,1)S(1)} %get-tuple-element.41), channel_id=1, source_target_pairs={{2,5},{0,7},{5,0},{6,9},{7,2},{4,11},{9,4},{10,13},{11,6},{8,15},{... | collective-permute-start | bytes 1105928 | tf_op jit(solution)/shard_map/ppermute | solution.py:218
  16.3 3.4 %collective-permute-done.3 = bf16[2,1,15,32,384]{4,3,2,1,0:T(8,128)(2,1)S(1)} collective-permute-done((bf16[2,1,15,32,384]{4,3,2,1,0:T(8,128)(2,1)S(1)}, bf16[2,1,15,32,384]{4,3,2,1,0:T(8,128)(2,1)S(1)}, u32[]{:S(2)}, u32[]{:S(2)}) %collective-permute-start.3) | collective-permute-done | bytes 737312 | tf_op jit(solution)/shard_map/ppermute | solution.py:218
  19.7 25.0 %shard_map.78 = (bf16[480,384]{1,0:T(8,128)(2,1)S(1)}, bf16[480,384]{1,0:T(8,128)(2,1)S(1)}, f32[384,1152]{1,0:T(8,128)S(1)}, f32[384,384]{1,0:T(8,128)S(1)}) custom-call(bf16[2,480,384]{2,1,0:T(8,128)(2,1)S(1)} %bitcast.39, bf16[2,480,384]{2,1,0:T(8,128)(2,1)S(1)} %bitcast.38, f32[384]{0:T(512)S(1)} %copy-done.5, bf16[384,1152]{1,0:T(8,128)(2,1)S(1)} %copy-done.3, ...), custom_call_target="tpu_custom_call" | custom-call | flops 7644119040 | bytes 8388608 | tf_op jit(solution)/shard_map/pallas_call | solution.py:171
  44.7 25.4 %shard_map.79 = (bf16[240,384]{1,0:T(8,128)(2,1)S(1)}, bf16[240,384]{1,0:T(8,128)(2,1)S(1)}, bf16[240,384]{1,0:T(8,128)(2,1)S(1)}, bf16[240,384]{1,0:T(8,128)(2,...) custom-call(bf16[2,240,384]{2,1,0:T(8,128)(2,1)S(1)} %bitcast.41, bf16[2,240,384]{2,1,0:T(8,128)(2,1)S(1)} %bitcast.42, ...), custom_call_target="tpu_custom_call" | custom-call | flops 7644119040 | bytes 8388608 | tf_op jit(solution)/shard_map/pallas_call | solution.py:171
  70.3 3.5 %collective-permute-start.9 = (bf16[15,16,384]{2,1,0:T(8,128)(2,1)S(1)}, bf16[15,16,384]{2,1,0:T(8,128)(2,1)S(1)}, u32[]{:S(2)}, u32[]{:S(2)}) collective-permute-start(bf16[15,16,384]{2,1,0:T(8,128)(2,1)S(1)} %bitcast.47), channel_id=1, source_target_pairs={{5,1},{7,3},{0,4},{9,5},{2,6},{11,7},{4,8},{13,9},{6,10},{15,11},{... | collective-permute-start | bytes 552968 | tf_op jit(solution)/shard_map/ppermute | solution.py:218
  73.8 3.5 %collective-permute-start.8 = (bf16[15,32,384]{2,1,0:T(8,128)(2,1)S(1)}, bf16[15,32,384]{2,1,0:T(8,128)(2,1)S(1)}, u32[]{:S(2)}, u32[]{:S(2)}) collective-permute-start(bf16[15,32,384]{2,1,0:T(8,128)(2,1)S(1)} %bitcast.40), channel_id=1, source_target_pairs={{5,1},{7,3},{0,4},{9,5},{2,6},{11,7},{4,8},{13,9},{6,10},{15,11},{... | collective-permute-start | bytes 1105928 | tf_op jit(solution)/shard_map/ppermute | solution.py:218
  77.4 1.0 convert_add_fusion.1
  78.4 1.0 convert_add_fusion
  79.6 2.6 %collective-permute-start.6 = (bf16[4,96,192]{2,1,0:T(8,128)(2,1)S(1)}, bf16[4,96,192]{2,1,0:T(8,128)(2,1)S(1)}, u32[]{:S(2)}, u32[]{:S(2)}) collective-permute-start(bf16[4,96,192]{2,1,0:T(8,128)(2,1)S(1)} %get-tuple-element.78), channel_id=1, source_target_pairs={{0,2},{1,3},{2,0},{3,1},{16,18},{17,19},{18,16},{19,17},{4,6},{5,7... | collective-permute-start | bytes 442376 | tf_op jit(solution)/shard_map/ppermute | solution.py:202
  82.2 1.9 %collective-permute-start.10 = (bf16[15,16,384]{2,1,0:T(8,128)(2,1)S(1)}, bf16[15,16,384]{2,1,0:T(8,128)(2,1)}, u32[]{:S(2)}, u32[]{:S(2)}) collective-permute-start(bf16[15,16,384]{2,1,0:T(8,128)(2,1)S(1)} %bitcast.45), channel_id=1, source_target_pairs={{5,2},{7,0},{0,5},{9,6},{2,7},{11,4},{4,9},{13,10},{6,11},{15,8},{... | collective-permute-start | bytes 552968 | tf_op jit(solution)/shard_map/ppermute | solution.py:218
  84.3 2.7 %collective-permute-start.7 = (bf16[4,96,192]{2,1,0:T(8,128)(2,1)S(1)}, bf16[4,96,192]{2,1,0:T(8,128)(2,1)S(1)}, u32[]{:S(2)}, u32[]{:S(2)}) collective-permute-start(bf16[4,96,192]{2,1,0:T(8,128)(2,1)S(1)} %get-tuple-element.77), channel_id=1, source_target_pairs={{0,18},{1,19},{2,16},{3,17},{16,2},{17,3},{18,0},{19,1},{4,22},{5,... | collective-permute-start | bytes 442376 | tf_op jit(solution)/shard_map/ppermute | solution.py:202
  88.2 4.8 %collective-permute-done.6 = bf16[4,96,192]{2,1,0:T(8,128)(2,1)S(1)} collective-permute-done((bf16[4,96,192]{2,1,0:T(8,128)(2,1)S(1)}, bf16[4,96,192]{2,1,0:T(8,128)(2,1)S(1)}, u32[]{:S(2)}, u32[]{:S(2)}) %collective-permute-start.6) | collective-permute-done | bytes 147488 | tf_op jit(solution)/shard_map/ppermute | solution.py:202
  93.0 1.8 %collective-permute-done.7 = bf16[4,96,192]{2,1,0:T(8,128)(2,1)S(1)} collective-permute-done((bf16[4,96,192]{2,1,0:T(8,128)(2,1)S(1)}, bf16[4,96,192]{2,1,0:T(8,128)(2,1)S(1)}, u32[]{:S(2)}, u32[]{:S(2)}) %collective-permute-start.7) | collective-permute-done | bytes 147488 | tf_op jit(solution)/shard_map/ppermute | solution.py:202
  94.9 2.2 %collective-permute-done.5 = bf16[4,96,192]{2,1,0:T(8,128)(2,1)S(1)} collective-permute-done((bf16[4,96,192]{2,1,0:T(8,128)(2,1)S(1)}, bf16[4,96,192]{2,1,0:T(8,128)(2,1)S(1)}, u32[]{:S(2)}, u32[]{:S(2)}) %collective-permute-start.5) | collective-permute-done | bytes 147488 | tf_op jit(solution)/shard_map/ppermute | solution.py:202
  97.3 1.5 %collective-permute-start.13 = (bf16[96,192]{1,0:T(8,128)(2,1)S(1)}, bf16[96,192]{1,0:T(8,128)(2,1)S(1)}, u32[]{:S(2)}, u32[]{:S(2)}) collective-permute-start(bf16[96,192]{1,0:T(8,128)(2,1)S(1)} %get-tuple-element.81), channel_id=1, source_target_pairs={{0,8},{4,12},{8,0},{12,4},{1,9},{5,13},{9,1},{13,5},{2,10},{6,14},... | collective-permute-start | bytes 110600 | tf_op jit(solution)/shard_map/ppermute | solution.py:202
  98.9 2.3 %collective-permute-start.14 = (bf16[96,192]{1,0:T(8,128)(2,1)S(1)}, bf16[96,192]{1,0:T(8,128)(2,1)S(1)}, u32[]{:S(2)}, u32[]{:S(2)}) collective-permute-start(bf16[96,192]{1,0:T(8,128)(2,1)S(1)} %get-tuple-element.80), channel_id=1, source_target_pairs={{0,12},{4,0},{8,4},{12,8},{1,13},{5,1},{9,5},{13,9},{2,14},{6,2},{... | collective-permute-start | bytes 110600 | tf_op jit(solution)/shard_map/ppermute | solution.py:202
  101.1 1.1 %broadcast_select_fusion.3 = (bf16[15,16,384]{2,1,0:T(8,128)(2,1)S(1)}, bf16[15,16,384]{2,1,0:T(8,128)(2,1)S(1)}, bf16[15,16,384]{2,1,0:T(8,128)(2,1)S(1)}, bf16[15,16,384]{2,1,0:T(8,128)(2,1)S(1)}) fusion(bf16[15,16,384]{2,1,0:T(8,128)(2,1)S(1)} %bitcast.37, bf16[15,16,384]{2,1,0:T(8,128)(2,1)S(1)} %collective-permute-done.9, pred[]{:T(512)S(6)} %eq.13, ...), kind=kLoop, calls=%fused_computation.16 | loop fusion | flops 368640 | bytes 1474562 | tf_op jit(solution)/shard_map/jit(_where)/select_n | solution.py:368
  102.5 1.2 %copy-done.1 = bf16[1,30,60,384]{3,2,1,0:T(8,128)(2,1)S(1)} copy-done((bf16[1,30,60,384]{3,2,1,0:T(8,128)(2,1)S(1)}, bf16[1,30,60,384]{3,2,1,0:T(8,128)(2,1)}, u32[]{:S(2)}) %copy-start.1) | copy-done | bytes 1382424
  103.7 1.9 %add_convert_fusion = bf16[1,30,60,384]{3,2,1,0:T(8,128)(2,1)} fusion(bf16[1,30,60,384]{3,2,1,0:T(8,128)(2,1)S(1)} %copy-done.1, bf16[1,30,15,384]{3,2,1,0:T(8,128)(2,1)S(1)} %fusion.1, bf16[1,30,30,384]{3,2,1,0:T(8,128)(2,1)S(1)} %fusion, bf16[1,30,15,384]{3,2,1,0:T(8,128)(2,1)S(1)} %fusion.2), kind=kLoop, calls=%fused_computation | loop fusion | flops 6220800 | bytes 4147200 | tf_op jit(solution)/shard_map/convert_element_type | solution.py:385
  (41 shorter events, 4.4 us)
Async XLA Ops:
  0.6 1.4 %copy-start = (bf16[1,30,60,384]{3,2,1,0:T(8,128)(2,1)S(1)}, bf16[1,30,60,384]{3,2,1,0:T(8,128)(2,1)}, u32[]{:S(2)}) copy-start(bf16[1,30,60,384]{3,2,1,0:T(8,128)(2,1)} %cot_ref.2) | copy-start | bytes 4147204
  2.0 1.4 %copy-start.2 = (bf16[1,30,60,384]{3,2,1,0:T(8,128)(2,1)S(1)}, bf16[1,30,60,384]{3,2,1,0:T(8,128)(2,1)}, u32[]{:S(2)}) copy-start(bf16[1,30,60,384]{3,2,1,0:T(8,128)(2,1)} %hid_ref.2) | copy-start | bytes 4147204
  3.6 16.0 %copy-start.3 = (bf16[384,1152]{1,0:T(8,128)(2,1)S(1)}, bf16[384,1152]{1,0:T(8,128)(2,1)}, u32[]{:S(2)}) copy-start(bf16[384,1152]{1,0:T(8,128)(2,1)} %refs_5_.1) | copy-start | bytes 2654212
  3.6 16.0 %copy-start.4 = (bf16[384,384]{1,0:T(8,128)(2,1)S(1)}, bf16[384,384]{1,0:T(8,128)(2,1)}, u32[]{:S(2)}) copy-start(bf16[384,384]{1,0:T(8,128)(2,1)} %refs_6_.1) | copy-start | bytes 884740
  3.6 16.0 %copy-start.5 = (f32[384]{0:T(512)S(1)}, f32[384]{0:T(512)}, u32[]{:S(2)}) copy-start(f32[384]{0:T(512)} %refs_4_.3) | copy-start | bytes 4612
  3.6 16.0 %collective-permute-start.3 = (bf16[2,1,15,32,384]{4,3,2,1,0:T(8,128)(2,1)S(1)}, bf16[2,1,15,32,384]{4,3,2,1,0:T(8,128)(2,1)S(1)}, u32[]{:S(2)}, u32[]{:S(2)}) collective-permute-start(bf16[2,1,15,32,384]{4,3,2,1,0:T(8,128)(2,1)S(1)} %shard_map.76), channel_id=1, source_target_pairs={{1,5},{3,7},{4,0},{5,9},{6,2},{7,11},{8,4},{9,13},{10,6},{11,15},{... | collective-permute-start | bytes 2211848 | tf_op jit(solution)/shard_map/ppermute | solution.py:218
  5.7 39.0 %collective-permute-start = (bf16[2,1,15,16,384]{4,3,2,1,0:T(8,128)(2,1)S(1)}, bf16[2,1,15,16,384]{4,3,2,1,0:T(8,128)(2,1)S(1)}, u32[]{:S(2)}, u32[]{:S(2)}) collective-permute-start(bf16[2,1,15,16,384]{4,3,2,1,0:T(8,128)(2,1)S(1)} %get-tuple-element.39), channel_id=1, source_target_pairs={{0,3},{1,0},{2,1},{3,2},{4,7},{5,4},{6,5},{7,6},{8,11},{9,8},{10,9... | collective-permute-start | bytes 1105928 | tf_op jit(solution)/shard_map/ppermute | solution.py:223
  10.2 34.6 %collective-permute-start.1 = (bf16[2,1,15,16,384]{4,3,2,1,0:T(8,128)(2,1)S(1)}, bf16[2,1,15,16,384]{4,3,2,1,0:T(8,128)(2,1)S(1)}, u32[]{:S(2)}, u32[]{:S(2)}) collective-permute-start(bf16[2,1,15,16,384]{4,3,2,1,0:T(8,128)(2,1)S(1)} %get-tuple-element.40), channel_id=1, source_target_pairs={{1,5},{3,7},{4,0},{5,9},{6,2},{7,11},{8,4},{9,13},{10,6},{11,15},{... | collective-permute-start | bytes 1105928 | tf_op jit(solution)/shard_map/ppermute | solution.py:218
  11.4 33.3 %collective-permute-start.2 = (bf16[2,1,15,16,384]{4,3,2,1,0:T(8,128)(2,1)S(1)}, bf16[2,1,15,16,384]{4,3,2,1,0:T(8,128)(2,1)S(1)}, u32[]{:S(2)}, u32[]{:S(2)}) collective-permute-start(bf16[2,1,15,16,384]{4,3,2,1,0:T(8,128)(2,1)S(1)} %get-tuple-element.41), channel_id=1, source_target_pairs={{2,5},{0,7},{5,0},{6,9},{7,2},{4,11},{9,4},{10,13},{11,6},{8,15},{... | collective-permute-start | bytes 1105928 | tf_op jit(solution)/shard_map/ppermute | solution.py:218
  70.1 7.2 %collective-permute-start.4 = (bf16[8,96,384]{2,1,0:T(8,128)(2,1)S(1)}, bf16[8,96,384]{2,1,0:T(8,128)(2,1)}, u32[]{:S(2)}, u32[]{:S(2)}) collective-permute-start(bf16[8,96,384]{2,1,0:T(8,128)(2,1)S(1)} %get-tuple-element.51), channel_id=1, source_target_pairs={{0,1},{1,0},{2,3},{3,2},{4,5},{5,4},{6,7},{7,6},{8,9},{9,8},{10,11... | collective-permute-start | bytes 1769480 | tf_op jit(solution)/shard_map/ppermute | solution.py:202
  70.3 14.0 %collective-permute-start.9 = (bf16[15,16,384]{2,1,0:T(8,128)(2,1)S(1)}, bf16[15,16,384]{2,1,0:T(8,128)(2,1)S(1)}, u32[]{:S(2)}, u32[]{:S(2)}) collective-permute-start(bf16[15,16,384]{2,1,0:T(8,128)(2,1)S(1)} %bitcast.47), channel_id=1, source_target_pairs={{5,1},{7,3},{0,4},{9,5},{2,6},{11,7},{4,8},{13,9},{6,10},{15,11},{... | collective-permute-start | bytes 552968 | tf_op jit(solution)/shard_map/ppermute | solution.py:218
  73.8 13.2 %collective-permute-start.8 = (bf16[15,32,384]{2,1,0:T(8,128)(2,1)S(1)}, bf16[15,32,384]{2,1,0:T(8,128)(2,1)S(1)}, u32[]{:S(2)}, u32[]{:S(2)}) collective-permute-start(bf16[15,32,384]{2,1,0:T(8,128)(2,1)S(1)} %bitcast.40), channel_id=1, source_target_pairs={{5,1},{7,3},{0,4},{9,5},{2,6},{11,7},{4,8},{13,9},{6,10},{15,11},{... | collective-permute-start | bytes 1105928 | tf_op jit(solution)/shard_map/ppermute | solution.py:218
  79.6 13.5 %collective-permute-start.6 = (bf16[4,96,192]{2,1,0:T(8,128)(2,1)S(1)}, bf16[4,96,192]{2,1,0:T(8,128)(2,1)S(1)}, u32[]{:S(2)}, u32[]{:S(2)}) collective-permute-start(bf16[4,96,192]{2,1,0:T(8,128)(2,1)S(1)} %get-tuple-element.78), channel_id=1, source_target_pairs={{0,2},{1,3},{2,0},{3,1},{16,18},{17,19},{18,16},{19,17},{4,6},{5,7... | collective-permute-start | bytes 442376 | tf_op jit(solution)/shard_map/ppermute | solution.py:202
  82.2 14.8 %collective-permute-start.11 = (bf16[15,16,384]{2,1,0:T(8,128)(2,1)S(1)}, bf16[15,16,384]{2,1,0:T(8,128)(2,1)}, u32[]{:S(2)}, u32[]{:S(2)}) collective-permute-start(bf16[15,16,384]{2,1,0:T(8,128)(2,1)S(1)} %bitcast.46), channel_id=1, source_target_pairs={{0,1},{1,2},{2,3},{3,0},{4,5},{5,6},{6,7},{7,4},{8,9},{9,10},{10,1... | collective-permute-start | bytes 552968 | tf_op jit(solution)/shard_map/ppermute | solution.py:223
  82.2 14.8 %collective-permute-start.10 = (bf16[15,16,384]{2,1,0:T(8,128)(2,1)S(1)}, bf16[15,16,384]{2,1,0:T(8,128)(2,1)}, u32[]{:S(2)}, u32[]{:S(2)}) collective-permute-start(bf16[15,16,384]{2,1,0:T(8,128)(2,1)S(1)} %bitcast.45), channel_id=1, source_target_pairs={{5,2},{7,0},{0,5},{9,6},{2,7},{11,4},{4,9},{13,10},{6,11},{15,8},{... | collective-permute-start | bytes 552968 | tf_op jit(solution)/shard_map/ppermute | solution.py:218
  84.3 10.6 %collective-permute-start.7 = (bf16[4,96,192]{2,1,0:T(8,128)(2,1)S(1)}, bf16[4,96,192]{2,1,0:T(8,128)(2,1)S(1)}, u32[]{:S(2)}, u32[]{:S(2)}) collective-permute-start(bf16[4,96,192]{2,1,0:T(8,128)(2,1)S(1)} %get-tuple-element.77), channel_id=1, source_target_pairs={{0,18},{1,19},{2,16},{3,17},{16,2},{17,3},{18,0},{19,1},{4,22},{5,... | collective-permute-start | bytes 442376 | tf_op jit(solution)/shard_map/ppermute | solution.py:202
  87.0 0.7 copy-start.6
  87.7 9.3 %collective-permute-start.5 = (bf16[4,96,192]{2,1,0:T(8,128)(2,1)S(1)}, bf16[4,96,192]{2,1,0:T(8,128)(2,1)S(1)}, u32[]{:S(2)}, u32[]{:S(2)}) collective-permute-start(bf16[4,96,192]{2,1,0:T(8,128)(2,1)S(1)} %dynamic-slice_convert_fusion.2), channel_id=1, source_target_pairs={{0,16},{1,17},{2,18},{3,19},{16,0},{17,1},{18,2},{19,3},{4,20},{5,... | collective-permute-start | bytes 442376 | tf_op jit(solution)/shard_map/ppermute | solution.py:202
  97.2 5.1 %copy-start.7 = (bf16[15,32,384]{2,1,0:T(8,128)(2,1)S(1)}, bf16[15,32,384]{2,1,0:T(8,128)(2,1)}, u32[]{:S(2)}) copy-start(bf16[15,32,384]{2,1,0:T(8,128)(2,1)} %copy-done.6) | copy-start | bytes 1105924
  97.3 8.4 %collective-permute-start.12 = (bf16[96,192]{1,0:T(8,128)(2,1)S(1)}, bf16[96,192]{1,0:T(8,128)(2,1)S(1)}, u32[]{:S(2)}, u32[]{:S(2)}) collective-permute-start(bf16[96,192]{1,0:T(8,128)(2,1)S(1)} %get-tuple-element.79), channel_id=1, source_target_pairs={{0,4},{4,8},{8,12},{12,0},{1,5},{5,9},{9,13},{13,1},{2,6},{6,10},{... | collective-permute-start | bytes 110600 | tf_op jit(solution)/shard_map/ppermute | solution.py:202
  97.3 8.3 %collective-permute-start.13 = (bf16[96,192]{1,0:T(8,128)(2,1)S(1)}, bf16[96,192]{1,0:T(8,128)(2,1)S(1)}, u32[]{:S(2)}, u32[]{:S(2)}) collective-permute-start(bf16[96,192]{1,0:T(8,128)(2,1)S(1)} %get-tuple-element.81), channel_id=1, source_target_pairs={{0,8},{4,12},{8,0},{12,4},{1,9},{5,13},{9,1},{13,5},{2,10},{6,14},... | collective-permute-start | bytes 110600 | tf_op jit(solution)/shard_map/ppermute | solution.py:202
  98.9 6.8 %collective-permute-start.14 = (bf16[96,192]{1,0:T(8,128)(2,1)S(1)}, bf16[96,192]{1,0:T(8,128)(2,1)S(1)}, u32[]{:S(2)}, u32[]{:S(2)}) collective-permute-start(bf16[96,192]{1,0:T(8,128)(2,1)S(1)} %get-tuple-element.80), channel_id=1, source_target_pairs={{0,12},{4,0},{8,4},{12,8},{1,13},{5,1},{9,5},{13,9},{2,14},{6,2},{... | collective-permute-start | bytes 110600 | tf_op jit(solution)/shard_map/ppermute | solution.py:202
  102.4 1.4 %copy-start.1 = (bf16[1,30,60,384]{3,2,1,0:T(8,128)(2,1)S(1)}, bf16[1,30,60,384]{3,2,1,0:T(8,128)(2,1)}, u32[]{:S(2)}) copy-start(bf16[1,30,60,384]{3,2,1,0:T(8,128)(2,1)} %cot_ref.2) | copy-start | bytes 4147204

commit v12 on v10

--- a/solution.py
+++ b/solution.py
@@ -329,7 +329,10 @@
     whole_inner = [[rest.pop(0) for _ in fixed] for _ in inner]
     whole_edge = [rest.pop(0) for _ in fixed]
     whole_side = [along_lon(rest.pop(0), -1) for _ in fixed]
-    own_side, edge_in, corner_in = along_lon(side_sent, -1), shared(edge_sent), shared(corner_sent, east=1)
+    own_side = along_lon(side_sent, -1)
+    if inner_in:
+        edge_sent, corner_sent, inner_in = lax.optimization_barrier((edge_sent, corner_sent, inner_in))
+    edge_in, corner_in = shared(edge_sent), shared(corner_sent, east=1)
 
     order = [(b, wr, wc) for b in range(samples) for wc in range(nc) for wr in range(nr)]
     sums = None

time: 102 us -> 107 us (1.049)
  waiting for transfers between devices: 6.44 us -> 10.1 us
  starting transfers between devices: 33.3 us -> 34.8 us
    ppermute x6, waiting for transfers between devices: 5.29 us -> 7.98 us  [shared(): return lax.ppermute(value, ('lat', 'lon'), pairs)]
    ppermute x6, starting transfers between devices: 17.1 us -> 19.4 us  [shared(): return lax.ppermute(value, ('lat', 'lon'), pairs)]
  transfers between devices with their start and end apart: 14 -> 14, of which waited for: 5 -> 2; matrix products, arithmetic and copies ran while one was open for 5% -> 5% of each run, Pallas kernels for 25% -> 24%
where the time goes in v12:
time: 107 us; the launch traced here: 106 us
  Pallas kernels  51.4 us (48%)
  starting transfers between devices  34.8 us (33%)
  waiting for transfers between devices  10.1 us (9%)
  other arithmetic  6.42 us (6%)
  local copies, waits for them, and re-layouts  2.91 us (3%)
    pallas_call x2, Pallas kernels, window_call(): pl.pallas_call(functools.partial(window_kernel, head, metas, (prev is not...  50.5 us
    ppermute x6, starting transfers between devices, shared(): return lax.ppermute(value, ('lat', 'lon'), pairs)  19.4 us
    ppermute x6, starting transfers between devices, permuted(): return lax.ppermute(value, tuple(axes), pairs)  11 us
    ppermute x6, waiting for transfers between devices, shared(): return lax.ppermute(value, ('lat', 'lon'), pairs)  7.98 us
    ppermute x2, starting transfers between devices, along_lon(): lax.ppermute(value, 'lon', [(j, (j + step) % count) for j in range(count)])  4.42 us
    unnamed x12, local copies, waits for them, and re-layouts  2.77 us
  transfers between devices with their start and end apart: 14, of which 2 were waited for; matrix products, arithmetic and copies ran while one was open for 5% of the time, Pallas kernels for 24%

profile of v12, /device:TPU:0, one launch (start us, length us, event | category | flops | bytes accessed | tf_op | source)
XLA Modules:
  0.0 106.5 jit_solution(4524088253804764587)
XLA Ops:
  0.6 1.4 %copy-done = bf16[1,30,60,384]{3,2,1,0:T(8,128)(2,1)S(1)} copy-done((bf16[1,30,60,384]{3,2,1,0:T(8,128)(2,1)S(1)}, bf16[1,30,60,384]{3,2,1,0:T(8,128)(2,1)}, u32[]{:S(2)}) %copy-start) | copy-done | bytes 1382424
  2.0 1.4 %copy-done.2 = bf16[1,30,60,384]{3,2,1,0:T(8,128)(2,1)S(1)} copy-done((bf16[1,30,60,384]{3,2,1,0:T(8,128)(2,1)S(1)}, bf16[1,30,60,384]{3,2,1,0:T(8,128)(2,1)}, u32[]{:S(2)}) %copy-start.2) | copy-done | bytes 1382424
  3.6 1.4 %collective-permute-start.1 = (bf16[2,1,15,32,384]{4,3,2,1,0:T(8,128)(2,1)S(1)}, bf16[2,1,15,32,384]{4,3,2,1,0:T(8,128)(2,1)S(1)}, u32[]{:S(2)}, u32[]{:S(2)}) collective-permute-start(bf16[2,1,15,32,384]{4,3,2,1,0:T(8,128)(2,1)S(1)} %shard_map.76), channel_id=1, source_target_pairs={{1,5},{3,7},{4,0},{5,9},{6,2},{7,11},{8,4},{9,13},{10,6},{11,15},{... | collective-permute-start | bytes 2211848 | tf_op jit(solution)/shard_map/ppermute | solution.py:218
  5.1 0.7 shard_map.77
  5.7 4.4 %collective-permute-start = (bf16[2,1,15,16,384]{4,3,2,1,0:T(8,128)(2,1)S(1)}, bf16[2,1,15,16,384]{4,3,2,1,0:T(8,128)(2,1)S(1)}, u32[]{:S(2)}, u32[]{:S(2)}) collective-permute-start(bf16[2,1,15,16,384]{4,3,2,1,0:T(8,128)(2,1)S(1)} %get-tuple-element.41), channel_id=1, source_target_pairs={{0,3},{1,0},{2,1},{3,2},{4,7},{5,4},{6,5},{7,6},{8,11},{9,8},{10,9... | collective-permute-start | bytes 1105928 | tf_op jit(solution)/shard_map/ppermute | solution.py:223
  10.2 8.0 %collective-permute-done.1 = bf16[2,1,15,32,384]{4,3,2,1,0:T(8,128)(2,1)S(1)} collective-permute-done((bf16[2,1,15,32,384]{4,3,2,1,0:T(8,128)(2,1)S(1)}, bf16[2,1,15,32,384]{4,3,2,1,0:T(8,128)(2,1)S(1)}, u32[]{:S(2)}, u32[]{:S(2)}) %collective-permute-start.1) | collective-permute-done | bytes 737312 | tf_op jit(solution)/shard_map/ppermute | solution.py:218
  18.1 1.3 %collective-permute-start.2 = (bf16[2,1,15,16,384]{4,3,2,1,0:T(8,128)(2,1)S(1)}, bf16[2,1,15,16,384]{4,3,2,1,0:T(8,128)(2,1)S(1)}, u32[]{:S(2)}, u32[]{:S(2)}) collective-permute-start(bf16[2,1,15,16,384]{4,3,2,1,0:T(8,128)(2,1)S(1)} %get-tuple-element.45), channel_id=1, source_target_pairs={{1,5},{3,7},{4,0},{5,9},{6,2},{7,11},{8,4},{9,13},{10,6},{11,15},{... | collective-permute-start | bytes 1105928 | tf_op jit(solution)/shard_map/ppermute | solution.py:218
  19.4 5.4 %collective-permute-start.3 = (bf16[2,1,15,16,384]{4,3,2,1,0:T(8,128)(2,1)S(1)}, bf16[2,1,15,16,384]{4,3,2,1,0:T(8,128)(2,1)S(1)}, u32[]{:S(2)}, u32[]{:S(2)}) collective-permute-start(bf16[2,1,15,16,384]{4,3,2,1,0:T(8,128)(2,1)S(1)} %get-tuple-element.46), channel_id=1, source_target_pairs={{2,5},{0,7},{5,0},{6,9},{7,2},{4,11},{9,4},{10,13},{11,6},{8,15},{... | collective-permute-start | bytes 1105928 | tf_op jit(solution)/shard_map/ppermute | solution.py:218
  24.8 25.1 %shard_map.78 = (bf16[480,384]{1,0:T(8,128)(2,1)S(1)}, bf16[480,384]{1,0:T(8,128)(2,1)S(1)}, f32[384,1152]{1,0:T(8,128)S(1)}, f32[384,384]{1,0:T(8,128)S(1)}) custom-call(bf16[2,480,384]{2,1,0:T(8,128)(2,1)S(1)} %bitcast.39, bf16[2,480,384]{2,1,0:T(8,128)(2,1)S(1)} %bitcast.38, f32[384]{0:T(512)S(1)} %copy-done.5, bf16[384,1152]{1,0:T(8,128)(2,1)S(1)} %copy-done.3, ...), custom_call_target="tpu_custom_call" | custom-call | flops 7644119040 | bytes 8388608 | tf_op jit(solution)/shard_map/pallas_call | solution.py:171
  49.9 25.4 %shard_map.79 = (bf16[240,384]{1,0:T(8,128)(2,1)S(1)}, bf16[240,384]{1,0:T(8,128)(2,1)S(1)}, bf16[240,384]{1,0:T(8,128)(2,1)S(1)}, bf16[240,384]{1,0:T(8,128)(2,...) custom-call(bf16[2,240,384]{2,1,0:T(8,128)(2,1)S(1)} %bitcast.41, bf16[2,240,384]{2,1,0:T(8,128)(2,1)S(1)} %bitcast.42, ...), custom_call_target="tpu_custom_call" | custom-call | flops 7644119040 | bytes 8388608 | tf_op jit(solution)/shard_map/pallas_call | solution.py:171
  75.4 4.0 %collective-permute-start.6 = (bf16[15,32,384]{2,1,0:T(8,128)(2,1)S(1)}, bf16[15,32,384]{2,1,0:T(8,128)(2,1)}, u32[]{:S(2)}, u32[]{:S(2)}) collective-permute-start(bf16[15,32,384]{2,1,0:T(8,128)(2,1)S(1)} %bitcast.40), channel_id=1, source_target_pairs={{5,1},{7,3},{0,4},{9,5},{2,6},{11,7},{4,8},{13,9},{6,10},{15,11},{... | collective-permute-start | bytes 1105928 | tf_op jit(solution)/shard_map/ppermute | solution.py:218
  79.4 0.8 add_convert_fusion.1
  80.6 3.3 %collective-permute-start.7 = (bf16[15,16,384]{2,1,0:T(8,128)(2,1)S(1)}, bf16[15,16,384]{2,1,0:T(8,128)(2,1)}, u32[]{:S(2)}, u32[]{:S(2)}) collective-permute-start(bf16[15,16,384]{2,1,0:T(8,128)(2,1)S(1)} %bitcast.47), channel_id=1, source_target_pairs={{5,1},{7,3},{0,4},{9,5},{2,6},{11,7},{4,8},{13,9},{6,10},{15,11},{... | collective-permute-start | bytes 552968 | tf_op jit(solution)/shard_map/ppermute | solution.py:218
  84.0 4.1 %collective-permute-start.9 = (bf16[15,16,384]{2,1,0:T(8,128)(2,1)S(1)}, bf16[15,16,384]{2,1,0:T(8,128)(2,1)S(1)}, u32[]{:S(2)}, u32[]{:S(2)}) collective-permute-start(bf16[15,16,384]{2,1,0:T(8,128)(2,1)S(1)} %bitcast.45), channel_id=1, source_target_pairs={{5,2},{7,0},{0,5},{9,6},{2,7},{11,4},{4,9},{13,10},{6,11},{15,8},{... | collective-permute-start | bytes 552968 | tf_op jit(solution)/shard_map/ppermute | solution.py:218
  88.3 1.5 %collective-permute-start.8 = (bf16[4,96,192]{2,1,0:T(8,128)(2,1)S(1)}, bf16[4,96,192]{2,1,0:T(8,128)(2,1)S(1)}, u32[]{:S(2)}, u32[]{:S(2)}) collective-permute-start(bf16[4,96,192]{2,1,0:T(8,128)(2,1)S(1)} %dynamic-slice_convert_fusion), channel_id=1, source_target_pairs={{0,16},{16,0},{1,17},{17,1},{2,18},{18,2},{3,19},{19,3},{4,20},{20... | collective-permute-start | bytes 442376 | tf_op jit(solution)/shard_map/ppermute | solution.py:202
  89.9 1.1 broadcast_select_fusion.1
  90.9 1.0 broadcast_select_fusion.3
  92.0 2.1 %collective-permute-done.8 = bf16[4,96,192]{2,1,0:T(8,128)(2,1)S(1)} collective-permute-done((bf16[4,96,192]{2,1,0:T(8,128)(2,1)S(1)}, bf16[4,96,192]{2,1,0:T(8,128)(2,1)S(1)}, u32[]{:S(2)}, u32[]{:S(2)}) %collective-permute-start.8) | collective-permute-done | bytes 147488 | tf_op jit(solution)/shard_map/ppermute | solution.py:202
  94.3 2.4 %collective-permute-start.11 = (bf16[96,192]{1,0:T(8,128)(2,1)S(1)}, bf16[96,192]{1,0:T(8,128)(2,1)S(1)}, u32[]{:S(2)}, u32[]{:S(2)}) collective-permute-start(bf16[96,192]{1,0:T(8,128)(2,1)S(1)} %get-tuple-element.81), channel_id=1, source_target_pairs={{0,4},{4,8},{8,12},{12,0},{1,5},{5,9},{9,13},{13,1},{2,6},{6,10},{... | collective-permute-start | bytes 110600 | tf_op jit(solution)/shard_map/ppermute | solution.py:202
  96.6 3.6 %collective-permute-start.12 = (bf16[96,192]{1,0:T(8,128)(2,1)S(1)}, bf16[96,192]{1,0:T(8,128)(2,1)S(1)}, u32[]{:S(2)}, u32[]{:S(2)}) collective-permute-start(bf16[96,192]{1,0:T(8,128)(2,1)S(1)} %get-tuple-element.83), channel_id=1, source_target_pairs={{0,8},{4,12},{8,0},{12,4},{1,9},{5,13},{9,1},{13,5},{2,10},{6,14},... | collective-permute-start | bytes 110600 | tf_op jit(solution)/shard_map/ppermute | solution.py:202
  100.3 2.8 %collective-permute-start.13 = (bf16[96,192]{1,0:T(8,128)(2,1)S(1)}, bf16[96,192]{1,0:T(8,128)(2,1)S(1)}, u32[]{:S(2)}, u32[]{:S(2)}) collective-permute-start(bf16[96,192]{1,0:T(8,128)(2,1)S(1)} %get-tuple-element.82), channel_id=1, source_target_pairs={{0,12},{4,0},{8,4},{12,8},{1,13},{5,1},{9,5},{13,9},{2,14},{6,2},{... | collective-permute-start | bytes 110600 | tf_op jit(solution)/shard_map/ppermute | solution.py:202
  103.3 1.9 %add_convert_fusion = bf16[1,30,60,384]{3,2,1,0:T(8,128)(2,1)} fusion(bf16[1,30,60,384]{3,2,1,0:T(8,128)(2,1)S(1)} %copy-done.1, bf16[1,30,15,384]{3,2,1,0:T(8,128)(2,1)S(1)} %get-tuple-element.84, bf16[1,30,30,384]{3,2,1,0:T(8,128)(2,1)S(1)} %fusion, bf16[1,30,15,384]{3,2,1,0:T(8,128)(2,1)S(1)} %get-tuple-element.85), kind=kLoop, calls=%fused_computation | loop fusion | flops 6220800 | bytes 4147200 | tf_op jit(solution)/shard_map/convert_element_type | solution.py:387
  105.2 0.6 fusion.6
  105.8 0.6 fusion.7
  (34 shorter events, 1.5 us)
Async XLA Ops:
  0.6 1.4 %copy-start = (bf16[1,30,60,384]{3,2,1,0:T(8,128)(2,1)S(1)}, bf16[1,30,60,384]{3,2,1,0:T(8,128)(2,1)}, u32[]{:S(2)}) copy-start(bf16[1,30,60,384]{3,2,1,0:T(8,128)(2,1)} %cot_ref.2) | copy-start | bytes 4147204
  2.0 1.4 %copy-start.2 = (bf16[1,30,60,384]{3,2,1,0:T(8,128)(2,1)S(1)}, bf16[1,30,60,384]{3,2,1,0:T(8,128)(2,1)}, u32[]{:S(2)}) copy-start(bf16[1,30,60,384]{3,2,1,0:T(8,128)(2,1)} %hid_ref.2) | copy-start | bytes 4147204
  3.6 21.2 %copy-start.3 = (bf16[384,1152]{1,0:T(8,128)(2,1)S(1)}, bf16[384,1152]{1,0:T(8,128)(2,1)}, u32[]{:S(2)}) copy-start(bf16[384,1152]{1,0:T(8,128)(2,1)} %refs_5_.1) | copy-start | bytes 2654212
  3.6 21.2 %copy-start.4 = (bf16[384,384]{1,0:T(8,128)(2,1)S(1)}, bf16[384,384]{1,0:T(8,128)(2,1)}, u32[]{:S(2)}) copy-start(bf16[384,384]{1,0:T(8,128)(2,1)} %refs_6_.1) | copy-start | bytes 884740
  3.6 21.2 %copy-start.5 = (f32[384]{0:T(512)S(1)}, f32[384]{0:T(512)}, u32[]{:S(2)}) copy-start(f32[384]{0:T(512)} %refs_4_.3) | copy-start | bytes 4612
  3.6 14.5 %collective-permute-start.1 = (bf16[2,1,15,32,384]{4,3,2,1,0:T(8,128)(2,1)S(1)}, bf16[2,1,15,32,384]{4,3,2,1,0:T(8,128)(2,1)S(1)}, u32[]{:S(2)}, u32[]{:S(2)}) collective-permute-start(bf16[2,1,15,32,384]{4,3,2,1,0:T(8,128)(2,1)S(1)} %shard_map.76), channel_id=1, source_target_pairs={{1,5},{3,7},{4,0},{5,9},{6,2},{7,11},{8,4},{9,13},{10,6},{11,15},{... | collective-permute-start | bytes 2211848 | tf_op jit(solution)/shard_map/ppermute | solution.py:218
  5.7 44.1 %collective-permute-start = (bf16[2,1,15,16,384]{4,3,2,1,0:T(8,128)(2,1)S(1)}, bf16[2,1,15,16,384]{4,3,2,1,0:T(8,128)(2,1)S(1)}, u32[]{:S(2)}, u32[]{:S(2)}) collective-permute-start(bf16[2,1,15,16,384]{4,3,2,1,0:T(8,128)(2,1)S(1)} %get-tuple-element.41), channel_id=1, source_target_pairs={{0,3},{1,0},{2,1},{3,2},{4,7},{5,4},{6,5},{7,6},{8,11},{9,8},{10,9... | collective-permute-start | bytes 1105928 | tf_op jit(solution)/shard_map/ppermute | solution.py:223
  18.1 31.8 %collective-permute-start.2 = (bf16[2,1,15,16,384]{4,3,2,1,0:T(8,128)(2,1)S(1)}, bf16[2,1,15,16,384]{4,3,2,1,0:T(8,128)(2,1)S(1)}, u32[]{:S(2)}, u32[]{:S(2)}) collective-permute-start(bf16[2,1,15,16,384]{4,3,2,1,0:T(8,128)(2,1)S(1)} %get-tuple-element.45), channel_id=1, source_target_pairs={{1,5},{3,7},{4,0},{5,9},{6,2},{7,11},{8,4},{9,13},{10,6},{11,15},{... | collective-permute-start | bytes 1105928 | tf_op jit(solution)/shard_map/ppermute | solution.py:218
  19.4 30.5 %collective-permute-start.3 = (bf16[2,1,15,16,384]{4,3,2,1,0:T(8,128)(2,1)S(1)}, bf16[2,1,15,16,384]{4,3,2,1,0:T(8,128)(2,1)S(1)}, u32[]{:S(2)}, u32[]{:S(2)}) collective-permute-start(bf16[2,1,15,16,384]{4,3,2,1,0:T(8,128)(2,1)S(1)} %get-tuple-element.46), channel_id=1, source_target_pairs={{2,5},{0,7},{5,0},{6,9},{7,2},{4,11},{9,4},{10,13},{11,6},{8,15},{... | collective-permute-start | bytes 1105928 | tf_op jit(solution)/shard_map/ppermute | solution.py:218
  75.3 4.0 %collective-permute-start.4 = (bf16[8,96,384]{2,1,0:T(8,128)(2,1)S(1)}, bf16[8,96,384]{2,1,0:T(8,128)(2,1)S(1)}, u32[]{:S(2)}, u32[]{:S(2)}) collective-permute-start(bf16[8,96,384]{2,1,0:T(8,128)(2,1)S(1)} %get-tuple-element.56), channel_id=1, source_target_pairs={{0,1},{1,0},{2,3},{3,2},{4,5},{5,4},{6,7},{7,6},{8,9},{9,8},{10,11... | collective-permute-start | bytes 1769480 | tf_op jit(solution)/shard_map/ppermute | solution.py:202
  75.4 12.6 %collective-permute-start.6 = (bf16[15,32,384]{2,1,0:T(8,128)(2,1)S(1)}, bf16[15,32,384]{2,1,0:T(8,128)(2,1)}, u32[]{:S(2)}, u32[]{:S(2)}) collective-permute-start(bf16[15,32,384]{2,1,0:T(8,128)(2,1)S(1)} %bitcast.40), channel_id=1, source_target_pairs={{5,1},{7,3},{0,4},{9,5},{2,6},{11,7},{4,8},{13,9},{6,10},{15,11},{... | collective-permute-start | bytes 1105928 | tf_op jit(solution)/shard_map/ppermute | solution.py:218
  80.2 7.9 %collective-permute-start.5 = (bf16[4,96,384]{2,1,0:T(8,128)(2,1)}, bf16[4,96,384]{2,1,0:T(8,128)(2,1)S(1)}, u32[]{:S(2)}, u32[]{:S(2)}) collective-permute-start(bf16[4,96,384]{2,1,0:T(8,128)(2,1)} %add_convert_fusion.1), channel_id=1, source_target_pairs={{0,2},{1,3},{2,0},{3,1},{4,6},{5,7},{6,4},{7,5},{8,10},{9,11},{10,... | collective-permute-start | bytes 884744 | tf_op jit(solution)/shard_map/ppermute | solution.py:202
  80.6 7.4 %collective-permute-start.7 = (bf16[15,16,384]{2,1,0:T(8,128)(2,1)S(1)}, bf16[15,16,384]{2,1,0:T(8,128)(2,1)}, u32[]{:S(2)}, u32[]{:S(2)}) collective-permute-start(bf16[15,16,384]{2,1,0:T(8,128)(2,1)S(1)} %bitcast.47), channel_id=1, source_target_pairs={{5,1},{7,3},{0,4},{9,5},{2,6},{11,7},{4,8},{13,9},{6,10},{15,11},{... | collective-permute-start | bytes 552968 | tf_op jit(solution)/shard_map/ppermute | solution.py:218
  84.0 8.0 %collective-permute-start.10 = (bf16[15,16,384]{2,1,0:T(8,128)(2,1)S(1)}, bf16[15,16,384]{2,1,0:T(8,128)(2,1)S(1)}, u32[]{:S(2)}, u32[]{:S(2)}) collective-permute-start(bf16[15,16,384]{2,1,0:T(8,128)(2,1)S(1)} %bitcast.46), channel_id=1, source_target_pairs={{0,1},{1,2},{2,3},{3,0},{4,5},{5,6},{6,7},{7,4},{8,9},{9,10},{10,1... | collective-permute-start | bytes 552968 | tf_op jit(solution)/shard_map/ppermute | solution.py:223
  84.0 8.0 %collective-permute-start.9 = (bf16[15,16,384]{2,1,0:T(8,128)(2,1)S(1)}, bf16[15,16,384]{2,1,0:T(8,128)(2,1)S(1)}, u32[]{:S(2)}, u32[]{:S(2)}) collective-permute-start(bf16[15,16,384]{2,1,0:T(8,128)(2,1)S(1)} %bitcast.45), channel_id=1, source_target_pairs={{5,2},{7,0},{0,5},{9,6},{2,7},{11,4},{4,9},{13,10},{6,11},{15,8},{... | collective-permute-start | bytes 552968 | tf_op jit(solution)/shard_map/ppermute | solution.py:218
  88.3 5.7 %collective-permute-start.8 = (bf16[4,96,192]{2,1,0:T(8,128)(2,1)S(1)}, bf16[4,96,192]{2,1,0:T(8,128)(2,1)S(1)}, u32[]{:S(2)}, u32[]{:S(2)}) collective-permute-start(bf16[4,96,192]{2,1,0:T(8,128)(2,1)S(1)} %dynamic-slice_convert_fusion), channel_id=1, source_target_pairs={{0,16},{16,0},{1,17},{17,1},{2,18},{18,2},{3,19},{19,3},{4,20},{20... | collective-permute-start | bytes 442376 | tf_op jit(solution)/shard_map/ppermute | solution.py:202
  94.2 9.0 %copy-start.1 = (bf16[1,30,60,384]{3,2,1,0:T(8,128)(2,1)S(1)}, bf16[1,30,60,384]{3,2,1,0:T(8,128)(2,1)}, u32[]{:S(2)}) copy-start(bf16[1,30,60,384]{3,2,1,0:T(8,128)(2,1)} %cot_ref.2) | copy-start | bytes 4147204
  94.3 10.9 %collective-permute-start.11 = (bf16[96,192]{1,0:T(8,128)(2,1)S(1)}, bf16[96,192]{1,0:T(8,128)(2,1)S(1)}, u32[]{:S(2)}, u32[]{:S(2)}) collective-permute-start(bf16[96,192]{1,0:T(8,128)(2,1)S(1)} %get-tuple-element.81), channel_id=1, source_target_pairs={{0,4},{4,8},{8,12},{12,0},{1,5},{5,9},{9,13},{13,1},{2,6},{6,10},{... | collective-permute-start | bytes 110600 | tf_op jit(solution)/shard_map/ppermute | solution.py:202
  96.6 8.5 %collective-permute-start.12 = (bf16[96,192]{1,0:T(8,128)(2,1)S(1)}, bf16[96,192]{1,0:T(8,128)(2,1)S(1)}, u32[]{:S(2)}, u32[]{:S(2)}) collective-permute-start(bf16[96,192]{1,0:T(8,128)(2,1)S(1)} %get-tuple-element.83), channel_id=1, source_target_pairs={{0,8},{4,12},{8,0},{12,4},{1,9},{5,13},{9,1},{13,5},{2,10},{6,14},... | collective-permute-start | bytes 110600 | tf_op jit(solution)/shard_map/ppermute | solution.py:202
  100.3 4.9 %collective-permute-start.13 = (bf16[96,192]{1,0:T(8,128)(2,1)S(1)}, bf16[96,192]{1,0:T(8,128)(2,1)S(1)}, u32[]{:S(2)}, u32[]{:S(2)}) collective-permute-start(bf16[96,192]{1,0:T(8,128)(2,1)S(1)} %get-tuple-element.82), channel_id=1, source_target_pairs={{0,12},{4,0},{8,4},{12,8},{1,13},{5,1},{9,5},{13,9},{2,14},{6,2},{... | collective-permute-start | bytes 110600 | tf_op jit(solution)/shard_map/ppermute | solution.py:202

commit v13 on v10

--- a/solution.py
+++ b/solution.py
@@ -179,7 +179,7 @@
             bytes_accessed=8 * 2**20,
             transcendentals=HEADS * cells * cells,
         ),
-        compiler_params=pltpu.CompilerParams(vmem_limit_bytes=32 * 2**20),
+        compiler_params=pltpu.CompilerParams(vmem_limit_bytes=26 * 2**20),
     )(*args)
     return outs[:len(sizes)], outs[-2:]
 

time: 102 us -> 102 us (level)
  no operation moved by 1% of the time
where the time goes in v13:
time: 102 us; the launch traced here: 101 us
  Pallas kernels  51.3 us (50%)
  starting transfers between devices  33.3 us (33%)
  waiting for transfers between devices  6.44 us (6%)
  other arithmetic  6.41 us (6%)
  local copies, waits for them, and re-layouts  2.91 us (3%)
    pallas_call x2, Pallas kernels, window_call(): pl.pallas_call(functools.partial(window_kernel, head, metas, (prev is not...  50.5 us
    ppermute x6, starting transfers between devices, shared(): return lax.ppermute(value, ('lat', 'lon'), pairs)  17.1 us
    ppermute x6, starting transfers between devices, permuted(): return lax.ppermute(value, tuple(axes), pairs)  11.8 us
    ppermute x6, waiting for transfers between devices, shared(): return lax.ppermute(value, ('lat', 'lon'), pairs)  5.29 us
    ppermute x2, starting transfers between devices, along_lon(): lax.ppermute(value, 'lon', [(j, (j + step) % count) for j in range(count)])  4.42 us
    unnamed x12, local copies, waits for them, and re-layouts  2.77 us
    select_n x3, other arithmetic, stacked(): above = jnp.where(upper, own, back)  2.07 us
  transfers between devices with their start and end apart: 14, of which 5 were waited for; matrix products, arithmetic and copies ran while one was open for 5% of the time, Pallas kernels for 25%

profile of v13, /device:TPU:0, one launch (start us, length us, event | category | flops | bytes accessed | tf_op | source)
XLA Modules:
  0.0 101.3 jit_solution(6833503280851400290)
XLA Ops:
  0.6 1.4 %copy-done = bf16[1,30,60,384]{3,2,1,0:T(8,128)(2,1)S(1)} copy-done((bf16[1,30,60,384]{3,2,1,0:T(8,128)(2,1)S(1)}, bf16[1,30,60,384]{3,2,1,0:T(8,128)(2,1)}, u32[]{:S(2)}) %copy-start) | copy-done | bytes 1382424
  2.0 1.4 %copy-done.2 = bf16[1,30,60,384]{3,2,1,0:T(8,128)(2,1)S(1)} copy-done((bf16[1,30,60,384]{3,2,1,0:T(8,128)(2,1)S(1)}, bf16[1,30,60,384]{3,2,1,0:T(8,128)(2,1)}, u32[]{:S(2)}) %copy-start.2) | copy-done | bytes 1382424
  3.6 1.4 %collective-permute-start.3 = (bf16[2,1,15,32,384]{4,3,2,1,0:T(8,128)(2,1)S(1)}, bf16[2,1,15,32,384]{4,3,2,1,0:T(8,128)(2,1)S(1)}, u32[]{:S(2)}, u32[]{:S(2)}) collective-permute-start(bf16[2,1,15,32,384]{4,3,2,1,0:T(8,128)(2,1)S(1)} %shard_map.76), channel_id=1, source_target_pairs={{1,5},{3,7},{4,0},{5,9},{6,2},{7,11},{8,4},{9,13},{10,6},{11,15},{... | collective-permute-start | bytes 2211848 | tf_op jit(solution)/shard_map/ppermute | solution.py:218
  5.1 0.7 shard_map.77
  5.7 4.4 %collective-permute-start = (bf16[2,1,15,16,384]{4,3,2,1,0:T(8,128)(2,1)S(1)}, bf16[2,1,15,16,384]{4,3,2,1,0:T(8,128)(2,1)S(1)}, u32[]{:S(2)}, u32[]{:S(2)}) collective-permute-start(bf16[2,1,15,16,384]{4,3,2,1,0:T(8,128)(2,1)S(1)} %get-tuple-element.38), channel_id=1, source_target_pairs={{0,3},{1,0},{2,1},{3,2},{4,7},{5,4},{6,5},{7,6},{8,11},{9,8},{10,9... | collective-permute-start | bytes 1105928 | tf_op jit(solution)/shard_map/ppermute | solution.py:223
  10.2 1.3 %collective-permute-start.1 = (bf16[2,1,15,16,384]{4,3,2,1,0:T(8,128)(2,1)S(1)}, bf16[2,1,15,16,384]{4,3,2,1,0:T(8,128)(2,1)S(1)}, u32[]{:S(2)}, u32[]{:S(2)}) collective-permute-start(bf16[2,1,15,16,384]{4,3,2,1,0:T(8,128)(2,1)S(1)} %get-tuple-element.39), channel_id=1, source_target_pairs={{1,5},{3,7},{4,0},{5,9},{6,2},{7,11},{8,4},{9,13},{10,6},{11,15},{... | collective-permute-start | bytes 1105928 | tf_op jit(solution)/shard_map/ppermute | solution.py:218
  11.4 4.8 %collective-permute-start.2 = (bf16[2,1,15,16,384]{4,3,2,1,0:T(8,128)(2,1)S(1)}, bf16[2,1,15,16,384]{4,3,2,1,0:T(8,128)(2,1)S(1)}, u32[]{:S(2)}, u32[]{:S(2)}) collective-permute-start(bf16[2,1,15,16,384]{4,3,2,1,0:T(8,128)(2,1)S(1)} %get-tuple-element.40), channel_id=1, source_target_pairs={{2,5},{0,7},{5,0},{6,9},{7,2},{4,11},{9,4},{10,13},{11,6},{8,15},{... | collective-permute-start | bytes 1105928 | tf_op jit(solution)/shard_map/ppermute | solution.py:218
  16.3 3.4 %collective-permute-done.3 = bf16[2,1,15,32,384]{4,3,2,1,0:T(8,128)(2,1)S(1)} collective-permute-done((bf16[2,1,15,32,384]{4,3,2,1,0:T(8,128)(2,1)S(1)}, bf16[2,1,15,32,384]{4,3,2,1,0:T(8,128)(2,1)S(1)}, u32[]{:S(2)}, u32[]{:S(2)}) %collective-permute-start.3) | collective-permute-done | bytes 737312 | tf_op jit(solution)/shard_map/ppermute | solution.py:218
  19.7 25.0 %shard_map.78 = (bf16[480,384]{1,0:T(8,128)(2,1)S(1)}, bf16[480,384]{1,0:T(8,128)(2,1)S(1)}, f32[384,1152]{1,0:T(8,128)S(1)}, f32[384,384]{1,0:T(8,128)S(1)}) custom-call(bf16[2,480,384]{2,1,0:T(8,128)(2,1)S(1)} %bitcast.39, bf16[2,480,384]{2,1,0:T(8,128)(2,1)S(1)} %bitcast.38, f32[384]{0:T(512)S(1)} %copy-done.5, bf16[384,1152]{1,0:T(8,128)(2,1)S(1)} %copy-done.3, ...), custom_call_target="tpu_custom_call" | custom-call | flops 7644119040 | bytes 8388608 | tf_op jit(solution)/shard_map/pallas_call | solution.py:171
  44.7 25.4 %shard_map.79 = (bf16[240,384]{1,0:T(8,128)(2,1)S(1)}, bf16[240,384]{1,0:T(8,128)(2,1)S(1)}, bf16[240,384]{1,0:T(8,128)(2,1)S(1)}, bf16[240,384]{1,0:T(8,128)(2,...) custom-call(bf16[2,240,384]{2,1,0:T(8,128)(2,1)S(1)} %bitcast.41, bf16[2,240,384]{2,1,0:T(8,128)(2,1)S(1)} %bitcast.42, ...), custom_call_target="tpu_custom_call" | custom-call | flops 7644119040 | bytes 8388608 | tf_op jit(solution)/shard_map/pallas_call | solution.py:171
  70.2 4.3 %collective-permute-start.6 = (bf16[15,32,384]{2,1,0:T(8,128)(2,1)S(1)}, bf16[15,32,384]{2,1,0:T(8,128)(2,1)}, u32[]{:S(2)}, u32[]{:S(2)}) collective-permute-start(bf16[15,32,384]{2,1,0:T(8,128)(2,1)S(1)} %bitcast.40), channel_id=1, source_target_pairs={{5,1},{7,3},{0,4},{9,5},{2,6},{11,7},{4,8},{13,9},{6,10},{15,11},{... | collective-permute-start | bytes 1105928 | tf_op jit(solution)/shard_map/ppermute | solution.py:218
  74.5 0.8 add_convert_fusion.1
  75.3 2.5 %collective-permute-start.5 = (bf16[4,96,384]{2,1,0:T(8,128)(2,1)}, bf16[4,96,384]{2,1,0:T(8,128)(2,1)S(1)}, u32[]{:S(2)}, u32[]{:S(2)}) collective-permute-start(bf16[4,96,384]{2,1,0:T(8,128)(2,1)} %add_convert_fusion.1), channel_id=1, source_target_pairs={{0,2},{1,3},{2,0},{3,1},{4,6},{5,7},{6,4},{7,5},{8,10},{9,11},{10,... | collective-permute-start | bytes 884744 | tf_op jit(solution)/shard_map/ppermute | solution.py:202
  77.8 3.5 %collective-permute-start.7 = (bf16[15,16,384]{2,1,0:T(8,128)(2,1)S(1)}, bf16[15,16,384]{2,1,0:T(8,128)(2,1)}, u32[]{:S(2)}, u32[]{:S(2)}) collective-permute-start(bf16[15,16,384]{2,1,0:T(8,128)(2,1)S(1)} %bitcast.47), channel_id=1, source_target_pairs={{5,1},{7,3},{0,4},{9,5},{2,6},{11,7},{4,8},{13,9},{6,10},{15,11},{... | collective-permute-start | bytes 552968 | tf_op jit(solution)/shard_map/ppermute | solution.py:218
  81.3 1.9 %collective-permute-start.9 = (bf16[15,16,384]{2,1,0:T(8,128)(2,1)S(1)}, bf16[15,16,384]{2,1,0:T(8,128)(2,1)S(1)}, u32[]{:S(2)}, u32[]{:S(2)}) collective-permute-start(bf16[15,16,384]{2,1,0:T(8,128)(2,1)S(1)} %bitcast.45), channel_id=1, source_target_pairs={{5,2},{7,0},{0,5},{9,6},{2,7},{11,4},{4,9},{13,10},{6,11},{15,8},{... | collective-permute-start | bytes 552968 | tf_op jit(solution)/shard_map/ppermute | solution.py:218
  83.9 1.6 %collective-permute-start.8 = (bf16[4,96,192]{2,1,0:T(8,128)(2,1)S(1)}, bf16[4,96,192]{2,1,0:T(8,128)(2,1)S(1)}, u32[]{:S(2)}, u32[]{:S(2)}) collective-permute-start(bf16[4,96,192]{2,1,0:T(8,128)(2,1)S(1)} %dynamic-slice_convert_fusion), channel_id=1, source_target_pairs={{0,16},{16,0},{1,17},{17,1},{2,18},{18,2},{3,19},{19,3},{4,20},{20... | collective-permute-start | bytes 442376 | tf_op jit(solution)/shard_map/ppermute | solution.py:202
  85.4 1.1 %broadcast_select_fusion.1 = (bf16[15,32,384]{2,1,0:T(8,128)(2,1)S(1)}, bf16[15,32,384]{2,1,0:T(8,128)(2,1)S(1)}) fusion(bf16[15,32,384]{2,1,0:T(8,128)(2,1)S(1)} %bitcast.36, bf16[15,32,384]{2,1,0:T(8,128)(2,1)} %collective-permute-done.6, pred[]{:T(512)S(6)} %eq.11), kind=kLoop, calls=%fused_computation.12 | loop fusion | flops 368640 | bytes 1474561 | tf_op jit(solution)/shard_map/jit(_where)/select_n | solution.py:367
  86.5 1.0 broadcast_select_fusion.3
  87.5 1.5 %collective-permute-done.9 = bf16[15,16,384]{2,1,0:T(8,128)(2,1)S(1)} collective-permute-done((bf16[15,16,384]{2,1,0:T(8,128)(2,1)S(1)}, bf16[15,16,384]{2,1,0:T(8,128)(2,1)S(1)}, u32[]{:S(2)}, u32[]{:S(2)}) %collective-permute-start.9) | collective-permute-done | bytes 184352 | tf_op jit(solution)/shard_map/ppermute | solution.py:218
  89.8 4.7 %collective-permute-start.11 = (bf16[96,192]{1,0:T(8,128)(2,1)S(1)}, bf16[96,192]{1,0:T(8,128)(2,1)S(1)}, u32[]{:S(2)}, u32[]{:S(2)}) collective-permute-start(bf16[96,192]{1,0:T(8,128)(2,1)S(1)} %get-tuple-element.75), channel_id=1, source_target_pairs={{0,4},{4,8},{8,12},{12,0},{1,5},{5,9},{9,13},{13,1},{2,6},{6,10},{... | collective-permute-start | bytes 110600 | tf_op jit(solution)/shard_map/ppermute | solution.py:202
  94.5 2.8 %collective-permute-start.13 = (bf16[96,192]{1,0:T(8,128)(2,1)S(1)}, bf16[96,192]{1,0:T(8,128)(2,1)S(1)}, u32[]{:S(2)}, u32[]{:S(2)}) collective-permute-start(bf16[96,192]{1,0:T(8,128)(2,1)S(1)} %get-tuple-element.76), channel_id=1, source_target_pairs={{0,12},{4,0},{8,4},{12,8},{1,13},{5,1},{9,5},{13,9},{2,14},{6,2},{... | collective-permute-start | bytes 110600 | tf_op jit(solution)/shard_map/ppermute | solution.py:202
  97.5 1.9 %add_convert_fusion = bf16[1,30,60,384]{3,2,1,0:T(8,128)(2,1)} fusion(bf16[1,30,60,384]{3,2,1,0:T(8,128)(2,1)S(1)} %copy-done.1, bf16[1,30,15,384]{3,2,1,0:T(8,128)(2,1)S(1)} %get-tuple-element.78, bf16[1,30,30,384]{3,2,1,0:T(8,128)(2,1)S(1)} %fusion, bf16[1,30,15,384]{3,2,1,0:T(8,128)(2,1)S(1)} %get-tuple-element.79), kind=kLoop, calls=%fused_computation | loop fusion | flops 6220800 | bytes 4147200 | tf_op jit(solution)/shard_map/convert_element_type | solution.py:384
  100.0 0.6 fusion.6
  100.7 0.6 fusion.7
  (34 shorter events, 2.6 us)
Async XLA Ops:
  0.6 1.4 %copy-start = (bf16[1,30,60,384]{3,2,1,0:T(8,128)(2,1)S(1)}, bf16[1,30,60,384]{3,2,1,0:T(8,128)(2,1)}, u32[]{:S(2)}) copy-start(bf16[1,30,60,384]{3,2,1,0:T(8,128)(2,1)} %cot_ref.2) | copy-start | bytes 4147204
  2.0 1.4 %copy-start.2 = (bf16[1,30,60,384]{3,2,1,0:T(8,128)(2,1)S(1)}, bf16[1,30,60,384]{3,2,1,0:T(8,128)(2,1)}, u32[]{:S(2)}) copy-start(bf16[1,30,60,384]{3,2,1,0:T(8,128)(2,1)} %hid_ref.2) | copy-start | bytes 4147204
  3.6 16.0 %copy-start.3 = (bf16[384,1152]{1,0:T(8,128)(2,1)S(1)}, bf16[384,1152]{1,0:T(8,128)(2,1)}, u32[]{:S(2)}) copy-start(bf16[384,1152]{1,0:T(8,128)(2,1)} %refs_5_.1) | copy-start | bytes 2654212
  3.6 16.0 %copy-start.4 = (bf16[384,384]{1,0:T(8,128)(2,1)S(1)}, bf16[384,384]{1,0:T(8,128)(2,1)}, u32[]{:S(2)}) copy-start(bf16[384,384]{1,0:T(8,128)(2,1)} %refs_6_.1) | copy-start | bytes 884740
  3.6 16.0 %copy-start.5 = (f32[384]{0:T(512)S(1)}, f32[384]{0:T(512)}, u32[]{:S(2)}) copy-start(f32[384]{0:T(512)} %refs_4_.3) | copy-start | bytes 4612
  3.6 16.0 %collective-permute-start.3 = (bf16[2,1,15,32,384]{4,3,2,1,0:T(8,128)(2,1)S(1)}, bf16[2,1,15,32,384]{4,3,2,1,0:T(8,128)(2,1)S(1)}, u32[]{:S(2)}, u32[]{:S(2)}) collective-permute-start(bf16[2,1,15,32,384]{4,3,2,1,0:T(8,128)(2,1)S(1)} %shard_map.76), channel_id=1, source_target_pairs={{1,5},{3,7},{4,0},{5,9},{6,2},{7,11},{8,4},{9,13},{10,6},{11,15},{... | collective-permute-start | bytes 2211848 | tf_op jit(solution)/shard_map/ppermute | solution.py:218
  5.7 39.0 %collective-permute-start = (bf16[2,1,15,16,384]{4,3,2,1,0:T(8,128)(2,1)S(1)}, bf16[2,1,15,16,384]{4,3,2,1,0:T(8,128)(2,1)S(1)}, u32[]{:S(2)}, u32[]{:S(2)}) collective-permute-start(bf16[2,1,15,16,384]{4,3,2,1,0:T(8,128)(2,1)S(1)} %get-tuple-element.38), channel_id=1, source_target_pairs={{0,3},{1,0},{2,1},{3,2},{4,7},{5,4},{6,5},{7,6},{8,11},{9,8},{10,9... | collective-permute-start | bytes 1105928 | tf_op jit(solution)/shard_map/ppermute | solution.py:223
  10.2 34.6 %collective-permute-start.1 = (bf16[2,1,15,16,384]{4,3,2,1,0:T(8,128)(2,1)S(1)}, bf16[2,1,15,16,384]{4,3,2,1,0:T(8,128)(2,1)S(1)}, u32[]{:S(2)}, u32[]{:S(2)}) collective-permute-start(bf16[2,1,15,16,384]{4,3,2,1,0:T(8,128)(2,1)S(1)} %get-tuple-element.39), channel_id=1, source_target_pairs={{1,5},{3,7},{4,0},{5,9},{6,2},{7,11},{8,4},{9,13},{10,6},{11,15},{... | collective-permute-start | bytes 1105928 | tf_op jit(solution)/shard_map/ppermute | solution.py:218
  11.4 33.3 %collective-permute-start.2 = (bf16[2,1,15,16,384]{4,3,2,1,0:T(8,128)(2,1)S(1)}, bf16[2,1,15,16,384]{4,3,2,1,0:T(8,128)(2,1)S(1)}, u32[]{:S(2)}, u32[]{:S(2)}) collective-permute-start(bf16[2,1,15,16,384]{4,3,2,1,0:T(8,128)(2,1)S(1)} %get-tuple-element.40), channel_id=1, source_target_pairs={{2,5},{0,7},{5,0},{6,9},{7,2},{4,11},{9,4},{10,13},{11,6},{8,15},{... | collective-permute-start | bytes 1105928 | tf_op jit(solution)/shard_map/ppermute | solution.py:218
  70.1 4.3 %collective-permute-start.4 = (bf16[8,96,384]{2,1,0:T(8,128)(2,1)S(1)}, bf16[8,96,384]{2,1,0:T(8,128)(2,1)S(1)}, u32[]{:S(2)}, u32[]{:S(2)}) collective-permute-start(bf16[8,96,384]{2,1,0:T(8,128)(2,1)S(1)} %get-tuple-element.50), channel_id=1, source_target_pairs={{0,1},{1,0},{2,3},{3,2},{4,5},{5,4},{6,7},{7,6},{8,9},{9,8},{10,11... | collective-permute-start | bytes 1769480 | tf_op jit(solution)/shard_map/ppermute | solution.py:202
  70.2 13.4 %collective-permute-start.6 = (bf16[15,32,384]{2,1,0:T(8,128)(2,1)S(1)}, bf16[15,32,384]{2,1,0:T(8,128)(2,1)}, u32[]{:S(2)}, u32[]{:S(2)}) collective-permute-start(bf16[15,32,384]{2,1,0:T(8,128)(2,1)S(1)} %bitcast.40), channel_id=1, source_target_pairs={{5,1},{7,3},{0,4},{9,5},{2,6},{11,7},{4,8},{13,9},{6,10},{15,11},{... | collective-permute-start | bytes 1105928 | tf_op jit(solution)/shard_map/ppermute | solution.py:218
  75.3 8.4 %collective-permute-start.5 = (bf16[4,96,384]{2,1,0:T(8,128)(2,1)}, bf16[4,96,384]{2,1,0:T(8,128)(2,1)S(1)}, u32[]{:S(2)}, u32[]{:S(2)}) collective-permute-start(bf16[4,96,384]{2,1,0:T(8,128)(2,1)} %add_convert_fusion.1), channel_id=1, source_target_pairs={{0,2},{1,3},{2,0},{3,1},{4,6},{5,7},{6,4},{7,5},{8,10},{9,11},{10,... | collective-permute-start | bytes 884744 | tf_op jit(solution)/shard_map/ppermute | solution.py:202
  77.8 5.8 %collective-permute-start.7 = (bf16[15,16,384]{2,1,0:T(8,128)(2,1)S(1)}, bf16[15,16,384]{2,1,0:T(8,128)(2,1)}, u32[]{:S(2)}, u32[]{:S(2)}) collective-permute-start(bf16[15,16,384]{2,1,0:T(8,128)(2,1)S(1)} %bitcast.47), channel_id=1, source_target_pairs={{5,1},{7,3},{0,4},{9,5},{2,6},{11,7},{4,8},{13,9},{6,10},{15,11},{... | collective-permute-start | bytes 552968 | tf_op jit(solution)/shard_map/ppermute | solution.py:218
  81.3 6.3 %collective-permute-start.10 = (bf16[15,16,384]{2,1,0:T(8,128)(2,1)S(1)}, bf16[15,16,384]{2,1,0:T(8,128)(2,1)S(1)}, u32[]{:S(2)}, u32[]{:S(2)}) collective-permute-start(bf16[15,16,384]{2,1,0:T(8,128)(2,1)S(1)} %bitcast.46), channel_id=1, source_target_pairs={{0,1},{1,2},{2,3},{3,0},{4,5},{5,6},{6,7},{7,4},{8,9},{9,10},{10,1... | collective-permute-start | bytes 552968 | tf_op jit(solution)/shard_map/ppermute | solution.py:223
  81.3 7.7 %collective-permute-start.9 = (bf16[15,16,384]{2,1,0:T(8,128)(2,1)S(1)}, bf16[15,16,384]{2,1,0:T(8,128)(2,1)S(1)}, u32[]{:S(2)}, u32[]{:S(2)}) collective-permute-start(bf16[15,16,384]{2,1,0:T(8,128)(2,1)S(1)} %bitcast.45), channel_id=1, source_target_pairs={{5,2},{7,0},{0,5},{9,6},{2,7},{11,4},{4,9},{13,10},{6,11},{15,8},{... | collective-permute-start | bytes 552968 | tf_op jit(solution)/shard_map/ppermute | solution.py:218
  83.9 5.7 %collective-permute-start.8 = (bf16[4,96,192]{2,1,0:T(8,128)(2,1)S(1)}, bf16[4,96,192]{2,1,0:T(8,128)(2,1)S(1)}, u32[]{:S(2)}, u32[]{:S(2)}) collective-permute-start(bf16[4,96,192]{2,1,0:T(8,128)(2,1)S(1)} %dynamic-slice_convert_fusion), channel_id=1, source_target_pairs={{0,16},{16,0},{1,17},{17,1},{2,18},{18,2},{3,19},{19,3},{4,20},{20... | collective-permute-start | bytes 442376 | tf_op jit(solution)/shard_map/ppermute | solution.py:202
  89.8 7.7 %copy-start.1 = (bf16[1,30,60,384]{3,2,1,0:T(8,128)(2,1)S(1)}, bf16[1,30,60,384]{3,2,1,0:T(8,128)(2,1)}, u32[]{:S(2)}) copy-start(bf16[1,30,60,384]{3,2,1,0:T(8,128)(2,1)} %cot_ref.2) | copy-start | bytes 4147204
  89.8 9.6 %collective-permute-start.11 = (bf16[96,192]{1,0:T(8,128)(2,1)S(1)}, bf16[96,192]{1,0:T(8,128)(2,1)S(1)}, u32[]{:S(2)}, u32[]{:S(2)}) collective-permute-start(bf16[96,192]{1,0:T(8,128)(2,1)S(1)} %get-tuple-element.75), channel_id=1, source_target_pairs={{0,4},{4,8},{8,12},{12,0},{1,5},{5,9},{9,13},{13,1},{2,6},{6,10},{... | collective-permute-start | bytes 110600 | tf_op jit(solution)/shard_map/ppermute | solution.py:202
  94.5 5.5 %collective-permute-start.12 = (bf16[96,192]{1,0:T(8,128)(2,1)S(1)}, bf16[96,192]{1,0:T(8,128)(2,1)S(1)}, u32[]{:S(2)}, u32[]{:S(2)}) collective-permute-start(bf16[96,192]{1,0:T(8,128)(2,1)S(1)} %get-tuple-element.77), channel_id=1, source_target_pairs={{0,8},{4,12},{8,0},{12,4},{1,9},{5,13},{9,1},{13,5},{2,10},{6,14},... | collective-permute-start | bytes 110600 | tf_op jit(solution)/shard_map/ppermute | solution.py:202
  94.5 5.4 %collective-permute-start.13 = (bf16[96,192]{1,0:T(8,128)(2,1)S(1)}, bf16[96,192]{1,0:T(8,128)(2,1)S(1)}, u32[]{:S(2)}, u32[]{:S(2)}) collective-permute-start(bf16[96,192]{1,0:T(8,128)(2,1)S(1)} %get-tuple-element.76), channel_id=1, source_target_pairs={{0,12},{4,0},{8,4},{12,8},{1,13},{5,1},{9,5},{13,9},{2,14},{6,2},{... | collective-permute-start | bytes 110600 | tf_op jit(solution)/shard_map/ppermute | solution.py:202
